TPU v7x, 32 devices: a whole 2x2x4 slice. The times are simulated.
32 devices in a mesh: seq: 8 (over z, y), ctx: 4 (over x, core).
Axes of the slice: x: 2, y: 2, z: 4, core: 2. Of those that a mesh axis runs over, the one named last changes fastest.
Arguments:
- tokens: bfloat16 [2, 8, 2048, 1088], P(None, 'seq', 'ctx'), may hold values from -6 to 6
- segments: int32 [2, 8, 2048], P(None, 'seq', 'ctx'), may hold values from 0 to 7, as said below
- adapter_index: int32 [2, 8], P(None, 'seq'), may hold values from 0 to 7, as said below
- norm_gains: float32 [2, 1088], replicated, may hold values from 0.25 to 1.75
- norm_shifts: float32 [2, 1088], replicated, may hold values from -4 to 4
- head_biases: float32 [2, 1088], replicated, may hold values from -4 to 4
- expand_bias: float32 [4352], replicated, may hold values from -6 to 6
- exit_biases: float32 [2, 1088], replicated, may hold values from -4 to 4
- mixing_weight: bfloat16 [1088, 3264], P('ctx', 'seq'), may hold values from -0.1875 to 0.1875
- output_weight: bfloat16 [1088, 1088], P('ctx', 'seq'), may hold values from -0.75 to 0.75
- expand_weight: bfloat16 [1088, 4352], P('ctx', 'seq'), may hold values from -0.1875 to 0.1875
- shrink_weight: bfloat16 [4352, 1088], P('ctx', 'seq'), may hold values from -0.09375 to 0.09375
- entry_adapters: bfloat16 [3, 8, 1088, 16], replicated, may hold values from -0.1875 to 0.1875
- mixing_adapters: bfloat16 [8, 16, 3264], replicated, may hold values from -0.75 to 0.75
- expand_adapters: bfloat16 [8, 16, 4352], replicated, may hold values from -0.75 to 0.75
- hidden_adapters: bfloat16 [8, 4352, 16], replicated, may hold values from -0.09375 to 0.09375
- exit_adapters: bfloat16 [2, 8, 16, 1088], replicated, may hold values from -1 to 1
- cotangent: bfloat16 [2, 8, 2048, 1088], P(None, 'seq', 'ctx'), may hold values from -6 to 6
Outputs:
- layer_output: bfloat16 [2, 8, 2048, 1088], P(None, 'seq', 'ctx')
- input_grad: bfloat16 [2, 8, 2048, 1088], P(None, 'seq', 'ctx')
- entry_grads: float32 [3, 8, 1088, 16], replicated
- mixing_grads: float32 [8, 16, 3264], replicated
- expand_grads: float32 [8, 16, 4352], replicated
- hidden_grads: float32 [8, 4352, 16], replicated
- exit_grads: float32 [2, 8, 16, 1088], replicated
Inputs may be any that keep to these rules, and one draw needn't show every extreme that they name: `segments`: within each sequence the numbers start at 0 and rise by one at the first token of each document. A sequence holds either a single document or exactly 8 documents. Of the 2 sequences at one index of seq, over all micro-batches together, exactly one is a single document. `adapter_index`: every one of the 8 adapters is used by at least one sequence.
All inputs are finite; a program needn't handle non-finite values.
Results may differ from a plain program's by a relative error of at most 0.015.
Values may be sent and summed in bfloat16 or wider, within the bound.
No kernel may reach another device: no remote copies, remote signals or barrier semaphores. Data moves between devices by JAX's collectives and lax.ppermute only.
A program may use at most 256 MiB of HBM per device.

v0:
```python
import jax
import jax.numpy as jnp
from jax import lax
from jax.sharding import PartitionSpec as P

HEADS = 17


EPS = 1e-05
NEGATIVE = -1e30
HIGH = lax.Precision.HIGHEST


def layer_norm(activations, scale_row, shift_row):
    middle = jnp.mean(activations, axis=-1, keepdims=True)
    centred = activations - middle
    spread = jnp.mean(centred * centred, axis=-1, keepdims=True)
    return centred * lax.rsqrt(spread + EPS) * scale_row + shift_row


def matmul(pattern, first_op, second_op):
    return jnp.einsum(pattern, first_op, second_op, preferred_element_type=jnp.float32)


def collect(shards):
    by_rows = (
        lax.all_gather(shards[0], "ctx", axis=0, tiled=True),
        lax.all_gather(shards[1], "ctx", axis=0, tiled=True),
        lax.all_gather(shards[2], "ctx", axis=0, tiled=True),
        lax.all_gather(shards[3], "ctx", axis=0, tiled=True),
    )
    return (
        lax.all_gather(by_rows[0], "seq", axis=1, tiled=True),
        lax.all_gather(by_rows[1], "seq", axis=1, tiled=True),
        lax.all_gather(by_rows[2], "seq", axis=1, tiled=True),
        lax.all_gather(by_rows[3], "seq", axis=1, tiled=True),
    )


def share_keys(key_rows, value_rows, segment_rows):
    return (
        lax.all_gather(key_rows, "ctx", axis=1, tiled=True),
        lax.all_gather(value_rows, "ctx", axis=1, tiled=True),
        lax.all_gather(segment_rows, "ctx", axis=1, tiled=True),
    )


def key_block(shared, query_segment, query_place, block_index, block_width, head_count):
    key_all, value_all, segment_all = shared
    seq_count = key_all.shape[0]
    first_key = block_index * block_width
    keys_here = lax.dynamic_slice_in_dim(key_all, first_key, block_width, 1).reshape(
        seq_count, block_width, head_count, -1
    )
    values_here = lax.dynamic_slice_in_dim(value_all, first_key, block_width, 1).reshape(
        seq_count, block_width, head_count, -1
    )
    segment_here = lax.dynamic_slice_in_dim(segment_all, first_key, block_width, 1)
    key_place = first_key + jnp.arange(block_width, dtype=jnp.int32)
    same_segment = query_segment[:, :, None] == segment_here[:, None, :]
    causal = query_place[:, None] >= key_place[None, :]
    return (keys_here, values_here, (same_segment & causal[None])[:, None])


def attention_forward(queries, shared, query_segment, query_place):
    seq_count, ctx_len, head_count, head_dim = queries.shape
    length = shared[0].shape[1]
    block_width = min(512, length)
    block_count = length // block_width

    def first_pass(block_index, running):
        keys_here, values_here, allowed = key_block(
            shared, query_segment, query_place, block_index, block_width, head_count
        )

        def first_visit_block(current):
            highest, exp_total = current
            scores = jnp.where(allowed, matmul("sqhe,skhe->shqk", queries, keys_here), NEGATIVE)
            new_highest = jnp.maximum(highest, jnp.max(scores, axis=-1))
            summed = jnp.sum(
                jnp.where(allowed, jnp.exp(scores - new_highest[..., None]), 0.0), axis=-1
            )
            return (new_highest, exp_total * jnp.exp(highest - new_highest) + summed)

        return lax.cond(jnp.any(allowed), first_visit_block, lambda kept: kept, running)

    initial = (
        jnp.full((seq_count, head_count, ctx_len), NEGATIVE, jnp.float32),
        jnp.zeros((seq_count, head_count, ctx_len), jnp.float32),
    )
    highest, exp_total = lax.fori_loop(0, block_count, first_pass, initial)
    log_total = highest + jnp.log(exp_total)

    def second_pass(block_index, running):
        keys_here, values_here, allowed = key_block(
            shared, query_segment, query_place, block_index, block_width, head_count
        )

        def second_visit_block(summed):
            scores = matmul("sqhe,skhe->shqk", queries, keys_here)
            weights = jnp.where(allowed, jnp.exp(scores - log_total[..., None]), 0.0).astype(
                jnp.bfloat16
            )
            return summed + matmul("shqk,skhe->sqhe", weights, values_here)

        return lax.cond(jnp.any(allowed), second_visit_block, lambda kept: kept, running)

    attended = lax.fori_loop(
        0,
        block_count,
        second_pass,
        jnp.zeros((seq_count, ctx_len, head_count, head_dim), jnp.float32),
    )
    return (attended.reshape(seq_count, ctx_len, head_count * head_dim), log_total)


def attention_backward(
    queries, shared, query_segment, query_place, log_total, delta, attended_grad
):
    seq_count, ctx_len, head_count, head_dim = queries.shape
    length = shared[0].shape[1]
    model_width = head_count * head_dim
    block_width = min(512, length)
    block_count = length // block_width
    grad_heads = attended_grad.reshape(queries.shape)

    def one_block(block_index, running):
        keys_here, values_here, allowed = key_block(
            shared, query_segment, query_place, block_index, block_width, head_count
        )

        def one_visit_block(current):
            query_grad, key_grad, value_grad = current
            scores = matmul("sqhe,skhe->shqk", queries, keys_here)
            probs = jnp.where(allowed, jnp.exp(scores - log_total[..., None]), 0.0)
            value_part = matmul("shqk,sqhe->skhe", probs.astype(jnp.bfloat16), grad_heads)
            prob_grad = matmul("sqhe,skhe->shqk", grad_heads, values_here)
            score_grad = (probs * (prob_grad - delta[..., None])).astype(jnp.bfloat16)
            query_grad = query_grad + matmul("shqk,skhe->sqhe", score_grad, keys_here)
            key_part = matmul("shqk,sqhe->skhe", score_grad, queries)
            first_key = block_index * block_width
            key_grad = lax.dynamic_update_slice_in_dim(
                key_grad, key_part.reshape(seq_count, block_width, model_width), first_key, 1
            )
            value_grad = lax.dynamic_update_slice_in_dim(
                value_grad, value_part.reshape(seq_count, block_width, model_width), first_key, 1
            )
            return (query_grad, key_grad, value_grad)

        return lax.cond(jnp.any(allowed), one_visit_block, lambda kept: kept, running)

    initial = (
        jnp.zeros(queries.shape, jnp.float32),
        jnp.zeros((seq_count, length, model_width), jnp.float32),
        jnp.zeros((seq_count, length, model_width), jnp.float32),
    )
    return lax.fori_loop(0, block_count, one_block, initial)


def per_device(
    tokens,
    segments,
    adapter_index,
    norm_gains,
    norm_shifts,
    head_biases,
    expand_bias,
    exit_biases,
    mixing_weight,
    output_weight,
    expand_weight,
    shrink_weight,
    entry_adapters,
    mixing_adapters,
    expand_adapters,
    hidden_adapters,
    exit_adapters,
    cotangent,
):
    micro_count, seq_count, ctx_len, model_width = tokens.shape
    adapter_count = entry_adapters.shape[1]
    query_place = lax.axis_index("ctx") * ctx_len + jnp.arange(ctx_len, dtype=jnp.int32)
    shards = (mixing_weight, output_weight, expand_weight, shrink_weight)
    grad_totals = tuple(
        (
            jnp.zeros(member.shape, jnp.float32)
            for member in (
                entry_adapters,
                mixing_adapters,
                expand_adapters,
                hidden_adapters,
                exit_adapters,
            )
        )
    )
    layer_rows = []
    input_rows = []
    for micro_index in range(micro_count):
        picked = (
            adapter_index[micro_index][:, None]
            == jnp.arange(adapter_count, dtype=jnp.int32)[None, :]
        )
        pick_low = picked.astype(jnp.bfloat16)
        pick_full = picked.astype(jnp.float32)
        chosen = matmul("sa,kadr->ksdr", pick_low, entry_adapters).astype(jnp.bfloat16)
        mix_up = matmul("sa,are->sre", pick_low, mixing_adapters).astype(jnp.bfloat16)
        expand_up = matmul("sa,arf->srf", pick_low, expand_adapters).astype(jnp.bfloat16)
        hidden_down = matmul("sa,afr->sfr", pick_low, hidden_adapters).astype(jnp.bfloat16)
        exit_up = matmul("sa,kard->ksrd", pick_low, exit_adapters).astype(jnp.bfloat16)
        weights_fwd = collect(shards)
        w_mix, w_out, w_expand, w_shrink = weights_fwd
        inputs = tokens[micro_index].astype(jnp.float32)
        segment_rows = segments[micro_index]
        first_norm, first_back = jax.vjp(
            lambda activations: layer_norm(activations, norm_gains[0], norm_shifts[0]), inputs
        )
        normed = first_norm.astype(jnp.bfloat16)
        narrow_mix = matmul("scd,sdr->scr", normed, chosen[0]).astype(jnp.bfloat16)
        mixed = matmul("scd,de->sce", normed, w_mix) + matmul("scr,sre->sce", narrow_mix, mix_up)
        queries = ((mixed[..., :model_width] + head_biases[0]) * 0.125).astype(jnp.bfloat16)
        key_rows = mixed[..., model_width : 2 * model_width].astype(jnp.bfloat16)
        value_rows = (mixed[..., 2 * model_width :] + head_biases[1]).astype(jnp.bfloat16)
        shared = share_keys(key_rows, value_rows, segment_rows)
        query_heads = queries.reshape(seq_count, ctx_len, HEADS, -1)
        attended, log_total = attention_forward(query_heads, shared, segment_rows, query_place)
        attended_low = attended.astype(jnp.bfloat16)
        narrow_out = matmul("scd,sdr->scr", attended_low, chosen[1]).astype(jnp.bfloat16)
        residual = (
            inputs
            + matmul("scd,de->sce", attended_low, w_out)
            + matmul("scr,srd->scd", narrow_out, exit_up[0])
            + exit_biases[0]
        )
        second_norm, second_back = jax.vjp(
            lambda activations: layer_norm(activations, norm_gains[1], norm_shifts[1]), residual
        )
        normed_two = second_norm.astype(jnp.bfloat16)
        narrow_up = matmul("scd,sdr->scr", normed_two, chosen[2]).astype(jnp.bfloat16)
        upward = (
            matmul("scd,df->scf", normed_two, w_expand)
            + matmul("scr,srf->scf", narrow_up, expand_up)
            + expand_bias
        )
        active_full, gelu_back = jax.vjp(jax.nn.gelu, upward)
        active = active_full.astype(jnp.bfloat16)
        narrow_down = matmul("scf,sfr->scr", active, hidden_down).astype(jnp.bfloat16)
        layer_out = (
            residual
            + matmul("scf,fd->scd", active, w_shrink)
            + matmul("scr,srd->scd", narrow_down, exit_up[1])
            + exit_biases[1]
        )
        layer_rows.append(layer_out.astype(jnp.bfloat16))
        weights_back = collect(shards)
        shared_back = share_keys(key_rows, value_rows, segment_rows)
        w_mix, w_out, w_expand, w_shrink = weights_back
        out_grad = cotangent[micro_index]
        narrow_down_grad = matmul("scd,srd->scr", out_grad, exit_up[1]).astype(jnp.bfloat16)
        active_grad = matmul("scd,fd->scf", out_grad, w_shrink) + matmul(
            "scr,sfr->scf", narrow_down_grad, hidden_down
        )
        upward_grad = gelu_back(active_grad)[0].astype(jnp.bfloat16)
        narrow_up_grad = matmul("scf,srf->scr", upward_grad, expand_up).astype(jnp.bfloat16)
        normed_two_grad = matmul("scf,df->scd", upward_grad, w_expand) + matmul(
            "scr,sdr->scd", narrow_up_grad, chosen[2]
        )
        residual_grad = out_grad.astype(jnp.float32) + second_back(normed_two_grad)[0]
        branch_grad = residual_grad.astype(jnp.bfloat16)
        narrow_out_grad = matmul("scd,srd->scr", branch_grad, exit_up[0]).astype(jnp.bfloat16)
        attended_grad = (
            matmul("scd,ed->sce", branch_grad, w_out)
            + matmul("scr,sdr->scd", narrow_out_grad, chosen[1])
        ).astype(jnp.bfloat16)
        delta = jnp.sum(
            attended_grad.reshape(query_heads.shape).astype(jnp.float32)
            * attended.reshape(query_heads.shape),
            axis=-1,
        )
        delta = jnp.swapaxes(delta, 1, 2)
        query_grad, key_full, value_full = attention_backward(
            query_heads, shared_back, segment_rows, query_place, log_total, delta, attended_grad
        )
        key_grad, value_grad = (
            lax.psum_scatter(
                key_full.astype(jnp.bfloat16), "ctx", scatter_dimension=1, tiled=True
            ).astype(jnp.float32),
            lax.psum_scatter(
                value_full.astype(jnp.bfloat16), "ctx", scatter_dimension=1, tiled=True
            ).astype(jnp.float32),
        )
        mixed_grad = jnp.concatenate(
            [
                query_grad.reshape(seq_count, ctx_len, model_width).astype(jnp.bfloat16) * 0.125,
                key_grad.astype(jnp.bfloat16),
                value_grad.astype(jnp.bfloat16),
            ],
            axis=-1,
        )
        narrow_mix_grad = matmul("sce,sre->scr", mixed_grad, mix_up).astype(jnp.bfloat16)
        normed_grad = matmul("sce,de->scd", mixed_grad, w_mix) + matmul(
            "scr,sdr->scd", narrow_mix_grad, chosen[0]
        )
        input_rows.append((residual_grad + first_back(normed_grad)[0]).astype(jnp.bfloat16))
        entry_seq = jnp.stack(
            [
                matmul("scd,scr->sdr", normed, narrow_mix_grad),
                matmul("scd,scr->sdr", attended_low, narrow_out_grad),
                matmul("scd,scr->sdr", normed_two, narrow_up_grad),
            ]
        )
        exit_seq = jnp.stack(
            [
                matmul("scr,scd->srd", narrow_out, branch_grad),
                matmul("scr,scd->srd", narrow_down, out_grad),
            ]
        )
        batch_grads = (
            jnp.einsum("sa,ksdr->kadr", pick_full, entry_seq, precision=HIGH),
            jnp.einsum(
                "sa,sre->are",
                pick_full,
                matmul("scr,sce->sre", narrow_mix, mixed_grad),
                precision=HIGH,
            ),
            jnp.einsum(
                "sa,srf->arf",
                pick_full,
                matmul("scr,scf->srf", narrow_up, upward_grad),
                precision=HIGH,
            ),
            jnp.einsum(
                "sa,sfr->afr",
                pick_full,
                matmul("scf,scr->sfr", active, narrow_down_grad),
                precision=HIGH,
            ),
            jnp.einsum("sa,ksrd->kard", pick_full, exit_seq, precision=HIGH),
        )
        grad_totals = tuple(
            (earlier + addition for earlier, addition in zip(grad_totals, batch_grads))
        )
    grad_totals = lax.psum(
        (grad_totals[0], grad_totals[1], grad_totals[2], grad_totals[3], grad_totals[4]),
        ("seq", "ctx"),
    )
    return (
        jnp.stack(layer_rows),
        jnp.stack(input_rows),
        grad_totals[0],
        grad_totals[1],
        grad_totals[2],
        grad_totals[3],
        grad_totals[4],
    )


def solution(mesh):
    in_specs = (
        P(None, "seq", "ctx", None),
        P(None, "seq", "ctx"),
        P(None, "seq"),
        P(),
        P(),
        P(),
        P(),
        P(),
        P("ctx", "seq"),
        P("ctx", "seq"),
        P("ctx", "seq"),
        P("ctx", "seq"),
        P(),
        P(),
        P(),
        P(),
        P(),
        P(None, "seq", "ctx", None),
    )
    out_specs = (P(None, "seq", "ctx", None), P(None, "seq", "ctx", None), P(), P(), P(), P(), P())
    return jax.shard_map(
        per_device, mesh=mesh, in_specs=in_specs, out_specs=out_specs, check_vma=False
    )
```

profile of v0, /device:TPU:5, one launch (start us, length us, event | category | flops | bytes accessed | tf_op | source)
XLA Modules:
  0.0 1461.1 jit_solution(17102734306764890602)
XLA Ops:
  8.0 11.1 all_gather.29
  43.5 100.9 %all-gather.15.cloned.1.call-done = bf16[1088,3264]{0,1:T(8,128)(2,1)} async-done(((bf16[1088,408]{0,1:T(8,128)(2,1)}), bf16[1088,3264]{0,1:T(8,128)(2,1)}) %all-gather.15.cloned.1.call-update) | async-done | bytes 7102480 | tf_op jit(solution)/shard_map/all_gather | solution.py:33
  191.4 11.3 fusion.158
  202.7 11.1 fusion.156
  217.6 14.5 copy.136
  232.1 14.2 copy.143
  265.9 38.0 %all-gather.27.cloned.1.call-done = bf16[4352,1088]{0,1:T(8,128)(2,1)} async-done(((bf16[4352,136]{0,1:T(8,128)(2,1)}), bf16[4352,1088]{0,1:T(8,128)(2,1)}) %all-gather.27.cloned.1.call-update) | async-done | bytes 9469968 | tf_op jit(solution)/shard_map/all_gather | solution.py:36
  303.9 12.4 fusion.136
  325.0 16.8 %all-gather.31.cloned.1.call-done = bf16[1,2048,1088]{1,2,0:T(8,128)(2,1)} async-done(((bf16[1,512,1088]{1,2,0:T(8,128)(2,1)}), bf16[1,2048,1088]{1,2,0:T(8,128)(2,1)}) %all-gather.31.cloned.1.call-update) | async-done | bytes 4456464 | tf_op jit(solution)/shard_map/all_gather | solution.py:42
  341.8 49.2 %while.104 = (s32[]{:T(128)}, f32[1,17,512]{2,1,0:T(8,128)S(1)}, f32[1,17,512]{2,1,0:T(8,128)S(1)}, s32[1,1,512]{2,1,0:T(1,128)S(1)}, s32[1,2048]{1,0:T(1,128)S(...) while((s32[]{:T(128)}, f32[1,17,512]{2,1,0:T(8,128)S(1)}, ...), condition=%wide.region_24.0_spmd.clone, body=%wide.region_18.24_spmd.clone.sunk | while | flops 598231040 | bytes 43460936 | solution.py:91
  343.6 21.9 %conditional.20 = ((f32[1,17,512]{2,1,0:T(8,128)S(1)}, f32[1,17,512]{2,1,0:T(8,128)S(1)})) conditional(s32[]{:T(128)} %convert_element_type.750, (f32[1,17,512]{2,1,0:T(8,128)S(1)}, f32[1,17,512]{2,1,0:T(8,128)S(1)}) %tuple.323, (pred[1,1,512,512]{2,3,1,0:T(8,128)(4,1)S(1)}, bf16[1,2048,1088]{1,2,0:T(8,128)(2,1)}, s32[]{:T(128)}, ...), branch_computations={%region_20.20_spmd, %region_21.23_spmd} | conditional | flops 597181440 | bytes 43182164 | solution.py:85
  345.7 10.0 fusion.20
  355.7 9.8 select_reduce_fusion.1
  367.2 20.5 %conditional.20 = ((f32[1,17,512]{2,1,0:T(8,128)S(1)}, f32[1,17,512]{2,1,0:T(8,128)S(1)})) conditional(s32[]{:T(128)} %convert_element_type.750, (f32[1,17,512]{2,1,0:T(8,128)S(1)}, f32[1,17,512]{2,1,0:T(8,128)S(1)}) %tuple.323, (pred[1,1,512,512]{2,3,1,0:T(8,128)(4,1)S(1)}, bf16[1,2048,1088]{1,2,0:T(8,128)(2,1)}, s32[]{:T(128)}, ...), branch_computations={%region_20.20_spmd, %region_21.23_spmd} | conditional | flops 597181440 | bytes 43182164 | solution.py:85
  377.9 9.7 select_reduce_fusion.1
  392.7 30.9 %while.105 = (s32[]{:T(128)}, f32[1,512,17,64]{1,3,2,0:T(8,128)}, s32[1,1,512]{2,1,0:T(1,128)S(1)}, s32[1,2048]{1,0:T(1,128)S(1)}, bf16[1,2048,1088]{1,2,0:T(8,1...) while((s32[]{:T(128)}, f32[1,512,17,64]{1,3,2,0:T(8,128)}, ...), condition=%wide.region_29.30_spmd.clone, body=%wide.region_25.29_spmd.clone.sunk | while | flops 1155826688 | bytes 12830977 | solution.py:108
  395.0 10.7 conditional.21
  408.1 10.7 conditional.21
  426.9 48.0 %while.102 = (s32[]{:T(128)}, f32[1,17,512]{2,1,0:T(8,128)S(1)}, f32[1,17,512]{2,1,0:T(8,128)S(1)}, s32[1,1,512]{2,1,0:T(1,128)S(1)}, s32[1,2048]{1,0:T(1,128)S(...) while((s32[]{:T(128)}, f32[1,17,512]{2,1,0:T(8,128)S(1)}, ...), condition=%wide.region_8.9_spmd.clone, body=%wide.region_2.8_spmd.clone.sunk | while | flops 598231040 | bytes 43460936 | solution.py:91
  428.6 20.7 %conditional.18 = ((f32[1,17,512]{2,1,0:T(8,128)S(1)}, f32[1,17,512]{2,1,0:T(8,128)S(1)})) conditional(s32[]{:T(128)} %convert_element_type.748, (f32[1,17,512]{2,1,0:T(8,128)S(1)}, f32[1,17,512]{2,1,0:T(8,128)S(1)}) %tuple.314, (pred[1,1,512,512]{2,3,1,0:T(8,128)(4,1)S(1)}, bf16[1,2048,1088]{1,2,0:T(8,128)(2,1)}, s32[]{:T(128)}, ...), branch_computations={%region_4.0_spmd, %region_5.7_spmd} | conditional | flops 597181440 | bytes 43182164 | solution.py:85
  439.4 9.8 select_reduce_fusion
  450.9 20.7 %conditional.18 = ((f32[1,17,512]{2,1,0:T(8,128)S(1)}, f32[1,17,512]{2,1,0:T(8,128)S(1)})) conditional(s32[]{:T(128)} %convert_element_type.748, (f32[1,17,512]{2,1,0:T(8,128)S(1)}, f32[1,17,512]{2,1,0:T(8,128)S(1)}) %tuple.314, (pred[1,1,512,512]{2,3,1,0:T(8,128)(4,1)S(1)}, bf16[1,2048,1088]{1,2,0:T(8,128)(2,1)}, s32[]{:T(128)}, ...), branch_computations={%region_4.0_spmd, %region_5.7_spmd} | conditional | flops 597181440 | bytes 43182164 | solution.py:85
  461.7 9.9 select_reduce_fusion
  476.6 28.3 %while.103 = (s32[]{:T(128)}, f32[1,512,17,64]{1,3,2,0:T(8,128)}, s32[1,1,512]{2,1,0:T(1,128)S(1)}, s32[1,2048]{1,0:T(1,128)S(1)}, bf16[1,2048,1088]{1,2,0:T(8,1...) while((s32[]{:T(128)}, f32[1,512,17,64]{1,3,2,0:T(8,128)}, ...), condition=%wide.region_13.14_spmd.clone, body=%wide.region_9.13_spmd.clone.sunk | while | flops 1155826688 | bytes 12830977 | solution.py:108
  491.0 9.4 conditional.19
  522.0 135.2 %all-gather.25.cloned.1.call-done = bf16[1088,4352]{0,1:T(8,128)(2,1)} async-done(((bf16[1088,544]{0,1:T(8,128)(2,1)}), bf16[1088,4352]{0,1:T(8,128)(2,1)}) %all-gather.25.cloned.1.call-update) | async-done | bytes 9469968 | tf_op jit(solution)/shard_map/all_gather | solution.py:35
  692.2 12.9 fusion.235
  723.7 9.6 fusion.238
  751.9 95.3 %while.106 = (s32[]{:T(128)}, f32[1,512,17,64]{1,3,2,0:T(8,128)}, bf16[1,2048,1088]{1,2,0:T(8,128)(2,1)}, bf16[1,2048,1088]{1,2,0:T(8,128)(2,1)}, s32[1,1,512]{2...) while((s32[]{:T(128)}, f32[1,512,17,64]{1,3,2,0:T(8,128)}, ...), condition=%wide.region_39.40_spmd.clone, body=%wide.region_35.39_spmd.clone.sunk | while | flops 2889384960 | bytes 159046160 | solution.py:157
  753.7 44.3 %conditional.22 = ((f32[1,512,17,64]{1,3,2,0:T(8,128)}, bf16[1,2048,1088]{1,2,0:T(8,128)(2,1)}, bf16[1,2048,1088]{1,2,0:T(8,128)(2,1)})) conditional(s32[]{:T(128)} %convert_element_type.752, (f32[1,512,17,64]{1,3,2,0:T(8,128)}, bf16[1,2048,1088]{1,2,0:T(8,128)(2,1)}, bf16[1,2048,1088]{1,2,0:T(8,128)(2,1)}) %tuple.332, ...), branch_computations={%region_37.37_spmd, %region_38.0_spmd} | conditional | flops 2888335360 | bytes 158767296 | solution.py:150
  765.0 9.7 fusion.28
  778.1 10.4 fusion.30
  799.6 44.3 %conditional.22 = ((f32[1,512,17,64]{1,3,2,0:T(8,128)}, bf16[1,2048,1088]{1,2,0:T(8,128)(2,1)}, bf16[1,2048,1088]{1,2,0:T(8,128)(2,1)})) conditional(s32[]{:T(128)} %convert_element_type.752, (f32[1,512,17,64]{1,3,2,0:T(8,128)}, bf16[1,2048,1088]{1,2,0:T(8,128)(2,1)}, bf16[1,2048,1088]{1,2,0:T(8,128)(2,1)}) %tuple.332, ...), branch_computations={%region_37.37_spmd, %region_38.0_spmd} | conditional | flops 2888335360 | bytes 158767296 | solution.py:150
  810.9 9.7 fusion.28
  824.1 10.4 fusion.30
  863.2 99.3 %while.107 = (s32[]{:T(128)}, f32[1,512,17,64]{1,3,2,0:T(8,128)}, bf16[1,2048,1088]{1,2,0:T(8,128)(2,1)}, bf16[1,2048,1088]{1,2,0:T(8,128)(2,1)}, s32[1,1,512]{2...) while((s32[]{:T(128)}, f32[1,512,17,64]{1,3,2,0:T(8,128)}, ...), condition=%wide.region_51.52_spmd.clone, body=%wide.region_47.51_spmd.clone.sunk | while | flops 2889384960 | bytes 159046160 | solution.py:157
  865.9 44.2 %conditional.23 = ((f32[1,512,17,64]{1,3,2,0:T(8,128)}, bf16[1,2048,1088]{1,2,0:T(8,128)(2,1)}, bf16[1,2048,1088]{1,2,0:T(8,128)(2,1)})) conditional(s32[]{:T(128)} %convert_element_type.753, (f32[1,512,17,64]{1,3,2,0:T(8,128)}, bf16[1,2048,1088]{1,2,0:T(8,128)(2,1)}, bf16[1,2048,1088]{1,2,0:T(8,128)(2,1)}) %tuple.337, ...), branch_computations={%region_49.49_spmd, %region_50.50_spmd} | conditional | flops 2888335360 | bytes 158767296 | solution.py:150
  877.2 9.7 fusion.42
  890.3 10.4 fusion.44
  912.4 45.6 %conditional.23 = ((f32[1,512,17,64]{1,3,2,0:T(8,128)}, bf16[1,2048,1088]{1,2,0:T(8,128)(2,1)}, bf16[1,2048,1088]{1,2,0:T(8,128)(2,1)})) conditional(s32[]{:T(128)} %convert_element_type.753, (f32[1,512,17,64]{1,3,2,0:T(8,128)}, bf16[1,2048,1088]{1,2,0:T(8,128)(2,1)}, bf16[1,2048,1088]{1,2,0:T(8,128)(2,1)}) %tuple.337, ...), branch_computations={%region_49.49_spmd, %region_50.50_spmd} | conditional | flops 2888335360 | bytes 158767296 | solution.py:150
  923.7 9.7 fusion.42
  936.8 11.5 fusion.44
  974.2 9.8 convolution_add_fusion.15
  991.2 10.4 convolution_add_fusion.14
  1017.2 12.7 reduce-scatter.7.cloned.1.call-done
  1034.4 151.2 %reduce-scatter.11.cloned.1.call-done = bf16[1,512,1088]{1,2,0:T(8,128)(2,1)} async-done(((bf16[1,2048,1088]{1,2,0:T(8,128)(2,1)}), bf16[1,512,1088]{1,2,0:T(8,128)(2,1)}) %reduce-scatter.11.cloned.1.call-update) | async-done | bytes 1114128 | tf_op jit(solution)/shard_map/reduce_scatter | solution.py:287
  1185.6 48.8 %reduce-scatter.9.cloned.1.call-done = bf16[1,512,1088]{1,2,0:T(8,128)(2,1)} async-done(((bf16[1,2048,1088]{1,2,0:T(8,128)(2,1)}), bf16[1,512,1088]{1,2,0:T(8,128)(2,1)}) %reduce-scatter.9.cloned.1.call-update) | async-done | bytes 1114128 | tf_op jit(solution)/shard_map/reduce_scatter | solution.py:284
  1271.2 172.4 %all-reduce.3.cloned.1.call-done = (f32[3,8,1088,16]{2,3,1,0:T(8,128)}, f32[8,16,3264]{2,1,0:T(8,128)}, f32[8,16,4352]{2,1,0:T(8,128)}, f32[8,4352,16]{1,2,0:T(8,128)}, f32[2,8,16,1088]{3,2,1,0:T(8,128)}) async-done(((f32[3,8,1088,16]{2,3,1,0:T(8,128)}, f32[8,16,3264]{2,1,0:T(8,128)}, f32[8,16,4352]{2,1,0:T(8,128)}, f32[8,4352,16]{1,2,0:T(8,128)}, f32[2,8,16,1088]{3,2,1,0:T(8,128)}), ...) | async-done | bytes 8912912 | tf_op jit(solution)/shard_map/psum | solution.py:342
  (752 shorter events, 512.3 us)
Async XLA Ops:
  7.2 184.2 %copy-start = (bf16[8,4352,16]{1,2,0:T(8,128)(2,1)S(1)}, bf16[8,4352,16]{1,2,0:T(8,128)(2,1)}, u32[]{:S(2)}) copy-start(bf16[8,4352,16]{1,2,0:T(8,128)(2,1)} %param.57) | copy-start | bytes 3342340
  7.2 21.9 %all-gather.33.cloned.1.call-start = ((), (), s32[]{:S(2)}) async-start(), calls=%async_computation.17 | async-start | bytes 1566720 | tf_op jit(solution)/shard_map/all_gather | solution.py:30
  7.9 136.4 %all-gather.15.cloned.1.call-start = ((), (), s32[]{:S(2)}) async-start(), calls=%async_computation.4 | async-start | bytes 8460288 | tf_op jit(solution)/shard_map/all_gather | solution.py:33
  20.6 193.2 %all-gather.23.cloned.1.call-start = ((), (), s32[]{:S(2)}) async-start(), calls=%async_computation.8 | async-start | bytes 1740800 | tf_op jit(solution)/shard_map/all_gather | solution.py:29
  21.4 282.5 %all-gather.27.cloned.1.call-start = ((), (), s32[]{:S(2)}) async-start(), calls=%async_computation.10 | async-start | bytes 10653696 | tf_op jit(solution)/shard_map/all_gather | solution.py:36
  35.5 306.3 %all-gather.31.cloned.1.call-start = ((), (), s32[]{:S(2)}) async-start(), calls=%async_computation.12 | async-start | bytes 5570560 | tf_op jit(solution)/shard_map/all_gather | solution.py:42
  42.3 109.1 %copy-start.85 = (bf16[1,16,3264]{2,0,1:T(2,128)(2,1)}, bf16[1,16,3264]{2,0,1:T(2,128)(2,1)S(1)}, u32[]{:S(2)}) copy-start(bf16[1,16,3264]{2,0,1:T(2,128)(2,1)S(1)} %fusion.168) | copy-start | bytes 313348
  156.5 234.6 %all-gather.29.cloned.1.call-start = ((), (), s32[]{:S(2)}) async-start(), calls=%async_computation.11 | async-start | bytes 5570560 | tf_op jit(solution)/shard_map/all_gather | solution.py:43
  173.9 252.9 %all-gather.19.cloned.1.call-start = ((), (), s32[]{:S(2)}) async-start(), calls=%async_computation.6 | async-start | bytes 5570560 | tf_op jit(solution)/shard_map/all_gather | solution.py:42
  177.1 297.9 %all-gather.17.cloned.1.call-start = ((), (), s32[]{:S(2)}) async-start(), calls=%async_computation.5 | async-start | bytes 5570560 | tf_op jit(solution)/shard_map/all_gather | solution.py:43
  177.8 332.1 %all-gather.21.cloned.1.call-start = ((), (), s32[]{:S(2)}) async-start(), calls=%async_computation.7 | async-start | bytes 2820096 | tf_op jit(solution)/shard_map/all_gather | solution.py:34
  188.4 468.7 %all-gather.25.cloned.1.call-start = ((), (), s32[]{:S(2)}) async-start(), calls=%async_computation.9 | async-start | bytes 11280384 | tf_op jit(solution)/shard_map/all_gather | solution.py:35
  216.4 800.8 %reduce-scatter.5.cloned.1.call-start = ((), (), s32[]{:S(2)}) async-start(), calls=%async_computation.13 | async-start | bytes 5570560 | tf_op jit(solution)/shard_map/reduce_scatter | solution.py:284
  217.5 42.4 %copy-start.69 = (bf16[1,2,16,1088]{3,2,1,0:T(8,128)(2,1)}, bf16[1,2,16,1088]{3,2,1,0:T(8,128)(2,1)S(1)}, u32[]{:S(2)}) copy-start(bf16[1,2,16,1088]{3,2,1,0:T(8,128)(2,1)S(1)} %copy.186) | copy-start | bytes 208900
  217.6 40.3 %copy-start.73 = (bf16[1,2,16,1088]{3,2,1,0:T(8,128)(2,1)}, bf16[1,2,16,1088]{3,2,1,0:T(8,128)(2,1)S(1)}, u32[]{:S(2)}) copy-start(bf16[1,2,16,1088]{3,2,1,0:T(8,128)(2,1)S(1)} %copy.187) | copy-start | bytes 208900
  232.1 14.2 copy-start.180
  232.1 25.1 %copy-start.167 = (f32[2,1088]{1,0:T(2,128)S(1)}, f32[2,1088]{1,0:T(2,128)}, u32[]{:S(2)}) copy-start(f32[2,1088]{1,0:T(2,128)} %param.49) | copy-start | bytes 26116
  246.2 15.8 %copy-start.55 = (bf16[8,16,4352]{2,1,0:T(8,128)(2,1)S(1)}, bf16[8,16,4352]{2,1,0:T(8,128)(2,1)}, u32[]{:S(2)}) copy-start(bf16[8,16,4352]{2,1,0:T(8,128)(2,1)} %param.56) | copy-start | bytes 3342340
  303.9 12.4 copy-start.16
  303.9 12.4 copy-start.29
  520.9 145.5 %copy-start.44 = (bf16[512,1088]{0,1:T(8,128)(2,1)}, bf16[512,1088]{0,1:T(8,128)(2,1)S(1)}, u32[]{:S(2)}) copy-start(bf16[512,1088]{0,1:T(8,128)(2,1)S(1)} %get-tuple-element.1856) | copy-start | bytes 3342340
  520.9 171.3 %copy-start.42 = (bf16[512,1088]{0,1:T(8,128)(2,1)}, bf16[512,1088]{0,1:T(8,128)(2,1)S(1)}, u32[]{:S(2)}) copy-start(bf16[512,1088]{0,1:T(8,128)(2,1)S(1)} %get-tuple-element.1857) | copy-start | bytes 3342340
  692.1 12.9 copy-start.122
  692.1 12.9 copy-start.76
  723.7 9.6 copy-start.98
  723.7 9.6 copy-start.20
  753.7 11.3 copy-start.52
  799.6 11.3 copy-start.52
  847.2 182.6 %reduce-scatter.7.cloned.1.call-start = ((), (), s32[]{:S(2)}) async-start(), calls=%async_computation.14 | async-start | bytes 5570560 | tf_op jit(solution)/shard_map/reduce_scatter | solution.py:287
  847.8 337.8 %reduce-scatter.11.cloned.1.call-start = ((), (), s32[]{:S(2)}) async-start(), calls=%async_computation.16 | async-start | bytes 5570560 | tf_op jit(solution)/shard_map/reduce_scatter | solution.py:287
  865.9 11.3 copy-start.53
  912.4 11.3 copy-start.53
  962.7 271.8 %reduce-scatter.9.cloned.1.call-start = ((), (), s32[]{:S(2)}) async-start(), calls=%async_computation.15 | async-start | bytes 5570560 | tf_op jit(solution)/shard_map/reduce_scatter | solution.py:284
  964.3 48.3 %copy-start.176 = (f32[8]{0:T(128)}, f32[8]{0:T(128)S(1)}, u32[]{:S(2)}) copy-start(f32[8]{0:T(128)S(1)} %get-tuple-element.1877) | copy-start | bytes 100
  964.3 48.3 %copy-start.178 = (f32[8]{0:T(128)}, f32[8]{0:T(128)S(1)}, u32[]{:S(2)}) copy-start(f32[8]{0:T(128)S(1)} %get-tuple-element.1878) | copy-start | bytes 100
  974.2 9.8 copy-start.43
  974.2 9.8 copy-start.99
  974.2 10.9 copy-start.18
  974.2 469.4 %all-reduce.3.cloned.1.call-start = ((), (), s32[]{:S(2)}) async-start(), calls=%async_computation.18 | async-start | bytes 18219008 | tf_op jit(solution)/shard_map/psum | solution.py:342
  991.2 10.4 copy-start.72
  1013.8 16.0 %copy-start.88 = (bf16[1,16,3264]{2,0,1:T(2,128)(2,1)S(1)}, bf16[1,16,3264]{2,0,1:T(2,128)(2,1)}, u32[]{:S(2)}) copy-start(bf16[1,16,3264]{2,0,1:T(2,128)(2,1)} %copy-done.87) | copy-start | bytes 313348
  1033.1 201.3 %copy-start.63 = (bf16[1,512,17,64]{1,3,2,0:T(8,128)(2,1)S(1)}, bf16[1,512,17,64]{1,3,2,0:T(8,128)(2,1)}, u32[]{:S(2)}) copy-start(bf16[1,512,17,64]{1,3,2,0:T(8,128)(2,1)} %convert_multiply_fusion) | copy-start | bytes 3342340
  1033.1 201.3 %copy-start.86 = (bf16[1,16,3264]{2,0,1:T(2,128)(2,1)S(1)}, bf16[1,16,3264]{2,0,1:T(2,128)(2,1)}, u32[]{:S(2)}) copy-start(bf16[1,16,3264]{2,0,1:T(2,128)(2,1)} %copy-done.85) | copy-start | bytes 313348
  1253.9 9.3 copy-start.28
  1253.9 9.3 copy-start.30
  1254.0 9.3 copy-start.112
  1254.0 9.3 copy-start.126
  1254.0 9.3 copy-start.130
  (178 other events, 570.9 us)
Sparse Core Ops, SparseCore 0:
  9.6 19.4 all-gather.32
  31.9 112.4 all-gather.14
  145.9 18.5 all-gather.22
  167.1 136.7 all-gather.26
  305.9 35.8 all-gather.30
  343.8 35.9 all-gather.28
  381.9 35.9 all-gather.18
  420.1 35.9 all-gather.16
  458.9 50.9 all-gather.20
  512.5 144.6 all-gather.24
  847.3 133.7 reduce-scatter.4
  983.6 46.1 reduce-scatter.6
  1032.4 153.1 reduce-scatter.10
  1188.1 46.2 reduce-scatter.8
  1254.1 189.5 all-reduce.2
where the time goes:
time: 1470 us; the launch traced here: 1460 us
  waiting for transfers between devices  688 us (47%)
  matrix products  456 us (31%)
  local copies, waits for them, and re-layouts  149 us (10%)
  other arithmetic  103 us (7%)
  blocking collectives  29.6 us (2%)
  loops' own time  18.2 us (1%)
  between operations  16.3 us (1%)
    dot_general x102, matrix products, matmul(): jnp.einsum(pattern, first_op, second_op, preferred_element_type=jnp.float32)  456 us
    psum x1, waiting for transfers between devices, per_device(): lax.psum((grad_totals[0], grad_totals[1], grad_totals[2], grad_totals[3],...  172 us
    reduce_scatter x2, waiting for transfers between devices, per_device(): lax.psum_scatter(value_full.astype(jnp.bfloat16), 'ctx', scatter_dimensio...  164 us
    all_gather x1, waiting for transfers between devices, collect(): lax.all_gather(by_rows[2], 'seq', axis=1, tiled=True)  135 us
    all_gather x1, waiting for transfers between devices, collect(): lax.all_gather(by_rows[0], 'seq', axis=1, tiled=True)  101 us
    reduce_scatter x2, waiting for transfers between devices, per_device(): lax.psum_scatter(key_full.astype(jnp.bfloat16), 'ctx', scatter_dimension=...  48.8 us
    reduce_sum x4, other arithmetic, first_visit_block(): jnp.sum(jnp.where(allowed, jnp.exp(scores - new_highest[..., None]), 0.0)...  39.1 us
    all_gather x1, waiting for transfers between devices, collect(): lax.all_gather(by_rows[3], 'seq', axis=1, tiled=True)  38 us
  transfers between devices with their start and end apart: 15, of which 10 were waited for; matrix products, arithmetic and copies ran while one was open for 32% of the time, Pallas kernels for 0%

commit v1 on v0

v1 whole, which is shorter than its diff:
```python
import functools

import jax
import jax.numpy as jnp
from jax import lax
from jax.experimental import pallas as pl
from jax.experimental.pallas import tpu as pltpu
from jax.sharding import PartitionSpec as P

HEADS = 17
EPS = 1e-05
NEG = -1e30
BF = jnp.bfloat16
F32 = jnp.float32
BOTH = ("seq", "ctx")


def dotg(a,b,ca,cb):
    return lax.dot_general(a,b,(((ca,),(cb,)),((),())),preferred_element_type=jnp.float32)

def ranges(meta_ref, r, qi, qn, QB, KB, ctx, L):
    smin=meta_ref[1+(r*qn+qi)*2]; smax=meta_ref[2+(r*qn+qi)*2]
    q0=ctx*L+qi*QB
    lo=smin//KB
    hi=(q0+QB-1)//KB+1
    f0=jnp.minimum((smax+KB-1)//KB,hi)
    f1=jnp.maximum((q0+1)//KB,f0)
    return lo,f0,f1,hi,q0

def fwd_kernel(meta_ref, start_ref, q_ref, k_ref, v_ref, o_ref, l_ref, vt_ref, acc_ref, st_ref, *, QB, KB, L, xorder):
    r=pl.program_id(0)
    ctx=meta_ref[0]
    qn=L//QB; per=L//KB
    vt_ref[...]=v_ref[0].T
    lane=lax.broadcasted_iota(jnp.int32,(1,128),1)
    for qi in range(qn):
        lo,f0,f1,hi,q0=ranges(meta_ref,r,qi,qn,QB,KB,ctx,L)
        q2=q_ref[0,qi*QB:(qi+1)*QB,:]
        qh=[jnp.where(lane<64,q2,0).astype(q2.dtype),jnp.where(lane>=64,q2,0).astype(q2.dtype)]
        start=start_ref[0,:,qi*QB:(qi+1)*QB]
        acc_ref[...]=jnp.zeros_like(acc_ref)
        st_ref[0:2,:]=jnp.full((2,QB),NEG,jnp.float32)
        st_ref[2:4,:]=jnp.zeros((2,QB),jnp.float32)
        def body(t,_,masked):
            b=t//per
            rel=(b^ctx) if xorder else b
            off=pl.multiple_of(rel*L+(t-b*per)*KB,KB)
            kt=k_ref[0,pl.ds(off,KB),:]
            if masked:
                kpos=lax.broadcasted_iota(jnp.int32,(KB,1),0)+t*KB
                qpos=lax.broadcasted_iota(jnp.int32,(1,QB),1)+q0
                ok=(kpos<=qpos)&(kpos>=start)
            for h in range(2):
                s=dotg(kt,qh[h],1,1)
                if masked: s=jnp.where(ok,s,NEG)
                m=st_ref[h:h+1,:]
                mn=jnp.maximum(m,jnp.max(s,axis=0,keepdims=True))
                al=jnp.exp(m-mn)
                p=jnp.exp(s-mn)
                if masked: p=jnp.where(ok,p,0.0)
                st_ref[2+h:3+h,:]=st_ref[2+h:3+h,:]*al+jnp.sum(p,axis=0,keepdims=True)
                st_ref[h:h+1,:]=mn
                vt=vt_ref[h*64:(h+1)*64,pl.ds(off,KB)]
                acc_ref[h*64:(h+1)*64,:]=acc_ref[h*64:(h+1)*64,:]*al+dotg(vt,p.astype(jnp.bfloat16),1,0)
            return 0
        lax.fori_loop(lo,f0,lambda t,c: body(t,c,True),0)
        lax.fori_loop(f0,f1,lambda t,c: body(t,c,False),0)
        lax.fori_loop(f1,hi,lambda t,c: body(t,c,True),0)
        for h in range(2):
            l=st_ref[2+h:3+h,:]
            l_ref[0,0,h:h+1,qi*QB:(qi+1)*QB]=st_ref[h:h+1,:]+jnp.log(l)
            acc_ref[h*64:(h+1)*64,:]=acc_ref[h*64:(h+1)*64,:]/l
        o_ref[0,qi*QB:(qi+1)*QB,:]=acc_ref[...].T.astype(o_ref.dtype)

def attn_fwd(meta,start,q,k,v,*,QB=256,KB=256,xorder=True):
    R,L,W=q.shape; T=k.shape[1]; NP=W//128
    kern=functools.partial(fwd_kernel,QB=QB,KB=KB,L=L,xorder=xorder)
    return pl.pallas_call(kern,
        grid_spec=pltpu.PrefetchScalarGridSpec(num_scalar_prefetch=1,grid=(R,NP),
            in_specs=[pl.BlockSpec((1,1,L),lambda r,p,m:(r,0,0)),
                      pl.BlockSpec((1,L,128),lambda r,p,m:(r,0,p)),
                      pl.BlockSpec((1,T,128),lambda r,p,m:(r,0,p)),
                      pl.BlockSpec((1,T,128),lambda r,p,m:(r,0,p))],
            out_specs=[pl.BlockSpec((1,L,128),lambda r,p,m:(r,0,p)),
                       pl.BlockSpec((1,1,2,L),lambda r,p,m:(r,p,0,0))],
            scratch_shapes=[pltpu.VMEM((128,T),jnp.bfloat16),pltpu.VMEM((128,QB),jnp.float32),pltpu.VMEM((8,QB),jnp.float32)]),
        out_shape=[jax.ShapeDtypeStruct((R,L,1088),jnp.bfloat16),jax.ShapeDtypeStruct((R,NP,2,L),jnp.float32)],
        compiler_params=pltpu.CompilerParams(dimension_semantics=("arbitrary","arbitrary"),vmem_limit_bytes=48<<20),
        cost_estimate=pl.CostEstimate(flops=R*4*L*T*W,bytes_accessed=R*(2*L+2*T)*W*2,transcendentals=R*L*T*18),
        name="attn_fwd")(meta,start,q,k,v)

def bwd_kernel(meta_ref, start_ref, q_ref, k_ref, v_ref, do_ref, o_ref, l_ref, dq_ref, dk_ref, dv_ref,
               kt_ref, dqt_ref, dkt_ref, dvt_ref, *, QB, KB, L, xorder, nheads, r0):
    r=pl.program_id(0)+r0
    ctx=meta_ref[0]
    qn=L//QB; per=L//KB
    kt_ref[...]=k_ref[0].T
    lane=lax.broadcasted_iota(jnp.int32,(1,128),1)
    lane_lim=nheads*64-pl.program_id(1)*128
    dkt_ref[...]=jnp.zeros_like(dkt_ref)
    dvt_ref[...]=jnp.zeros_like(dvt_ref)
    for qi in range(qn):
        lo,f0,f1,hi,q0=ranges(meta_ref,r,qi,qn,QB,KB,ctx,L)
        q2=q_ref[0,qi*QB:(qi+1)*QB,:]
        do2=do_ref[0,qi*QB:(qi+1)*QB,:]
        do2=jnp.where(lane<lane_lim,do2,0).astype(do2.dtype)
        o2=o_ref[0,qi*QB:(qi+1)*QB,:]
        o2=jnp.where(lane<lane_lim,o2,0).astype(o2.dtype)
        qh=[jnp.where(lane<64,q2,0).astype(q2.dtype),jnp.where(lane>=64,q2,0).astype(q2.dtype)]
        dh=[jnp.where(lane<64,do2,0).astype(q2.dtype),jnp.where(lane>=64,do2,0).astype(q2.dtype)]
        qt=q2.T; dot_=do2.T
        prod=(do2.astype(jnp.float32)*o2.astype(jnp.float32)).T
        dl=[jnp.sum(prod[h*64:(h+1)*64],axis=0,keepdims=True) for h in range(2)]
        lrow=[l_ref[0,0,h:h+1,qi*QB:(qi+1)*QB] for h in range(2)]
        start=start_ref[0,:,qi*QB:(qi+1)*QB]
        dqt_ref[...]=jnp.zeros_like(dqt_ref)
        def body(t,_,masked):
            b=t//per
            rel=(b^ctx) if xorder else b
            off=pl.multiple_of(rel*L+(t-b*per)*KB,KB)
            kt=k_ref[0,pl.ds(off,KB),:]
            vt=v_ref[0,pl.ds(off,KB),:]
            if masked:
                kpos=lax.broadcasted_iota(jnp.int32,(KB,1),0)+t*KB
                qpos=lax.broadcasted_iota(jnp.int32,(1,QB),1)+q0
                ok=(kpos<=qpos)&(kpos>=start)
            for h in range(2):
                hs=slice(h*64,(h+1)*64)
                s=dotg(kt,qh[h],1,1)
                dp=dotg(vt,dh[h],1,1)
                p=jnp.exp(s-lrow[h])
                if masked: p=jnp.where(ok,p,0.0)
                pb=p.astype(jnp.bfloat16)
                ds=(p*(dp-dl[h])).astype(jnp.bfloat16)
                dvt_ref[hs,pl.ds(off,KB)]+=dotg(dot_[hs],pb,1,1)
                dkt_ref[hs,pl.ds(off,KB)]+=dotg(qt[hs],ds,1,1)
                dqt_ref[hs,:]+=dotg(kt_ref[hs,pl.ds(off,KB)],ds,1,0)
            return 0
        lax.fori_loop(lo,f0,lambda t,c: body(t,c,True),0)
        lax.fori_loop(f0,f1,lambda t,c: body(t,c,False),0)
        lax.fori_loop(f1,hi,lambda t,c: body(t,c,True),0)
        dq_ref[0,qi*QB:(qi+1)*QB,:]=(dqt_ref[...].T).astype(dq_ref.dtype)*jnp.bfloat16(0.125)
    dk_ref[0]=dkt_ref[...].T.astype(dk_ref.dtype)
    dv_ref[0]=dvt_ref[...].T.astype(dv_ref.dtype)

def attn_bwd(meta,start,q,k,v,do,o,lse,*,QB=256,KB=256,xorder=True,nheads=17,r0=0):
    _,L,W=q.shape; T=k.shape[1]; NP=W//128; R=1
    kern=functools.partial(bwd_kernel,QB=QB,KB=KB,L=L,xorder=xorder,nheads=nheads,r0=r0)
    full=lambda r,p,m:(r+r0,0,p)
    return pl.pallas_call(kern,
        grid_spec=pltpu.PrefetchScalarGridSpec(num_scalar_prefetch=1,grid=(R,NP),
            in_specs=[pl.BlockSpec((1,1,L),lambda r,p,m:(r+r0,0,0)),
                      pl.BlockSpec((1,L,128),full),
                      pl.BlockSpec((1,T,128),full),
                      pl.BlockSpec((1,T,128),full),
                      pl.BlockSpec((1,L,128),full),
                      pl.BlockSpec((1,L,128),full),
                      pl.BlockSpec((1,1,2,L),lambda r,p,m:(r+r0,p,0,0))],
            out_specs=[pl.BlockSpec((1,L,128),lambda r,p,m:(r,0,p)),
                       pl.BlockSpec((1,T,128),lambda r,p,m:(r,0,p)),
                       pl.BlockSpec((1,T,128),lambda r,p,m:(r,0,p))],
            scratch_shapes=[pltpu.VMEM((128,T),jnp.bfloat16),pltpu.VMEM((128,QB),jnp.float32),
                            pltpu.VMEM((128,T),jnp.float32),pltpu.VMEM((128,T),jnp.float32)]),
        out_shape=[jax.ShapeDtypeStruct((R,L,W),jnp.bfloat16),jax.ShapeDtypeStruct((R,T,W),jnp.bfloat16),jax.ShapeDtypeStruct((R,T,W),jnp.bfloat16)],
        compiler_params=pltpu.CompilerParams(dimension_semantics=("arbitrary","arbitrary"),vmem_limit_bytes=48<<20),
        cost_estimate=pl.CostEstimate(flops=R*10*L*T*W,bytes_accessed=R*(3*L+4*T)*W*2,transcendentals=R*L*T*18),
        name="attn_bwd")(meta,start,q,k,v,do,o,lse)


def mm(pattern, a, b):
    return jnp.einsum(pattern, a, b, preferred_element_type=F32)


def unpack_kernel(w_ref, *outs, pieces, rows, halves):
    for half in range(halves):
        for out, (first, width, places, pad) in zip(outs, pieces):
            whole = [
                w_ref[s, 0, :, half * (w_ref.shape[3] // halves) + first : half * (w_ref.shape[3] // halves) + first + width]
                for s in range(w_ref.shape[0])
            ]
            joined = jnp.concatenate(whole, axis=1)
            if pad:
                zero = jnp.zeros((rows, pad), joined.dtype)
                step = joined.shape[1] // places
                joined = jnp.concatenate(
                    [x for i in range(places) for x in (joined[:, i * step : (i + 1) * step], zero)], axis=1
                )
            out[0, half] = joined


def layer_stats(v):
    middle = jnp.mean(v, axis=-1, keepdims=True)
    centred = v - middle
    inv = lax.rsqrt(jnp.mean(centred * centred, axis=-1, keepdims=True) + EPS)
    return centred * inv, inv


def norm_back(e, z, inv):
    return (e - jnp.mean(e, -1, keepdims=True) - z * jnp.mean(e * z, -1, keepdims=True)) * inv


def swap(x, axis, bit, needed):
    n = lax.axis_size(axis)
    return lax.ppermute(x, axis, [(d ^ bit, d) for d in range(n) if needed(d)])


def blocks_of(x, bits):
    found = {0: x}
    for bit in reversed(bits):
        for j in sorted(found):
            found[j | bit] = swap(found[j], "ctx", bit, lambda d, k=j | bit: (d ^ k) < d)
    return [found[j] for j in sorted(found)]


def blocks_back(parts, bits):
    held = dict(enumerate(parts))
    for bit in bits:
        for j in sorted(held):
            if j & bit:
                sent = held.pop(j)
                got = swap(sent, "ctx", bit, lambda d, k=j, b=bit: ((d ^ b) ^ k) < (d ^ b))
                held[j ^ bit] = held[j ^ bit] + got
    return held[0]


def ctx_sum_rows(g, bits):
    n = lax.axis_size("ctx")
    me = lax.axis_index("ctx")
    for bit in reversed(bits):
        half = g.shape[0] // 2
        mine = (me & bit) != 0
        low, high = g[:half], g[half:]
        got = lax.ppermute(jnp.where(mine, low, high), "ctx", [(d, d ^ bit) for d in range(n)])
        g = jnp.where(mine, high, low) + got
    return g


def slots_kernel(index_ref, g_ref, *refs, count, spans):
    outs, total = refs[:-1], refs[-1]
    total[...] = jnp.zeros_like(total)

    def one(i, carry):
        a = index_ref[i]
        total[a] = total[a] + g_ref[i].astype(F32)
        return carry

    lax.fori_loop(0, count, one, 0)
    for out, (first, width) in zip(outs, spans):
        out[...] = total[:, :, first : first + width]


def to_slots(index, g, adapters, widths):
    count, rank, wide = g.shape
    rows = 8
    spans, at = [], 0
    for w in widths:
        spans.append((at, w))
        at += w
    return pl.pallas_call(
        functools.partial(slots_kernel, count=count, spans=spans),
        grid_spec=pltpu.PrefetchScalarGridSpec(
            num_scalar_prefetch=1,
            grid=(rank // rows,),
            in_specs=[pl.BlockSpec((count, rows, wide), lambda i, m: (0, i, 0))],
            out_specs=[pl.BlockSpec((adapters, rows, w), lambda i, m: (0, i, 0)) for w in widths],
            scratch_shapes=[pltpu.VMEM((adapters, rows, wide), F32)],
        ),
        out_shape=[jax.ShapeDtypeStruct((adapters, rank, w), F32) for w in widths],
        compiler_params=pltpu.CompilerParams(vmem_limit_bytes=48 << 20),
        cost_estimate=pl.CostEstimate(
            flops=count * rank * wide, bytes_accessed=count * rank * wide * 2 + adapters * rank * wide * 4, transcendentals=0
        ),
        name="to_slots",
    )(index, g)


def per_device(
    tokens, segments, adapter_index, norm_gains, norm_shifts, head_biases, expand_bias, exit_biases,
    mixing_weight, output_weight, expand_weight, shrink_weight,
    entry_adapters, mixing_adapters, expand_adapters, hidden_adapters, exit_adapters, cotangent,
):
    micro, seqs, L, D = tokens.shape
    R = micro * seqs
    adapters, rank = mixing_adapters.shape[:2]
    FF = expand_bias.shape[0]
    C = lax.axis_size("ctx")
    S = lax.axis_size("seq")
    bits = [1 << i for i in range(C.bit_length() - 1)]
    me = lax.axis_index("ctx")
    T = C * L
    W = -(-D // 128) * 128
    pad = W - D

    rows = mixing_weight.shape[0]
    cm, co, ce = mixing_weight.shape[1], output_weight.shape[1], expand_weight.shape[1]
    first = jnp.concatenate([mixing_weight, output_weight], 1)
    first = jnp.concatenate([first[: rows // 2], first[rows // 2 :]], 1)
    second = jnp.concatenate([expand_weight[: rows // 2], expand_weight[rows // 2 :]], 1)
    third = shrink_weight.T
    g1 = lax.all_gather(first, BOTH)
    if second.shape[1] == third.shape[1]:
        g2 = lax.all_gather(jnp.concatenate([second, third], 0), BOTH)
        g2, g3 = g2[:, : rows // 2], g2[:, rows // 2 :]
    else:
        g2, g3 = lax.all_gather(second, BOTH), lax.all_gather(third, BOTH)

    def join(g, width):
        r = g.shape[1]
        g = g.reshape(S, C, r, 2, width).transpose(1, 3, 2, 0, 4)
        return g.reshape(C * 2 * r, S, width)

    w1 = join(g1, cm + co)
    w_mix = w1[:, :, :cm].reshape(D, 3 * D)
    w_out = w1[:, :, cm:].reshape(D, D)
    padded = lambda m: jnp.pad(m, [(0, 0)] * (m.ndim - 1) + [(0, pad)])
    w_q, w_k, w_v = (padded(w_mix[:, i * D : (i + 1) * D]) for i in range(3))
    w_exp = join(g2, ce).reshape(D, FF)
    w_shr_t = g3.reshape(S, C, D // S, FF // C).transpose(0, 2, 1, 3).reshape(D, FF)

    index = adapter_index.reshape(R)
    take = lambda table, axis: jnp.stack(
        [lax.dynamic_index_in_dim(table, index[r], axis, keepdims=False) for r in range(R)], axis
    )
    entry = take(entry_adapters, 1)
    mix_up = take(mixing_adapters, 0)
    exp_up = take(expand_adapters, 0)
    hid = take(hidden_adapters, 0)
    exit_up = take(exit_adapters, 1)
    m_q, m_k, m_v = (padded(mix_up[..., i * D : (i + 1) * D]) for i in range(3))
    all_index = lax.all_gather(index, "seq").reshape(S * R)

    seg = segments.reshape(R, L)
    seg_blocks = blocks_of(seg, bits)
    start = jnp.zeros((R, L), jnp.int32)
    for j, other in enumerate(seg_blocks):
        ok = (me ^ j) <= me
        start = start + jnp.sum(((other[:, None, :] < seg[:, :, None]) & ok).astype(jnp.int32), -1)
    QB = KB = min(512, L)
    meta = jnp.concatenate(
        [me[None].astype(jnp.int32)]
        + [start[r, (qi + e) * QB - e][None] for r in range(R) for qi in range(L // QB) for e in (0, 1)]
    )
    start = start[:, None, :]

    x = tokens.reshape(R, L, D).astype(F32)
    dy = cotangent.reshape(R, L, D)
    z1, inv1 = layer_stats(x)
    n1 = (z1 * norm_gains[0] + norm_shifts[0]).astype(BF)
    n1_all = jnp.concatenate(blocks_of(n1, bits), 1)
    l1_all = mm("rtd,rdk->rtk", n1_all, entry[0]).astype(BF)
    l1 = l1_all[:, :L]
    q = ((mm("rtd,de->rte", n1, w_q) + mm("rtk,rke->rte", l1, m_q) + padded(head_biases[0])) * 0.125).astype(BF)
    k = (mm("rtd,de->rte", n1_all, w_k) + mm("rtk,rke->rte", l1_all, m_k)).astype(BF)
    v = (mm("rtd,de->rte", n1_all, w_v) + mm("rtk,rke->rte", l1_all, m_v) + padded(head_biases[1])).astype(BF)

    o, lse = attn_fwd(meta, start, q, k, v, QB=QB, KB=KB)

    lo = mm("rtd,rdk->rtk", o, entry[1]).astype(BF)
    res = x + mm("rtd,de->rte", o, w_out) + mm("rtk,rke->rte", lo, exit_up[0]) + exit_biases[0]
    z2, inv2 = layer_stats(res)
    n2 = (z2 * norm_gains[1] + norm_shifts[1]).astype(BF)
    l3 = mm("rtd,rdk->rtk", n2, entry[2]).astype(BF)
    h = mm("rtd,df->rtf", n2, w_exp) + mm("rtk,rkf->rtf", l3, exp_up) + expand_bias
    c0 = 0.7978845608028654
    hh = h * h
    th = jnp.tanh(c0 * h * (1.0 + 0.044715 * hh))
    g = (0.5 * h * (1.0 + th)).astype(BF)
    slope = 0.5 * (1.0 + th) + 0.5 * h * (1.0 - th * th) * (c0 * (1.0 + 3 * 0.044715 * hh))
    l4 = mm("rtf,rfk->rtk", g, hid).astype(BF)
    out = res + mm("rtf,df->rtd", g, w_shr_t) + mm("rtk,rkd->rtd", l4, exit_up[1]) + exit_biases[1]
    layer_output = out.astype(BF).reshape(tokens.shape)

    dl4 = mm("rtd,rkd->rtk", dy, exit_up[1]).astype(BF)
    dg = mm("rtd,df->rtf", dy, w_shr_t) + mm("rtk,rfk->rtf", dl4, hid)
    dh = (dg * slope).astype(BF)
    dl3 = mm("rtf,rkf->rtk", dh, exp_up).astype(BF)
    dn2 = mm("rtf,df->rtd", dh, w_exp) + mm("rtk,rdk->rtd", dl3, entry[2])
    dr = dy.astype(F32) + norm_back(norm_gains[1] * dn2, z2, inv2)
    drb = dr.astype(BF)
    dl2 = mm("rtd,rkd->rtk", drb, exit_up[0]).astype(BF)
    do = (mm("rtd,ed->rte", drb, w_out) + mm("rtk,rdk->rtd", dl2, entry[1])).astype(BF)

    early = jnp.concatenate(
        [
            mm("rtk,rtd->rkd", dl2, o),
            mm("rtk,rtd->rkd", dl3, n2),
            mm("rtk,rtf->rkf", l3, dh),
            mm("rtk,rtf->rkf", dl4, g),
            mm("rtk,rtd->rkd", lo, drb),
            mm("rtk,rtd->rkd", l4, dy),
        ],
        -1,
    ).reshape(R * rank, -1)
    early = ctx_sum_rows(early, bits).astype(BF)
    early = lax.all_gather(early, BOTH).reshape(S * R, rank, -1)
    entry1_g, entry2_g, expand_g, hidden_g, exit0_g, exit1_g = to_slots(
        all_index, early, adapters, (D, D, FF, FF, D, D)
    )

    own, late = [], []
    for r in range(R):
        dq, dk, dv = attn_bwd(meta, start, q, k, v, do, o, lse, QB=QB, KB=KB, r0=r)
        dq, dk, dv = dq[0], dk[0], dv[0]
        dl1 = mm("te,ke->tk", dk, m_k[r]) + mm("te,ke->tk", dv, m_v[r])
        dl1 = jnp.concatenate([dl1[:L] + mm("te,ke->tk", dq, m_q[r]), dl1[L:]], 0).astype(BF)
        part = mm("te,de->td", dk, w_k) + mm("te,de->td", dv, w_v) + mm("tk,dk->td", dl1, entry[0, r])
        mine = part[:L] + mm("te,de->td", dq, w_q)
        others = part[L:].astype(BF)
        parts = [mine] + [others[(j - 1) * L : j * L] for j in range(1, C)]
        own.append(blocks_back(parts, bits))
        late.append(
            jnp.concatenate(
                [
                    mm("tk,te->ke", l1[r], dq)[:, :D],
                    mm("tk,te->ke", l1_all[r], dk)[:, :D],
                    mm("tk,te->ke", l1_all[r], dv)[:, :D],
                    mm("tk,td->kd", dl1, n1_all[r]),
                ],
                -1,
            )
        )
    late = ctx_sum_rows(jnp.concatenate(late, 0), bits).astype(BF)
    late = lax.all_gather(late, BOTH).reshape(S * R, rank, -1)
    mixing_g, entry0_g = to_slots(all_index, late, adapters, (3 * D, D))

    dn1 = jnp.stack(own)
    input_grad = (dr + norm_back(norm_gains[0] * dn1, z1, inv1)).astype(BF).reshape(tokens.shape)

    flip = lambda m: jnp.swapaxes(m, -1, -2)
    return (
        layer_output,
        input_grad,
        jnp.stack([flip(entry0_g), flip(entry1_g), flip(entry2_g)]),
        mixing_g,
        expand_g,
        flip(hidden_g),
        jnp.stack([exit0_g, exit1_g]),
    )


def solution(mesh):
    rows = P(None, "seq", "ctx", None)
    weight = P("ctx", "seq")
    in_specs = (
        (rows, P(None, "seq", "ctx"), P(None, "seq")) + (P(),) * 5 + (weight,) * 4 + (P(),) * 5 + (rows,)
    )
    out_specs = (rows, rows) + (P(),) * 5
    return jax.shard_map(per_device, mesh=mesh, in_specs=in_specs, out_specs=out_specs, check_vma=False)
```

time: 1470 us -> 989 us (0.67)
  waiting for transfers between devices: 688 us -> 117 us
  Pallas kernels: 0 us -> 156 us
  matrix products: 456 us -> 307 us
  starting transfers between devices: 1.07 us -> 122 us
  other arithmetic: 103 us -> 38.9 us
  local copies, waits for them, and re-layouts: 149 us -> 208 us
  blocking collectives: 29.6 us -> 10.9 us
  loops' own time: 18.2 us -> 0 us
    all_gather x10 -> x4, waiting for transfers between devices: 300 us -> 0.01 us  [the longest x1 0.01 us: per_device(): g1 = lax.all_gather(first, BOTH)]
    reduce_scatter x4 -> x0, waiting for transfers between devices: 213 us -> none  [the longest x2 164 us: per_device(): lax.psum_scatter(value_full.astype(jnp.bfloat16), 'ctx', scatter_dimensio...]
    psum x1 -> x0, waiting for transfers between devices: 172 us -> none  [per_device(): lax.psum((grad_totals[0], grad_totals[1], grad_totals[2], grad_totals[3],...]
    pallas_call x0 -> x5, Pallas kernels: none -> 156 us  [the longest x2 80.9 us: attn_bwd(): pl.pallas_call(kern, grid_spec=pltpu.PrefetchScalarGridSpec(num_scalar_pr...]
    dot_general x102 -> x53, matrix products: 456 us -> 307 us  [mm(): return jnp.einsum(pattern, a, b, preferred_element_type=F32)]
    ppermute x0 -> x16, starting transfers between devices: none -> 122 us  [the longest x4 101 us: ctx_sum_rows(): lax.ppermute(jnp.where(mine, low, high), 'ctx', [(d, d ^ bit) for d in ra...]
    ppermute x0 -> x16, waiting for transfers between devices: none -> 117 us  [the longest x12 98.2 us: swap(): return lax.ppermute(x, axis, [(d ^ bit, d) for d in range(n) if needed(d)])]
    reshape x0 -> x3, local copies, waits for them, and re-layouts: none -> 64.2 us  [the longest x2 47.6 us: join(): g = g.reshape(S, C, r, 2, width).transpose(1, 3, 2, 0, 4)]
  transfers between devices with their start and end apart: 15 -> 20, of which waited for: 10 -> 4; matrix products, arithmetic and copies ran while one was open for 32% -> 30% of each run, Pallas kernels for 0% -> 7%
where the time goes in v1:
time: 989 us; the launch traced here: 980 us
  matrix products  307 us (31%)
  local copies, waits for them, and re-layouts  208 us (21%)
  Pallas kernels  156 us (16%)
  starting transfers between devices  122 us (12%)
  waiting for transfers between devices  117 us (12%)
  other arithmetic  38.9 us (4%)
  between operations  20 us (2%)
  blocking collectives  10.9 us (1%)
    dot_general x53, matrix products, mm(): return jnp.einsum(pattern, a, b, preferred_element_type=F32)  307 us
    ppermute x4, starting transfers between devices, ctx_sum_rows(): lax.ppermute(jnp.where(mine, low, high), 'ctx', [(d, d ^ bit) for d in ra...  101 us
    ppermute x12, waiting for transfers between devices, swap(): return lax.ppermute(x, axis, [(d ^ bit, d) for d in range(n) if needed(d)])  98.2 us
    pallas_call x2, Pallas kernels, attn_bwd(): pl.pallas_call(kern, grid_spec=pltpu.PrefetchScalarGridSpec(num_scalar_pr...  80.9 us
    pallas_call x1, Pallas kernels, attn_fwd(): pl.pallas_call(kern, grid_spec=pltpu.PrefetchScalarGridSpec(num_scalar_pr...  65.8 us
    reshape x2, local copies, waits for them, and re-layouts, join(): g = g.reshape(S, C, r, 2, width).transpose(1, 3, 2, 0, 4)  47.6 us
    transpose x2, local copies, waits for them, and re-layouts, join(): g = g.reshape(S, C, r, 2, width).transpose(1, 3, 2, 0, 4)  23.6 us
    unnamed x205, local copies, waits for them, and re-layouts  21.5 us
  transfers between devices with their start and end apart: 20, of which 4 were waited for; matrix products, arithmetic and copies ran while one was open for 30% of the time, Pallas kernels for 7%

profile of v1, /device:TPU:5, one launch (start us, length us, event | category | flops | bytes accessed | tf_op | source)
XLA Modules:
  0.0 979.8 jit_solution(13278600924057644599)
XLA Ops:
  33.8 51.0 %collective-permute-done.4 = bf16[2,512,1088]{1,2,0:T(8,128)(2,1)S(1)} collective-permute-done((bf16[2,512,1088]{1,2,0:T(8,128)(2,1)}, bf16[2,512,1088]{1,2,0:T(8,128)(2,1)S(1)}, u32[]{:S(2)}, u32[]{:S(2)}) %collective-permute-start.4) | collective-permute-done | bytes 2228256 | tf_op jit(solution)/shard_map/ppermute | solution.py:204
  93.6 10.9 %all-reduce.6.index_ref = s32[16]{0:T(128)S(1)} all-reduce(s32[16]{0:T(128)S(1)} %bitcast_dynamic-update-slice_fusion), channel_id=4, replica_groups=mesh['seq'=8,'ctx'=4] {'seq'}, use_global_device_ids=true, to_apply=%add.6 | all-reduce | flops 16 | bytes 128 | tf_op jit(solution)/shard_map/reshape | solution.py:330
  109.2 3.9 pad_maximum_fusion
  116.6 7.8 fusion.84
  124.5 7.9 fusion.153
  132.4 23.8 %reshape.149 = bf16[8,4,136,2,544]{4,3,2,1,0:T(2,128)(2,1)} reshape(bf16[4352,1088]{1,0:T(8,128)(2,1)} %all-gather.10.cloned.1.call-done) | data formatting | bytes 18939904 | tf_op jit(solution)/shard_map/reshape | solution.py:309
  156.2 10.3 %copy.94 = bf16[4,2,136,8,544]{4,3,2,1,0:T(8,128)(2,1)S(1)} copy(bf16[4,2,136,8,544]{4,1,2,0,3:T(2,128)(2,1)} %bitcast.287) | data formatting | bytes 18939904 | tf_op jit(solution)/shard_map/transpose | solution.py:309
  166.5 3.9 slice.336
  174.0 12.3 %copy.95 = bf16[1088,8,408]{0,2,1:T(8,128)(2,1)} copy(bf16[1088,8,408]{2,1,0:T(8,128)(2,1)} %slice.336) | data formatting | bytes 14204928 | tf_op jit(solution)/shard_map/slice | solution.py:313
  186.3 6.5 fusion.144
  192.8 5.2 copy.119
  198.0 5.1 copy.120
  203.1 6.8 copy.99
  209.9 6.2 fusion.36
  216.9 22.6 %add_convert_fusion.1.k_ref = bf16[2,2048,1152]{2,1,0:T(8,128)(2,1)} fusion(f32[2,2048,1152]{2,1,0:T(8,128)} %fusion.84, bf16[2,2048,1088]{1,2,0:T(8,128)(2,1)} %copy-done.6, bf16[1088,1088]{1,0:T(8,128)(2,1)} %copy.119), kind=kOutput, calls=%fused_computation.1 | convolution fusion | flops 10277093376 | bytes 39591936 | tf_op jit(solution)/shard_map/rtd,de->rte/dot_general | solution.py:171
  239.6 22.9 %add_convert_fusion.v_ref = bf16[2,2048,1152]{2,1,0:T(8,128)(2,1)} fusion(f32[2,2048,1152]{2,1,0:T(8,128)} %fusion.153, bf16[2,2048,1088]{1,2,0:T(8,128)(2,1)} %copy-done.6, f32[1152]{0:T(1024)S(1)} %pad.34, bf16[1088,1088]{1,0:T(8,128)(2,1)} %copy.120), kind=kOutput, calls=%fused_computation | convolution fusion | flops 10281811968 | bytes 39596544 | tf_op jit(solution)/shard_map/rtd,de->rte/dot_general | solution.py:171
  262.4 65.8 %attn_fwd.1 = (bf16[2,512,1088]{2,1,0:T(8,128)(2,1)S(1)}, f32[2,9,2,512]{3,2,1,0:T(2,128)S(1)}) custom-call(s32[5]{0:T(128)S(1)} %concatenate.35.meta_ref, s32[2,1,512]{2,1,0:T(1,128)S(1)} %add.261.start_ref, bf16[2,512,1152]{2,1,0:T(8,128)(2,1)S(1)} %fusion.33.q_ref, bf16[2,2048,1152]{2,1,0:T(8,128)(2,1)} %add_convert_fusion.1.k_ref, ...), custom_call_target="tpu_custom_call" | custom-call | flops 9663676416 | bytes 23592960 | tf_op jit(solution)/shard_map/attn_fwd/pallas_call | solution.py:78
  335.7 8.6 fusion.67
  344.3 15.0 %fusion.143 = (bf16[32,136,1088]{2,1,0:T(8,128)(2,1)}, bf16[32,136,1088]{2,1,0:T(8,128)(2,1)}) fusion(bf16[32,272,1088]{2,1,0:T(8,128)(2,1)} %bitcast.308), kind=kLoop, calls=%fused_computation.251 | loop fusion | bytes 37879808 | tf_op jit(solution)/shard_map/slice | solution.py:303
  359.2 23.8 %reshape.153 = bf16[8,4,136,2,544]{4,3,2,1,0:T(2,128)(2,1)} reshape(bf16[32,136,1088]{2,1,0:T(8,128)(2,1)} %get-tuple-element.91) | data formatting | bytes 18939904 | tf_op jit(solution)/shard_map/reshape | solution.py:309
  383.0 13.2 %copy.102 = bf16[4,2,136,8,544]{4,3,2,1,0:T(8,128)(2,1)} copy(bf16[4,2,136,8,544]{4,1,2,0,3:T(2,128)(2,1)} %bitcast.288) | data formatting | bytes 18939904 | tf_op jit(solution)/shard_map/transpose | solution.py:309
  396.2 18.1 %reshape.181 = bf16[1088,4352,1]{1,0,2:T(8,128)(2,1)} reshape(bf16[4,2,136,8,544]{4,3,2,1,0:T(8,128)(2,1)} %copy.102) | data formatting | bytes 18939904 | tf_op jit(solution)/shard_map/reshape;reshape | solution.py:317
  414.4 9.5 copy.103
  423.9 16.6 %reshape.182 = bf16[1088,4352,1]{1,0,2:T(8,128)(2,1)} reshape(bf16[8,136,4,1088]{3,2,1,0:T(4,128)(2,1)} %copy.103) | data formatting | bytes 18939904 | tf_op jit(solution)/shard_map/reshape | solution.py:318
  440.5 19.3 %fusion.45 = f32[4352,2,512]{0,2,1:T(8,128)} fusion(bf16[1088,4352,1]{1,0,2:T(8,128)(2,1)} %reshape.182, bf16[2,1,512,1088]{2,3,1,0:T(8,128)(2,1)} %param.35), kind=kOutput, calls=%fused_computation.77 | convolution fusion | flops 9697230848 | bytes 29523968 | tf_op jit(solution)/shard_map/rtd,df->rtf/dot_general | solution.py:171
  459.8 25.9 %multiply_convert_fusion = (bf16[2,512,4352]{2,1,0:T(8,128)(2,1)}, f32[2,512,4352]{2,1,0:T(8,128)}) fusion(f32[4352]{0:T(1024)S(1)} %copy-done.70, f32[2,512,4352]{2,1,0:T(8,128)} %fusion.67, bf16[2,512,1088]{1,2,0:T(8,128)(2,1)S(1)} %add_convert_fusion.2, bf16[1088,4352,1]{1,0,2:T(8,128)(2,1)} %reshape.181), kind=kOutput, calls=%fused_computation.5 | convolution fusion | flops 9746251776 | bytes 56280064 | tf_op jit(solution)/shard_map/rtd,df->rtf/dot_general | solution.py:171
  485.7 19.6 %fusion.1 = bf16[2,512,4352]{2,1,0:T(8,128)(2,1)} fusion(f32[4352,2,512]{0,2,1:T(8,128)} %fusion.45, f32[2,512,4352]{2,1,0:T(8,128)} %get-tuple-element.121, bf16[2,16,512]{2,1,0:T(8,128)(2,1)S(1)} %copy-done.41, bf16[1,4352,16]{1,2,0:T(8,128)(2,1)S(1)} %copy-done.40, bf16[1,4352,16]{1,2,0:T(8,128)(2,1)S(1)} %copy-done.39), kind=kOutput, calls=%fused_computation.4 | convolution fusion | flops 227418112 | bytes 44875776 | tf_op jit(solution)/shard_map/rtk,rfk->rtf/dot_general | solution.py:171
  505.3 6.1 convolution_convert_fusion.1
  514.3 15.9 %fusion.142 = (f32[2,512]{1,0:T(2,128)S(1)}, f32[2,512]{1,0:T(2,128)S(1)}, f32[2,512,1088]{1,2,0:T(8,128)}) fusion(f32[2,512]{1,0:T(2,128)S(1)} %add_rsqrt_fusion, f32[2,512,1088]{1,2,0:T(8,128)} %copy-done.7, f32[2,512]{1,0:T(2,128)S(1)} %broadcast_multiply_fusion.4, f32[2,512,1088]{1,2,0:T(8,128)} %fusion.137, bf16[2,512,4352]{2,1,0:T(8,128)(2,1)S(1)} %copy-done.9, ...), kind=kOutput, calls=%fused_computation.250 | convolution fusion | flops 9705027584 | bytes 31772928 | tf_op jit(solution)/shard_map/rtf,df->rtd/dot_general | solution.py:171
  544.4 41.0 %attn_bwd.3 = (bf16[1,512,1152]{2,1,0:T(8,128)(2,1)S(1)}, bf16[1,2048,1152]{2,1,0:T(8,128)(2,1)}, bf16[1,2048,1152]{2,1,0:T(8,128)(2,1)}) custom-call(s32[5]{0:T(128)S(1)} %concatenate.35.meta_ref, s32[2,1,512]{2,1,0:T(1,128)S(1)} %add.261.start_ref, bf16[2,512,1152]{2,1,0:T(8,128)(2,1)S(1)} %copy-done.3, bf16[2,2048,1152]{2,1,0:T(8,128)(2,1)} %add_convert_fusion.1.k_ref, ...), custom_call_target="tpu_custom_call" | custom-call | flops 12079595520 | bytes 22413312 | tf_op jit(solution)/shard_map/attn_bwd/pallas_call | solution.py:150
  585.5 39.9 %attn_bwd.2 = (bf16[1,512,1152]{2,1,0:T(8,128)(2,1)S(1)}, bf16[1,2048,1152]{2,1,0:T(8,128)(2,1)}, bf16[1,2048,1152]{2,1,0:T(8,128)(2,1)}) custom-call(s32[5]{0:T(128)S(1)} %concatenate.35.meta_ref, s32[2,1,512]{2,1,0:T(1,128)S(1)} %add.261.start_ref, bf16[2,512,1152]{2,1,0:T(8,128)(2,1)S(1)} %copy-done.3, bf16[2,2048,1152]{2,1,0:T(8,128)(2,1)} %add_convert_fusion.1.k_ref, ...), custom_call_target="tpu_custom_call" | custom-call | flops 12079595520 | bytes 22413312 | tf_op jit(solution)/shard_map/attn_bwd/pallas_call | solution.py:150
  627.8 5.0 fusion.156
  632.8 6.0 convolution_convert_fusion.2
  642.4 3.8 fusion.90
  671.4 99.0 %collective-permute-start.12 = (f32[16,4352]{1,0:T(8,128)}, f32[16,4352]{1,0:T(8,128)}, u32[]{:S(2)}, u32[]{:S(2)}) collective-permute-start(f32[16,4352]{1,0:T(8,128)} %broadcast_select_fusion), channel_id=1, source_target_pairs={{0,2},{1,3},{2,0},{3,1},{4,6},{5,7},{6,4},{7,5},{8,10},{9,11},{10,... | collective-permute-start | bytes 835592 | tf_op jit(solution)/shard_map/ppermute | solution.py:233
  776.3 11.2 %fusion.51 = f32[2048,1088]{0,1:T(8,128)} fusion(bf16[1088,1088]{1,0:T(8,128)(2,1)} %copy.119, bf16[1,2048,1152]{2,1,0:T(8,128)(2,1)} %get-tuple-element.28), kind=kOutput, calls=%fused_computation.89 | convolution fusion | flops 5133828096 | bytes 15998976 | tf_op jit(solution)/shard_map/te,de->td/dot_general | solution.py:171
  789.3 18.6 %collective-permute-done.14 = f32[16,13056]{1,0:T(8,128)S(1)} collective-permute-done((f32[16,13056]{1,0:T(8,128)}, f32[16,13056]{1,0:T(8,128)S(1)}, u32[]{:S(2)}, u32[]{:S(2)}) %collective-permute-start.14) | collective-permute-done | bytes 835616 | tf_op jit(solution)/shard_map/ppermute | solution.py:233
  811.0 12.1 %convolution_add_fusion.2 = f32[2048,1088]{0,1:T(8,128)} fusion(f32[2048,1088]{0,1:T(8,128)} %fusion.51, bf16[1088,1088]{1,0:T(8,128)(2,1)S(1)} %copy-done.22, bf16[1,2048,1152]{2,1,0:T(8,128)(2,1)} %get-tuple-element.29), kind=kOutput, calls=%fused_computation.10 | convolution fusion | flops 5136056320 | bytes 24911872 | tf_op jit(solution)/shard_map/te,de->td/dot_general | solution.py:171
  823.9 8.5 fusion.151
  839.0 10.9 %fusion.53 = f32[2048,1088]{0,1:T(8,128)} fusion(bf16[1088,1088]{1,0:T(8,128)(2,1)S(1)} %copy-done.21, bf16[1,2048,1152]{2,1,0:T(8,128)(2,1)} %get-tuple-element.25), kind=kOutput, calls=%fused_computation.91 | convolution fusion | flops 5133828096 | bytes 15998976 | tf_op jit(solution)/shard_map/te,de->td/dot_general | solution.py:171
  849.9 10.7 %convolution_add_fusion.3 = f32[2048,1088]{0,1:T(8,128)} fusion(f32[2048,1088]{0,1:T(8,128)} %fusion.53, bf16[1088,1088]{1,0:T(8,128)(2,1)S(1)} %copy-done.23, bf16[1,2048,1152]{2,1,0:T(8,128)(2,1)S(1)} %bitcast.294), kind=kOutput, calls=%fused_computation.11 | convolution fusion | flops 5136056320 | bytes 24911872 | tf_op jit(solution)/shard_map/te,de->td/dot_general | solution.py:171
  860.6 8.5 fusion.152
  876.9 14.5 %fusion.35 = bf16[2,1,512,1088]{2,3,1,0:T(8,128)(2,1)} fusion(f32[2,512,1088]{1,2,0:T(8,128)} %fusion.94, f32[2,512,1088]{1,2,0:T(8,128)S(1)} %bitcast.276, bf16[2,512,4352]{2,1,0:T(8,128)(2,1)S(1)} %bitcast.284, bf16[1088,4352,1]{1,0,2:T(8,128)(2,1)} %reshape.182, f32[1088]{0:T(1024)S(1)} %copy-done.65), kind=kOutput, calls=%fused_computation.63 | convolution fusion | flops 9701687296 | bytes 29528320 | tf_op jit(solution)/shard_map/rtf,df->rtd/dot_general | solution.py:171
  891.4 4.2 convolution_add_fusion.9
  901.7 4.3 convolution_add_fusion.10
  906.0 25.4 %collective-permute-done.11 = bf16[512,1088]{0,1:T(8,128)(2,1)S(1)} collective-permute-done((bf16[512,1088]{0,1:T(8,128)(2,1)S(1)}, bf16[512,1088]{0,1:T(8,128)(2,1)S(1)}, u32[]{:S(2)}, u32[]{:S(2)}) %collective-permute-start.11) | collective-permute-done | bytes 1114144 | tf_op jit(solution)/shard_map/ppermute | solution.py:204
  933.4 21.8 %collective-permute-done.8 = bf16[512,1088]{0,1:T(8,128)(2,1)S(1)} collective-permute-done((bf16[512,1088]{0,1:T(8,128)(2,1)S(1)}, bf16[512,1088]{0,1:T(8,128)(2,1)S(1)}, u32[]{:S(2)}, u32[]{:S(2)}) %collective-permute-start.8) | collective-permute-done | bytes 1114144 | tf_op jit(solution)/shard_map/ppermute | solution.py:204
  964.2 6.4 to_slots.3
  (346 shorter events, 143.8 us)
Async XLA Ops:
  7.2 125.2 %all-gather.10.cloned.1.call-start = ((), (), s32[]{:S(2)}) async-start(), calls=%async_computation | async-start | bytes 10340352 | tf_op jit(solution)/shard_map/all_gather | solution.py:300
  11.2 333.1 %all-gather.12.cloned.1.call-start = ((), (), s32[]{:S(2)}) async-start(), calls=%async_computation.1 | async-start | bytes 20680704 | tf_op jit(solution)/shard_map/all_gather | solution.py:302
  14.2 945.9 %all-gather.14.cloned.1.call-start = ((), (), s32[]{:S(2)}) async-start(), calls=%async_computation.2 | async-start | bytes 2297856 | tf_op jit(solution)/shard_map/all_gather | solution.py:423
  14.8 74.8 %copy-start.57 = (f32[2,512]{1,0:T(2,128)}, f32[2,512]{1,0:T(2,128)S(1)}, u32[]{:S(2)}) copy-start(f32[2,512]{1,0:T(2,128)S(1)} %broadcast_multiply_fusion.5) | copy-start | bytes 12292
  15.4 76.8 %copy-start.63 = (f32[2,1088]{1,0:T(2,128)S(1)}, f32[2,1088]{1,0:T(2,128)}, u32[]{:S(2)}) copy-start(f32[2,1088]{1,0:T(2,128)} %param.25) | copy-start | bytes 26116
  15.4 78.1 %copy-start.64 = (f32[2,1088]{1,0:T(2,128)S(1)}, f32[2,1088]{1,0:T(2,128)}, u32[]{:S(2)}) copy-start(f32[2,1088]{1,0:T(2,128)} %param.23) | copy-start | bytes 26116
  17.7 67.2 %collective-permute-start.4 = (bf16[2,512,1088]{1,2,0:T(8,128)(2,1)}, bf16[2,512,1088]{1,2,0:T(8,128)(2,1)S(1)}, u32[]{:S(2)}, u32[]{:S(2)}) collective-permute-start(bf16[2,512,1088]{1,2,0:T(8,128)(2,1)} %fusion.24), channel_id=1, source_target_pairs={{0,2},{1,3},{4,6},{5,7},{8,10},{9,11},{12,14},{13,15},{16,18},{17,... | collective-permute-start | bytes 6684680 | tf_op jit(solution)/shard_map/ppermute | solution.py:204
  20.9 83.6 %collective-permute-start = (s32[2,512]{1,0:T(2,128)S(1)}, s32[2,512]{1,0:T(2,128)S(1)}, u32[]{:S(2)}, u32[]{:S(2)}) collective-permute-start(s32[2,512]{1,0:T(2,128)S(1)} %bitcast.313), channel_id=1, source_target_pairs={{0,1},{2,3},{4,5},{6,7},{8,9},{10,11},{12,13},{14,15},{16,17},{18,... | collective-permute-start | bytes 12296 | tf_op jit(solution)/shard_map/ppermute | solution.py:204
  22.2 70.7 %collective-permute-start.1 = (s32[2,512]{1,0:T(2,128)S(1)}, s32[2,512]{1,0:T(2,128)S(1)}, u32[]{:S(2)}, u32[]{:S(2)}) collective-permute-start(s32[2,512]{1,0:T(2,128)S(1)} %bitcast.314), channel_id=1, source_target_pairs={{0,2},{1,3},{4,6},{5,7},{8,10},{9,11},{12,14},{13,15},{16,18},{17,... | collective-permute-start | bytes 12296 | tf_op jit(solution)/shard_map/ppermute | solution.py:204
  23.5 85.7 %collective-permute-start.3 = (bf16[2,512,1088]{1,2,0:T(8,128)(2,1)}, bf16[2,512,1088]{1,2,0:T(8,128)(2,1)}, u32[]{:S(2)}, u32[]{:S(2)}) collective-permute-start(bf16[2,512,1088]{1,2,0:T(8,128)(2,1)} %fusion.24), channel_id=1, source_target_pairs={{0,1},{2,3},{4,5},{6,7},{8,9},{10,11},{12,13},{14,15},{16,17},{18,... | collective-permute-start | bytes 6684680 | tf_op jit(solution)/shard_map/ppermute | solution.py:204
  31.7 82.7 %copy-start.31 = (bf16[2,16,1088]{2,1,0:T(8,128)(2,1)}, bf16[2,16,1088]{2,1,0:T(8,128)(2,1)S(1)}, u32[]{:S(2)}) copy-start(bf16[2,16,1088]{2,1,0:T(8,128)(2,1)S(1)} %fusion.74) | copy-start | bytes 208900
  32.7 299.4 %copy-start.26 = (bf16[2,1,16,1088]{3,2,1,0:T(8,128)(2,1)}, bf16[2,1,16,1088]{3,2,1,0:T(8,128)(2,1)S(1)}, u32[]{:S(2)}) copy-start(bf16[2,1,16,1088]{3,2,1,0:T(8,128)(2,1)S(1)} %get-tuple-element.106) | copy-start | bytes 208900
  32.7 299.4 %copy-start.28 = (bf16[2,1,16,1088]{3,2,1,0:T(8,128)(2,1)}, bf16[2,1,16,1088]{3,2,1,0:T(8,128)(2,1)S(1)}, u32[]{:S(2)}) copy-start(bf16[2,1,16,1088]{3,2,1,0:T(8,128)(2,1)S(1)} %get-tuple-element.107) | copy-start | bytes 208900
  33.8 90.6 %copy-start.37 = (bf16[2,16,1152]{2,1,0:T(8,128)(2,1)}, bf16[2,16,1152]{2,1,0:T(8,128)(2,1)S(1)}, u32[]{:S(2)}) copy-start(bf16[2,16,1152]{2,1,0:T(8,128)(2,1)S(1)} %get-tuple-element.110) | copy-start | bytes 221188
  33.8 182.2 %copy-start.35 = (bf16[2,16,1152]{2,1,0:T(8,128)(2,1)}, bf16[2,16,1152]{2,1,0:T(8,128)(2,1)S(1)}, u32[]{:S(2)}) copy-start(bf16[2,16,1152]{2,1,0:T(8,128)(2,1)S(1)} %get-tuple-element.111) | copy-start | bytes 221188
  84.8 24.4 %collective-permute-start.5 = (bf16[2,512,1088]{1,2,0:T(8,128)(2,1)S(1)}, bf16[2,512,1088]{1,2,0:T(8,128)(2,1)}, u32[]{:S(2)}, u32[]{:S(2)}) collective-permute-start(bf16[2,512,1088]{1,2,0:T(8,128)(2,1)S(1)} %collective-permute-done.4), channel_id=1, source_target_pairs={{3,2},{2,3},{7,6},{6,7},{11,10},{10,11},{15,14},{14,15},{19,18},{1... | collective-permute-start | bytes 6684680 | tf_op jit(solution)/shard_map/ppermute | solution.py:204
  92.9 11.7 %collective-permute-start.2 = (s32[2,512]{1,0:T(2,128)S(1)}, s32[2,512]{1,0:T(2,128)S(1)}, u32[]{:S(2)}, u32[]{:S(2)}) collective-permute-start(s32[2,512]{1,0:T(2,128)S(1)} %collective-permute-done.1), channel_id=1, source_target_pairs={{3,2},{2,3},{7,6},{6,7},{11,10},{10,11},{15,14},{14,15},{19,18},{1... | collective-permute-start | bytes 12296 | tf_op jit(solution)/shard_map/ppermute | solution.py:204
  116.6 99.5 %copy-start.19 = (bf16[2,2048,16]{1,2,0:T(8,128)(2,1)}, bf16[2,2048,16]{1,2,0:T(8,128)(2,1)S(1)}, u32[]{:S(2)}) copy-start(bf16[2,2048,16]{1,2,0:T(8,128)(2,1)S(1)} %convolution_convert_fusion) | copy-start | bytes 393220
  216.9 45.5 %copy-start.2 = (bf16[2,512,1152]{2,1,0:T(8,128)(2,1)}, bf16[2,512,1152]{2,1,0:T(8,128)(2,1)S(1)}, u32[]{:S(2)}) copy-start(bf16[2,512,1152]{2,1,0:T(8,128)(2,1)S(1)} %fusion.33.q_ref) | copy-start | bytes 7077892
  262.4 66.5 %copy-start.11 = (bf16[2,1,512,1088]{2,3,1,0:T(8,128)(2,1)S(1)}, bf16[2,1,512,1088]{2,3,1,0:T(8,128)(2,1)}, u32[]{:S(2)}) copy-start(bf16[2,1,512,1088]{2,3,1,0:T(8,128)(2,1)} %param.18) | copy-start | bytes 6684676
  262.4 66.5 %copy-start.24 = (bf16[1088,8,136]{0,2,1:T(8,128)(2,1)S(1)}, bf16[1088,8,136]{0,2,1:T(8,128)(2,1)}, u32[]{:S(2)}) copy-start(bf16[1088,8,136]{0,2,1:T(8,128)(2,1)} %copy.99) | copy-start | bytes 7102468
  335.3 124.5 %copy-start.13 = (bf16[2,512,1088]{1,2,0:T(8,128)(2,1)}, bf16[2,512,1088]{1,2,0:T(8,128)(2,1)S(1)}, u32[]{:S(2)}) copy-start(bf16[2,512,1088]{1,2,0:T(8,128)(2,1)S(1)} %add_convert_fusion.2) | copy-start | bytes 6684676
  459.8 25.9 %copy-start.39 = (bf16[1,4352,16]{1,2,0:T(8,128)(2,1)S(1)}, bf16[1,4352,16]{1,2,0:T(8,128)(2,1)}, u32[]{:S(2)}) copy-start(bf16[1,4352,16]{1,2,0:T(8,128)(2,1)} %get-tuple-element.98) | copy-start | bytes 417796
  459.8 25.9 %copy-start.40 = (bf16[1,4352,16]{1,2,0:T(8,128)(2,1)S(1)}, bf16[1,4352,16]{1,2,0:T(8,128)(2,1)}, u32[]{:S(2)}) copy-start(bf16[1,4352,16]{1,2,0:T(8,128)(2,1)} %get-tuple-element.99) | copy-start | bytes 417796
  459.8 25.9 %copy-start.41 = (bf16[2,16,512]{2,1,0:T(8,128)(2,1)S(1)}, bf16[2,16,512]{2,1,0:T(8,128)(2,1)}, u32[]{:S(2)}) copy-start(bf16[2,16,512]{2,1,0:T(8,128)(2,1)} %fusion.60) | copy-start | bytes 98308
  505.3 24.9 %slice-start.3 = ((s8[4456448]{0:T(1024)(128)(4,1)}), s8[4194304]{0:T(1024)(128)(4,1)S(1)}, s32[]{:S(2)}) async-start(s8[4456448]{0:T(1024)(128)(4,1)} %bitcast.273), calls=%async_computation.7 | async-start | bytes 8388608
  585.5 39.9 %copy-start.1 = (bf16[2,512,1088]{2,1,0:T(8,128)(2,1)S(1)}, bf16[2,512,1088]{2,1,0:T(8,128)(2,1)}, u32[]{:S(2)}) copy-start(bf16[2,512,1088]{2,1,0:T(8,128)(2,1)} %copy-done) | copy-start | bytes 6684676
  585.5 41.0 %copy-start.14 = (bf16[2,512,1088]{1,2,0:T(8,128)(2,1)S(1)}, bf16[2,512,1088]{1,2,0:T(8,128)(2,1)}, u32[]{:S(2)}) copy-start(bf16[2,512,1088]{1,2,0:T(8,128)(2,1)} %copy-done.13) | copy-start | bytes 6684676
  671.4 103.7 %collective-permute-start.12 = (f32[16,4352]{1,0:T(8,128)}, f32[16,4352]{1,0:T(8,128)}, u32[]{:S(2)}, u32[]{:S(2)}) collective-permute-start(f32[16,4352]{1,0:T(8,128)} %broadcast_select_fusion), channel_id=1, source_target_pairs={{0,2},{1,3},{2,0},{3,1},{4,6},{5,7},{6,4},{7,5},{8,10},{9,11},{10,... | collective-permute-start | bytes 835592 | tf_op jit(solution)/shard_map/ppermute | solution.py:233
  776.2 12.3 %collective-permute-start.13 = (f32[8,4352]{1,0:T(8,128)S(1)}, f32[8,4352]{1,0:T(8,128)S(1)}, u32[]{:S(2)}, u32[]{:S(2)}) collective-permute-start(f32[8,4352]{1,0:T(8,128)S(1)} %slice_select_fusion.2), channel_id=1, source_target_pairs={{0,1},{1,0},{2,3},{3,2},{4,5},{5,4},{6,7},{7,6},{8,9},{9,8},{10,11... | collective-permute-start | bytes 417800 | tf_op jit(solution)/shard_map/ppermute | solution.py:233
  787.5 20.4 %collective-permute-start.14 = (f32[16,13056]{1,0:T(8,128)}, f32[16,13056]{1,0:T(8,128)S(1)}, u32[]{:S(2)}, u32[]{:S(2)}) collective-permute-start(f32[16,13056]{1,0:T(8,128)} %select_bitcast_fusion), channel_id=1, source_target_pairs={{0,2},{1,3},{2,0},{3,1},{4,6},{5,7},{6,4},{7,5},{8,10},{9,11},{10,... | collective-permute-start | bytes 2506760 | tf_op jit(solution)/shard_map/ppermute | solution.py:233
  789.2 175.0 %all-gather.16.cloned.1.call-start = ((), (), s32[]{:S(2)}) async-start(), calls=%async_computation.3 | async-start | bytes 6893568 | tf_op jit(solution)/shard_map/all_gather | solution.py:395
  809.6 13.5 %collective-permute-start.15 = (f32[8,13056]{1,0:T(8,128)S(1)}, f32[8,13056]{1,0:T(8,128)S(1)}, u32[]{:S(2)}, u32[]{:S(2)}) collective-permute-start(f32[8,13056]{1,0:T(8,128)S(1)} %slice_select_fusion.1), channel_id=1, source_target_pairs={{0,1},{1,0},{2,3},{3,2},{4,5},{5,4},{6,7},{7,6},{8,9},{9,8},{10,11... | collective-permute-start | bytes 1253384 | tf_op jit(solution)/shard_map/ppermute | solution.py:233
  833.9 61.7 %collective-permute-start.10 = (bf16[512,1088]{0,1:T(8,128)(2,1)}, bf16[512,1088]{0,1:T(8,128)(2,1)}, u32[]{:S(2)}, u32[]{:S(2)}) collective-permute-start(bf16[512,1088]{0,1:T(8,128)(2,1)} %get-tuple-element.97), channel_id=1, source_target_pairs={{3,2},{2,3},{7,6},{6,7},{11,10},{10,11},{15,14},{14,15},{19,18},{1... | collective-permute-start | bytes 3342344 | tf_op jit(solution)/shard_map/ppermute | solution.py:204
  835.7 70.3 %collective-permute-start.9 = (bf16[512,1088]{0,1:T(8,128)(2,1)}, bf16[512,1088]{0,1:T(8,128)(2,1)}, u32[]{:S(2)}, u32[]{:S(2)}) collective-permute-start(bf16[512,1088]{0,1:T(8,128)(2,1)} %get-tuple-element.96), channel_id=1, source_target_pairs={{1,0},{3,2},{5,4},{7,6},{9,8},{11,10},{13,12},{15,14},{17,16},{19,... | collective-permute-start | bytes 3342344 | tf_op jit(solution)/shard_map/ppermute | solution.py:204
  839.0 37.9 %slice-start.5 = ((s8[4456448]{0:T(1024)(128)(4,1)}), s8[4194304]{0:T(1024)(128)(4,1)S(1)}, s32[]{:S(2)}) async-start(s8[4456448]{0:T(1024)(128)(4,1)} %bitcast.275), calls=%async_computation.9 | async-start | bytes 8388608
  849.9 27.0 %slice-start.6 = ((s8[4456448]{0:T(1024)(128)(4,1)}), s8[262144]{0:T(1024)(128)(4,1)S(1)}, s32[]{:S(2)}) async-start(s8[4456448]{0:T(1024)(128)(4,1)} %bitcast.275), calls=%async_computation.10 | async-start | bytes 524288
  849.9 27.0 %slice-start.14 = ((s8[8912896]{0:T(1024)(128)(4,1)}), s8[4194304]{0:T(1024)(128)(4,1)S(1)}, s32[]{:S(2)}) async-start(s8[8912896]{0:T(1024)(128)(4,1)} %bitcast.283), calls=%async_computation.18 | async-start | bytes 8388608
  849.9 27.0 %slice-start.15 = ((s8[8912896]{0:T(1024)(128)(4,1)}), s8[4194304]{0:T(1024)(128)(4,1)S(1)}, s32[]{:S(2)}) async-start(s8[8912896]{0:T(1024)(128)(4,1)} %bitcast.283), calls=%async_computation.19 | async-start | bytes 8388608
  870.7 28.0 %collective-permute-start.7 = (bf16[512,1088]{0,1:T(8,128)(2,1)}, bf16[512,1088]{0,1:T(8,128)(2,1)}, u32[]{:S(2)}, u32[]{:S(2)}) collective-permute-start(bf16[512,1088]{0,1:T(8,128)(2,1)} %get-tuple-element.95), channel_id=1, source_target_pairs={{3,2},{2,3},{7,6},{6,7},{11,10},{10,11},{15,14},{14,15},{19,18},{1... | collective-permute-start | bytes 3342344 | tf_op jit(solution)/shard_map/ppermute | solution.py:204
  872.4 61.0 %collective-permute-start.6 = (bf16[512,1088]{0,1:T(8,128)(2,1)}, bf16[512,1088]{0,1:T(8,128)(2,1)S(1)}, u32[]{:S(2)}, u32[]{:S(2)}) collective-permute-start(bf16[512,1088]{0,1:T(8,128)(2,1)} %get-tuple-element.94), channel_id=1, source_target_pairs={{1,0},{3,2},{5,4},{7,6},{9,8},{11,10},{13,12},{15,14},{17,16},{19,... | collective-permute-start | bytes 3342344 | tf_op jit(solution)/shard_map/ppermute | solution.py:204
  897.4 34.0 %collective-permute-start.11 = (bf16[512,1088]{0,1:T(8,128)(2,1)S(1)}, bf16[512,1088]{0,1:T(8,128)(2,1)S(1)}, u32[]{:S(2)}, u32[]{:S(2)}) collective-permute-start(bf16[512,1088]{0,1:T(8,128)(2,1)S(1)} %slice_add_fusion), channel_id=1, source_target_pairs={{2,0},{3,1},{6,4},{7,5},{10,8},{11,9},{14,12},{15,13},{18,16},{19,... | collective-permute-start | bytes 3342344 | tf_op jit(solution)/shard_map/ppermute | solution.py:204
  900.4 54.7 %collective-permute-start.8 = (bf16[512,1088]{0,1:T(8,128)(2,1)S(1)}, bf16[512,1088]{0,1:T(8,128)(2,1)S(1)}, u32[]{:S(2)}, u32[]{:S(2)}) collective-permute-start(bf16[512,1088]{0,1:T(8,128)(2,1)S(1)} %slice_add_fusion.1), channel_id=1, source_target_pairs={{2,0},{3,1},{6,4},{7,5},{10,8},{11,9},{14,12},{15,13},{18,16},{19,... | collective-permute-start | bytes 3342344 | tf_op jit(solution)/shard_map/ppermute | solution.py:204
  931.4 25.8 %slice-start.9 = ((s8[4456448]{0:T(1024)(128)(4,1)}), s8[4194304]{0:T(1024)(128)(4,1)S(1)}, s32[]{:S(2)}) async-start(s8[4456448]{0:T(1024)(128)(4,1)} %bitcast.279), calls=%async_computation.13 | async-start | bytes 8388608
  933.3 22.3 %copy-start.12 = (bf16[2,1,512,1088]{2,3,1,0:T(8,128)(2,1)S(1)}, bf16[2,1,512,1088]{2,3,1,0:T(8,128)(2,1)}, u32[]{:S(2)}) copy-start(bf16[2,1,512,1088]{2,3,1,0:T(8,128)(2,1)} %param.18) | copy-start | bytes 6684676
  933.4 22.3 %copy-start.56 = (f32[1088]{0:T(1024)S(1)}, f32[1088]{0:T(1024)}, u32[]{:S(2)}) copy-start(f32[1088]{0:T(1024)} %copy-done.55) | copy-start | bytes 13060
  933.4 22.3 %copy-start.58 = (f32[2,512]{1,0:T(2,128)S(1)}, f32[2,512]{1,0:T(2,128)}, u32[]{:S(2)}) copy-start(f32[2,512]{1,0:T(2,128)} %copy-done.57) | copy-start | bytes 12292
  933.4 23.8 %slice-start.10 = ((s8[4456448]{0:T(1024)(128)(4,1)}), s8[262144]{0:T(1024)(128)(4,1)S(1)}, s32[]{:S(2)}) async-start(s8[4456448]{0:T(1024)(128)(4,1)} %bitcast.279), calls=%async_computation.14 | async-start | bytes 524288
  (71 other events, 585.1 us)
Sparse Core Ops, SparseCore 0:
  11.5 97.1 all-gather.9
  112.2 135.5 all-gather.11
  789.3 54.7 all-gather.13
  847.5 83.2 all-gather.15

commit v2 on v1

--- a/solution.py
+++ b/solution.py
@@ -167,25 +167,433 @@
         name="attn_bwd")(meta,start,q,k,v,do,o,lse)
 
 
+def dot_nn(a, b):
+    return lax.dot_general(a, b, (((1,), (0,)), ((), ())), preferred_element_type=F32)
+
+
+def dot_nt(a, b):
+    return lax.dot_general(a, b, (((1,), (1,)), ((), ())), preferred_element_type=F32)
+
+
+def turned(x):
+    rank = x.shape[1]
+    eye = (
+        lax.broadcasted_iota(jnp.int32, (rank, rank), 0) == lax.broadcasted_iota(jnp.int32, (rank, rank), 1)
+    ).astype(F32).astype(BF)
+    return dot_nt(eye, x).astype(BF)
+
+
+def whole_spec(shape, **kw):
+    return pl.BlockSpec(shape, lambda *_: (0,) * len(shape), pipeline_mode=pl.Buffered(1))
+
+
+def unpack_kernel(g_ref, mix_ref, out_ref, *, cm, co, D, W):
+    S = g_ref.shape[0]
+    rows = mix_ref.shape[2]
+    half_width = cm + co
+    for half in range(2):
+        at = half * half_width
+        mix = jnp.concatenate([g_ref[s, 0, :rows, at : at + cm] for s in range(S)], axis=1)
+        out = jnp.concatenate([g_ref[s, 0, :rows, at + cm : at + half_width] for s in range(S)], axis=1)
+        zero = jnp.zeros((mix.shape[0], W - D), mix.dtype)
+        for i in range(3):
+            mix_ref[0, half, :, i * W : (i + 1) * W] = jnp.concatenate([mix[:, i * D : (i + 1) * D], zero], axis=1)
+        out_ref[0, half] = out
+
+
+def unpack(g, S, C, rows2, cm, co, D, W):
+    g = g.reshape(S, C, -1, 2 * (cm + co))
+    mix, out = pl.pallas_call(
+        functools.partial(unpack_kernel, cm=cm, co=co, D=D, W=W),
+        grid=(C,),
+        in_specs=[pl.BlockSpec((S, 1) + g.shape[2:], lambda c: (0, c, 0, 0))],
+        out_specs=[
+            pl.BlockSpec((1, 2, rows2, 3 * W), lambda c: (c, 0, 0, 0)),
+            pl.BlockSpec((1, 2, rows2, D), lambda c: (c, 0, 0, 0)),
+        ],
+        out_shape=[
+            jax.ShapeDtypeStruct((C, 2, rows2, 3 * W), BF),
+            jax.ShapeDtypeStruct((C, 2, rows2, D), BF),
+        ],
+        compiler_params=pltpu.CompilerParams(vmem_limit_bytes=48 << 20),
+        cost_estimate=pl.CostEstimate(flops=0, bytes_accessed=4 * g.size, transcendentals=0),
+        name="unpack",
+    )(g)
+    return mix.reshape(D, 3 * W), out.reshape(D, D)
+
+
+def qkv_kernel(meta_ref, *refs, W, count):
+    n_refs = refs[:count]
+    w_ref, e_ref, m_ref, b_ref, q_ref, k_ref, v_ref, l_ref, n_ref = refs[count:]
+    j = pl.program_id(1)
+    me = meta_ref[0]
+    for jj in range(count):
+
+        @pl.when(j == jj)
+        def _(jj=jj):
+            n_ref[...] = n_refs[jj][0, :, : n_ref.shape[1]]
+
+    @pl.when((me ^ j) <= me)
+    def _():
+        n = n_ref[...]
+        low = dot_nt(n, e_ref[0]).astype(BF)
+        l_ref[0] = low
+
+        def part(i):
+            s = slice(i * W, (i + 1) * W)
+            return dot_nn(n, w_ref[:, s]) + dot_nn(low, m_ref[0, :, s]) + b_ref[:, s]
+
+        k_ref[0] = part(1).astype(BF)
+        v_ref[0] = part(2).astype(BF)
+
+        @pl.when(j == 0)
+        def _():
+            q_ref[0] = (part(0) * 0.125).astype(BF)
+
+    @pl.when((me ^ j) > me)
+    def _():
+        l_ref[0] = jnp.zeros_like(l_ref[0])
+
+
+def qkv(meta, n_parts, w, e_t, m, b):
+    count = len(n_parts)
+    R, L, W = n_parts[0].shape
+    D = w.shape[0]
+    T = count * L
+    rank = m.shape[1]
+    row = lambda r, j, _: (r, j, 0)
+    one = lambda r, j, _: (r, 0, 0)
+    return pl.pallas_call(
+        functools.partial(qkv_kernel, W=W, count=count),
+        grid_spec=pltpu.PrefetchScalarGridSpec(
+            num_scalar_prefetch=1,
+            grid=(R, count),
+            in_specs=[pl.BlockSpec((1, L, W), one)] * count
+            + [
+                whole_spec(w.shape),
+                pl.BlockSpec((1, rank, D), one),
+                pl.BlockSpec((1, rank, 3 * W), one),
+                whole_spec(b.shape),
+            ],
+            out_specs=[
+                pl.BlockSpec((1, L, W), one),
+                pl.BlockSpec((1, L, W), row),
+                pl.BlockSpec((1, L, W), row),
+                pl.BlockSpec((1, L, rank), row),
+            ],
+            scratch_shapes=[pltpu.VMEM((L, D), BF)],
+        ),
+        out_shape=[
+            jax.ShapeDtypeStruct((R, L, W), BF),
+            jax.ShapeDtypeStruct((R, T, W), BF),
+            jax.ShapeDtypeStruct((R, T, W), BF),
+            jax.ShapeDtypeStruct((R, T, rank), BF),
+        ],
+        compiler_params=pltpu.CompilerParams(vmem_limit_bytes=56 << 20),
+        cost_estimate=pl.CostEstimate(
+            flops=2 * R * T * D * 2 * W, bytes_accessed=2 * (R * T * D + w.size + 2 * R * T * W), transcendentals=0
+        ),
+        name="qkv",
+    )(meta, *n_parts, w, e_t, m, b)
+
+
+def ffn_kernel(
+    n2_ref, dy_ref, res_ref, o_ref, lo_ref, l3_ref, wexp_ref, wshr_ref, rexp_ref, rshr_ref, eu_ref, eur_ref,
+    hd_ref, hdr_ref, b_ref, br_ref, x0_ref, x1_ref, e1_ref, e2_ref, wout_ref, gain_ref, xb_ref,
+    y_ref, dr_ref, do_ref, g1_ref, g2_ref, gx0_ref, gx1_ref, ge_ref, ger_ref, gh_ref, ghr_ref,
+    out_acc, dn_acc, l4_acc, dl3_acc, dl4_ref, dl4t_ref, l3t_ref, shr_ref, *, R, per, co,
+):
+    f = pl.program_id(0)
+    last = pl.num_programs(0) - 1
+    D = dy_ref.shape[2]
+
+    def block(r, wexp, wshr, eu, hd, b, ge, gh):
+        n2, dy = n2_ref[r], dy_ref[r]
+        h = dot_nn(n2, wexp) + dot_nn(l3_ref[r], eu) + b
+        hh = h * h
+        th = jnp.tanh(h * (0.7978845608028654 + (0.7978845608028654 * 0.044715) * hh))
+        half = 0.5 * (1.0 + th)
+        g = (h * half).astype(BF)
+        slope = half + (0.5 * h) * (1.0 - th * th) * (0.7978845608028654 + (3 * 0.7978845608028654 * 0.044715) * hh)
+        dg = dot_nn(dy, wshr) + dot_nn(dl4_ref[r], hd)
+        dh = (dg * slope).astype(BF)
+        out_acc[r] += dot_nt(g, wshr)
+        dn_acc[r] += dot_nt(dh, wexp)
+        l4_acc[r] += dot_nt(g, hd)
+        dl3_acc[r] += dot_nt(dh, eu)
+        gh[r] = dot_nn(dl4t_ref[r], g)
+        ge[r] = dot_nn(l3t_ref[r], dh)
+
+    if per:
+        for part in range(per):
+
+            @pl.when(lax.rem(f, per) == part)
+            def _(part=part):
+                for s in range(wshr_ref.shape[0]):
+                    shr_ref[s * co : (s + 1) * co] = wshr_ref[s, 0, part * co : (part + 1) * co]
+
+    else:
+        shr_ref = wshr_ref.at[0]
+
+    def rows(r, carry):
+        @pl.when(f == 0)
+        def _():
+            dl4 = dot_nt(dy_ref[r], x1_ref[r]).astype(BF)
+            dl4_ref[r] = dl4
+            dl4t_ref[r] = turned(dl4)
+            l3t_ref[r] = turned(l3_ref[r])
+            out_acc[r] = jnp.zeros_like(out_acc[r])
+            dn_acc[r] = jnp.zeros_like(dn_acc[r])
+            l4_acc[r] = jnp.zeros_like(l4_acc[r])
+            dl3_acc[r] = jnp.zeros_like(dl3_acc[r])
+
+        block(r, wexp_ref[...].reshape(D, -1), shr_ref[...], eu_ref[r], hd_ref[r], b_ref[...], ge_ref, gh_ref)
+
+        @pl.when(f == last)
+        def _():
+            block(r, rexp_ref[...], rshr_ref[...], eur_ref[r], hdr_ref[r], br_ref[...], ger_ref, ghr_ref)
+            l4 = l4_acc[r].astype(BF)
+            res = res_ref[r]
+            y_ref[r] = (res + out_acc[r] + dot_nn(l4, x1_ref[r]) + xb_ref[...]).astype(BF).T
+            gx1_ref[r] = dot_nn(turned(l4), dy_ref[r])
+            dl3 = dl3_acc[r].astype(BF)
+            g2_ref[r] = dot_nn(turned(dl3), n2_ref[r])
+            e = (dn_acc[r] + dot_nn(dl3, e2_ref[r])) * gain_ref[...]
+            z, inv = layer_stats(res)
+            dr = dy_ref[r].astype(F32) + norm_back(e, z, inv)
+            dr_ref[r] = dr
+            drb = dr.astype(BF)
+            dl2 = dot_nt(drb, x0_ref[r]).astype(BF)
+            do_ref[r] = (dot_nt(drb, wout_ref[...]) + dot_nn(dl2, e1_ref[r])).astype(BF)
+            g1_ref[r] = dot_nn(turned(dl2), o_ref[r])
+            gx0_ref[r] = dot_nn(turned(lo_ref[r]), drb)
+
+        return carry
+
+    lax.fori_loop(0, R, rows, 0)
+
+
+def ffn(n2, dy, res, o, lo, l3, wexp, wshr, rexp, rshr, eu, eur, hd, hdr, b, br, x0, x1, e1, e2, wout, gain, xb):
+    R, L, D = n2.shape
+    rank = x0.shape[1]
+    width, rem = wexp.shape[-1], rexp.shape[1]
+    blocks = eu.shape[2] // width
+    cols = lambda *lead: pl.BlockSpec(lead + (width,), lambda f: (0,) * len(lead) + (f,))
+    if wexp.ndim == 4:
+        S, C = wexp.shape[:2]
+        per, co = S // C, D // S
+        wexp_spec = pl.BlockSpec((1, C, D // C, width), lambda f: (f, 0, 0, 0))
+        wshr_spec = pl.BlockSpec((S, 1, D // C, width), lambda f: (0, f // per, 1, 0))
+    else:
+        per = co = 0
+        wexp_spec = wshr_spec = pl.BlockSpec((1, D, width), lambda f: (f, 0, 0))
+    shapes = [
+        ((R, D, L), BF), ((R, L, D), F32), ((R, L, D), BF),
+        ((R, rank, D), F32), ((R, rank, D), F32), ((R, rank, D), F32), ((R, rank, D), F32),
+        ((R, rank, blocks * width), F32), ((R, rank, rem), F32), ((R, rank, blocks * width), F32), ((R, rank, rem), F32),
+    ]
+    out_specs = [whole_spec(s) for s, _ in shapes]
+    out_specs[7] = out_specs[9] = cols(R, rank)
+    ff = blocks * width + rem
+    return pl.pallas_call(
+        functools.partial(ffn_kernel, R=R, per=per, co=co),
+        grid=(blocks,),
+        in_specs=[whole_spec(a.shape) for a in (n2, dy, res, o, lo, l3)]
+        + [wexp_spec, wshr_spec, whole_spec(rexp.shape), whole_spec(rshr.shape)]
+        + [cols(R, rank), whole_spec(eur.shape), cols(R, rank), whole_spec(hdr.shape), cols(1), whole_spec(br.shape)]
+        + [whole_spec(a.shape) for a in (x0, x1, e1, e2, wout, gain, xb)],
+        out_specs=out_specs,
+        out_shape=[jax.ShapeDtypeStruct(s, d) for s, d in shapes],
+        scratch_shapes=[
+            pltpu.VMEM((R, L, D), F32), pltpu.VMEM((R, L, D), F32), pltpu.VMEM((R, L, rank), F32),
+            pltpu.VMEM((R, L, rank), F32), pltpu.VMEM((R, L, rank), BF), pltpu.VMEM((R, rank, L), BF),
+            pltpu.VMEM((R, rank, L), BF), pltpu.VMEM((D, width), BF),
+        ],
+        compiler_params=pltpu.CompilerParams(vmem_limit_bytes=60 << 20),
+        cost_estimate=pl.CostEstimate(
+            flops=8 * R * L * D * ff, bytes_accessed=4 * D * ff + 24 * R * L * D, transcendentals=R * L * ff
+        ),
+        name="ffn",
+    )(n2, dy, res, o, lo, l3, wexp, wshr, rexp, rshr, eu, eur, hd, hdr, b, br, x0, x1, e1, e2, wout, gain, xb)
+
+
+def project_kernel(meta_ref, dq_ref, dk_ref, dv_ref, w_ref, m_ref, e_ref, low_ref, *refs, W, count):
+    n_refs, refs = refs[:count], refs[count:]
+    mine_ref, o_refs, g_ref, n_ref, t_ref = refs[0], refs[1:count], refs[count], refs[count + 1], refs[count + 2]
+    j = pl.program_id(0)
+    me = meta_ref[0]
+    D = n_ref.shape[1]
+    for jj in range(count):
+
+        @pl.when(j == jj)
+        def _(jj=jj):
+            n_ref[...] = n_refs[jj][0, :, :D]
+
+    @pl.when(j == 0)
+    def _():
+        g_ref[...] = jnp.zeros_like(g_ref)
+
+    def work(pieces):
+        low_t = turned(low_ref[0])
+        dl = sum(dot_nt(d[0], m_ref[0, :, i * W : (i + 1) * W]) for i, d in pieces).astype(BF)
+        total = dot_nn(dl, e_ref[0])
+        for i, d in pieces:
+            total = total + dot_nt(d[0], w_ref[:, i * W : (i + 1) * W])
+            g_ref[i] += dot_nn(low_t, d[0])
+        g_ref[3, :, :D] += dot_nn(turned(dl), n_ref[...])
+        return total
+
+    @pl.when(j == 0)
+    def _():
+        mine_ref[...] = work([(0, dq_ref), (1, dk_ref), (2, dv_ref)])
+
+    @pl.when((j > 0) & ((me ^ j) < me))
+    def _():
+        t_ref[:, :D] = work([(1, dk_ref), (2, dv_ref)]).astype(BF)
+
+    for jj in range(1, count):
+
+        @pl.when(j == jj)
+        def _(jj=jj):
+            o_refs[jj - 1][...] = t_ref[...]
+
+
+def project(meta, dq, dk, dv, w, m, e_t, low, n_parts, r):
+    count = len(n_parts)
+    _, L, W = dq.shape
+    D = w.shape[0]
+    T = count * L
+    rank = m.shape[1]
+    out = pl.pallas_call(
+        functools.partial(project_kernel, W=W, count=count),
+        grid_spec=pltpu.PrefetchScalarGridSpec(
+            num_scalar_prefetch=1,
+            grid=(count,),
+            in_specs=[
+                whole_spec(dq.shape),
+                pl.BlockSpec((1, L, W), lambda j, _: (0, j, 0)),
+                pl.BlockSpec((1, L, W), lambda j, _: (0, j, 0)),
+                whole_spec(w.shape),
+                pl.BlockSpec((1, rank, 3 * W), lambda j, _: (r, 0, 0)),
+                pl.BlockSpec((1, rank, D), lambda j, _: (r, 0, 0)),
+                pl.BlockSpec((1, L, rank), lambda j, _: (r, j, 0)),
+            ]
+            + [pl.BlockSpec((1, L, W), lambda j, _: (r, 0, 0))] * count,
+            out_specs=[whole_spec((L, D))] + [whole_spec((L, W))] * (count - 1) + [whole_spec((4, rank, W))],
+            scratch_shapes=[pltpu.VMEM((L, D), BF), pltpu.VMEM((L, W), BF)],
+        ),
+        out_shape=[jax.ShapeDtypeStruct((L, D), F32)]
+        + [jax.ShapeDtypeStruct((L, W), BF)] * (count - 1)
+        + [jax.ShapeDtypeStruct((4, rank, W), F32)],
+        compiler_params=pltpu.CompilerParams(vmem_limit_bytes=56 << 20),
+        cost_estimate=pl.CostEstimate(
+            flops=2 * T * D * 2 * W, bytes_accessed=2 * (w.size + 2 * T * W + 2 * T * D), transcendentals=0
+        ),
+        name="project",
+    )(meta, dq, dk, dv, w, m, e_t, low, *n_parts)
+    return out[:count], out[count]
+
+
+def norm_kernel(x_ref, dy_ref, gain_ref, shift_ref, n_ref, xr_ref, dyr_ref):
+    x = x_ref[0].astype(F32)
+    centred = x - jnp.mean(x, axis=0, keepdims=True)
+    inv = lax.rsqrt(jnp.mean(centred * centred, axis=0, keepdims=True) + EPS)
+    n = (centred * inv * gain_ref[...] + shift_ref[...]).astype(BF).T
+    n_ref[0] = jnp.concatenate([n, jnp.zeros((n.shape[0], n_ref.shape[2] - n.shape[1]), BF)], axis=1)
+    xr_ref[0] = x_ref[0].T
+    dyr_ref[0] = dy_ref[0].T
+
+
+def first_norm(x_t, dy_t, gain, shift, W):
+    R, D, L = x_t.shape
+    col = pl.BlockSpec((1, D, L), lambda r: (r, 0, 0))
+    row = pl.BlockSpec((1, L, D), lambda r: (r, 0, 0))
+    return pl.pallas_call(
+        norm_kernel,
+        grid=(R,),
+        in_specs=[col, col, whole_spec((D, 1)), whole_spec((D, 1))],
+        out_specs=[pl.BlockSpec((1, L, W), lambda r: (r, 0, 0)), row, row],
+        out_shape=[jax.ShapeDtypeStruct((R, L, W), BF)] + [jax.ShapeDtypeStruct((R, L, D), BF)] * 2,
+        compiler_params=pltpu.CompilerParams(vmem_limit_bytes=48 << 20),
+        cost_estimate=pl.CostEstimate(flops=10 * x_t.size, bytes_accessed=10 * x_t.size, transcendentals=0),
+        name="first_norm",
+    )(x_t, dy_t, gain[:, None], shift[:, None])
+
+
+def last_kernel(*refs, count, alias):
+    if alias:
+        refs = refs[1:]
+    terms, (dr_ref, x_ref, gain_ref, o_ref) = refs[:count], refs[count:]
+    D = x_ref.shape[2]
+    dn = terms[0][...]
+    for t in terms[1:]:
+        dn = dn + t[:, :D].astype(F32)
+    z, inv = layer_stats(x_ref[0].astype(F32))
+    o_ref[0] = (dr_ref[0] + norm_back(dn * gain_ref[...], z, inv)).astype(BF).T
+
+
+def last(r, before, terms, dr, x, gain):
+    R, L, D = x.shape
+    alias = before is not None
+    return pl.pallas_call(
+        functools.partial(last_kernel, count=len(terms), alias=alias),
+        grid=(1,),
+        in_specs=[pl.BlockSpec(memory_space=pl.ANY)] * alias
+        + [whole_spec(t.shape) for t in terms]
+        + [pl.BlockSpec((1, L, D), lambda i: (r, 0, 0))] * 2
+        + [whole_spec((1, D))],
+        out_specs=pl.BlockSpec((1, D, L), lambda i: (r, 0, 0)),
+        out_shape=jax.ShapeDtypeStruct((R, D, L), BF),
+        input_output_aliases={0: 0} if alias else {},
+        compiler_params=pltpu.CompilerParams(vmem_limit_bytes=48 << 20),
+        cost_estimate=pl.CostEstimate(flops=20 * L * D, bytes_accessed=12 * L * D, transcendentals=0),
+        name="last",
+    )(*([before] if alias else []), *terms, dr, x, gain)
+
+
+def late_kernel(slot_ref, part_ref, *refs, R, parts, D, W):
+    g_refs, mix_ref, entry_ref, total = refs[:R], refs[R], refs[R + 1], refs[R + 2]
+    total[...] = jnp.zeros_like(total)
+    count = g_refs[0].shape[0]
+    for r in range(R):
+
+        def one(i, carry):
+            a = slot_ref[r * count + i]
+            c = part_ref[i]
+            total[a, c] = total[a, c] + g_refs[r][i].astype(F32)
+            return carry
+
+        lax.fori_loop(0, count, one, 0)
+    per = parts // 4
+    wide = [jnp.concatenate([total[:, i * per + p] for p in range(per)], axis=-1) for i in range(4)]
+    mix_ref[...] = jnp.concatenate([w[:, :, :D] for w in wide[:3]], axis=-1)
+    entry_ref[...] = wide[3][:, :, :D]
+
+
+def late_slots(slot, part, gs, adapters, parts, D, W):
+    R = len(gs)
+    _, rank, width = gs[0].shape
+    return pl.pallas_call(
+        functools.partial(late_kernel, R=R, parts=parts, D=D, W=W),
+        grid_spec=pltpu.PrefetchScalarGridSpec(
+            num_scalar_prefetch=2,
+            grid=(1,),
+            in_specs=[whole_spec(g.shape) for g in gs],
+            out_specs=[whole_spec((adapters, rank, 3 * D)), whole_spec((adapters, rank, D))],
+            scratch_shapes=[pltpu.VMEM((adapters, parts, rank, width), F32)],
+        ),
+        out_shape=[
+            jax.ShapeDtypeStruct((adapters, rank, 3 * D), F32),
+            jax.ShapeDtypeStruct((adapters, rank, D), F32),
+        ],
+        compiler_params=pltpu.CompilerParams(vmem_limit_bytes=48 << 20),
+        cost_estimate=pl.CostEstimate(flops=0, bytes_accessed=8 << 20, transcendentals=0),
+        name="late_slots",
+    )(slot, part, *gs)
+
+
 def mm(pattern, a, b):
     return jnp.einsum(pattern, a, b, preferred_element_type=F32)
-
-
-def unpack_kernel(w_ref, *outs, pieces, rows, halves):
-    for half in range(halves):
-        for out, (first, width, places, pad) in zip(outs, pieces):
-            whole = [
-                w_ref[s, 0, :, half * (w_ref.shape[3] // halves) + first : half * (w_ref.shape[3] // halves) + first + width]
-                for s in range(w_ref.shape[0])
-            ]
-            joined = jnp.concatenate(whole, axis=1)
-            if pad:
-                zero = jnp.zeros((rows, pad), joined.dtype)
-                step = joined.shape[1] // places
-                joined = jnp.concatenate(
-                    [x for i in range(places) for x in (joined[:, i * step : (i + 1) * step], zero)], axis=1
-                )
-            out[0, half] = joined
 
 
 def layer_stats(v):
@@ -213,13 +621,14 @@
 
 
 def blocks_back(parts, bits):
-    held = dict(enumerate(parts))
+    held = {j: [p] for j, p in enumerate(parts)}
     for bit in bits:
         for j in sorted(held):
             if j & bit:
                 sent = held.pop(j)
+                sent = sent[0] if len(sent) == 1 else sum(t.astype(F32) for t in sent).astype(BF)
                 got = swap(sent, "ctx", bit, lambda d, k=j, b=bit: ((d ^ b) ^ k) < (d ^ b))
-                held[j ^ bit] = held[j ^ bit] + got
+                held[j ^ bit].append(got)
     return held[0]
 
 
@@ -235,6 +644,18 @@
     return g
 
 
+def gather_all(x, seq_count, ctx_count):
+    n = seq_count * ctx_count
+    seq_bits = [ctx_count << i for i in range(seq_count.bit_length() - 1)]
+    ctx_bits = [1 << i for i in range(ctx_count.bit_length() - 1)]
+    held, order = x[None], [0]
+    for bit in seq_bits + ctx_bits[::-1]:
+        got = lax.ppermute(held, BOTH, [(d, d ^ bit) for d in range(n)])
+        held = jnp.concatenate([held, got], 0)
+        order = order + [o ^ bit for o in order]
+    return held, order
+
+
 def slots_kernel(index_ref, g_ref, *refs, count, spans):
     outs, total = refs[:-1], refs[-1]
     total[...] = jnp.zeros_like(total)
@@ -245,17 +666,15 @@
         return carry
 
     lax.fori_loop(0, count, one, 0)
-    for out, (first, width) in zip(outs, spans):
-        out[...] = total[:, :, first : first + width]
-
-
-def to_slots(index, g, adapters, widths):
+    for out, pieces in zip(outs, spans):
+        parts = [total[:, :, first : first + width] for first, width in pieces]
+        out[...] = parts[0] if len(parts) == 1 else jnp.concatenate(parts, axis=-1)
+
+
+def to_slots(index, g, adapters, spans):
     count, rank, wide = g.shape
     rows = 8
-    spans, at = [], 0
-    for w in widths:
-        spans.append((at, w))
-        at += w
+    widths = [sum(w for _, w in pieces) for pieces in spans]
     return pl.pallas_call(
         functools.partial(slots_kernel, count=count, spans=spans),
         grid_spec=pltpu.PrefetchScalarGridSpec(
@@ -295,27 +714,31 @@
     cm, co, ce = mixing_weight.shape[1], output_weight.shape[1], expand_weight.shape[1]
     first = jnp.concatenate([mixing_weight, output_weight], 1)
     first = jnp.concatenate([first[: rows // 2], first[rows // 2 :]], 1)
-    second = jnp.concatenate([expand_weight[: rows // 2], expand_weight[rows // 2 :]], 1)
-    third = shrink_weight.T
+    main = ce // 128 * 128
+    rem = ce - main
+    per = S // C
+    shr_t = shrink_weight.T.reshape(co, per, ce).transpose(1, 0, 2)
+    rest = jnp.concatenate([expand_weight[:, main:].reshape(-1), shr_t[:, :, main:].reshape(-1)])
+    rest_rows = -(-rest.shape[0] // first.shape[1])
+    rest = jnp.pad(rest, (0, rest_rows * first.shape[1] - rest.shape[0])).reshape(rest_rows, -1)
+    first = jnp.concatenate([first, rest], 0)
+    second = jnp.concatenate([expand_weight[:, :main], shr_t[:, :, :main].reshape(per * co, main)], 0)
     g1 = lax.all_gather(first, BOTH)
-    if second.shape[1] == third.shape[1]:
-        g2 = lax.all_gather(jnp.concatenate([second, third], 0), BOTH)
-        g2, g3 = g2[:, : rows // 2], g2[:, rows // 2 :]
+    g2 = lax.all_gather(second, BOTH).reshape(S, C, -1, main)
+    w_mix, w_out = unpack(g1, S, C, rows // 2, cm, co, D, W)
+    if rows % 16 == 0 and per * co == rows and co % 8 == 0:
+        w_exp = w_shr = g2
     else:
-        g2, g3 = lax.all_gather(second, BOTH), lax.all_gather(third, BOTH)
-
-    def join(g, width):
-        r = g.shape[1]
-        g = g.reshape(S, C, r, 2, width).transpose(1, 3, 2, 0, 4)
-        return g.reshape(C * 2 * r, S, width)
-
-    w1 = join(g1, cm + co)
-    w_mix = w1[:, :, :cm].reshape(D, 3 * D)
-    w_out = w1[:, :, cm:].reshape(D, D)
-    padded = lambda m: jnp.pad(m, [(0, 0)] * (m.ndim - 1) + [(0, pad)])
-    w_q, w_k, w_v = (padded(w_mix[:, i * D : (i + 1) * D]) for i in range(3))
-    w_exp = join(g2, ce).reshape(D, FF)
-    w_shr_t = g3.reshape(S, C, D // S, FF // C).transpose(0, 2, 1, 3).reshape(D, FF)
+        w_exp = g2[:, :, :rows].reshape(S, D, main)
+        w_shr = g2[:, :, rows:].reshape(S, C, per, co, main).transpose(1, 2, 0, 3, 4).reshape(S, D, main)
+    flat = g1[:, rows // 2 :].reshape(S, C, -1)
+    r_exp = flat[..., : rows * rem].reshape(S, C, rows, rem).transpose(1, 2, 0, 3).reshape(D, S * rem)
+    r_shr = flat[..., rows * rem : rows * rem + per * co * rem].reshape(S, C, per, co, rem)
+    r_shr = r_shr.transpose(0, 3, 1, 2, 4).reshape(D, S * rem)
+
+    def split_ff(m):
+        m = m.reshape(m.shape[:-1] + (S, ce))
+        return m[..., :main].reshape(m.shape[:-2] + (S * main,)), m[..., main:].reshape(m.shape[:-2] + (S * rem,))
 
     index = adapter_index.reshape(R)
     take = lambda table, axis: jnp.stack(
@@ -326,8 +749,15 @@
     exp_up = take(expand_adapters, 0)
     hid = take(hidden_adapters, 0)
     exit_up = take(exit_adapters, 1)
-    m_q, m_k, m_v = (padded(mix_up[..., i * D : (i + 1) * D]) for i in range(3))
-    all_index = lax.all_gather(index, "seq").reshape(S * R)
+    pad_heads = lambda m: jnp.concatenate([padded(m[..., i * D : (i + 1) * D]) for i in range(3)], -1)
+    padded = lambda m: jnp.pad(m, [(0, 0)] * (m.ndim - 1) + [(0, pad)])
+    mix_up = pad_heads(mix_up)
+    flip = lambda m: jnp.swapaxes(m, -1, -2)
+    entry_t = flip(entry)
+    exp_main, exp_rest = split_ff(exp_up)
+    hid_main, hid_rest = split_ff(flip(hid))
+    bias_main, bias_rest = split_ff(expand_bias[None])
+    head_bias = pad_heads(jnp.concatenate([head_biases[0], jnp.zeros_like(head_biases[0]), head_biases[1]])[None])
 
     seg = segments.reshape(R, L)
     seg_blocks = blocks_of(seg, bits)
@@ -342,91 +772,57 @@
     )
     start = start[:, None, :]
 
-    x = tokens.reshape(R, L, D).astype(F32)
-    dy = cotangent.reshape(R, L, D)
-    z1, inv1 = layer_stats(x)
-    n1 = (z1 * norm_gains[0] + norm_shifts[0]).astype(BF)
-    n1_all = jnp.concatenate(blocks_of(n1, bits), 1)
-    l1_all = mm("rtd,rdk->rtk", n1_all, entry[0]).astype(BF)
-    l1 = l1_all[:, :L]
-    q = ((mm("rtd,de->rte", n1, w_q) + mm("rtk,rke->rte", l1, m_q) + padded(head_biases[0])) * 0.125).astype(BF)
-    k = (mm("rtd,de->rte", n1_all, w_k) + mm("rtk,rke->rte", l1_all, m_k)).astype(BF)
-    v = (mm("rtd,de->rte", n1_all, w_v) + mm("rtk,rke->rte", l1_all, m_v) + padded(head_biases[1])).astype(BF)
+    n1, x, dy = first_norm(
+        flip(tokens.reshape(R, L, D)), flip(cotangent.reshape(R, L, D)), norm_gains[0], norm_shifts[0], W
+    )
+    n1_parts = blocks_of(n1, bits)
+    q, k, v, l1_all = qkv(meta, n1_parts, w_mix, entry_t[0], mix_up, head_bias)
 
     o, lse = attn_fwd(meta, start, q, k, v, QB=QB, KB=KB)
 
     lo = mm("rtd,rdk->rtk", o, entry[1]).astype(BF)
-    res = x + mm("rtd,de->rte", o, w_out) + mm("rtk,rke->rte", lo, exit_up[0]) + exit_biases[0]
+    res = x.astype(F32) + mm("rtd,de->rte", o, w_out) + mm("rtk,rke->rte", lo, exit_up[0]) + exit_biases[0]
     z2, inv2 = layer_stats(res)
     n2 = (z2 * norm_gains[1] + norm_shifts[1]).astype(BF)
     l3 = mm("rtd,rdk->rtk", n2, entry[2]).astype(BF)
-    h = mm("rtd,df->rtf", n2, w_exp) + mm("rtk,rkf->rtf", l3, exp_up) + expand_bias
-    c0 = 0.7978845608028654
-    hh = h * h
-    th = jnp.tanh(c0 * h * (1.0 + 0.044715 * hh))
-    g = (0.5 * h * (1.0 + th)).astype(BF)
-    slope = 0.5 * (1.0 + th) + 0.5 * h * (1.0 - th * th) * (c0 * (1.0 + 3 * 0.044715 * hh))
-    l4 = mm("rtf,rfk->rtk", g, hid).astype(BF)
-    out = res + mm("rtf,df->rtd", g, w_shr_t) + mm("rtk,rkd->rtd", l4, exit_up[1]) + exit_biases[1]
-    layer_output = out.astype(BF).reshape(tokens.shape)
-
-    dl4 = mm("rtd,rkd->rtk", dy, exit_up[1]).astype(BF)
-    dg = mm("rtd,df->rtf", dy, w_shr_t) + mm("rtk,rfk->rtf", dl4, hid)
-    dh = (dg * slope).astype(BF)
-    dl3 = mm("rtf,rkf->rtk", dh, exp_up).astype(BF)
-    dn2 = mm("rtf,df->rtd", dh, w_exp) + mm("rtk,rdk->rtd", dl3, entry[2])
-    dr = dy.astype(F32) + norm_back(norm_gains[1] * dn2, z2, inv2)
-    drb = dr.astype(BF)
-    dl2 = mm("rtd,rkd->rtk", drb, exit_up[0]).astype(BF)
-    do = (mm("rtd,ed->rte", drb, w_out) + mm("rtk,rdk->rtd", dl2, entry[1])).astype(BF)
-
-    early = jnp.concatenate(
-        [
-            mm("rtk,rtd->rkd", dl2, o),
-            mm("rtk,rtd->rkd", dl3, n2),
-            mm("rtk,rtf->rkf", l3, dh),
-            mm("rtk,rtf->rkf", dl4, g),
-            mm("rtk,rtd->rkd", lo, drb),
-            mm("rtk,rtd->rkd", l4, dy),
-        ],
-        -1,
-    ).reshape(R * rank, -1)
+    y, dr, do, g1, g2_, gx0, gx1, ge, ger, gh, ghr = ffn(
+        n2, dy, res, o, lo, l3, w_exp, w_shr, r_exp, r_shr, exp_main, exp_rest, hid_main, hid_rest, bias_main, bias_rest,
+        exit_up[0], exit_up[1], entry_t[1], entry_t[2], w_out, norm_gains[1][None], exit_biases[1][None],
+    )
+    layer_output = flip(y).reshape(tokens.shape)
+
+    number = jnp.broadcast_to((index.astype(F32) / C)[:, None, None], (R, rank, 128))
+    early = jnp.concatenate([g1, g2_, gx0, gx1, ge, ger, gh, ghr, number], -1).reshape(R * rank, -1)
     early = ctx_sum_rows(early, bits).astype(BF)
     early = lax.all_gather(early, BOTH).reshape(S * R, rank, -1)
-    entry1_g, entry2_g, expand_g, hidden_g, exit0_g, exit1_g = to_slots(
-        all_index, early, adapters, (D, D, FF, FF, D, D)
-    )
-
-    own, late = [], []
+    all_index = early[:, 0, -1].astype(jnp.int32)
+    spans = [[(i * D, D)] for i in range(4)]
+    for at in (4 * D, 4 * D + FF):
+        spans.append(
+            [p for i in range(S) for p in ((at + i * main, main), (at + S * main + i * rem, rem))]
+        )
+    entry1_g, entry2_g, exit0_g, exit1_g, expand_g, hidden_g = to_slots(all_index, early, adapters, spans)
+
+    input_grad, late, terms = None, [], []
     for r in range(R):
         dq, dk, dv = attn_bwd(meta, start, q, k, v, do, o, lse, QB=QB, KB=KB, r0=r)
-        dq, dk, dv = dq[0], dk[0], dv[0]
-        dl1 = mm("te,ke->tk", dk, m_k[r]) + mm("te,ke->tk", dv, m_v[r])
-        dl1 = jnp.concatenate([dl1[:L] + mm("te,ke->tk", dq, m_q[r]), dl1[L:]], 0).astype(BF)
-        part = mm("te,de->td", dk, w_k) + mm("te,de->td", dv, w_v) + mm("tk,dk->td", dl1, entry[0, r])
-        mine = part[:L] + mm("te,de->td", dq, w_q)
-        others = part[L:].astype(BF)
-        parts = [mine] + [others[(j - 1) * L : j * L] for j in range(1, C)]
-        own.append(blocks_back(parts, bits))
-        late.append(
-            jnp.concatenate(
-                [
-                    mm("tk,te->ke", l1[r], dq)[:, :D],
-                    mm("tk,te->ke", l1_all[r], dk)[:, :D],
-                    mm("tk,te->ke", l1_all[r], dv)[:, :D],
-                    mm("tk,td->kd", dl1, n1_all[r]),
-                ],
-                -1,
-            )
-        )
-    late = ctx_sum_rows(jnp.concatenate(late, 0), bits).astype(BF)
-    late = lax.all_gather(late, BOTH).reshape(S * R, rank, -1)
-    mixing_g, entry0_g = to_slots(all_index, late, adapters, (3 * D, D))
-
-    dn1 = jnp.stack(own)
-    input_grad = (dr + norm_back(norm_gains[0] * dn1, z1, inv1)).astype(BF).reshape(tokens.shape)
-
-    flip = lambda m: jnp.swapaxes(m, -1, -2)
+        if r:
+            dk, terms[r - 1] = lax.optimization_barrier((dk, terms[r - 1]))
+        parts, g = project(meta, dq, dk, dv, w_mix, mix_up, entry_t[0], l1_all, n1_parts, r)
+        if r + 1 < R:
+            do, parts = lax.optimization_barrier((do, parts))
+        terms.append(blocks_back(parts, bits))
+        g = g.reshape(4, rank, C // 4, -1).transpose(0, 2, 1, 3).reshape(C, rank, -1)
+        late.append(gather_all(ctx_sum_rows(g, bits)[0].astype(BF), S, C))
+    for r in range(R):
+        input_grad = last(r, input_grad, terms[r], dr, x, norm_gains[0][None])
+    device = lax.axis_index("seq") * C + me
+    order = device ^ jnp.array(late[0][1], jnp.int32)
+    by_row = all_index.reshape(S, R)
+    slot = jnp.concatenate([jnp.sum(jnp.where((order // C)[:, None] == jnp.arange(S), by_row[:, r], 0), 1) for r in range(R)])
+    mixing_g, entry0_g = late_slots(slot, order % C, [g for g, _ in late], adapters, C, D, W)
+    input_grad = flip(input_grad).reshape(tokens.shape)
+
     return (
         layer_output,
         input_grad,

time: 989 us -> 760 us (0.77)
  matrix products: 307 us -> 8.03 us
  Pallas kernels: 156 us -> 357 us
  local copies, waits for them, and re-layouts: 208 us -> 55.3 us
  starting transfers between devices: 122 us -> 171 us
  other arithmetic: 38.9 us -> 17.7 us
  blocking collectives: 10.9 us -> 0 us
    dot_general x53 -> x4, matrix products: 307 us -> 8.03 us  [mm(): return jnp.einsum(pattern, a, b, preferred_element_type=F32)]
    pallas_call x0 -> x9, Pallas kernels: none -> 203 us  [the longest x1 90.2 us: ffn(): pl.pallas_call(functools.partial(ffn_kernel, R=R, per=per, co=co), grid=(...]
    reshape x3 -> x16, local copies, waits for them, and re-layouts: 64.2 us -> 15.9 us  [the longest x1 3.06 us: per_device(): flat = g1[:, rows // 2:].reshape(S, C, -1)]
    slice x12 -> x17, local copies, waits for them, and re-layouts: 52.9 us -> 6.81 us  [the longest x2 2.5 us: per_device(): flat[..., rows * rem:rows * rem + per * co * rem]]
    ppermute x0 -> x10, starting transfers between devices: none -> 41.5 us  [gather_all(): got = lax.ppermute(held, BOTH, [(d, d ^ bit) for d in range(n)])]
    transpose x3 -> x2, local copies, waits for them, and re-layouts: 33.1 us -> 3.84 us  [the longest x1 2.16 us: per_device(): flat[..., :rows * rem].reshape(S, C, rows, rem).transpose(1, 2, 0, 3)]
    ppermute x0 -> x10, waiting for transfers between devices: none -> 24.7 us  [gather_all(): got = lax.ppermute(held, BOTH, [(d, d ^ bit) for d in range(n)])]
    ppermute x12, waiting for transfers between devices: 98.2 us -> 77.3 us  [swap(): return lax.ppermute(x, axis, [(d ^ bit, d) for d in range(n) if needed(d)])]
  transfers between devices with their start and end apart: 20 -> 31, of which waited for: 4 -> 15; matrix products, arithmetic and copies ran while one was open for 30% -> 7% of each run, Pallas kernels for 7% -> 34%
where the time goes in v2:
time: 760 us; the launch traced here: 750 us
  Pallas kernels  357 us (47%)
  starting transfers between devices  171 us (22%)
  waiting for transfers between devices  122 us (16%)
  local copies, waits for them, and re-layouts  55.3 us (7%)
  between operations  18.9 us (2%)
  other arithmetic  17.7 us (2%)
  matrix products  8.03 us (1%)
    ppermute x6, starting transfers between devices, ctx_sum_rows(): lax.ppermute(jnp.where(mine, low, high), 'ctx', [(d, d ^ bit) for d in ra...  110 us
    pallas_call x1, Pallas kernels, ffn(): pl.pallas_call(functools.partial(ffn_kernel, R=R, per=per, co=co), grid=(...  90.2 us
    pallas_call x2, Pallas kernels, attn_bwd(): pl.pallas_call(kern, grid_spec=pltpu.PrefetchScalarGridSpec(num_scalar_pr...  81 us
    ppermute x12, waiting for transfers between devices, swap(): return lax.ppermute(x, axis, [(d ^ bit, d) for d in range(n) if needed(d)])  77.3 us
    pallas_call x1, Pallas kernels, attn_fwd(): pl.pallas_call(kern, grid_spec=pltpu.PrefetchScalarGridSpec(num_scalar_pr...  65.7 us
    pallas_call x2, Pallas kernels, project(): pl.pallas_call(functools.partial(project_kernel, W=W, count=count), grid_...  48.1 us
    ppermute x10, starting transfers between devices, gather_all(): got = lax.ppermute(held, BOTH, [(d, d ^ bit) for d in range(n)])  41.5 us
    pallas_call x1, Pallas kernels, qkv(): pl.pallas_call(functools.partial(qkv_kernel, W=W, count=count), grid_spec...  37.3 us
  transfers between devices with their start and end apart: 31, of which 15 were waited for; matrix products, arithmetic and copies ran while one was open for 7% of the time, Pallas kernels for 34%

profile of v2, /device:TPU:5, one launch (start us, length us, event | category | flops | bytes accessed | tf_op | source)
XLA Modules:
  0.0 749.8 jit_solution(12725046706862049837)
XLA Ops:
  12.9 3.1 collective-permute-start.1
  20.1 4.8 first_norm.1
  24.9 2.7 collective-permute-start.4
  40.8 54.6 %collective-permute-done.4.refs_2_ = bf16[2,512,1152]{2,1,0:T(8,128)(2,1)} collective-permute-done((bf16[2,512,1152]{2,1,0:T(8,128)(2,1)}, bf16[2,512,1152]{2,1,0:T(8,128)(2,1)}, u32[]{:S(2)}, u32[]{:S(2)}) %collective-permute-start.4) | collective-permute-done | bytes 2359328 | tf_op jit(solution)/shard_map/ppermute | solution.py:612
  95.4 2.1 collective-permute-start.5
  106.3 3.3 concatenate.75.meta_ref
  109.6 4.3 all-gather.7.cloned.1.call-done
  113.8 9.7 %unpack.1 = (bf16[4,2,136,3456]{3,2,1,0:T(8,128)(2,1)}, bf16[4,2,136,1088]{3,2,1,0:T(8,128)(2,1)S(1)}) custom-call(bf16[8,4,152,1088]{3,2,1,0:T(8,128)(2,1)} %bitcast.119), custom_call_target="tpu_custom_call" | custom-call | bytes 21168128 | tf_op jit(solution)/shard_map/unpack/pallas_call | solution.py:206
  125.0 37.3 %qkv.1 = (bf16[2,512,1152]{2,1,0:T(8,128)(2,1)}, bf16[2,2048,1152]{2,1,0:T(8,128)(2,1)}, bf16[2,2048,1152]{2,1,0:T(8,128)(2,1)}, bf16[2,2048,16]{2,1,0:T(8,128)(2,1)}) custom-call(s32[5]{0:T(128)} %concatenate.75.meta_ref, bf16[2,512,1152]{2,1,0:T(8,128)(2,1)} %get-tuple-element.63.refs_0_, bf16[2,512,1152]{2,1,0:T(8,128)(2,1)} %collective-permute-done.3.refs_1_, ...), custom_call_target="tpu_custom_call" | custom-call | flops 20535312384 | bytes 35307520 | tf_op jit(solution)/shard_map/qkv/pallas_call | solution.py:266
  162.4 1.7 copy-done.12
  164.0 65.7 %attn_fwd.1 = (bf16[2,512,1088]{2,1,0:T(8,128)(2,1)S(1)}, f32[2,9,2,512]{3,2,1,0:T(2,128)S(1)}) custom-call(s32[5]{0:T(128)S(1)} %copy-done.7, s32[2,1,512]{2,1,0:T(1,128)S(1)} %add.136.start_ref, bf16[2,512,1152]{2,1,0:T(8,128)(2,1)S(1)} %copy-done.12, bf16[2,2048,1152]{2,1,0:T(8,128)(2,1)} %get-tuple-element.66.k_ref, ...), custom_call_target="tpu_custom_call" | custom-call | flops 9663676416 | bytes 23592960 | tf_op jit(solution)/shard_map/attn_fwd/pallas_call | solution.py:78
  231.3 5.4 fusion.36
  242.5 2.4 slice.270
  244.9 3.1 reshape.178
  248.0 2.4 fusion.29
  252.0 1.7 copy.110
  257.4 2.2 copy.108
  261.1 90.2 %ffn.1 = (bf16[2,1088,512]{2,1,0:T(8,128)(2,1)}, f32[2,512,1088]{2,1,0:T(8,128)}, bf16[2,512,1088]{2,1,0:T(8,128)(2,1)}, f32[2,16,1088]{2,1,0:T(8,128)}, f32[2,1...) custom-call(bf16[2,512,1088]{2,1,0:T(8,128)(2,1)} %copy-done.18, ...), custom_call_target="tpu_custom_call" | custom-call | flops 38788923392 | bytes 45678592 | tf_op jit(solution)/shard_map/ffn/pallas_call | solution.py:398
  353.1 66.3 %collective-permute-start.12 = (f32[16,13184]{1,0:T(8,128)S(1)}, f32[16,13184]{1,0:T(8,128)S(1)}, u32[]{:S(2)}, u32[]{:S(2)}) collective-permute-start(f32[16,13184]{1,0:T(8,128)S(1)} %select_bitcast_fusion), channel_id=1, source_target_pairs={{0,2},{1,3},{2,0},{3,1},{4,6},{5,7},{6,4},{7,5},{8,10},{9,11},{10,... | collective-permute-start | bytes 2531336 | tf_op jit(solution)/shard_map/ppermute | solution.py:642
  419.3 10.0 %collective-permute-done.12 = f32[16,13184]{1,0:T(8,128)S(1)} collective-permute-done((f32[16,13184]{1,0:T(8,128)S(1)}, f32[16,13184]{1,0:T(8,128)S(1)}, u32[]{:S(2)}, u32[]{:S(2)}) %collective-permute-start.12) | collective-permute-done | bytes 843808 | tf_op jit(solution)/shard_map/ppermute | solution.py:642
  429.6 1.8 collective-permute-done.13
  432.1 1.7 copy-done.14
  433.8 39.5 %attn_bwd.2 = (bf16[1,512,1152]{2,1,0:T(8,128)(2,1)S(1)}, bf16[1,2048,1152]{2,1,0:T(8,128)(2,1)}, bf16[1,2048,1152]{2,1,0:T(8,128)(2,1)}) custom-call(s32[5]{0:T(128)S(1)} %copy-done.7, s32[2,1,512]{2,1,0:T(1,128)S(1)} %add.136.start_ref, bf16[2,512,1152]{2,1,0:T(8,128)(2,1)S(1)} %copy-done.13, bf16[2,2048,1152]{2,1,0:T(8,128)(2,1)} %get-tuple-element.66.k_ref, ...), custom_call_target="tpu_custom_call" | custom-call | flops 12079595520 | bytes 22413312 | tf_op jit(solution)/shard_map/attn_bwd/pallas_call | solution.py:150
  474.3 24.5 %project.2 = (f32[512,1088]{1,0:T(8,128)}, bf16[512,1152]{1,0:T(8,128)(2,1)}, bf16[512,1152]{1,0:T(8,128)(2,1)}, bf16[512,1152]{1,0:T(8,128)(2,1)}, f32[4,16,1152]{2,1,0:T(8,128)}) custom-call(s32[5]{0:T(128)} %concatenate.75.meta_ref, bf16[1,512,1152]{2,1,0:T(8,128)(2,1)} %copy-done.11, bf16[1,2048,1152]{2,1,0:T(8,128)(2,1)} %get-tuple-element.75.dk_ref, ...), custom_call_target="tpu_custom_call" | custom-call | flops 10267656192 | bytes 25870336 | tf_op jit(solution)/shard_map/project/pallas_call | solution.py:467
  499.8 35.5 %collective-permute-start.14 = (f32[2,16,1152]{2,1,0:T(8,128)S(1)}, f32[2,16,1152]{2,1,0:T(8,128)S(1)}, u32[]{:S(2)}, u32[]{:S(2)}) collective-permute-start(f32[2,16,1152]{2,1,0:T(8,128)S(1)} %slice_select_fusion.2), channel_id=1, source_target_pairs={{0,2},{1,3},{2,0},{3,1},{4,6},{5,7},{6,4},{7,5},{8,10},{9,11},{10,... | collective-permute-start | bytes 442376 | tf_op jit(solution)/shard_map/ppermute | solution.py:642
  536.1 1.8 collective-permute-done.14
  539.0 1.7 copy-done.15
  540.7 41.5 %attn_bwd.3 = (bf16[1,512,1152]{2,1,0:T(8,128)(2,1)S(1)}, bf16[1,2048,1152]{2,1,0:T(8,128)(2,1)}, bf16[1,2048,1152]{2,1,0:T(8,128)(2,1)}) custom-call(s32[5]{0:T(128)S(1)} %copy-done.8, s32[2,1,512]{2,1,0:T(1,128)S(1)} %add.136.start_ref, bf16[2,512,1152]{2,1,0:T(8,128)(2,1)S(1)} %copy-done.13, bf16[2,2048,1152]{2,1,0:T(8,128)(2,1)} %get-tuple-element.66.k_ref, ...), custom_call_target="tpu_custom_call" | custom-call | flops 12079595520 | bytes 22413312 | tf_op jit(solution)/shard_map/attn_bwd/pallas_call | solution.py:150
  587.2 2.5 collective-permute-done.17
  591.3 4.9 collective-permute-done.18
  596.3 28.0 %collective-permute-start.19 = (bf16[8,16,1152]{2,1,0:T(8,128)(2,1)S(1)}, bf16[8,16,1152]{2,1,0:T(8,128)(2,1)S(1)}, u32[]{:S(2)}, u32[]{:S(2)}) collective-permute-start(bf16[8,16,1152]{2,1,0:T(8,128)(2,1)S(1)} %pad_maximum_fusion.5), channel_id=1, source_target_pairs={{0,2},{1,3},{2,0},{3,1},{4,6},{5,7},{6,4},{7,5},{8,10},{9,11},{10,... | collective-permute-start | bytes 884744 | tf_op jit(solution)/shard_map/ppermute | solution.py:653
  624.3 5.5 collective-permute-done.8.refs_2_
  629.8 23.6 %project.3 = (f32[512,1088]{1,0:T(8,128)}, bf16[512,1152]{1,0:T(8,128)(2,1)}, bf16[512,1152]{1,0:T(8,128)(2,1)}, bf16[512,1152]{1,0:T(8,128)(2,1)}, f32[4,16,1152]{2,1,0:T(8,128)}) custom-call(s32[5]{0:T(128)} %concatenate.75.meta_ref, bf16[1,512,1152]{2,1,0:T(8,128)(2,1)} %copy-done.10, bf16[1,2048,1152]{2,1,0:T(8,128)(2,1)} %get-tuple-element.93.dk_ref, ...), custom_call_target="tpu_custom_call" | custom-call | flops 10267656192 | bytes 25870336 | tf_op jit(solution)/shard_map/project/pallas_call | solution.py:467
  654.5 8.2 %collective-permute-start.21 = (f32[2,16,1152]{2,1,0:T(8,128)S(1)}, f32[2,16,1152]{2,1,0:T(8,128)S(1)}, u32[]{:S(2)}, u32[]{:S(2)}) collective-permute-start(f32[2,16,1152]{2,1,0:T(8,128)S(1)} %slice_select_fusion.1), channel_id=1, source_target_pairs={{0,2},{1,3},{2,0},{3,1},{4,6},{5,7},{6,4},{7,5},{8,10},{9,11},{10,... | collective-permute-start | bytes 442376 | tf_op jit(solution)/shard_map/ppermute | solution.py:642
  662.7 2.5 collective-permute-done.21
  667.7 2.0 collective-permute-start.9
  669.7 1.8 collective-permute-start.23
  674.1 2.5 collective-permute-done.24
  678.2 7.8 %collective-permute-done.25 = bf16[4,16,1152]{2,1,0:T(8,128)(2,1)S(1)} collective-permute-done((bf16[4,16,1152]{2,1,0:T(8,128)(2,1)S(1)}, bf16[4,16,1152]{2,1,0:T(8,128)(2,1)S(1)}, u32[]{:S(2)}, u32[]{:S(2)}) %collective-permute-start.25) | collective-permute-done | bytes 147488 | tf_op jit(solution)/shard_map/ppermute | solution.py:653
  686.1 3.2 collective-permute-start.26
  691.3 4.4 collective-permute-done.26
  695.8 2.7 collective-permute-start.27
  698.7 5.1 last.2.refs_0_
  703.8 17.2 %collective-permute-done.11.refs_3_ = bf16[512,1152]{1,0:T(8,128)(2,1)S(1)} collective-permute-done((bf16[512,1152]{1,0:T(8,128)(2,1)S(1)}, bf16[512,1152]{1,0:T(8,128)(2,1)S(1)}, u32[]{:S(2)}, u32[]{:S(2)}) %collective-permute-start.11) | collective-permute-done | bytes 1179680 | tf_op jit(solution)/shard_map/ppermute | solution.py:612
  721.0 4.9 last.3
  727.1 7.2 to_slots.1
  736.3 2.3 pad_maximum_fusion.1
  738.8 3.0 late_slots.1
  (228 shorter events, 71.1 us)
Async XLA Ops:
  7.2 106.7 %all-gather.7.cloned.1.call-start = ((), (), s32[]{:S(2)}) async-start(), calls=%async_computation | async-start | bytes 11556864 | tf_op jit(solution)/shard_map/all_gather | solution.py:726
  11.8 249.3 %all-gather.9.cloned.1.call-start = ((), (), s32[]{:S(2)}) async-start(), calls=%async_computation.1 | async-start | bytes 18382848 | tf_op jit(solution)/shard_map/all_gather | solution.py:727
  12.8 713.1 %all-gather.11.cloned.1.call-start = ((), (), s32[]{:S(2)}) async-start(), calls=%async_computation.2 | async-start | bytes 6961152 | tf_op jit(solution)/shard_map/all_gather | solution.py:797
  12.9 85.3 %collective-permute-start.1 = (s32[2,512]{1,0:T(2,128)S(1)}, s32[2,512]{1,0:T(2,128)S(1)}, u32[]{:S(2)}, u32[]{:S(2)}) collective-permute-start(s32[2,512]{1,0:T(2,128)S(1)} %bitcast.130), channel_id=1, source_target_pairs={{0,2},{1,3},{4,6},{5,7},{8,10},{9,11},{12,14},{13,15},{16,18},{17,... | collective-permute-start | bytes 12296 | tf_op jit(solution)/shard_map/ppermute | solution.py:612
  16.0 88.4 %collective-permute-start = (s32[2,512]{1,0:T(2,128)S(1)}, s32[2,512]{1,0:T(2,128)S(1)}, u32[]{:S(2)}, u32[]{:S(2)}) collective-permute-start(s32[2,512]{1,0:T(2,128)S(1)} %bitcast.131), channel_id=1, source_target_pairs={{0,1},{2,3},{4,5},{6,7},{8,9},{10,11},{12,13},{14,15},{16,17},{18,... | collective-permute-start | bytes 12296 | tf_op jit(solution)/shard_map/ppermute | solution.py:612
  20.1 8.8 %copy-start.32 = (s32[2,1]{0,1:T(1,128)S(1)}, s32[2,1]{0,1:T(1,128)}, u32[]{:S(2)}) copy-start(s32[2,1]{0,1:T(1,128)} %param.21) | copy-start | bytes 28
  20.1 12.0 %copy-start.25 = (f32[2,1088]{1,0:T(2,128)S(1)}, f32[2,1088]{1,0:T(2,128)}, u32[]{:S(2)}) copy-start(f32[2,1088]{1,0:T(2,128)} %param.24) | copy-start | bytes 26116
  20.1 15.5 %copy-start.29 = (pred[1,1152]{1,0:T(4,128)(4,1)S(1)}, pred[1,1152]{1,0:T(4,128)(4,1)}, u32[]{:S(2)}) copy-start(pred[1,1152]{1,0:T(4,128)(4,1)} %constant.87.clone.1) | copy-start | bytes 3460
  20.1 17.0 %copy-start.31 = (pred[1152]{0:T(1024)(128)(4,1)S(1)}, pred[1152]{0:T(1024)(128)(4,1)}, u32[]{:S(2)}) copy-start(pred[1152]{0:T(1024)(128)(4,1)} %constant.85.clone.1) | copy-start | bytes 3460
  20.1 17.2 %copy-start.24 = (f32[4352]{0:T(1024)S(1)}, f32[4352]{0:T(1024)}, u32[]{:S(2)}) copy-start(f32[4352]{0:T(1024)} %param.25) | copy-start | bytes 52228
  24.9 70.5 %collective-permute-start.4 = (bf16[2,512,1152]{2,1,0:T(8,128)(2,1)}, bf16[2,512,1152]{2,1,0:T(8,128)(2,1)}, u32[]{:S(2)}, u32[]{:S(2)}) collective-permute-start(bf16[2,512,1152]{2,1,0:T(8,128)(2,1)} %get-tuple-element.63.refs_0_), channel_id=1, source_target_pairs={{0,2},{1,3},{4,6},{5,7},{8,10},{9,11},{12,14},{13,15},{16,18},{17,... | collective-permute-start | bytes 7077896 | tf_op jit(solution)/shard_map/ppermute | solution.py:612
  27.6 97.4 %collective-permute-start.3 = (bf16[2,512,1152]{2,1,0:T(8,128)(2,1)}, bf16[2,512,1152]{2,1,0:T(8,128)(2,1)}, u32[]{:S(2)}, u32[]{:S(2)}) collective-permute-start(bf16[2,512,1152]{2,1,0:T(8,128)(2,1)} %get-tuple-element.63.refs_0_), channel_id=1, source_target_pairs={{0,1},{2,3},{4,5},{6,7},{8,9},{10,11},{12,13},{14,15},{16,17},{18,... | collective-permute-start | bytes 7077896 | tf_op jit(solution)/shard_map/ppermute | solution.py:612
  95.4 29.6 %collective-permute-start.5 = (bf16[2,512,1152]{2,1,0:T(8,128)(2,1)}, bf16[2,512,1152]{2,1,0:T(8,128)(2,1)}, u32[]{:S(2)}, u32[]{:S(2)}) collective-permute-start(bf16[2,512,1152]{2,1,0:T(8,128)(2,1)} %collective-permute-done.4.refs_2_), channel_id=1, source_target_pairs={{3,2},{2,3},{7,6},{6,7},{11,10},{10,11},{15,14},{14,15},{19,18},{1... | collective-permute-start | bytes 7077896 | tf_op jit(solution)/shard_map/ppermute | solution.py:612
  98.1 138.6 %copy-start.23 = (bf16[2,16,1088]{2,1,0:T(8,128)(2,1)}, bf16[2,16,1088]{2,1,0:T(8,128)(2,1)S(1)}, u32[]{:S(2)}) copy-start(bf16[2,16,1088]{2,1,0:T(8,128)(2,1)S(1)} %get-tuple-element.194.x0_ref) | copy-start | bytes 208900
  98.2 6.2 collective-permute-start.2
  125.0 37.3 %copy-start.7 = (s32[5]{0:T(128)S(1)}, s32[5]{0:T(128)}, u32[]{:S(2)}) copy-start(s32[5]{0:T(128)} %concatenate.75.meta_ref) | copy-start | bytes 64
  229.7 7.0 copy-start.1
  353.1 76.2 %collective-permute-start.12 = (f32[16,13184]{1,0:T(8,128)S(1)}, f32[16,13184]{1,0:T(8,128)S(1)}, u32[]{:S(2)}, u32[]{:S(2)}) collective-permute-start(f32[16,13184]{1,0:T(8,128)S(1)} %select_bitcast_fusion), channel_id=1, source_target_pairs={{0,2},{1,3},{2,0},{3,1},{4,6},{5,7},{6,4},{7,5},{8,10},{9,11},{10,... | collective-permute-start | bytes 2531336 | tf_op jit(solution)/shard_map/ppermute | solution.py:642
  429.5 1.8 collective-permute-start.13
  474.3 64.7 %copy-start.8 = (s32[5]{0:T(128)S(1)}, s32[5]{0:T(128)}, u32[]{:S(2)}) copy-start(s32[5]{0:T(128)} %concatenate.75.meta_ref) | copy-start | bytes 64
  499.8 38.0 %collective-permute-start.14 = (f32[2,16,1152]{2,1,0:T(8,128)S(1)}, f32[2,16,1152]{2,1,0:T(8,128)S(1)}, u32[]{:S(2)}, u32[]{:S(2)}) collective-permute-start(f32[2,16,1152]{2,1,0:T(8,128)S(1)} %slice_select_fusion.2), channel_id=1, source_target_pairs={{0,2},{1,3},{2,0},{3,1},{4,6},{5,7},{6,4},{7,5},{8,10},{9,11},{10,... | collective-permute-start | bytes 442376 | tf_op jit(solution)/shard_map/ppermute | solution.py:642
  535.3 48.3 %collective-permute-start.7 = (bf16[512,1152]{1,0:T(8,128)(2,1)}, bf16[512,1152]{1,0:T(8,128)(2,1)S(1)}, u32[]{:S(2)}, u32[]{:S(2)}) collective-permute-start(bf16[512,1152]{1,0:T(8,128)(2,1)} %get-tuple-element.87), channel_id=1, source_target_pairs={{3,2},{2,3},{7,6},{6,7},{11,10},{10,11},{15,14},{14,15},{19,18},{1... | collective-permute-start | bytes 3538952 | tf_op jit(solution)/shard_map/ppermute | solution.py:612
  538.9 44.6 %collective-permute-start.15 = (f32[1,16,1152]{2,1,0:T(8,128)S(1)}, f32[1,16,1152]{2,1,0:T(8,128)S(1)}, u32[]{:S(2)}, u32[]{:S(2)}) collective-permute-start(f32[1,16,1152]{2,1,0:T(8,128)S(1)} %slice_select_fusion.4), channel_id=1, source_target_pairs={{0,1},{1,0},{2,3},{3,2},{4,5},{5,4},{6,7},{7,6},{8,9},{9,8},{10,11... | collective-permute-start | bytes 221192 | tf_op jit(solution)/shard_map/ppermute | solution.py:642
  540.7 41.5 %copy-start.35 = (bf16[512,1152]{1,0:T(8,128)(2,1)S(1)}, bf16[512,1152]{1,0:T(8,128)(2,1)}, u32[]{:S(2)}) copy-start(bf16[512,1152]{1,0:T(8,128)(2,1)} %get-tuple-element.85) | copy-start | bytes 3538948
  540.7 43.0 %copy-start.21 = (bf16[512,1152]{1,0:T(8,128)(2,1)S(1)}, bf16[512,1152]{1,0:T(8,128)(2,1)}, u32[]{:S(2)}) copy-start(bf16[512,1152]{1,0:T(8,128)(2,1)} %get-tuple-element.86) | copy-start | bytes 3538948
  582.1 7.6 %copy-start.10 = (bf16[1,512,1152]{2,1,0:T(8,128)(2,1)}, bf16[1,512,1152]{2,1,0:T(8,128)(2,1)S(1)}, u32[]{:S(2)}) copy-start(bf16[1,512,1152]{2,1,0:T(8,128)(2,1)S(1)} %get-tuple-element.92.dq_ref) | copy-start | bytes 3538948
  582.1 42.2 %collective-permute-start.6 = (bf16[512,1152]{1,0:T(8,128)(2,1)S(1)}, bf16[512,1152]{1,0:T(8,128)(2,1)S(1)}, u32[]{:S(2)}, u32[]{:S(2)}) collective-permute-start(bf16[512,1152]{1,0:T(8,128)(2,1)S(1)} %copy-done.35), channel_id=1, source_target_pairs={{1,0},{3,2},{5,4},{7,6},{9,8},{11,10},{13,12},{15,14},{17,16},{19,... | collective-permute-start | bytes 3538952 | tf_op jit(solution)/shard_map/ppermute | solution.py:612
  583.5 2.9 collective-permute-start.16
  583.9 45.9 %collective-permute-start.8 = (bf16[512,1152]{1,0:T(8,128)(2,1)S(1)}, bf16[512,1152]{1,0:T(8,128)(2,1)S(1)}, u32[]{:S(2)}, u32[]{:S(2)}) collective-permute-start(bf16[512,1152]{1,0:T(8,128)(2,1)S(1)} %add_convert_fusion.2), channel_id=1, source_target_pairs={{2,0},{3,1},{6,4},{7,5},{10,8},{11,9},{14,12},{15,13},{18,16},{19,... | collective-permute-start | bytes 3538952 | tf_op jit(solution)/shard_map/ppermute | solution.py:612
  586.4 3.3 collective-permute-start.17
  589.7 6.5 collective-permute-start.18
  596.3 70.0 %collective-permute-start.19 = (bf16[8,16,1152]{2,1,0:T(8,128)(2,1)S(1)}, bf16[8,16,1152]{2,1,0:T(8,128)(2,1)S(1)}, u32[]{:S(2)}, u32[]{:S(2)}) collective-permute-start(bf16[8,16,1152]{2,1,0:T(8,128)(2,1)S(1)} %pad_maximum_fusion.5), channel_id=1, source_target_pairs={{0,2},{1,3},{2,0},{3,1},{4,6},{5,7},{6,4},{7,5},{8,10},{9,11},{10,... | collective-permute-start | bytes 884744 | tf_op jit(solution)/shard_map/ppermute | solution.py:653
  653.4 13.5 %copy-start.34 = (bf16[512,1152]{1,0:T(8,128)(2,1)S(1)}, bf16[512,1152]{1,0:T(8,128)(2,1)}, u32[]{:S(2)}) copy-start(bf16[512,1152]{1,0:T(8,128)(2,1)} %get-tuple-element.98) | copy-start | bytes 3538948
  654.5 10.7 %collective-permute-start.21 = (f32[2,16,1152]{2,1,0:T(8,128)S(1)}, f32[2,16,1152]{2,1,0:T(8,128)S(1)}, u32[]{:S(2)}, u32[]{:S(2)}) collective-permute-start(f32[2,16,1152]{2,1,0:T(8,128)S(1)} %slice_select_fusion.1), channel_id=1, source_target_pairs={{0,2},{1,3},{2,0},{3,1},{4,6},{5,7},{6,4},{7,5},{8,10},{9,11},{10,... | collective-permute-start | bytes 442376 | tf_op jit(solution)/shard_map/ppermute | solution.py:642
  662.7 26.7 %copy-start.20 = (bf16[512,1152]{1,0:T(8,128)(2,1)S(1)}, bf16[512,1152]{1,0:T(8,128)(2,1)}, u32[]{:S(2)}) copy-start(bf16[512,1152]{1,0:T(8,128)(2,1)} %get-tuple-element.97) | copy-start | bytes 3538948
  666.2 3.5 collective-permute-start.22
  666.4 32.2 %collective-permute-start.20 = (bf16[16,16,1152]{2,1,0:T(8,128)(2,1)S(1)}, bf16[16,16,1152]{2,1,0:T(8,128)(2,1)S(1)}, u32[]{:S(2)}, u32[]{:S(2)}) collective-permute-start(bf16[16,16,1152]{2,1,0:T(8,128)(2,1)S(1)} %get-tuple-element.182), channel_id=1, source_target_pairs={{0,1},{1,0},{2,3},{3,2},{4,5},{5,4},{6,7},{7,6},{8,9},{9,8},{10,11... | collective-permute-start | bytes 1769480 | tf_op jit(solution)/shard_map/ppermute | solution.py:653
  667.0 22.4 %collective-permute-start.10 = (bf16[512,1152]{1,0:T(8,128)(2,1)S(1)}, bf16[512,1152]{1,0:T(8,128)(2,1)S(1)}, u32[]{:S(2)}, u32[]{:S(2)}) collective-permute-start(bf16[512,1152]{1,0:T(8,128)(2,1)S(1)} %copy-done.34), channel_id=1, source_target_pairs={{3,2},{2,3},{7,6},{6,7},{11,10},{10,11},{15,14},{14,15},{19,18},{1... | collective-permute-start | bytes 3538952 | tf_op jit(solution)/shard_map/ppermute | solution.py:612
  667.7 36.1 %collective-permute-start.9 = (bf16[512,1152]{1,0:T(8,128)(2,1)}, bf16[512,1152]{1,0:T(8,128)(2,1)S(1)}, u32[]{:S(2)}, u32[]{:S(2)}) collective-permute-start(bf16[512,1152]{1,0:T(8,128)(2,1)} %get-tuple-element.96), channel_id=1, source_target_pairs={{1,0},{3,2},{5,4},{7,6},{9,8},{11,10},{13,12},{15,14},{17,16},{19,... | collective-permute-start | bytes 3538952 | tf_op jit(solution)/shard_map/ppermute | solution.py:612
  669.7 3.1 collective-permute-start.23
  672.9 3.7 collective-permute-start.24
  676.6 9.4 %collective-permute-start.25 = (bf16[4,16,1152]{2,1,0:T(8,128)(2,1)S(1)}, bf16[4,16,1152]{2,1,0:T(8,128)(2,1)S(1)}, u32[]{:S(2)}, u32[]{:S(2)}) collective-permute-start(bf16[4,16,1152]{2,1,0:T(8,128)(2,1)S(1)} %pad_maximum_fusion.10), channel_id=1, source_target_pairs={{0,16},{1,17},{2,18},{3,19},{4,20},{5,21},{6,22},{7,23},{8,24},{9,... | collective-permute-start | bytes 442376 | tf_op jit(solution)/shard_map/ppermute | solution.py:653
  686.1 9.6 %collective-permute-start.26 = (bf16[8,16,1152]{2,1,0:T(8,128)(2,1)S(1)}, bf16[8,16,1152]{2,1,0:T(8,128)(2,1)S(1)}, u32[]{:S(2)}, u32[]{:S(2)}) collective-permute-start(bf16[8,16,1152]{2,1,0:T(8,128)(2,1)S(1)} %pad_maximum_fusion.6), channel_id=1, source_target_pairs={{0,2},{1,3},{2,0},{3,1},{4,6},{5,7},{6,4},{7,5},{8,10},{9,11},{10,... | collective-permute-start | bytes 884744 | tf_op jit(solution)/shard_map/ppermute | solution.py:653
  689.4 9.2 %copy-start.33 = (s32[32]{0:T(128)S(1)}, s32[32]{0:T(128)}, u32[]{:S(2)}) copy-start(s32[32]{0:T(128)} %constant.96.clone) | copy-start | bytes 388
  689.4 9.3 %copy-start = (f32[512,1088]{1,0:T(8,128)S(1)}, f32[512,1088]{1,0:T(8,128)}, u32[]{:S(2)}) copy-start(f32[512,1088]{1,0:T(8,128)} %get-tuple-element.88.refs_0_) | copy-start | bytes 6684676
  689.7 31.3 %collective-permute-start.11 = (bf16[512,1152]{1,0:T(8,128)(2,1)S(1)}, bf16[512,1152]{1,0:T(8,128)(2,1)S(1)}, u32[]{:S(2)}, u32[]{:S(2)}) collective-permute-start(bf16[512,1152]{1,0:T(8,128)(2,1)S(1)} %add_convert_fusion.1), channel_id=1, source_target_pairs={{2,0},{3,1},{6,4},{7,5},{10,8},{11,9},{14,12},{15,13},{18,16},{19,... | collective-permute-start | bytes 3538952 | tf_op jit(solution)/shard_map/ppermute | solution.py:612
  695.8 8.0 %collective-permute-start.27 = (bf16[16,16,1152]{2,1,0:T(8,128)(2,1)S(1)}, bf16[16,16,1152]{2,1,0:T(8,128)(2,1)S(1)}, u32[]{:S(2)}, u32[]{:S(2)}) collective-permute-start(bf16[16,16,1152]{2,1,0:T(8,128)(2,1)S(1)} %get-tuple-element.180), channel_id=1, source_target_pairs={{0,1},{1,0},{2,3},{3,2},{4,5},{5,4},{6,7},{7,6},{8,9},{9,8},{10,11... | collective-permute-start | bytes 1769480 | tf_op jit(solution)/shard_map/ppermute | solution.py:653
  698.7 22.4 %copy-start.2 = (f32[512,1088]{1,0:T(8,128)S(1)}, f32[512,1088]{1,0:T(8,128)}, u32[]{:S(2)}) copy-start(f32[512,1088]{1,0:T(8,128)} %get-tuple-element.95.refs_1_) | copy-start | bytes 6684676
  (20 other events, 61.7 us)
Sparse Core Ops, SparseCore 0:
  12.0 101.8 all-gather.6
  117.3 130.0 all-gather.8
  432.2 70.9 all-gather.10

commit v3 on v2

v3 whole, which is shorter than its diff:
```python
import functools

import jax
import jax.numpy as jnp
from jax import lax
from jax.experimental import pallas as pl
from jax.experimental.pallas import tpu as pltpu
from jax.sharding import PartitionSpec as P

HEADS = 17
EPS = 1e-05
NEG = -1e30
BF = jnp.bfloat16
F32 = jnp.float32
BOTH = ("seq", "ctx")


FAR = -1e30


def product(a, b, ca, cb):
    return lax.dot_general(a, b, (((ca,), (cb,)), ((), ())), preferred_element_type=F32)


def thirds(x):
    a = x.astype(BF)
    b = (x - a.astype(F32)).astype(BF)
    c = (x - a.astype(F32) - b.astype(F32)).astype(BF)
    return a, b, c


def lanes_of(h, lane):
    return (lane < 64) if h == 0 else (lane >= 64)


def attn_fwd_kernel(
    meta_ref, q_ref, k_ref, v_ref, qa_ref, ka_ref, o_ref, a_ref, kh_ref, vt_ref, s_ref, acc_ref, st_ref, *, L
):
    r = pl.program_id(0)
    me = meta_ref[0]
    lo = meta_ref[1 + r]
    lane = lax.broadcasted_iota(jnp.int32, (1, 128), 1)
    vt_ref[...] = v_ref[0].T
    q2, qa = q_ref[0], qa_ref[0]
    qh = [jnp.where(lanes_of(h, lane), q2, qa) for h in range(2)]
    for h in range(2):
        kh_ref[h] = jnp.where(lanes_of(h, lane), k_ref[0], ka_ref[0])
        st_ref[h] = jnp.concatenate([jnp.full((1, L), NEG, F32), jnp.zeros((7, L), F32)], axis=0)
    acc_ref[...] = jnp.zeros_like(acc_ref)

    def at(t):
        return pl.multiple_of((t ^ me) * L, L)

    def scores(t, h):
        s_ref[h] = product(kh_ref[h, pl.ds(at(t), L), :], qh[h], 1, 1)

    def gather(t, h, diagonal):
        s = s_ref[h]
        if diagonal:
            ok = lax.broadcasted_iota(jnp.int32, (L, L), 0) <= lax.broadcasted_iota(jnp.int32, (L, L), 1)
            s = jnp.where(ok, s, NEG)
        m = st_ref[h, 0:1]
        new = jnp.maximum(m, jnp.max(s, axis=0, keepdims=True))
        scale = jnp.exp(m - new)
        p = jnp.exp(s - new)
        st_ref[h, 1:2] = st_ref[h, 1:2] * scale + jnp.sum(p, axis=0, keepdims=True)
        st_ref[h, 0:1] = new
        rows = slice(h * 64, (h + 1) * 64)
        acc_ref[rows] = acc_ref[rows] * scale + product(vt_ref[rows, pl.ds(at(t), L)], p.astype(BF), 1, 0)

    scores(lo, 0)

    def body(t, carry):
        scores(t, 1)
        gather(t, 0, False)
        scores(t + 1, 0)
        gather(t, 1, False)
        return carry

    lax.fori_loop(lo, me, body, 0)
    scores(me, 1)
    gather(me, 0, True)
    gather(me, 1, True)
    rows = []
    for h in range(2):
        total = st_ref[h, 1:2]
        sl = slice(h * 64, (h + 1) * 64)
        acc_ref[sl] = acc_ref[sl] / total
        rows.append(thirds(-(st_ref[h, 0:1] + jnp.log(total))))
    o_ref[0] = acc_ref[...].T.astype(o_ref.dtype)
    sub = lax.broadcasted_iota(jnp.int32, (128, 1), 0)
    extra = jnp.zeros((128, L), F32)
    for h in range(2):
        for i in range(3):
            extra = jnp.where(sub == (1 - h) * 64 + 8 + i, rows[h][i].astype(F32), extra)
    a_ref[0, 0] = (qa.astype(F32) + extra.T).astype(BF)


def attn_fwd(meta, q, k, v, qa, ka, D):
    R, L, W = q.shape
    T = k.shape[1]
    NP = W // 128
    col = lambda r, p, m: (r, 0, p)
    one = lambda r, p, m: (r, 0, 0)
    return pl.pallas_call(
        functools.partial(attn_fwd_kernel, L=L),
        grid_spec=pltpu.PrefetchScalarGridSpec(
            num_scalar_prefetch=1,
            grid=(R, NP),
            in_specs=[
                pl.BlockSpec((1, L, 128), col),
                pl.BlockSpec((1, T, 128), col),
                pl.BlockSpec((1, T, 128), col),
                pl.BlockSpec((1, L, 128), one),
                pl.BlockSpec((1, T, 128), one),
            ],
            out_specs=[pl.BlockSpec((1, L, 128), col), pl.BlockSpec((1, 1, L, 128), lambda r, p, m: (r, p, 0, 0))],
            scratch_shapes=[
                pltpu.VMEM((2, T, 128), BF),
                pltpu.VMEM((128, T), BF),
                pltpu.VMEM((2, L, L), F32),
                pltpu.VMEM((128, L), F32),
                pltpu.VMEM((2, 8, L), F32),
            ],
        ),
        out_shape=[jax.ShapeDtypeStruct((R, L, D), BF), jax.ShapeDtypeStruct((R, NP, L, 128), BF)],
        compiler_params=pltpu.CompilerParams(vmem_limit_bytes=48 << 20),
        cost_estimate=pl.CostEstimate(
            flops=R * 40 * L * T * W, bytes_accessed=R * (2 * L + 2 * T) * W * 2, transcendentals=R * L * T * 18
        ),
        name="attn_fwd",
    )(meta, q, k, v, qa, ka)


def attn_bwd_kernel(
    meta_ref, q_ref, k_ref, v_ref, do_ref, o_ref, a_ref, ka_ref, dq_ref, dk_ref, dv_ref,
    kh_ref, vh_ref, kt_ref, s_ref, dp_ref, dqt_ref, dkt_ref, dvt_ref, *, L, r0, D,
):
    me = meta_ref[0]
    lo = meta_ref[1 + r0]
    lane = lax.broadcasted_iota(jnp.int32, (1, 128), 1)
    limit = D - pl.program_id(0) * 128
    kt_ref[...] = k_ref[0].T
    ones = jnp.where((lane % 64 >= 8) & (lane % 64 < 11), 1.0, 0.0).astype(BF)
    do2 = jnp.where(lane < limit, do_ref[0], jnp.zeros((), BF))
    o2 = jnp.where(lane < limit, o_ref[0], jnp.zeros((), BF))
    q2 = q_ref[0]
    prod = do2.astype(F32) * o2.astype(F32)
    qh, dh = [], []
    for h in range(2):
        mine = lanes_of(h, lane)
        parts = thirds(-jnp.sum(jnp.where(mine, prod, 0.0), axis=1, keepdims=True))
        extra = jnp.zeros((1, 128), BF)
        for i in range(3):
            extra = jnp.where(lane == (1 - h) * 64 + 8 + i, parts[i], extra)
        dh.append(jnp.where(mine, do2, extra))
        qh.append(jnp.where(mine, q2, a_ref[0, 0]))
        kh_ref[h] = jnp.where(mine, k_ref[0], ka_ref[0])
        vh_ref[h] = jnp.where(mine, v_ref[0], ones)
    qt, dot_ = q2.T, do2.T
    dqt_ref[...] = jnp.zeros_like(dqt_ref)

    def at(t):
        return pl.multiple_of((t ^ me) * L, L)

    def scores(t, h):
        s_ref[h] = product(kh_ref[h, pl.ds(at(t), L), :], qh[h], 1, 1)
        dp_ref[h] = product(vh_ref[h, pl.ds(at(t), L), :], dh[h], 1, 1)

    def gather(t, h, diagonal):
        p = jnp.exp(s_ref[h])
        if diagonal:
            ok = lax.broadcasted_iota(jnp.int32, (L, L), 0) <= lax.broadcasted_iota(jnp.int32, (L, L), 1)
            p = jnp.where(ok, p, 0.0)
        ds = (p * dp_ref[h]).astype(BF)
        rows = slice(h * 64, (h + 1) * 64)
        here = pl.ds(at(t), L)
        dvt_ref[rows, :] = product(dot_[rows], p.astype(BF), 1, 1)
        dkt_ref[rows, :] = product(qt[rows], ds, 1, 1)
        dqt_ref[rows] += product(kt_ref[rows, here], ds, 1, 0)

    def store(t):
        here = pl.ds(at(t), L)
        dk_ref[0, here, :] = dkt_ref[...].astype(BF).T
        dv_ref[0, here, :] = dvt_ref[...].astype(BF).T

    def none(t, carry):
        dk_ref[0, pl.ds(at(t), L), :] = jnp.zeros((L, 128), BF)
        dv_ref[0, pl.ds(at(t), L), :] = jnp.zeros((L, 128), BF)
        return carry

    lax.fori_loop(0, lo, none, 0)
    scores(lo, 0)

    def body(t, carry):
        scores(t, 1)
        gather(t, 0, False)
        scores(t + 1, 0)
        gather(t, 1, False)
        store(t)
        return carry

    lax.fori_loop(lo, me, body, 0)
    scores(me, 1)
    gather(me, 0, True)
    gather(me, 1, True)
    store(me)
    dq_ref[0] = dqt_ref[...].astype(BF).T * jnp.asarray(0.125, BF)


def attn_bwd(meta, q, k, v, do, o, extra, ka, r0):
    R, L, W = q.shape
    T, D = k.shape[1], do.shape[2]
    NP = W // 128
    col = lambda p, m: (r0, 0, p)
    out = lambda p, m: (0, 0, p)
    return pl.pallas_call(
        functools.partial(attn_bwd_kernel, L=L, r0=r0, D=D),
        grid_spec=pltpu.PrefetchScalarGridSpec(
            num_scalar_prefetch=1,
            grid=(NP,),
            in_specs=[
                pl.BlockSpec((1, L, 128), col),
                pl.BlockSpec((1, T, 128), col),
                pl.BlockSpec((1, T, 128), col),
                pl.BlockSpec((1, L, 128), col),
                pl.BlockSpec((1, L, 128), col),
                pl.BlockSpec((1, 1, L, 128), lambda p, m: (r0, p, 0, 0)),
                pl.BlockSpec((1, T, 128), lambda p, m: (r0, 0, 0)),
            ],
            out_specs=[pl.BlockSpec((1, L, 128), out), pl.BlockSpec((1, T, 128), out), pl.BlockSpec((1, T, 128), out)],
            scratch_shapes=[
                pltpu.VMEM((2, T, 128), BF),
                pltpu.VMEM((2, T, 128), BF),
                pltpu.VMEM((128, T), BF),
                pltpu.VMEM((2, L, L), F32),
                pltpu.VMEM((2, L, L), F32),
                pltpu.VMEM((128, L), F32),
                pltpu.VMEM((128, L), F32),
                pltpu.VMEM((128, L), F32),
            ],
        ),
        out_shape=[
            jax.ShapeDtypeStruct((1, L, W), BF),
            jax.ShapeDtypeStruct((1, T, W), BF),
            jax.ShapeDtypeStruct((1, T, W), BF),
        ],
        compiler_params=pltpu.CompilerParams(vmem_limit_bytes=48 << 20),
        cost_estimate=pl.CostEstimate(
            flops=60 * L * T * W, bytes_accessed=(3 * L + 4 * T) * W * 2, transcendentals=L * T * 18
        ),
        name="attn_bwd",
    )(meta, q, k, v, do, o, extra, ka)


def document_lanes(seg_q, seg_k):
    number = jnp.arange(64, dtype=jnp.int32)
    two = lambda m: jnp.concatenate([m, m], -1).astype(BF)
    qa = jnp.where((number < 8) & (number != seg_q[..., None]), FAR, 0.0)
    ka = jnp.where((number == seg_k[..., None]) | ((number >= 8) & (number < 11)), 1.0, 0.0)
    return two(qa), two(ka)


def dot_nn(a, b):
    return lax.dot_general(a, b, (((1,), (0,)), ((), ())), preferred_element_type=F32)


def dot_nt(a, b):
    return lax.dot_general(a, b, (((1,), (1,)), ((), ())), preferred_element_type=F32)


def turned(x):
    rank = x.shape[1]
    eye = (
        lax.broadcasted_iota(jnp.int32, (rank, rank), 0) == lax.broadcasted_iota(jnp.int32, (rank, rank), 1)
    ).astype(F32).astype(BF)
    return dot_nt(eye, x).astype(BF)


def place(x, first, width):
    rank = x.shape[1]
    to = lax.broadcasted_iota(jnp.int32, (rank, width), 1) == lax.broadcasted_iota(jnp.int32, (rank, width), 0) + first
    return dot_nn(x, to.astype(F32).astype(BF)).astype(BF)


def taken(x, first, rank):
    width = x.shape[1]
    to = lax.broadcasted_iota(jnp.int32, (rank, width), 1) == lax.broadcasted_iota(jnp.int32, (rank, width), 0) + first
    return dot_nt(to.astype(F32).astype(BF), x).astype(BF)


def whole_spec(shape, **kw):
    return pl.BlockSpec(shape, lambda *_: (0,) * len(shape), pipeline_mode=pl.Buffered(1))


def unpack_kernel(g_ref, mix_ref, out_ref, *, cm, co, D, W):
    S = g_ref.shape[0]
    rows = mix_ref.shape[2]
    half_width = cm + co
    for half in range(2):
        at = half * half_width
        mix = jnp.concatenate([g_ref[s, 0, :rows, at : at + cm] for s in range(S)], axis=1)
        out = jnp.concatenate([g_ref[s, 0, :rows, at + cm : at + half_width] for s in range(S)], axis=1)
        zero = jnp.zeros((mix.shape[0], W - D), mix.dtype)
        for i in range(3):
            mix_ref[0, half, :, i * W : (i + 1) * W] = jnp.concatenate([mix[:, i * D : (i + 1) * D], zero], axis=1)
        out_ref[0, half] = out


def unpack(g, S, C, rows2, cm, co, D, W):
    g = g.reshape(S, C, -1, 2 * (cm + co))
    mix, out = pl.pallas_call(
        functools.partial(unpack_kernel, cm=cm, co=co, D=D, W=W),
        grid=(C,),
        in_specs=[pl.BlockSpec((S, 1) + g.shape[2:], lambda c: (0, c, 0, 0))],
        out_specs=[
            pl.BlockSpec((1, 2, rows2, 3 * W), lambda c: (c, 0, 0, 0)),
            pl.BlockSpec((1, 2, rows2, D), lambda c: (c, 0, 0, 0)),
        ],
        out_shape=[
            jax.ShapeDtypeStruct((C, 2, rows2, 3 * W), BF),
            jax.ShapeDtypeStruct((C, 2, rows2, D), BF),
        ],
        compiler_params=pltpu.CompilerParams(vmem_limit_bytes=48 << 20),
        cost_estimate=pl.CostEstimate(flops=0, bytes_accessed=4 * g.size, transcendentals=0),
        name="unpack",
    )(g)
    return mix.reshape(D, 3 * W), out.reshape(D, D)


def qkv_kernel(meta_ref, *refs, count, W, R):
    n_refs = refs[:count]
    w_ref, m_ref, b_ref, q_ref, k_ref, v_ref, n_ref, wa_ref = refs[count:]
    j = pl.program_id(0)
    me = meta_ref[0]
    D = w_ref.shape[0]
    rank = m_ref.shape[1]
    for jj in range(count):

        @pl.when(j == jj)
        def _(jj=jj):
            n_ref[...] = n_refs[jj][...].reshape(n_ref.shape)

    @pl.when(j == 0)
    def _():
        wa_ref[:D] = w_ref[...]
        for r in range(R):
            wa_ref[D + r * rank : D + (r + 1) * rank] = m_ref[r]
        wa_ref[D + R * rank :] = jnp.zeros((W - D - R * rank, 3 * W), BF)

    def part(i):
        s = slice(i * W, (i + 1) * W)
        return (dot_nn(n_ref[...], wa_ref[:, s]) + b_ref[:, s]).reshape(R, -1, W)

    @pl.when(j == 0)
    def _():
        q_ref[...] = (part(0) * 0.125).astype(BF)

    @pl.when((me ^ j) <= me)
    def _():
        k_ref[...] = part(1).astype(BF)
        v_ref[...] = part(2).astype(BF)


def qkv(meta, n_parts, w, m, b):
    count = len(n_parts)
    R, L, W = n_parts[0].shape
    T = count * L
    row = pl.BlockSpec((R, L, W), lambda j, _: (0, j, 0))
    return pl.pallas_call(
        functools.partial(qkv_kernel, W=W, count=count, R=R),
        grid_spec=pltpu.PrefetchScalarGridSpec(
            num_scalar_prefetch=1,
            grid=(count,),
            in_specs=[whole_spec(x.shape) for x in (*n_parts, w, m, b)],
            out_specs=[whole_spec((R, L, W)), row, row],
            scratch_shapes=[pltpu.VMEM((R * L, W), BF), pltpu.VMEM((W, 3 * W), BF)],
        ),
        out_shape=[
            jax.ShapeDtypeStruct((R, L, W), BF),
            jax.ShapeDtypeStruct((R, T, W), BF),
            jax.ShapeDtypeStruct((R, T, W), BF),
        ],
        compiler_params=pltpu.CompilerParams(vmem_limit_bytes=60 << 20),
        cost_estimate=pl.CostEstimate(
            flops=4 * R * T * W * 2 * W, bytes_accessed=2 * (R * T * W + w.size + 2 * R * T * W), transcendentals=0
        ),
        name="qkv",
    )(meta, *n_parts, w, m, b)


def mid_kernel(
    o_ref, x_ref, dy_ref, wout_ref, e1_ref, e2_ref, x0_ref, x1_ref, gain_ref, shift_ref, xb_ref,
    res_ref, na_ref, da_ref, lo_ref,
):
    r = pl.program_id(0)
    D, W = o_ref.shape[2], na_ref.shape[2]
    rank = e1_ref.shape[1]
    o, dy = o_ref[0], dy_ref[0]
    lo = dot_nt(o, e1_ref[0]).astype(BF)
    lo_ref[0] = lo
    res = x_ref[0].astype(F32) + dot_nn(o, wout_ref[...]) + dot_nn(lo, x0_ref[0]) + xb_ref[...]
    res_ref[0] = res
    z, _ = layer_stats(res)
    n2 = (z * gain_ref[...] + shift_ref[...]).astype(BF)
    l3 = dot_nt(n2, e2_ref[0]).astype(BF)
    na_ref[0] = jnp.concatenate([n2, place(l3, r * rank, W - D)], axis=1)
    dl4 = dot_nt(dy, x1_ref[0]).astype(BF)
    da_ref[0] = jnp.concatenate([dy, place(dl4, r * rank, W - D)], axis=1)


def mid(o, x, dy, wout, e1, e2, x0, x1, gain, shift, xb, W):
    R, L, D = o.shape
    rank = e1.shape[1]
    row = pl.BlockSpec((1, L, D), lambda r: (r, 0, 0))
    wide = pl.BlockSpec((1, L, W), lambda r: (r, 0, 0))
    small = pl.BlockSpec((1, rank, D), lambda r: (r, 0, 0))
    return pl.pallas_call(
        mid_kernel,
        grid=(R,),
        in_specs=[row] * 3 + [whole_spec(wout.shape)] + [small] * 4 + [whole_spec((1, D))] * 3,
        out_specs=[row, wide, wide, pl.BlockSpec((1, L, rank), lambda r: (r, 0, 0))],
        out_shape=[
            jax.ShapeDtypeStruct((R, L, D), F32),
            jax.ShapeDtypeStruct((R, L, W), BF),
            jax.ShapeDtypeStruct((R, L, W), BF),
            jax.ShapeDtypeStruct((R, L, rank), BF),
        ],
        compiler_params=pltpu.CompilerParams(vmem_limit_bytes=48 << 20),
        cost_estimate=pl.CostEstimate(flops=2 * R * L * D * D, bytes_accessed=16 * R * L * D, transcendentals=0),
        name="mid",
    )(o, x, dy, wout, e1, e2, x0, x1, gain, shift, xb)


def ffn_kernel(
    na_ref, da_ref, res_ref, o_ref, lo_ref, wexp_ref, wshr_ref, rexp_ref, rshr_ref, eu_ref, eur_ref,
    hd_ref, hdr_ref, b_ref, br_ref, x0_ref, x1_ref, e1_ref, e2_ref, wout_ref, gain_ref, xb_ref,
    y_ref, dr_ref, do_ref, g1_ref, g2_ref, gx0_ref, gx1_ref, ge_ref, ger_ref, gh_ref, ghr_ref,
    out_acc, dn_acc, we_ref, ws_ref, l3_ref, dl4_ref, *, R, per, co,
):
    f = pl.program_id(0)
    last = pl.num_programs(0) - 1
    N, W = na_ref.shape
    L, D, rank = N // R, res_ref.shape[2], x0_ref.shape[1]

    @pl.when(f == 0)
    def _():
        out_acc[...] = jnp.zeros_like(out_acc)
        dn_acc[...] = jnp.zeros_like(dn_acc)
        we_ref[D:] = jnp.zeros((W - D, we_ref.shape[1]), BF)
        ws_ref[D:] = jnp.zeros((W - D, ws_ref.shape[1]), BF)
        for r in range(R):
            l3_ref[r] = taken(na_ref[r * L : (r + 1) * L, D // 128 * 128 :], D % 128 + r * rank, rank)
            dl4_ref[r] = taken(da_ref[r * L : (r + 1) * L, D // 128 * 128 :], D % 128 + r * rank, rank)

    def narrow(eu, hd, width):
        for r in range(R):
            we_ref[D + r * rank : D + (r + 1) * rank, :width] = eu[r]
            ws_ref[D + r * rank : D + (r + 1) * rank, :width] = hd[r]

    def block(width, b, ge, gh):
        we, ws = we_ref[:, :width], ws_ref[:, :width]
        h = dot_nn(na_ref[...], we) + b
        dg = dot_nn(da_ref[...], ws)
        c0, c1 = 0.7978845608028654, 0.7978845608028654 * 0.044715
        hh = h * h
        th = jnp.tanh(h * (c0 + c1 * hh))
        half = 0.5 + 0.5 * th
        g = (h * half).astype(BF)
        slope = half + (h * (0.5 - 0.5 * (th * th))) * (c0 + (3 * c1) * hh)
        dh = (dg * slope).astype(BF)
        out_acc[...] += dot_nt(g, ws)
        dn_acc[...] += dot_nt(dh, we)
        for r in range(R):
            gh[r] = dot_nn(dl4_ref[r], g[r * L : (r + 1) * L])
            ge[r] = dot_nn(l3_ref[r], dh[r * L : (r + 1) * L])

    we_ref[:D] = wexp_ref[...].reshape(D, -1)
    if per:
        for part in range(per):

            @pl.when(lax.rem(f, per) == part)
            def _(part=part):
                for s in range(wshr_ref.shape[0]):
                    ws_ref[s * co : (s + 1) * co] = wshr_ref[s, 0, part * co : (part + 1) * co]

    else:
        ws_ref[:D] = wshr_ref[0]
    narrow(eu_ref, hd_ref, we_ref.shape[1])
    block(we_ref.shape[1], b_ref[...], ge_ref, gh_ref)

    @pl.when(f == last)
    def _():
        width = rexp_ref.shape[1]
        we_ref[:D, :width] = rexp_ref[...]
        ws_ref[:D, :width] = rshr_ref[...]
        narrow(eur_ref, hdr_ref, width)
        block(width, br_ref[...], ger_ref, ghr_ref)

        def rows(r, carry):
            here = pl.ds(pl.multiple_of(r * L, L), L)
            edge = D // 128 * 128
            dy = da_ref[here, :D]
            l4_t = taken(out_acc[here, edge:].astype(BF), D % 128 + r * rank, rank)
            dl3_t = taken(dn_acc[here, edge:].astype(BF), D % 128 + r * rank, rank)
            gx1_ref[r] = dot_nn(l4_t, dy)
            g2_ref[r] = dot_nn(dl3_t, na_ref[here, :D])
            res = res_ref[r]
            low = lambda t, w: lax.dot_general(t, w, (((0,), (0,)), ((), ())), preferred_element_type=F32)
            y_ref[r] = (res + out_acc[here, :D] + low(l4_t, x1_ref[r]) + xb_ref[...]).astype(BF).T
            e = (dn_acc[here, :D] + low(dl3_t, e2_ref[r])) * gain_ref[...]
            z, inv = layer_stats(res)
            dr = dy.astype(F32) + norm_back(e, z, inv)
            dr_ref[r] = dr
            drb = dr.astype(BF)
            dl2 = dot_nt(drb, x0_ref[r]).astype(BF)
            do_ref[r] = (dot_nt(drb, wout_ref[...]) + dot_nn(dl2, e1_ref[r])).astype(BF)
            g1_ref[r] = dot_nn(turned(dl2), o_ref[r])
            gx0_ref[r] = dot_nn(turned(lo_ref[r]), drb)
            return carry

        lax.fori_loop(0, R, rows, 0)


def ffn(na, da, res, o, lo, wexp, wshr, rexp, rshr, eu, eur, hd, hdr, b, br, x0, x1, e1, e2, wout, gain, xb):
    R, L, D = res.shape
    N, W = na.shape
    rank = x0.shape[1]
    width, rem = wexp.shape[-1], rexp.shape[1]
    blocks = eu.shape[2] // width
    cols = lambda *lead: pl.BlockSpec(lead + (width,), lambda f: (0,) * len(lead) + (f,))
    if wexp.ndim == 4:
        S, C = wexp.shape[:2]
        per, co = S // C, D // S
        wexp_spec = pl.BlockSpec((1, C, D // C, width), lambda f: (f, 0, 0, 0))
        wshr_spec = pl.BlockSpec((S, 1, D // C, width), lambda f: (0, f // per, 1, 0))
    else:
        per = co = 0
        wexp_spec = wshr_spec = pl.BlockSpec((1, D, width), lambda f: (f, 0, 0))
    shapes = [
        ((R, D, L), BF), ((R, L, D), F32), ((R, L, D), BF),
        ((R, rank, D), F32), ((R, rank, D), F32), ((R, rank, D), F32), ((R, rank, D), F32),
        ((R, rank, blocks * width), F32), ((R, rank, rem), F32), ((R, rank, blocks * width), F32), ((R, rank, rem), F32),
    ]
    out_specs = [whole_spec(s) for s, _ in shapes]
    out_specs[7] = out_specs[9] = cols(R, rank)
    ff = blocks * width + rem
    return pl.pallas_call(
        functools.partial(ffn_kernel, R=R, per=per, co=co),
        grid=(blocks,),
        in_specs=[whole_spec(a.shape) for a in (na, da, res, o, lo)]
        + [wexp_spec, wshr_spec, whole_spec(rexp.shape), whole_spec(rshr.shape)]
        + [cols(R, rank), whole_spec(eur.shape), cols(R, rank), whole_spec(hdr.shape), cols(1), whole_spec(br.shape)]
        + [whole_spec(a.shape) for a in (x0, x1, e1, e2, wout, gain, xb)],
        out_specs=out_specs,
        out_shape=[jax.ShapeDtypeStruct(s, d) for s, d in shapes],
        scratch_shapes=[
            pltpu.VMEM((N, W), F32), pltpu.VMEM((N, W), F32), pltpu.VMEM((W, width), BF), pltpu.VMEM((W, width), BF),
            pltpu.VMEM((R, rank, L), BF), pltpu.VMEM((R, rank, L), BF),
        ],
        compiler_params=pltpu.CompilerParams(vmem_limit_bytes=60 << 20),
        cost_estimate=pl.CostEstimate(
            flops=16 * N * D * ff, bytes_accessed=4 * D * ff + 24 * N * D, transcendentals=N * ff
        ),
        name="ffn",
    )(na, da, res, o, lo, wexp, wshr, rexp, rshr, eu, eur, hd, hdr, b, br, x0, x1, e1, e2, wout, gain, xb)


def project_kernel(meta_ref, dq_ref, dk_ref, dv_ref, w_ref, m_ref, *refs, W, count, r):
    n_refs, refs = refs[:count], refs[count:]
    mine_ref, o_refs, g_ref, n_ref, t_ref, wa_ref = refs[0], refs[1:count], refs[count], *refs[count + 1 :]
    j = pl.program_id(0)
    me = meta_ref[0]
    D = w_ref.shape[0]
    rank = m_ref.shape[1]
    edge = D // 128 * 128
    for jj in range(count):

        @pl.when(j == jj)
        def _(jj=jj):
            n_ref[...] = n_refs[jj][0]

    @pl.when(j == 0)
    def _():
        g_ref[...] = jnp.zeros_like(g_ref)
        wa_ref[:D] = w_ref[...]
        wa_ref[D : D + rank] = m_ref[0]
        wa_ref[D + rank :] = jnp.zeros((W - D - rank, 3 * W), BF)

    def work(pieces):
        low_t = taken(n_ref[:, edge:], D % 128 + r * rank, rank)
        total = sum(dot_nt(d[0], wa_ref[:, i * W : (i + 1) * W]) for i, d in pieces)
        for i, d in pieces:
            g_ref[i] += dot_nn(low_t, d[0])
        g_ref[3] += dot_nn(taken(total[:, edge:].astype(BF), D % 128, rank), n_ref[...])
        return total

    @pl.when(j == 0)
    def _():
        mine_ref[...] = work([(0, dq_ref), (1, dk_ref), (2, dv_ref)])

    @pl.when((j > 0) & ((me ^ j) < me))
    def _():
        t_ref[...] = work([(1, dk_ref), (2, dv_ref)]).astype(BF)

    for jj in range(1, count):

        @pl.when(j == jj)
        def _(jj=jj):
            o_refs[jj - 1][...] = t_ref[...]


def project(meta, dq, dk, dv, w, m, n_parts, r):
    count = len(n_parts)
    _, L, W = dq.shape
    T = count * L
    rank = m.shape[1]
    out = pl.pallas_call(
        functools.partial(project_kernel, W=W, count=count, r=r),
        grid_spec=pltpu.PrefetchScalarGridSpec(
            num_scalar_prefetch=1,
            grid=(count,),
            in_specs=[
                whole_spec(dq.shape),
                pl.BlockSpec((1, L, W), lambda j, _: (0, j, 0)),
                pl.BlockSpec((1, L, W), lambda j, _: (0, j, 0)),
                whole_spec(w.shape),
                pl.BlockSpec((1, rank, 3 * W), lambda j, _: (r, 0, 0)),
            ]
            + [pl.BlockSpec((1, L, W), lambda j, _: (r, 0, 0))] * count,
            out_specs=[whole_spec((L, W))] * count + [whole_spec((4, rank, W))],
            scratch_shapes=[pltpu.VMEM((L, W), BF), pltpu.VMEM((L, W), BF), pltpu.VMEM((W, 3 * W), BF)],
        ),
        out_shape=[jax.ShapeDtypeStruct((L, W), F32)]
        + [jax.ShapeDtypeStruct((L, W), BF)] * (count - 1)
        + [jax.ShapeDtypeStruct((4, rank, W), F32)],
        compiler_params=pltpu.CompilerParams(vmem_limit_bytes=60 << 20),
        cost_estimate=pl.CostEstimate(
            flops=6 * T * W * 2 * W, bytes_accessed=2 * (w.size + 2 * T * W + 2 * T * W), transcendentals=0
        ),
        name="project",
    )(meta, dq, dk, dv, w, m, *n_parts)
    return out[:count], out[count]


def norm_kernel(x_ref, dy_ref, gain_ref, shift_ref, e_ref, n_ref, xr_ref, dyr_ref):
    x = x_ref[0].astype(F32)
    centred = x - jnp.mean(x, axis=0, keepdims=True)
    inv = lax.rsqrt(jnp.mean(centred * centred, axis=0, keepdims=True) + EPS)
    n = (centred * inv * gain_ref[...] + shift_ref[...]).astype(BF).T
    low = dot_nt(n, e_ref[0]).astype(BF)
    narrow = place(low, pl.program_id(0) * low.shape[1], n_ref.shape[2] - n.shape[1])
    n_ref[0] = jnp.concatenate([n, narrow], axis=1)
    xr_ref[0] = x_ref[0].T
    dyr_ref[0] = dy_ref[0].T


def first_norm(x_t, dy_t, gain, shift, e_t, W):
    R, D, L = x_t.shape
    col = pl.BlockSpec((1, D, L), lambda r: (r, 0, 0))
    row = pl.BlockSpec((1, L, D), lambda r: (r, 0, 0))
    return pl.pallas_call(
        norm_kernel,
        grid=(R,),
        in_specs=[col, col, whole_spec((D, 1)), whole_spec((D, 1)), pl.BlockSpec((1,) + e_t.shape[1:], lambda r: (r, 0, 0))],
        out_specs=[pl.BlockSpec((1, L, W), lambda r: (r, 0, 0)), row, row],
        out_shape=[jax.ShapeDtypeStruct((R, L, W), BF)] + [jax.ShapeDtypeStruct((R, L, D), BF)] * 2,
        compiler_params=pltpu.CompilerParams(vmem_limit_bytes=48 << 20),
        cost_estimate=pl.CostEstimate(flops=10 * x_t.size, bytes_accessed=10 * x_t.size, transcendentals=0),
        name="first_norm",
    )(x_t, dy_t, gain[:, None], shift[:, None], e_t)


def last_kernel(*refs, count, alias):
    if alias:
        refs = refs[1:]
    terms, (dr_ref, x_ref, gain_ref, e_ref, o_ref) = refs[:count], refs[count:]
    D = x_ref.shape[2]
    dn = terms[0][...]
    for t in terms[1:]:
        dn = dn + t[...].astype(F32)
    edge = D // 128 * 128
    rank = e_ref.shape[1]
    low_t = taken(dn[:, edge:].astype(BF), D % 128, rank)
    dn = dn[:, :D] + lax.dot_general(low_t, e_ref[0], (((0,), (0,)), ((), ())), preferred_element_type=F32)
    z, inv = layer_stats(x_ref[0].astype(F32))
    o_ref[0] = (dr_ref[0] + norm_back(dn * gain_ref[...], z, inv)).astype(BF).T


def last(r, before, terms, dr, x, gain, e_t):
    R, L, D = x.shape
    alias = before is not None
    return pl.pallas_call(
        functools.partial(last_kernel, count=len(terms), alias=alias),
        grid=(1,),
        in_specs=[pl.BlockSpec(memory_space=pl.ANY)] * alias
        + [whole_spec(t.shape) for t in terms]
        + [pl.BlockSpec((1, L, D), lambda i: (r, 0, 0))] * 2
        + [whole_spec((1, D)), pl.BlockSpec((1,) + e_t.shape[1:], lambda i: (r, 0, 0))],
        out_specs=pl.BlockSpec((1, D, L), lambda i: (r, 0, 0)),
        out_shape=jax.ShapeDtypeStruct((R, D, L), BF),
        input_output_aliases={0: 0} if alias else {},
        compiler_params=pltpu.CompilerParams(vmem_limit_bytes=48 << 20),
        cost_estimate=pl.CostEstimate(flops=20 * L * D, bytes_accessed=12 * L * D, transcendentals=0),
        name="last",
    )(*([before] if alias else []), *terms, dr, x, gain, e_t)


def late_kernel(slot_ref, part_ref, *refs, R, parts, D, W):
    g_refs, mix_ref, entry_ref, total = refs[:R], refs[R], refs[R + 1], refs[R + 2]
    total[...] = jnp.zeros_like(total)
    count = g_refs[0].shape[0]
    for r in range(R):

        def one(i, carry):
            a = slot_ref[r * count + i]
            c = part_ref[i]
            total[a, c] = total[a, c] + g_refs[r][i].astype(F32)
            return carry

        lax.fori_loop(0, count, one, 0)
    per = parts // 4
    wide = [jnp.concatenate([total[:, i * per + p] for p in range(per)], axis=-1) for i in range(4)]
    mix_ref[...] = jnp.concatenate([w[:, :, :D] for w in wide[:3]], axis=-1)
    entry_ref[...] = wide[3][:, :, :D]


def late_slots(slot, part, gs, adapters, parts, D, W):
    R = len(gs)
    _, rank, width = gs[0].shape
    return pl.pallas_call(
        functools.partial(late_kernel, R=R, parts=parts, D=D, W=W),
        grid_spec=pltpu.PrefetchScalarGridSpec(
            num_scalar_prefetch=2,
            grid=(1,),
            in_specs=[whole_spec(g.shape) for g in gs],
            out_specs=[whole_spec((adapters, rank, 3 * D)), whole_spec((adapters, rank, D))],
            scratch_shapes=[pltpu.VMEM((adapters, parts, rank, width), F32)],
        ),
        out_shape=[
            jax.ShapeDtypeStruct((adapters, rank, 3 * D), F32),
            jax.ShapeDtypeStruct((adapters, rank, D), F32),
        ],
        compiler_params=pltpu.CompilerParams(vmem_limit_bytes=48 << 20),
        cost_estimate=pl.CostEstimate(flops=0, bytes_accessed=8 << 20, transcendentals=0),
        name="late_slots",
    )(slot, part, *gs)


def mm(pattern, a, b):
    return jnp.einsum(pattern, a, b, preferred_element_type=F32)


def layer_stats(v):
    middle = jnp.mean(v, axis=-1, keepdims=True)
    centred = v - middle
    inv = lax.rsqrt(jnp.mean(centred * centred, axis=-1, keepdims=True) + EPS)
    return centred * inv, inv


def norm_back(e, z, inv):
    return (e - jnp.mean(e, -1, keepdims=True) - z * jnp.mean(e * z, -1, keepdims=True)) * inv


def swap(x, axis, bit, needed):
    n = lax.axis_size(axis)
    return lax.ppermute(x, axis, [(d ^ bit, d) for d in range(n) if needed(d)])


def blocks_of(x, bits):
    found = {0: x}
    for bit in reversed(bits):
        for j in sorted(found):
            found[j | bit] = swap(found[j], "ctx", bit, lambda d, k=j | bit: (d ^ k) < d)
    return [found[j] for j in sorted(found)]


def blocks_back(parts, bits):
    held = {j: [p] for j, p in enumerate(parts)}
    for bit in bits:
        for j in sorted(held):
            if j & bit:
                sent = held.pop(j)
                sent = sent[0] if len(sent) == 1 else sum(t.astype(F32) for t in sent).astype(BF)
                got = swap(sent, "ctx", bit, lambda d, k=j, b=bit: ((d ^ b) ^ k) < (d ^ b))
                held[j ^ bit].append(got)
    return held[0]


def ctx_sum_rows(g, bits):
    n = lax.axis_size("ctx")
    me = lax.axis_index("ctx")
    for bit in reversed(bits):
        half = g.shape[0] // 2
        mine = (me & bit) != 0
        low, high = g[:half], g[half:]
        got = lax.ppermute(jnp.where(mine, low, high), "ctx", [(d, d ^ bit) for d in range(n)])
        g = jnp.where(mine, high, low) + got
    return g


def gather_all(x, seq_count, ctx_count):
    n = seq_count * ctx_count
    seq_bits = [ctx_count << i for i in range(seq_count.bit_length() - 1)]
    ctx_bits = [1 << i for i in range(ctx_count.bit_length() - 1)]
    held, order = x[None], [0]
    for bit in seq_bits + ctx_bits[::-1]:
        got = lax.ppermute(held, BOTH, [(d, d ^ bit) for d in range(n)])
        held = jnp.concatenate([held, got], 0)
        order = order + [o ^ bit for o in order]
    return held, order


def slots_kernel(index_ref, g_ref, *refs, count, spans):
    outs, total = refs[:-1], refs[-1]
    total[...] = jnp.zeros_like(total)

    def one(i, carry):
        a = index_ref[i]
        total[a] = total[a] + g_ref[i].astype(F32)
        return carry

    lax.fori_loop(0, count, one, 0)
    for out, pieces in zip(outs, spans):
        parts = [total[:, :, first : first + width] for first, width in pieces]
        out[...] = parts[0] if len(parts) == 1 else jnp.concatenate(parts, axis=-1)


def to_slots(index, g, adapters, spans):
    count, rank, wide = g.shape
    rows = 8
    widths = [sum(w for _, w in pieces) for pieces in spans]
    return pl.pallas_call(
        functools.partial(slots_kernel, count=count, spans=spans),
        grid_spec=pltpu.PrefetchScalarGridSpec(
            num_scalar_prefetch=1,
            grid=(rank // rows,),
            in_specs=[pl.BlockSpec((count, rows, wide), lambda i, m: (0, i, 0))],
            out_specs=[pl.BlockSpec((adapters, rows, w), lambda i, m: (0, i, 0)) for w in widths],
            scratch_shapes=[pltpu.VMEM((adapters, rows, wide), F32)],
        ),
        out_shape=[jax.ShapeDtypeStruct((adapters, rank, w), F32) for w in widths],
        compiler_params=pltpu.CompilerParams(vmem_limit_bytes=48 << 20),
        cost_estimate=pl.CostEstimate(
            flops=count * rank * wide, bytes_accessed=count * rank * wide * 2 + adapters * rank * wide * 4, transcendentals=0
        ),
        name="to_slots",
    )(index, g)


def per_device(
    tokens, segments, adapter_index, norm_gains, norm_shifts, head_biases, expand_bias, exit_biases,
    mixing_weight, output_weight, expand_weight, shrink_weight,
    entry_adapters, mixing_adapters, expand_adapters, hidden_adapters, exit_adapters, cotangent,
):
    micro, seqs, L, D = tokens.shape
    R = micro * seqs
    adapters, rank = mixing_adapters.shape[:2]
    FF = expand_bias.shape[0]
    C = lax.axis_size("ctx")
    S = lax.axis_size("seq")
    bits = [1 << i for i in range(C.bit_length() - 1)]
    me = lax.axis_index("ctx")
    T = C * L
    W = -(-D // 128) * 128
    pad = W - D

    rows = mixing_weight.shape[0]
    cm, co, ce = mixing_weight.shape[1], output_weight.shape[1], expand_weight.shape[1]
    first = jnp.concatenate([mixing_weight, output_weight], 1)
    first = jnp.concatenate([first[: rows // 2], first[rows // 2 :]], 1)
    main = ce // 128 * 128
    rem = ce - main
    per = S // C
    shr_t = shrink_weight.T.reshape(co, per, ce).transpose(1, 0, 2)
    rest = jnp.concatenate([expand_weight[:, main:].reshape(-1), shr_t[:, :, main:].reshape(-1)])
    rest_rows = -(-rest.shape[0] // first.shape[1])
    rest = jnp.pad(rest, (0, rest_rows * first.shape[1] - rest.shape[0])).reshape(rest_rows, -1)
    first = jnp.concatenate([first, rest], 0)
    second = jnp.concatenate([expand_weight[:, :main], shr_t[:, :, :main].reshape(per * co, main)], 0)
    g1 = lax.all_gather(first, BOTH)
    g2 = lax.all_gather(second, BOTH).reshape(S, C, -1, main)
    w_mix, w_out = unpack(g1, S, C, rows // 2, cm, co, D, W)
    if rows % 16 == 0 and per * co == rows and co % 8 == 0:
        w_exp = w_shr = g2
    else:
        w_exp = g2[:, :, :rows].reshape(S, D, main)
        w_shr = g2[:, :, rows:].reshape(S, C, per, co, main).transpose(1, 2, 0, 3, 4).reshape(S, D, main)
    flat = g1[:, rows // 2 :].reshape(S, C, -1)
    r_exp = flat[..., : rows * rem].reshape(S, C, rows, rem).transpose(1, 2, 0, 3).reshape(D, S * rem)
    r_shr = flat[..., rows * rem : rows * rem + per * co * rem].reshape(S, C, per, co, rem)
    r_shr = r_shr.transpose(0, 3, 1, 2, 4).reshape(D, S * rem)

    def split_ff(m):
        m = m.reshape(m.shape[:-1] + (S, ce))
        return m[..., :main].reshape(m.shape[:-2] + (S * main,)), m[..., main:].reshape(m.shape[:-2] + (S * rem,))

    index = adapter_index.reshape(R)
    take = lambda table, axis: jnp.stack(
        [lax.dynamic_index_in_dim(table, index[r], axis, keepdims=False) for r in range(R)], axis
    )
    entry = take(entry_adapters, 1)
    mix_up = take(mixing_adapters, 0)
    exp_up = take(expand_adapters, 0)
    hid = take(hidden_adapters, 0)
    exit_up = take(exit_adapters, 1)
    pad_heads = lambda m: jnp.concatenate([padded(m[..., i * D : (i + 1) * D]) for i in range(3)], -1)
    padded = lambda m: jnp.pad(m, [(0, 0)] * (m.ndim - 1) + [(0, pad)])
    mix_up = pad_heads(mix_up)
    flip = lambda m: jnp.swapaxes(m, -1, -2)
    entry_t = flip(entry)
    exp_main, exp_rest = split_ff(exp_up)
    hid_main, hid_rest = split_ff(flip(hid))
    bias_main, bias_rest = split_ff(expand_bias[None])
    head_bias = pad_heads(jnp.concatenate([head_biases[0], jnp.zeros_like(head_biases[0]), head_biases[1]])[None])

    seg = segments.reshape(R, L)
    seg_blocks = blocks_of(seg, bits)
    first_block = me * jnp.ones((R,), jnp.int32)
    for j, other in enumerate(seg_blocks):
        reached = ((me ^ j) <= me) & jnp.any(other == seg[:, :1], axis=1)
        first_block = jnp.where(reached, jnp.minimum(first_block, me ^ j), first_block)
    meta = jnp.concatenate([me[None], first_block]).astype(jnp.int32)
    qa, ka = document_lanes(seg, jnp.concatenate(seg_blocks, 1))

    n1, x, dy = first_norm(
        flip(tokens.reshape(R, L, D)), flip(cotangent.reshape(R, L, D)), norm_gains[0], norm_shifts[0],
        entry_t[0], W,
    )
    n1_parts = blocks_of(n1, bits)
    q, k, v = qkv(meta, n1_parts, w_mix, mix_up, head_bias)
    o, extra = attn_fwd(meta, q, k, v, qa, ka, D)

    res, na, da, lo = mid(
        o, x, dy, w_out, entry_t[1], entry_t[2], exit_up[0], exit_up[1], norm_gains[1][None], norm_shifts[1][None],
        exit_biases[0][None], W,
    )
    y, dr, do, g1, g2_, gx0, gx1, ge, ger, gh, ghr = ffn(
        na.reshape(R * L, W), da.reshape(R * L, W), res, o, lo, w_exp, w_shr, r_exp, r_shr,
        exp_main, exp_rest, hid_main, hid_rest, bias_main, bias_rest,
        exit_up[0], exit_up[1], entry_t[1], entry_t[2], w_out, norm_gains[1][None], exit_biases[1][None],
    )
    layer_output = flip(y).reshape(tokens.shape)

    number = jnp.broadcast_to((index.astype(F32) / C)[:, None, None], (R, rank, 128))
    early = jnp.concatenate([g1, g2_, gx0, gx1, ge, ger, gh, ghr, number], -1).reshape(R * rank, -1)
    early = ctx_sum_rows(early, bits).astype(BF)
    early = lax.all_gather(early, BOTH).reshape(S * R, rank, -1)
    all_index = early[:, 0, -1].astype(jnp.int32)
    spans = [[(i * D, D)] for i in range(4)]
    for at in (4 * D, 4 * D + FF):
        spans.append(
            [p for i in range(S) for p in ((at + i * main, main), (at + S * main + i * rem, rem))]
        )
    entry1_g, entry2_g, exit0_g, exit1_g, expand_g, hidden_g = to_slots(all_index, early, adapters, spans)

    input_grad, late, terms = None, [], []
    for r in range(R):
        dq, dk, dv = attn_bwd(meta, q, k, v, do, o, extra, ka, r)
        if r:
            dk, terms[r - 1] = lax.optimization_barrier((dk, terms[r - 1]))
        parts, g = project(meta, dq, dk, dv, w_mix, mix_up, n1_parts, r)
        if r + 1 < R:
            do, parts = lax.optimization_barrier((do, parts))
        terms.append(blocks_back(parts, bits))
        g = g.reshape(4, rank, C // 4, -1).transpose(0, 2, 1, 3).reshape(C, rank, -1)
        late.append(gather_all(ctx_sum_rows(g, bits)[0].astype(BF), S, C))
    for r in range(R):
        input_grad = last(r, input_grad, terms[r], dr, x, norm_gains[0][None], entry_t[0])
    device = lax.axis_index("seq") * C + me
    order = device ^ jnp.array(late[0][1], jnp.int32)
    by_row = all_index.reshape(S, R)
    slot = jnp.concatenate([jnp.sum(jnp.where((order // C)[:, None] == jnp.arange(S), by_row[:, r], 0), 1) for r in range(R)])
    mixing_g, entry0_g = late_slots(slot, order % C, [g for g, _ in late], adapters, C, D, W)
    input_grad = flip(input_grad).reshape(tokens.shape)

    return (
        layer_output,
        input_grad,
        jnp.stack([flip(entry0_g), flip(entry1_g), flip(entry2_g)]),
        mixing_g,
        expand_g,
        flip(hidden_g),
        jnp.stack([exit0_g, exit1_g]),
    )


def solution(mesh):
    rows = P(None, "seq", "ctx", None)
    weight = P("ctx", "seq")
    in_specs = (
        (rows, P(None, "seq", "ctx"), P(None, "seq")) + (P(),) * 5 + (weight,) * 4 + (P(),) * 5 + (rows,)
    )
    out_specs = (rows, rows) + (P(),) * 5
    return jax.shard_map(per_device, mesh=mesh, in_specs=in_specs, out_specs=out_specs, check_vma=False)
```

time: 760 us -> 694 us (0.913)
  starting transfers between devices: 171 us -> 128 us
  Pallas kernels: 357 us -> 317 us
  waiting for transfers between devices: 122 us -> 139 us
  matrix products: 8.03 us -> 0 us
    ppermute x6, starting transfers between devices: 110 us -> 79.3 us  [ctx_sum_rows(): lax.ppermute(jnp.where(mine, low, high), 'ctx', [(d, d ^ bit) for d in ra...]
    pallas_call x6 -> x7, Pallas kernels: 232 us -> 206 us  [the longest x2 79.4 us: attn_bwd(): pl.pallas_call(functools.partial(attn_bwd_kernel, L=L, r0=r0, D=D), grid_...]
    all_gather x1, waiting for transfers between devices: 0.01 us -> 16.8 us  [per_device(): g2 = lax.all_gather(second, BOTH).reshape(S, C, -1, main)]
    pallas_call x1, Pallas kernels: 90.2 us -> 76.2 us  [ffn(): pl.pallas_call(functools.partial(ffn_kernel, R=R, per=per, co=co), grid=(...]
    ppermute x10, starting transfers between devices: 41.5 us -> 27.7 us  [gather_all(): got = lax.ppermute(held, BOTH, [(d, d ^ bit) for d in range(n)])]
    ppermute x6, waiting for transfers between devices: 16.1 us -> 3.68 us  [ctx_sum_rows(): lax.ppermute(jnp.where(mine, low, high), 'ctx', [(d, d ^ bit) for d in ra...]
    ppermute x10, waiting for transfers between devices: 24.7 us -> 35.3 us  [gather_all(): got = lax.ppermute(held, BOTH, [(d, d ^ bit) for d in range(n)])]
    dot_general x4 -> x0, matrix products: 8.03 us -> none  [mm(): return jnp.einsum(pattern, a, b, preferred_element_type=F32)]
  transfers between devices with their start and end apart: 31 -> 31, of which waited for: 15 -> 15; matrix products, arithmetic and copies ran while one was open for 7% -> 8% of each run, Pallas kernels for 34% -> 34%
where the time goes in v3:
time: 694 us; the launch traced here: 683 us
  Pallas kernels  317 us (46%)
  waiting for transfers between devices  139 us (20%)
  starting transfers between devices  128 us (18%)
  local copies, waits for them, and re-layouts  56 us (8%)
  other arithmetic  23.7 us (3%)
  between operations  19.1 us (3%)
    ppermute x12, waiting for transfers between devices, swap(): return lax.ppermute(x, axis, [(d ^ bit, d) for d in range(n) if needed(d)])  81.1 us
    pallas_call x2, Pallas kernels, attn_bwd(): pl.pallas_call(functools.partial(attn_bwd_kernel, L=L, r0=r0, D=D), grid_...  79.4 us
    ppermute x6, starting transfers between devices, ctx_sum_rows(): lax.ppermute(jnp.where(mine, low, high), 'ctx', [(d, d ^ bit) for d in ra...  79.3 us
    pallas_call x1, Pallas kernels, ffn(): pl.pallas_call(functools.partial(ffn_kernel, R=R, per=per, co=co), grid=(...  76.2 us
    pallas_call x2, Pallas kernels, project(): pl.pallas_call(functools.partial(project_kernel, W=W, count=count, r=r),...  42.3 us
    pallas_call x1, Pallas kernels, attn_fwd(): pl.pallas_call(functools.partial(attn_fwd_kernel, L=L), grid_spec=pltpu.P...  40.5 us
    ppermute x10, waiting for transfers between devices, gather_all(): got = lax.ppermute(held, BOTH, [(d, d ^ bit) for d in range(n)])  35.3 us
    pallas_call x1, Pallas kernels, qkv(): pl.pallas_call(functools.partial(qkv_kernel, W=W, count=count, R=R), grid...  30.9 us
  transfers between devices with their start and end apart: 31, of which 15 were waited for; matrix products, arithmetic and copies ran while one was open for 8% of the time, Pallas kernels for 34%

profile of v3, /device:TPU:5, one launch (start us, length us, event | category | flops | bytes accessed | tf_op | source)
XLA Modules:
  0.0 682.7 jit_solution(6101440190441410609)
XLA Ops:
  11.2 3.1 collective-permute-start
  24.1 1.7 copy-done.5
  25.8 5.1 first_norm.1
  30.9 2.9 collective-permute-start.4
  49.2 59.2 %collective-permute-done.4.refs_2_ = bf16[2,512,1152]{2,1,0:T(8,128)(2,1)} collective-permute-done((bf16[2,512,1152]{2,1,0:T(8,128)(2,1)}, bf16[2,512,1152]{2,1,0:T(8,128)(2,1)}, u32[]{:S(2)}, u32[]{:S(2)}) %collective-permute-start.4) | collective-permute-done | bytes 2359328 | tf_op jit(solution)/shard_map/ppermute | solution.py:767
  108.5 2.3 collective-permute-start.5
  111.9 1.9 all-gather.7.cloned.1.call-done
  113.8 9.4 %unpack.1 = (bf16[4,2,136,3456]{3,2,1,0:T(8,128)(2,1)}, bf16[4,2,136,1088]{3,2,1,0:T(8,128)(2,1)S(1)}) custom-call(bf16[8,4,152,1088]{3,2,1,0:T(8,128)(2,1)} %bitcast.105), custom_call_target="tpu_custom_call" | custom-call | bytes 21168128 | tf_op jit(solution)/shard_map/unpack/pallas_call | solution.py:312
  126.0 2.0 reshape.155
  128.0 2.4 fusion.21
  130.6 2.5 reshape.158
  133.0 3.3 copy.61
  138.5 2.5 reshape.156
  141.0 3.3 copy.59
  145.8 30.9 %qkv.1 = (bf16[2,512,1152]{2,1,0:T(8,128)(2,1)}, bf16[2,2048,1152]{2,1,0:T(8,128)(2,1)}, bf16[2,2048,1152]{2,1,0:T(8,128)(2,1)}) custom-call(s32[3]{0:T(128)} %pad_add_fusion.1.meta_ref, bf16[2,512,1152]{2,1,0:T(8,128)(2,1)} %get-tuple-element.65.refs_0_, bf16[2,512,1152]{2,1,0:T(8,128)(2,1)} %collective-permute-done.3.refs_1_, ...), custom_call_target="tpu_custom_call" | custom-call | flops 43486543872 | bytes 35831808 | tf_op jit(solution)/shard_map/qkv/pallas_call | solution.py:370
  176.7 40.5 %attn_fwd.1 = (bf16[2,512,1088]{2,1,0:T(8,128)(2,1)S(1)}, bf16[2,9,512,128]{3,2,1,0:T(8,128)(2,1)S(1)}) custom-call(s32[3]{0:T(128)S(1)} %copy-done.20, bf16[2,512,1152]{2,1,0:T(8,128)(2,1)} %get-tuple-element.67.q_ref, bf16[2,2048,1152]{2,1,0:T(8,128)(2,1)} %get-tuple-element.68.k_ref, bf16[2,2048,1152]{2,1,0:T(8,128)(2,1)} %get-tuple-element.69.v_ref, ...), custom_call_target="tpu_custom_call" | custom-call | flops 96636764160 | bytes 23592960 | tf_op jit(solution)/shard_map/attn_fwd/pallas_call | solution.py:105
  220.1 13.1 %mid.1 = (f32[2,512,1088]{2,1,0:T(8,128)}, bf16[2,512,1152]{2,1,0:T(8,128)(2,1)S(1)}, bf16[2,512,1152]{2,1,0:T(8,128)(2,1)S(1)}, bf16[2,512,16]{2,1,0:T(8,128)(2,1)S(1)}) custom-call(bf16[2,512,1088]{2,1,0:T(8,128)(2,1)} %copy-done.3, bf16[2,512,1088]{2,1,0:T(8,128)(2,1)} %get-tuple-element.71.x_ref.refs_4_.refs_5_, ...), custom_call_target="tpu_custom_call" | custom-call | flops 2424307712 | bytes 17825792 | tf_op jit(solution)/shard_map/mid/pallas_call | solution.py:418
  236.7 16.8 %all-gather.9.cloned.1.call-done = bf16[17408,512]{1,0:T(8,128)(2,1)} async-done(((bf16[544,512]{1,0:T(8,128)(2,1)}), bf16[17408,512]{1,0:T(8,128)(2,1)}) %all-gather.9.cloned.1.call-update) | async-done | bytes 17825808 | tf_op jit(solution)/shard_map/all_gather | solution.py:882
  253.6 76.2 %ffn.1 = (bf16[2,1088,512]{2,1,0:T(8,128)(2,1)}, f32[2,512,1088]{2,1,0:T(8,128)}, bf16[2,512,1088]{2,1,0:T(8,128)(2,1)}, f32[2,16,1088]{2,1,0:T(8,128)}, f32[2,1...) custom-call(bf16[1024,1152]{1,0:T(8,128)(2,1)} %bitcast.103, ...), custom_call_target="tpu_custom_call" | custom-call | flops 77577846784 | bytes 45678592 | tf_op jit(solution)/shard_map/ffn/pallas_call | solution.py:548
  329.8 1.6 concatenate.99
  332.9 37.8 %collective-permute-start.12 = (f32[16,13184]{1,0:T(8,128)}, f32[16,13184]{1,0:T(8,128)}, u32[]{:S(2)}, u32[]{:S(2)}) collective-permute-start(f32[16,13184]{1,0:T(8,128)} %select_bitcast_fusion), channel_id=1, source_target_pairs={{0,2},{1,3},{2,0},{3,1},{4,6},{5,7},{6,4},{7,5},{8,10},{9,11},{10,... | collective-permute-start | bytes 2531336 | tf_op jit(solution)/shard_map/ppermute | solution.py:797
  370.7 39.6 %attn_bwd.2 = (bf16[1,512,1152]{2,1,0:T(8,128)(2,1)S(1)}, bf16[1,2048,1152]{2,1,0:T(8,128)(2,1)}, bf16[1,2048,1152]{2,1,0:T(8,128)(2,1)}) custom-call(s32[3]{0:T(128)S(1)} %copy-done.20, bf16[2,512,1152]{2,1,0:T(8,128)(2,1)S(1)} %copy-done.24, bf16[2,2048,1152]{2,1,0:T(8,128)(2,1)} %get-tuple-element.68.k_ref, ...), custom_call_target="tpu_custom_call" | custom-call | flops 72477573120 | bytes 22413312 | tf_op jit(solution)/shard_map/attn_bwd/pallas_call | solution.py:217
  411.4 21.2 %project.2 = (f32[512,1152]{1,0:T(8,128)}, bf16[512,1152]{1,0:T(8,128)(2,1)}, bf16[512,1152]{1,0:T(8,128)(2,1)}, bf16[512,1152]{1,0:T(8,128)(2,1)}, f32[4,16,1152]{2,1,0:T(8,128)}) custom-call(s32[3]{0:T(128)} %pad_add_fusion.1.meta_ref, bf16[1,512,1152]{2,1,0:T(8,128)(2,1)} %copy-done.23, bf16[1,2048,1152]{2,1,0:T(8,128)(2,1)} %get-tuple-element.82.dk_ref, ...), custom_call_target="tpu_custom_call" | custom-call | flops 32614907904 | bytes 26394624 | tf_op jit(solution)/shard_map/project/pallas_call | solution.py:618
  433.6 34.3 %collective-permute-start.14 = (f32[2,16,1152]{2,1,0:T(8,128)S(1)}, f32[2,16,1152]{2,1,0:T(8,128)S(1)}, u32[]{:S(2)}, u32[]{:S(2)}) collective-permute-start(f32[2,16,1152]{2,1,0:T(8,128)S(1)} %slice_select_fusion.2), channel_id=1, source_target_pairs={{0,2},{1,3},{2,0},{3,1},{4,6},{5,7},{6,4},{7,5},{8,10},{9,11},{10,... | collective-permute-start | bytes 442376 | tf_op jit(solution)/shard_map/ppermute | solution.py:797
  467.9 1.9 collective-permute-start.7
  475.5 1.7 copy-done.25
  477.2 39.8 %attn_bwd.3 = (bf16[1,512,1152]{2,1,0:T(8,128)(2,1)S(1)}, bf16[1,2048,1152]{2,1,0:T(8,128)(2,1)}, bf16[1,2048,1152]{2,1,0:T(8,128)(2,1)}) custom-call(s32[3]{0:T(128)S(1)} %copy-done.21, bf16[2,512,1152]{2,1,0:T(8,128)(2,1)S(1)} %copy-done.25, bf16[2,2048,1152]{2,1,0:T(8,128)(2,1)} %get-tuple-element.68.k_ref, ...), custom_call_target="tpu_custom_call" | custom-call | flops 72477573120 | bytes 22413312 | tf_op jit(solution)/shard_map/attn_bwd/pallas_call | solution.py:217
  524.6 7.4 %collective-permute-done.17 = bf16[2,16,1152]{2,1,0:T(8,128)(2,1)S(1)} collective-permute-done((bf16[2,16,1152]{2,1,0:T(8,128)(2,1)S(1)}, bf16[2,16,1152]{2,1,0:T(8,128)(2,1)S(1)}, u32[]{:S(2)}, u32[]{:S(2)}) %collective-permute-start.17) | collective-permute-done | bytes 73760 | tf_op jit(solution)/shard_map/ppermute | solution.py:808
  532.7 12.4 %collective-permute-done.18 = bf16[4,16,1152]{2,1,0:T(8,128)(2,1)S(1)} collective-permute-done((bf16[4,16,1152]{2,1,0:T(8,128)(2,1)S(1)}, bf16[4,16,1152]{2,1,0:T(8,128)(2,1)S(1)}, u32[]{:S(2)}, u32[]{:S(2)}) %collective-permute-start.18) | collective-permute-done | bytes 147488 | tf_op jit(solution)/shard_map/ppermute | solution.py:808
  545.9 15.5 %collective-permute-start.19 = (bf16[8,16,1152]{2,1,0:T(8,128)(2,1)}, bf16[8,16,1152]{2,1,0:T(8,128)(2,1)S(1)}, u32[]{:S(2)}, u32[]{:S(2)}) collective-permute-start(bf16[8,16,1152]{2,1,0:T(8,128)(2,1)} %pad_maximum_fusion.6), channel_id=1, source_target_pairs={{0,2},{1,3},{2,0},{3,1},{4,6},{5,7},{6,4},{7,5},{8,10},{9,11},{10,... | collective-permute-start | bytes 884744 | tf_op jit(solution)/shard_map/ppermute | solution.py:808
  561.4 5.9 collective-permute-done.8.refs_2_
  567.3 21.1 %project.3 = (f32[512,1152]{1,0:T(8,128)}, bf16[512,1152]{1,0:T(8,128)(2,1)}, bf16[512,1152]{1,0:T(8,128)(2,1)}, bf16[512,1152]{1,0:T(8,128)(2,1)}, f32[4,16,1152]{2,1,0:T(8,128)}) custom-call(s32[3]{0:T(128)} %pad_add_fusion.1.meta_ref, bf16[1,512,1152]{2,1,0:T(8,128)(2,1)} %copy-done.22, bf16[1,2048,1152]{2,1,0:T(8,128)(2,1)} %get-tuple-element.99.dk_ref, ...), custom_call_target="tpu_custom_call" | custom-call | flops 32614907904 | bytes 26394624 | tf_op jit(solution)/shard_map/project/pallas_call | solution.py:618
  589.5 6.5 collective-permute-start.21
  596.6 1.8 collective-permute-done.21
  601.6 2.1 collective-permute-start.9
  608.0 2.1 collective-permute-done.24
  610.2 1.9 collective-permute-start.25
  612.1 7.1 %collective-permute-done.25 = bf16[4,16,1152]{2,1,0:T(8,128)(2,1)S(1)} collective-permute-done((bf16[4,16,1152]{2,1,0:T(8,128)(2,1)S(1)}, bf16[4,16,1152]{2,1,0:T(8,128)(2,1)S(1)}, u32[]{:S(2)}, u32[]{:S(2)}) %collective-permute-start.25) | collective-permute-done | bytes 147488 | tf_op jit(solution)/shard_map/ppermute | solution.py:808
  619.3 3.1 collective-permute-start.26
  622.7 1.6 collective-permute-start.11
  624.4 4.0 collective-permute-done.26
  628.4 3.6 collective-permute-start.27
  632.2 5.4 last.2.refs_0_
  637.6 16.0 %collective-permute-done.11.refs_3_ = bf16[512,1152]{1,0:T(8,128)(2,1)S(1)} collective-permute-done((bf16[512,1152]{1,0:T(8,128)(2,1)S(1)}, bf16[512,1152]{1,0:T(8,128)(2,1)S(1)}, u32[]{:S(2)}, u32[]{:S(2)}) %collective-permute-start.11) | collective-permute-done | bytes 1179680 | tf_op jit(solution)/shard_map/ppermute | solution.py:767
  653.6 5.2 last.3
  660.0 7.2 %to_slots.1 = (f32[8,16,1088]{2,1,0:T(8,128)S(1)}, f32[8,16,1088]{2,1,0:T(8,128)S(1)}, f32[8,16,1088]{2,1,0:T(8,128)S(1)}, f32[8,16,1088]{2,1,0:T(8,128)S(1)}, f...) custom-call(s32[16]{0:T(128)S(1)} %fusion.20.index_ref, bf16[16,16,13184]{2,1,0:T(8,128)(2,1)} %bitcast.111), custom_call_target="tpu_custom_call" | custom-call | flops 3375104 | bytes 13500416 | tf_op jit(solution)/shard_map/to_slots/pallas_call | solution.py:833
  669.0 2.3 pad_maximum_fusion.1
  671.6 3.0 late_slots.1
  (252 shorter events, 71.7 us)
Async XLA Ops:
  7.2 106.6 %all-gather.7.cloned.1.call-start = ((), (), s32[]{:S(2)}) async-start(), calls=%async_computation | async-start | bytes 11556864 | tf_op jit(solution)/shard_map/all_gather | solution.py:881
  10.1 243.5 %all-gather.9.cloned.1.call-start = ((), (), s32[]{:S(2)}) async-start(), calls=%async_computation.1 | async-start | bytes 18382848 | tf_op jit(solution)/shard_map/all_gather | solution.py:882
  11.1 647.7 %all-gather.11.cloned.1.call-start = ((), (), s32[]{:S(2)}) async-start(), calls=%async_computation.2 | async-start | bytes 6961152 | tf_op jit(solution)/shard_map/all_gather | solution.py:948
  11.2 30.6 %collective-permute-start = (s32[2,512]{1,0:T(2,128)S(1)}, s32[2,512]{1,0:T(2,128)S(1)}, u32[]{:S(2)}, u32[]{:S(2)}) collective-permute-start(s32[2,512]{1,0:T(2,128)S(1)} %bitcast.116), channel_id=1, source_target_pairs={{0,2},{1,3},{4,6},{5,7},{8,10},{9,11},{12,14},{13,15},{16,18},{17,... | collective-permute-start | bytes 12296 | tf_op jit(solution)/shard_map/ppermute | solution.py:767
  14.3 33.7 %collective-permute-start.2 = (s32[2,512]{1,0:T(2,128)S(1)}, s32[2,512]{1,0:T(2,128)S(1)}, u32[]{:S(2)}, u32[]{:S(2)}) collective-permute-start(s32[2,512]{1,0:T(2,128)S(1)} %bitcast.117), channel_id=1, source_target_pairs={{0,1},{2,3},{4,5},{6,7},{8,9},{10,11},{12,13},{14,15},{16,17},{18,... | collective-permute-start | bytes 12296 | tf_op jit(solution)/shard_map/ppermute | solution.py:767
  19.4 200.6 %copy-start.16 = (f32[1,1088]{1,0:T(1,128)}, f32[1,1088]{1,0:T(1,128)S(1)}, u32[]{:S(2)}) copy-start(f32[1,1088]{1,0:T(1,128)S(1)} %get-tuple-element.205.gain_ref) | copy-start | bytes 13060
  24.1 196.0 %copy-start.12 = (bf16[2,16,1088]{2,1,0:T(8,128)(2,1)}, bf16[2,16,1088]{2,1,0:T(8,128)(2,1)S(1)}, u32[]{:S(2)}) copy-start(bf16[2,16,1088]{2,1,0:T(8,128)(2,1)S(1)} %get-tuple-element.191.x1_ref) | copy-start | bytes 208900
  24.1 196.0 %copy-start.13 = (bf16[2,16,1088]{2,1,0:T(8,128)(2,1)}, bf16[2,16,1088]{2,1,0:T(8,128)(2,1)S(1)}, u32[]{:S(2)}) copy-start(bf16[2,16,1088]{2,1,0:T(8,128)(2,1)S(1)} %get-tuple-element.192.x0_ref) | copy-start | bytes 208900
  30.9 77.5 %collective-permute-start.4 = (bf16[2,512,1152]{2,1,0:T(8,128)(2,1)}, bf16[2,512,1152]{2,1,0:T(8,128)(2,1)}, u32[]{:S(2)}, u32[]{:S(2)}) collective-permute-start(bf16[2,512,1152]{2,1,0:T(8,128)(2,1)} %get-tuple-element.65.refs_0_), channel_id=1, source_target_pairs={{0,2},{1,3},{4,6},{5,7},{8,10},{9,11},{12,14},{13,15},{16,18},{17,... | collective-permute-start | bytes 7077896 | tf_op jit(solution)/shard_map/ppermute | solution.py:767
  33.8 112.0 %collective-permute-start.3 = (bf16[2,512,1152]{2,1,0:T(8,128)(2,1)}, bf16[2,512,1152]{2,1,0:T(8,128)(2,1)}, u32[]{:S(2)}, u32[]{:S(2)}) collective-permute-start(bf16[2,512,1152]{2,1,0:T(8,128)(2,1)} %get-tuple-element.65.refs_0_), channel_id=1, source_target_pairs={{0,1},{2,3},{4,5},{6,7},{8,9},{10,11},{12,13},{14,15},{16,17},{18,... | collective-permute-start | bytes 7077896 | tf_op jit(solution)/shard_map/ppermute | solution.py:767
  41.7 6.3 collective-permute-start.1
  108.5 37.3 %collective-permute-start.5 = (bf16[2,512,1152]{2,1,0:T(8,128)(2,1)}, bf16[2,512,1152]{2,1,0:T(8,128)(2,1)}, u32[]{:S(2)}, u32[]{:S(2)}) collective-permute-start(bf16[2,512,1152]{2,1,0:T(8,128)(2,1)} %collective-permute-done.4.refs_2_), channel_id=1, source_target_pairs={{3,2},{2,3},{7,6},{6,7},{11,10},{10,11},{15,14},{14,15},{19,18},{1... | collective-permute-start | bytes 7077896 | tf_op jit(solution)/shard_map/ppermute | solution.py:767
  145.8 30.9 %copy-start.20 = (s32[3]{0:T(128)S(1)}, s32[3]{0:T(128)}, u32[]{:S(2)}) copy-start(s32[3]{0:T(128)} %pad_add_fusion.1.meta_ref) | copy-start | bytes 40
  176.7 43.4 %copy-start.14 = (bf16[2,16,1088]{2,1,0:T(8,128)(2,1)S(1)}, bf16[2,16,1088]{2,1,0:T(8,128)(2,1)}, u32[]{:S(2)}) copy-start(bf16[2,16,1088]{2,1,0:T(8,128)(2,1)} %get-tuple-element.213.e1_ref) | copy-start | bytes 208900
  176.7 43.4 %copy-start.15 = (bf16[2,16,1088]{2,1,0:T(8,128)(2,1)S(1)}, bf16[2,16,1088]{2,1,0:T(8,128)(2,1)}, u32[]{:S(2)}) copy-start(bf16[2,16,1088]{2,1,0:T(8,128)(2,1)} %get-tuple-element.214.e2_ref) | copy-start | bytes 208900
  253.6 76.2 %copy-start.45 = (f32[2]{0:T(128)S(1)}, f32[2]{0:T(128)}, u32[]{:S(2)}) copy-start(f32[2]{0:T(128)} %multiply_bitcast_fusion) | copy-start | bytes 28
  331.4 39.3 %copy-start.24 = (bf16[2,512,1152]{2,1,0:T(8,128)(2,1)S(1)}, bf16[2,512,1152]{2,1,0:T(8,128)(2,1)}, u32[]{:S(2)}) copy-start(bf16[2,512,1152]{2,1,0:T(8,128)(2,1)} %get-tuple-element.67.q_ref) | copy-start | bytes 7077892
  332.9 138.6 %collective-permute-start.12 = (f32[16,13184]{1,0:T(8,128)}, f32[16,13184]{1,0:T(8,128)}, u32[]{:S(2)}, u32[]{:S(2)}) collective-permute-start(f32[16,13184]{1,0:T(8,128)} %select_bitcast_fusion), channel_id=1, source_target_pairs={{0,2},{1,3},{2,0},{3,1},{4,6},{5,7},{6,4},{7,5},{8,10},{9,11},{10,... | collective-permute-start | bytes 2531336 | tf_op jit(solution)/shard_map/ppermute | solution.py:797
  411.4 60.1 %copy-start.28 = (f32[2,16,13184]{2,1,0:T(8,128)S(1)}, f32[2,16,13184]{2,1,0:T(8,128)}, u32[]{:S(2)}) copy-start(f32[2,16,13184]{2,1,0:T(8,128)} %copy-done.27) | copy-start | bytes 5062660
  433.6 36.9 %collective-permute-start.14 = (f32[2,16,1152]{2,1,0:T(8,128)S(1)}, f32[2,16,1152]{2,1,0:T(8,128)S(1)}, u32[]{:S(2)}, u32[]{:S(2)}) collective-permute-start(f32[2,16,1152]{2,1,0:T(8,128)S(1)} %slice_select_fusion.2), channel_id=1, source_target_pairs={{0,2},{1,3},{2,0},{3,1},{4,6},{5,7},{6,4},{7,5},{8,10},{9,11},{10,... | collective-permute-start | bytes 442376 | tf_op jit(solution)/shard_map/ppermute | solution.py:797
  467.9 52.0 %collective-permute-start.7 = (bf16[512,1152]{1,0:T(8,128)(2,1)}, bf16[512,1152]{1,0:T(8,128)(2,1)}, u32[]{:S(2)}, u32[]{:S(2)}) collective-permute-start(bf16[512,1152]{1,0:T(8,128)(2,1)} %get-tuple-element.93), channel_id=1, source_target_pairs={{3,2},{2,3},{7,6},{6,7},{11,10},{10,11},{15,14},{14,15},{19,18},{1... | collective-permute-start | bytes 3538952 | tf_op jit(solution)/shard_map/ppermute | solution.py:767
  472.9 1.8 collective-permute-start.13
  472.9 46.3 %collective-permute-start.15 = (f32[1,16,1152]{2,1,0:T(8,128)S(1)}, f32[1,16,1152]{2,1,0:T(8,128)S(1)}, u32[]{:S(2)}, u32[]{:S(2)}) collective-permute-start(f32[1,16,1152]{2,1,0:T(8,128)S(1)} %slice_select_fusion.4), channel_id=1, source_target_pairs={{0,1},{1,0},{2,3},{3,2},{4,5},{5,4},{6,7},{7,6},{8,9},{9,8},{10,11... | collective-permute-start | bytes 221192 | tf_op jit(solution)/shard_map/ppermute | solution.py:797
  477.1 40.8 %copy-start.47 = (bf16[512,1152]{1,0:T(8,128)(2,1)S(1)}, bf16[512,1152]{1,0:T(8,128)(2,1)}, u32[]{:S(2)}) copy-start(bf16[512,1152]{1,0:T(8,128)(2,1)} %get-tuple-element.91) | copy-start | bytes 3538948
  477.1 42.8 %copy-start.31 = (bf16[512,1152]{1,0:T(8,128)(2,1)S(1)}, bf16[512,1152]{1,0:T(8,128)(2,1)}, u32[]{:S(2)}) copy-start(bf16[512,1152]{1,0:T(8,128)(2,1)} %get-tuple-element.92) | copy-start | bytes 3538948
  517.9 43.5 %collective-permute-start.6 = (bf16[512,1152]{1,0:T(8,128)(2,1)S(1)}, bf16[512,1152]{1,0:T(8,128)(2,1)S(1)}, u32[]{:S(2)}, u32[]{:S(2)}) collective-permute-start(bf16[512,1152]{1,0:T(8,128)(2,1)S(1)} %copy-done.47), channel_id=1, source_target_pairs={{1,0},{3,2},{5,4},{7,6},{9,8},{11,10},{13,12},{15,14},{17,16},{19,... | collective-permute-start | bytes 3538952 | tf_op jit(solution)/shard_map/ppermute | solution.py:767
  519.9 3.6 collective-permute-start.16
  521.5 45.8 %collective-permute-start.8 = (bf16[512,1152]{1,0:T(8,128)(2,1)S(1)}, bf16[512,1152]{1,0:T(8,128)(2,1)S(1)}, u32[]{:S(2)}, u32[]{:S(2)}) collective-permute-start(bf16[512,1152]{1,0:T(8,128)(2,1)S(1)} %add_convert_fusion.1), channel_id=1, source_target_pairs={{2,0},{3,1},{6,4},{7,5},{10,8},{11,9},{14,12},{15,13},{18,16},{19,... | collective-permute-start | bytes 3538952 | tf_op jit(solution)/shard_map/ppermute | solution.py:767
  523.6 8.4 %collective-permute-start.17 = (bf16[2,16,1152]{2,1,0:T(8,128)(2,1)S(1)}, bf16[2,16,1152]{2,1,0:T(8,128)(2,1)S(1)}, u32[]{:S(2)}, u32[]{:S(2)}) collective-permute-start(bf16[2,16,1152]{2,1,0:T(8,128)(2,1)S(1)} %pad_maximum_fusion.13), channel_id=1, source_target_pairs={{0,8},{1,9},{2,10},{3,11},{4,12},{5,13},{6,14},{7,15},{8,0},{9,1},... | collective-permute-start | bytes 221192 | tf_op jit(solution)/shard_map/ppermute | solution.py:808
  532.0 13.1 %collective-permute-start.18 = (bf16[4,16,1152]{2,1,0:T(8,128)(2,1)S(1)}, bf16[4,16,1152]{2,1,0:T(8,128)(2,1)S(1)}, u32[]{:S(2)}, u32[]{:S(2)}) collective-permute-start(bf16[4,16,1152]{2,1,0:T(8,128)(2,1)S(1)} %pad_maximum_fusion.10), channel_id=1, source_target_pairs={{0,16},{1,17},{2,18},{3,19},{4,20},{5,21},{6,22},{7,23},{8,24},{9,... | collective-permute-start | bytes 442376 | tf_op jit(solution)/shard_map/ppermute | solution.py:808
  545.9 53.7 %collective-permute-start.19 = (bf16[8,16,1152]{2,1,0:T(8,128)(2,1)}, bf16[8,16,1152]{2,1,0:T(8,128)(2,1)S(1)}, u32[]{:S(2)}, u32[]{:S(2)}) collective-permute-start(bf16[8,16,1152]{2,1,0:T(8,128)(2,1)} %pad_maximum_fusion.6), channel_id=1, source_target_pairs={{0,2},{1,3},{2,0},{3,1},{4,6},{5,7},{6,4},{7,5},{8,10},{9,11},{10,... | collective-permute-start | bytes 884744 | tf_op jit(solution)/shard_map/ppermute | solution.py:808
  567.3 21.1 %copy-start.8 = (bf16[512,1152]{1,0:T(8,128)(2,1)}, bf16[512,1152]{1,0:T(8,128)(2,1)S(1)}, u32[]{:S(2)}) copy-start(bf16[512,1152]{1,0:T(8,128)(2,1)S(1)} %collective-permute-done.8.refs_2_) | copy-start | bytes 3538948
  588.4 12.5 %copy-start.48 = (bf16[512,1152]{1,0:T(8,128)(2,1)S(1)}, bf16[512,1152]{1,0:T(8,128)(2,1)}, u32[]{:S(2)}) copy-start(bf16[512,1152]{1,0:T(8,128)(2,1)} %get-tuple-element.104) | copy-start | bytes 3538948
  589.5 12.1 %copy-start.46 = (bf16[512,1152]{1,0:T(8,128)(2,1)S(1)}, bf16[512,1152]{1,0:T(8,128)(2,1)}, u32[]{:S(2)}) copy-start(bf16[512,1152]{1,0:T(8,128)(2,1)} %get-tuple-element.102) | copy-start | bytes 3538948
  589.5 9.0 %collective-permute-start.21 = (f32[2,16,1152]{2,1,0:T(8,128)S(1)}, f32[2,16,1152]{2,1,0:T(8,128)S(1)}, u32[]{:S(2)}, u32[]{:S(2)}) collective-permute-start(f32[2,16,1152]{2,1,0:T(8,128)S(1)} %slice_select_fusion.1), channel_id=1, source_target_pairs={{0,2},{1,3},{2,0},{3,1},{4,6},{5,7},{6,4},{7,5},{8,10},{9,11},{10,... | collective-permute-start | bytes 442376 | tf_op jit(solution)/shard_map/ppermute | solution.py:797
  599.5 4.2 collective-permute-start.22
  600.4 22.0 %copy-start.30 = (bf16[512,1152]{1,0:T(8,128)(2,1)S(1)}, bf16[512,1152]{1,0:T(8,128)(2,1)}, u32[]{:S(2)}) copy-start(bf16[512,1152]{1,0:T(8,128)(2,1)} %get-tuple-element.103) | copy-start | bytes 3538948
  600.4 31.7 %collective-permute-start.20 = (bf16[16,16,1152]{2,1,0:T(8,128)(2,1)}, bf16[16,16,1152]{2,1,0:T(8,128)(2,1)S(1)}, u32[]{:S(2)}, u32[]{:S(2)}) collective-permute-start(bf16[16,16,1152]{2,1,0:T(8,128)(2,1)} %get-tuple-element.180), channel_id=1, source_target_pairs={{0,1},{1,0},{2,3},{3,2},{4,5},{5,4},{6,7},{7,6},{8,9},{9,8},{10,11... | collective-permute-start | bytes 1769480 | tf_op jit(solution)/shard_map/ppermute | solution.py:808
  600.9 21.5 %collective-permute-start.10 = (bf16[512,1152]{1,0:T(8,128)(2,1)S(1)}, bf16[512,1152]{1,0:T(8,128)(2,1)S(1)}, u32[]{:S(2)}, u32[]{:S(2)}) collective-permute-start(bf16[512,1152]{1,0:T(8,128)(2,1)S(1)} %copy-done.48), channel_id=1, source_target_pairs={{3,2},{2,3},{7,6},{6,7},{11,10},{10,11},{15,14},{14,15},{19,18},{1... | collective-permute-start | bytes 3538952 | tf_op jit(solution)/shard_map/ppermute | solution.py:767
  601.6 36.0 %collective-permute-start.9 = (bf16[512,1152]{1,0:T(8,128)(2,1)S(1)}, bf16[512,1152]{1,0:T(8,128)(2,1)S(1)}, u32[]{:S(2)}, u32[]{:S(2)}) collective-permute-start(bf16[512,1152]{1,0:T(8,128)(2,1)S(1)} %copy-done.46), channel_id=1, source_target_pairs={{1,0},{3,2},{5,4},{7,6},{9,8},{11,10},{13,12},{15,14},{17,16},{19,... | collective-permute-start | bytes 3538952 | tf_op jit(solution)/shard_map/ppermute | solution.py:767
  603.8 3.1 collective-permute-start.23
  606.9 3.3 collective-permute-start.24
  610.2 9.0 %collective-permute-start.25 = (bf16[4,16,1152]{2,1,0:T(8,128)(2,1)S(1)}, bf16[4,16,1152]{2,1,0:T(8,128)(2,1)S(1)}, u32[]{:S(2)}, u32[]{:S(2)}) collective-permute-start(bf16[4,16,1152]{2,1,0:T(8,128)(2,1)S(1)} %pad_maximum_fusion.11), channel_id=1, source_target_pairs={{0,16},{1,17},{2,18},{3,19},{4,20},{5,21},{6,22},{7,23},{8,24},{9,... | collective-permute-start | bytes 442376 | tf_op jit(solution)/shard_map/ppermute | solution.py:808
  619.3 9.0 %collective-permute-start.26 = (bf16[8,16,1152]{2,1,0:T(8,128)(2,1)S(1)}, bf16[8,16,1152]{2,1,0:T(8,128)(2,1)S(1)}, u32[]{:S(2)}, u32[]{:S(2)}) collective-permute-start(bf16[8,16,1152]{2,1,0:T(8,128)(2,1)S(1)} %pad_maximum_fusion.7), channel_id=1, source_target_pairs={{0,2},{1,3},{2,0},{3,1},{4,6},{5,7},{6,4},{7,5},{8,10},{9,11},{10,... | collective-permute-start | bytes 884744 | tf_op jit(solution)/shard_map/ppermute | solution.py:808
  622.4 9.7 %copy-start.2 = (f32[512,1152]{1,0:T(8,128)S(1)}, f32[512,1152]{1,0:T(8,128)}, u32[]{:S(2)}) copy-start(f32[512,1152]{1,0:T(8,128)} %get-tuple-element.94.refs_0_) | copy-start | bytes 7077892
  622.7 30.9 %collective-permute-start.11 = (bf16[512,1152]{1,0:T(8,128)(2,1)S(1)}, bf16[512,1152]{1,0:T(8,128)(2,1)S(1)}, u32[]{:S(2)}, u32[]{:S(2)}) collective-permute-start(bf16[512,1152]{1,0:T(8,128)(2,1)S(1)} %add_convert_fusion), channel_id=1, source_target_pairs={{2,0},{3,1},{6,4},{7,5},{10,8},{11,9},{14,12},{15,13},{18,16},{19,... | collective-permute-start | bytes 3538952 | tf_op jit(solution)/shard_map/ppermute | solution.py:767
  628.4 9.2 %collective-permute-start.27 = (bf16[16,16,1152]{2,1,0:T(8,128)(2,1)S(1)}, bf16[16,16,1152]{2,1,0:T(8,128)(2,1)S(1)}, u32[]{:S(2)}, u32[]{:S(2)}) collective-permute-start(bf16[16,16,1152]{2,1,0:T(8,128)(2,1)S(1)} %get-tuple-element.178), channel_id=1, source_target_pairs={{0,1},{1,0},{2,3},{3,2},{4,5},{5,4},{6,7},{7,6},{8,9},{9,8},{10,11... | collective-permute-start | bytes 1769480 | tf_op jit(solution)/shard_map/ppermute | solution.py:808
  632.2 21.4 %copy-start.1 = (f32[512,1152]{1,0:T(8,128)S(1)}, f32[512,1152]{1,0:T(8,128)}, u32[]{:S(2)}) copy-start(f32[512,1152]{1,0:T(8,128)} %get-tuple-element.101.refs_1_) | copy-start | bytes 7077892
  (35 other events, 145.1 us)
Sparse Core Ops, SparseCore 0:
  11.5 102.2 all-gather.6
  117.2 136.2 all-gather.8
  475.6 72.8 all-gather.10

commit v4 on v3

--- a/solution.py
+++ b/solution.py
@@ -42,7 +42,7 @@
     lane = lax.broadcasted_iota(jnp.int32, (1, 128), 1)
     vt_ref[...] = v_ref[0].T
     q2, qa = q_ref[0], qa_ref[0]
-    qh = [jnp.where(lanes_of(h, lane), q2, qa) for h in range(2)]
+    qh = [jnp.where(lanes_of(h, lane), q2, qa).T for h in range(2)]
     for h in range(2):
         kh_ref[h] = jnp.where(lanes_of(h, lane), k_ref[0], ka_ref[0])
         st_ref[h] = jnp.concatenate([jnp.full((1, L), NEG, F32), jnp.zeros((7, L), F32)], axis=0)
@@ -52,7 +52,7 @@
         return pl.multiple_of((t ^ me) * L, L)
 
     def scores(t, h):
-        s_ref[h] = product(kh_ref[h, pl.ds(at(t), L), :], qh[h], 1, 1)
+        s_ref[h] = product(kh_ref[h, pl.ds(at(t), L), :], qh[h], 1, 0)
 
     def gather(t, h, diagonal):
         s = s_ref[h]
@@ -133,15 +133,15 @@
 
 
 def attn_bwd_kernel(
-    meta_ref, q_ref, k_ref, v_ref, do_ref, o_ref, a_ref, ka_ref, dq_ref, dk_ref, dv_ref,
-    kh_ref, vh_ref, kt_ref, s_ref, dp_ref, dqt_ref, dkt_ref, dvt_ref, *, L, r0, D,
+    meta_ref, q_ref, k_ref, v_ref, do_ref, o_ref, a_ref, ka_ref, *refs, L, r0, D, first,
 ):
+    dq_ref, dk_ref, dv_ref, kh_ref, vh_ref, kt_ref, s_ref, dp_ref, dqt_ref, dkt_ref, dvt_ref = refs[-11:]
     me = meta_ref[0]
     lo = meta_ref[1 + r0]
     lane = lax.broadcasted_iota(jnp.int32, (1, 128), 1)
-    limit = D - pl.program_id(0) * 128
-    kt_ref[...] = k_ref[0].T
-    ones = jnp.where((lane % 64 >= 8) & (lane % 64 < 11), 1.0, 0.0).astype(BF)
+    row = lax.broadcasted_iota(jnp.int32, (128, 1), 0)
+    limit = D - (pl.program_id(0) + first) * 128
+    ones = jnp.where((row % 64 >= 8) & (row % 64 < 11), 1.0, 0.0).astype(BF)
     do2 = jnp.where(lane < limit, do_ref[0], jnp.zeros((), BF))
     o2 = jnp.where(lane < limit, o_ref[0], jnp.zeros((), BF))
     q2 = q_ref[0]
@@ -155,29 +155,36 @@
             extra = jnp.where(lane == (1 - h) * 64 + 8 + i, parts[i], extra)
         dh.append(jnp.where(mine, do2, extra))
         qh.append(jnp.where(mine, q2, a_ref[0, 0]))
-        kh_ref[h] = jnp.where(mine, k_ref[0], ka_ref[0])
-        vh_ref[h] = jnp.where(mine, v_ref[0], ones)
     qt, dot_ = q2.T, do2.T
     dqt_ref[...] = jnp.zeros_like(dqt_ref)
 
     def at(t):
         return pl.multiple_of((t ^ me) * L, L)
 
+    def turn(t):
+        here = pl.ds(at(t), L)
+        kt = k_ref[0, here, :].T
+        vt = v_ref[0, here, :].T
+        kt_ref[:, here] = kt
+        for h in range(2):
+            kh_ref[h, :, here] = jnp.where(lanes_of(h, row), kt, ka_ref[0, :, here])
+            vh_ref[h, :, here] = jnp.where(lanes_of(h, row), vt, ones)
+
     def scores(t, h):
-        s_ref[h] = product(kh_ref[h, pl.ds(at(t), L), :], qh[h], 1, 1)
-        dp_ref[h] = product(vh_ref[h, pl.ds(at(t), L), :], dh[h], 1, 1)
+        here = pl.ds(at(t), L)
+        s_ref[h] = product(qh[h], kh_ref[h, :, here], 1, 0)
+        dp_ref[h] = product(dh[h], vh_ref[h, :, here], 1, 0)
 
     def gather(t, h, diagonal):
         p = jnp.exp(s_ref[h])
         if diagonal:
-            ok = lax.broadcasted_iota(jnp.int32, (L, L), 0) <= lax.broadcasted_iota(jnp.int32, (L, L), 1)
+            ok = lax.broadcasted_iota(jnp.int32, (L, L), 1) <= lax.broadcasted_iota(jnp.int32, (L, L), 0)
             p = jnp.where(ok, p, 0.0)
         ds = (p * dp_ref[h]).astype(BF)
         rows = slice(h * 64, (h + 1) * 64)
-        here = pl.ds(at(t), L)
-        dvt_ref[rows, :] = product(dot_[rows], p.astype(BF), 1, 1)
-        dkt_ref[rows, :] = product(qt[rows], ds, 1, 1)
-        dqt_ref[rows] += product(kt_ref[rows, here], ds, 1, 0)
+        dvt_ref[rows] = product(dot_[rows], p.astype(BF), 1, 0)
+        dkt_ref[rows] = product(qt[rows], ds, 1, 0)
+        dqt_ref[rows] += product(kt_ref[rows, pl.ds(at(t), L)], ds, 1, 1)
 
     def store(t):
         here = pl.ds(at(t), L)
@@ -190,10 +197,12 @@
         return carry
 
     lax.fori_loop(0, lo, none, 0)
+    turn(lo)
     scores(lo, 0)
 
     def body(t, carry):
         scores(t, 1)
+        turn(t + 1)
         gather(t, 0, False)
         scores(t + 1, 0)
         gather(t, 1, False)
@@ -208,30 +217,30 @@
     dq_ref[0] = dqt_ref[...].astype(BF).T * jnp.asarray(0.125, BF)
 
 
-def attn_bwd(meta, q, k, v, do, o, extra, ka, r0):
+def attn_bwd(meta, q, k, v, do, o, extra, ka_t, r0, first, count, before=()):
     R, L, W = q.shape
     T, D = k.shape[1], do.shape[2]
-    NP = W // 128
-    col = lambda p, m: (r0, 0, p)
-    out = lambda p, m: (0, 0, p)
+    col = lambda p, m: (r0, 0, p + first)
+    out = lambda p, m: (0, 0, p + first)
     return pl.pallas_call(
-        functools.partial(attn_bwd_kernel, L=L, r0=r0, D=D),
+        functools.partial(attn_bwd_kernel, L=L, r0=r0, D=D, first=first),
         grid_spec=pltpu.PrefetchScalarGridSpec(
             num_scalar_prefetch=1,
-            grid=(NP,),
+            grid=(count,),
             in_specs=[
                 pl.BlockSpec((1, L, 128), col),
                 pl.BlockSpec((1, T, 128), col),
                 pl.BlockSpec((1, T, 128), col),
                 pl.BlockSpec((1, L, 128), col),
                 pl.BlockSpec((1, L, 128), col),
-                pl.BlockSpec((1, 1, L, 128), lambda p, m: (r0, p, 0, 0)),
-                pl.BlockSpec((1, T, 128), lambda p, m: (r0, 0, 0)),
-            ],
+                pl.BlockSpec((1, 1, L, 128), lambda p, m: (r0, p + first, 0, 0)),
+                pl.BlockSpec((1, 128, T), lambda p, m: (r0, 0, 0)),
+            ]
+            + [pl.BlockSpec(memory_space=pl.ANY) for _ in before],
             out_specs=[pl.BlockSpec((1, L, 128), out), pl.BlockSpec((1, T, 128), out), pl.BlockSpec((1, T, 128), out)],
             scratch_shapes=[
-                pltpu.VMEM((2, T, 128), BF),
-                pltpu.VMEM((2, T, 128), BF),
+                pltpu.VMEM((2, 128, T), BF),
+                pltpu.VMEM((2, 128, T), BF),
                 pltpu.VMEM((128, T), BF),
                 pltpu.VMEM((2, L, L), F32),
                 pltpu.VMEM((2, L, L), F32),
@@ -246,11 +255,12 @@
             jax.ShapeDtypeStruct((1, T, W), BF),
         ],
         compiler_params=pltpu.CompilerParams(vmem_limit_bytes=48 << 20),
+        input_output_aliases={8 + i: i for i in range(len(before))},
         cost_estimate=pl.CostEstimate(
-            flops=60 * L * T * W, bytes_accessed=(3 * L + 4 * T) * W * 2, transcendentals=L * T * 18
+            flops=60 * L * T * 128 * count, bytes_accessed=(3 * L + 4 * T) * 256 * count, transcendentals=L * T * 2 * count
         ),
         name="attn_bwd",
-    )(meta, q, k, v, do, o, extra, ka)
+    )(meta, q, k, v, do, o, extra, ka_t, *before)
 
 
 def document_lanes(seg_q, seg_k):
@@ -293,7 +303,7 @@
     return pl.BlockSpec(shape, lambda *_: (0,) * len(shape), pipeline_mode=pl.Buffered(1))
 
 
-def unpack_kernel(g_ref, mix_ref, out_ref, *, cm, co, D, W):
+def unpack_kernel(g_ref, mix_ref, out_ref, rexp_ref, rshr_ref, *, cm, co, D, W, rem, per):
     S = g_ref.shape[0]
     rows = mix_ref.shape[2]
     half_width = cm + co
@@ -305,27 +315,31 @@
         for i in range(3):
             mix_ref[0, half, :, i * W : (i + 1) * W] = jnp.concatenate([mix[:, i * D : (i + 1) * D], zero], axis=1)
         out_ref[0, half] = out
-
-
-def unpack(g, S, C, rows2, cm, co, D, W):
+    for s in range(S):
+        for i in range(rem // 8):
+            rexp_ref[0, s * rem + i * 8 : s * rem + i * 8 + 8] = g_ref[
+                s, 0, rows : rows + 8, i * 2 * rows : (i + 1) * 2 * rows
+            ]
+    for i in range(per * rem // 8):
+        rshr_ref[0, i * 8 : i * 8 + 8] = jnp.concatenate(
+            [g_ref[s, 0, rows + 8 : rows + 16, i * co : (i + 1) * co] for s in range(S)], axis=1
+        )
+
+
+def unpack(g, S, C, rows2, cm, co, D, W, rem, per):
     g = g.reshape(S, C, -1, 2 * (cm + co))
-    mix, out = pl.pallas_call(
-        functools.partial(unpack_kernel, cm=cm, co=co, D=D, W=W),
+    shapes = [(C, 2, rows2, 3 * W), (C, 2, rows2, D), (C, S * rem, 2 * rows2), (C, per * rem, D)]
+    mix, out, rexp, rshr = pl.pallas_call(
+        functools.partial(unpack_kernel, cm=cm, co=co, D=D, W=W, rem=rem, per=per),
         grid=(C,),
         in_specs=[pl.BlockSpec((S, 1) + g.shape[2:], lambda c: (0, c, 0, 0))],
-        out_specs=[
-            pl.BlockSpec((1, 2, rows2, 3 * W), lambda c: (c, 0, 0, 0)),
-            pl.BlockSpec((1, 2, rows2, D), lambda c: (c, 0, 0, 0)),
-        ],
-        out_shape=[
-            jax.ShapeDtypeStruct((C, 2, rows2, 3 * W), BF),
-            jax.ShapeDtypeStruct((C, 2, rows2, D), BF),
-        ],
+        out_specs=[pl.BlockSpec((1,) + s[1:], lambda c, n=len(s): (c,) + (0,) * (n - 1)) for s in shapes],
+        out_shape=[jax.ShapeDtypeStruct(s, BF) for s in shapes],
         compiler_params=pltpu.CompilerParams(vmem_limit_bytes=48 << 20),
         cost_estimate=pl.CostEstimate(flops=0, bytes_accessed=4 * g.size, transcendentals=0),
         name="unpack",
     )(g)
-    return mix.reshape(D, 3 * W), out.reshape(D, D)
+    return mix.reshape(D, 3 * W), out.reshape(D, D), rexp, rshr.reshape(C * per * rem, D)
 
 
 def qkv_kernel(meta_ref, *refs, count, W, R):
@@ -491,9 +505,9 @@
 
     @pl.when(f == last)
     def _():
-        width = rexp_ref.shape[1]
-        we_ref[:D, :width] = rexp_ref[...]
-        ws_ref[:D, :width] = rshr_ref[...]
+        width = rshr_ref.shape[0]
+        we_ref[:D, :width] = jnp.concatenate([rexp_ref[c] for c in range(rexp_ref.shape[0])], axis=1).T
+        ws_ref[:D, :width] = rshr_ref[...].T
         narrow(eur_ref, hdr_ref, width)
         block(width, br_ref[...], ger_ref, ghr_ref)
 
@@ -526,7 +540,7 @@
     R, L, D = res.shape
     N, W = na.shape
     rank = x0.shape[1]
-    width, rem = wexp.shape[-1], rexp.shape[1]
+    width, rem = wexp.shape[-1], rshr.shape[0]
     blocks = eu.shape[2] // width
     cols = lambda *lead: pl.BlockSpec(lead + (width,), lambda f: (0,) * len(lead) + (f,))
     if wexp.ndim == 4:
@@ -566,21 +580,23 @@
     )(na, da, res, o, lo, wexp, wshr, rexp, rshr, eu, eur, hd, hdr, b, br, x0, x1, e1, e2, wout, gain, xb)
 
 
-def project_kernel(meta_ref, dq_ref, dk_ref, dv_ref, w_ref, m_ref, *refs, W, count, r):
-    n_refs, refs = refs[:count], refs[count:]
-    mine_ref, o_refs, g_ref, n_ref, t_ref, wa_ref = refs[0], refs[1:count], refs[count], *refs[count + 1 :]
-    j = pl.program_id(0)
+def project_kernel(meta_ref, dq_ref, dk_ref, dv_ref, w_ref, m_ref, *refs, W, js, r):
+    count = len(js)
+    n_refs, o_refs = refs[:count], refs[count : 2 * count]
+    g_ref, n_ref, t_ref, wa_ref = refs[2 * count :]
+    step = pl.program_id(0)
+    j = step + js[0]
     me = meta_ref[0]
     D = w_ref.shape[0]
     rank = m_ref.shape[1]
     edge = D // 128 * 128
-    for jj in range(count):
-
-        @pl.when(j == jj)
-        def _(jj=jj):
-            n_ref[...] = n_refs[jj][0]
-
-    @pl.when(j == 0)
+    for i in range(count):
+
+        @pl.when(step == i)
+        def _(i=i):
+            n_ref[...] = n_refs[i][0]
+
+    @pl.when(step == 0)
     def _():
         g_ref[...] = jnp.zeros_like(g_ref)
         wa_ref[:D] = w_ref[...]
@@ -595,35 +611,39 @@
         g_ref[3] += dot_nn(taken(total[:, edge:].astype(BF), D % 128, rank), n_ref[...])
         return total
 
-    @pl.when(j == 0)
-    def _():
-        mine_ref[...] = work([(0, dq_ref), (1, dk_ref), (2, dv_ref)])
-
-    @pl.when((j > 0) & ((me ^ j) < me))
-    def _():
-        t_ref[...] = work([(1, dk_ref), (2, dv_ref)]).astype(BF)
-
-    for jj in range(1, count):
-
-        @pl.when(j == jj)
-        def _(jj=jj):
-            o_refs[jj - 1][...] = t_ref[...]
-
-
-def project(meta, dq, dk, dv, w, m, n_parts, r):
-    count = len(n_parts)
+    if js[0] == 0:
+
+        @pl.when(j == 0)
+        def _():
+            o_refs[0][...] = work([(0, dq_ref), (1, dk_ref), (2, dv_ref)])
+
+    if js[-1] > 0:
+
+        @pl.when((j > 0) & ((me ^ j) < me))
+        def _():
+            t_ref[...] = work([(1, dk_ref), (2, dv_ref)]).astype(BF)
+
+    for i in range(count):
+        if js[i] > 0:
+
+            @pl.when(step == i)
+            def _(i=i):
+                o_refs[i][...] = t_ref[...]
+
+
+def project(meta, dq, dk, dv, w, m, n_parts, r, js):
     _, L, W = dq.shape
-    T = count * L
     rank = m.shape[1]
+    count = len(js)
     out = pl.pallas_call(
-        functools.partial(project_kernel, W=W, count=count, r=r),
+        functools.partial(project_kernel, W=W, js=tuple(js), r=r),
         grid_spec=pltpu.PrefetchScalarGridSpec(
             num_scalar_prefetch=1,
             grid=(count,),
             in_specs=[
                 whole_spec(dq.shape),
-                pl.BlockSpec((1, L, W), lambda j, _: (0, j, 0)),
-                pl.BlockSpec((1, L, W), lambda j, _: (0, j, 0)),
+                pl.BlockSpec((1, L, W), lambda j, _: (0, j + js[0], 0)),
+                pl.BlockSpec((1, L, W), lambda j, _: (0, j + js[0], 0)),
                 whole_spec(w.shape),
                 pl.BlockSpec((1, rank, 3 * W), lambda j, _: (r, 0, 0)),
             ]
@@ -631,16 +651,15 @@
             out_specs=[whole_spec((L, W))] * count + [whole_spec((4, rank, W))],
             scratch_shapes=[pltpu.VMEM((L, W), BF), pltpu.VMEM((L, W), BF), pltpu.VMEM((W, 3 * W), BF)],
         ),
-        out_shape=[jax.ShapeDtypeStruct((L, W), F32)]
-        + [jax.ShapeDtypeStruct((L, W), BF)] * (count - 1)
+        out_shape=[jax.ShapeDtypeStruct((L, W), BF if j else F32) for j in js]
         + [jax.ShapeDtypeStruct((4, rank, W), F32)],
         compiler_params=pltpu.CompilerParams(vmem_limit_bytes=60 << 20),
         cost_estimate=pl.CostEstimate(
-            flops=6 * T * W * 2 * W, bytes_accessed=2 * (w.size + 2 * T * W + 2 * T * W), transcendentals=0
+            flops=8 * count * L * W * 2 * W, bytes_accessed=2 * (w.size + 4 * count * L * W), transcendentals=0
         ),
         name="project",
-    )(meta, dq, dk, dv, w, m, *n_parts)
-    return out[:count], out[count]
+    )(meta, dq, dk, dv, w, m, *[n_parts[j] for j in js])
+    return list(out[:count]), out[count]
 
 
 def norm_kernel(x_ref, dy_ref, gain_ref, shift_ref, e_ref, n_ref, xr_ref, dyr_ref):
@@ -707,44 +726,53 @@
 
 
 def late_kernel(slot_ref, part_ref, *refs, R, parts, D, W):
-    g_refs, mix_ref, entry_ref, total = refs[:R], refs[R], refs[R + 1], refs[R + 2]
+    g_refs, mix_ref, entry_ref, total = refs[:R], refs[R + 1], refs[R + 2], refs[R + 3]
     total[...] = jnp.zeros_like(total)
     count = g_refs[0].shape[0]
     for r in range(R):
 
         def one(i, carry):
             a = slot_ref[r * count + i]
-            c = part_ref[i]
-            total[a, c] = total[a, c] + g_refs[r][i].astype(F32)
+            if r + 1 < R:
+                total[a] = total[a] + g_refs[r][i].astype(F32)
+            else:
+                c = part_ref[i]
+                total[a, c] = total[a, c] + g_refs[r][i].astype(F32)
             return carry
 
         lax.fori_loop(0, count, one, 0)
     per = parts // 4
     wide = [jnp.concatenate([total[:, i * per + p] for p in range(per)], axis=-1) for i in range(4)]
     mix_ref[...] = jnp.concatenate([w[:, :, :D] for w in wide[:3]], axis=-1)
-    entry_ref[...] = wide[3][:, :, :D]
-
-
-def late_slots(slot, part, gs, adapters, parts, D, W):
+    entry_ref[0] = wide[3][:, :, :D]
+
+
+def late_slots(slot, part, gs, entry, D, W):
     R = len(gs)
-    _, rank, width = gs[0].shape
+    adapters = entry.shape[1]
+    _, rank, width = gs[-1].shape
+    parts = 4 * W // width
     return pl.pallas_call(
         functools.partial(late_kernel, R=R, parts=parts, D=D, W=W),
         grid_spec=pltpu.PrefetchScalarGridSpec(
             num_scalar_prefetch=2,
             grid=(1,),
-            in_specs=[whole_spec(g.shape) for g in gs],
-            out_specs=[whole_spec((adapters, rank, 3 * D)), whole_spec((adapters, rank, D))],
+            in_specs=[whole_spec(g.shape) for g in gs] + [pl.BlockSpec(memory_space=pl.ANY)],
+            out_specs=[
+                whole_spec((adapters, rank, 3 * D)),
+                pl.BlockSpec((1, adapters, rank, D), lambda i, *_: (0, 0, 0, 0)),
+            ],
             scratch_shapes=[pltpu.VMEM((adapters, parts, rank, width), F32)],
         ),
         out_shape=[
             jax.ShapeDtypeStruct((adapters, rank, 3 * D), F32),
-            jax.ShapeDtypeStruct((adapters, rank, D), F32),
+            jax.ShapeDtypeStruct(entry.shape, F32),
         ],
-        compiler_params=pltpu.CompilerParams(vmem_limit_bytes=48 << 20),
-        cost_estimate=pl.CostEstimate(flops=0, bytes_accessed=8 << 20, transcendentals=0),
+        input_output_aliases={2 + R: 1},
+        compiler_params=pltpu.CompilerParams(vmem_limit_bytes=60 << 20),
+        cost_estimate=pl.CostEstimate(flops=0, bytes_accessed=12 << 20, transcendentals=0),
         name="late_slots",
-    )(slot, part, *gs)
+    )(slot, part, *gs, entry)
 
 
 def mm(pattern, a, b):
@@ -775,40 +803,50 @@
     return [found[j] for j in sorted(found)]
 
 
-def blocks_back(parts, bits):
-    held = {j: [p] for j, p in enumerate(parts)}
-    for bit in bits:
-        for j in sorted(held):
-            if j & bit:
-                sent = held.pop(j)
-                sent = sent[0] if len(sent) == 1 else sum(t.astype(F32) for t in sent).astype(BF)
-                got = swap(sent, "ctx", bit, lambda d, k=j, b=bit: ((d ^ b) ^ k) < (d ^ b))
-                held[j ^ bit].append(got)
-    return held[0]
-
-
-def ctx_sum_rows(g, bits):
+def block_sum(terms):
+    return terms[0] if len(terms) == 1 else sum(t.astype(F32) for t in terms).astype(BF)
+
+
+def blocks_back(held, bit):
+    held = dict(held)
+    for j in sorted(held):
+        if j & bit:
+            sent = block_sum(held.pop(j))
+            got = swap(sent, "ctx", bit, lambda d, k=j, b=bit: ((d ^ b) ^ k) < (d ^ b))
+            held[j ^ bit] = held[j ^ bit] + [got]
+    return held
+
+
+def turned_order(bits):
+    count = 2 * bits[-1]
+    return sorted(range(count), key=lambda c: [c & b for b in bits])
+
+
+def ctx_sum_stage(g, bit):
     n = lax.axis_size("ctx")
-    me = lax.axis_index("ctx")
-    for bit in reversed(bits):
-        half = g.shape[0] // 2
-        mine = (me & bit) != 0
-        low, high = g[:half], g[half:]
-        got = lax.ppermute(jnp.where(mine, low, high), "ctx", [(d, d ^ bit) for d in range(n)])
-        g = jnp.where(mine, high, low) + got
-    return g
-
-
-def gather_all(x, seq_count, ctx_count):
+    half = g.shape[0] // 2
+    mine = (lax.axis_index("ctx") & bit) != 0
+    low, high = g[:half], g[half:]
+    got = lax.ppermute(jnp.where(mine, low, high), "ctx", [(d, d ^ bit) for d in range(n)])
+    return jnp.where(mine, high, low) + got
+
+
+def gather_all(x, seq_count, ctx_count, at, beside):
     n = seq_count * ctx_count
     seq_bits = [ctx_count << i for i in range(seq_count.bit_length() - 1)]
     ctx_bits = [1 << i for i in range(ctx_count.bit_length() - 1)]
-    held, order = x[None], [0]
-    for bit in seq_bits + ctx_bits[::-1]:
+    steps = seq_bits[::-1] + ctx_bits[::-1]
+    held, order, beside = x[None], [0], list(beside)
+    for i, bit in enumerate(steps):
+        k = i - at
+        if 0 <= k < len(beside):
+            if callable(beside[k]):
+                beside[k] = beside[k](beside[k - 1])
+            held, beside[k] = lax.optimization_barrier((held, beside[k]))
         got = lax.ppermute(held, BOTH, [(d, d ^ bit) for d in range(n)])
         held = jnp.concatenate([held, got], 0)
         order = order + [o ^ bit for o in order]
-    return held, order
+    return held, order, beside
 
 
 def slots_kernel(index_ref, g_ref, *refs, count, spans):
@@ -821,25 +859,27 @@
         return carry
 
     lax.fori_loop(0, count, one, 0)
-    for out, pieces in zip(outs, spans):
-        parts = [total[:, :, first : first + width] for first, width in pieces]
-        out[...] = parts[0] if len(parts) == 1 else jnp.concatenate(parts, axis=-1)
+    for out, layers in zip(outs, spans):
+        for i, pieces in enumerate(layers):
+            parts = [total[:, :, first : first + width] for first, width in pieces]
+            if parts:
+                out[i] = parts[0] if len(parts) == 1 else jnp.concatenate(parts, axis=-1)
 
 
 def to_slots(index, g, adapters, spans):
     count, rank, wide = g.shape
     rows = 8
-    widths = [sum(w for _, w in pieces) for pieces in spans]
+    shapes = [(len(layers), adapters, rank, sum(w for _, w in layers[-1])) for layers in spans]
     return pl.pallas_call(
         functools.partial(slots_kernel, count=count, spans=spans),
         grid_spec=pltpu.PrefetchScalarGridSpec(
             num_scalar_prefetch=1,
             grid=(rank // rows,),
             in_specs=[pl.BlockSpec((count, rows, wide), lambda i, m: (0, i, 0))],
-            out_specs=[pl.BlockSpec((adapters, rows, w), lambda i, m: (0, i, 0)) for w in widths],
+            out_specs=[pl.BlockSpec(s[:2] + (rows, s[3]), lambda i, m: (0, 0, i, 0)) for s in shapes],
             scratch_shapes=[pltpu.VMEM((adapters, rows, wide), F32)],
         ),
-        out_shape=[jax.ShapeDtypeStruct((adapters, rank, w), F32) for w in widths],
+        out_shape=[jax.ShapeDtypeStruct(s, F32) for s in shapes],
         compiler_params=pltpu.CompilerParams(vmem_limit_bytes=48 << 20),
         cost_estimate=pl.CostEstimate(
             flops=count * rank * wide, bytes_accessed=count * rank * wide * 2 + adapters * rank * wide * 4, transcendentals=0
@@ -865,6 +905,7 @@
     W = -(-D // 128) * 128
     pad = W - D
 
+    flip = lambda m: jnp.swapaxes(m, -1, -2)
     rows = mixing_weight.shape[0]
     cm, co, ce = mixing_weight.shape[1], output_weight.shape[1], expand_weight.shape[1]
     first = jnp.concatenate([mixing_weight, output_weight], 1)
@@ -873,23 +914,22 @@
     rem = ce - main
     per = S // C
     shr_t = shrink_weight.T.reshape(co, per, ce).transpose(1, 0, 2)
-    rest = jnp.concatenate([expand_weight[:, main:].reshape(-1), shr_t[:, :, main:].reshape(-1)])
-    rest_rows = -(-rest.shape[0] // first.shape[1])
-    rest = jnp.pad(rest, (0, rest_rows * first.shape[1] - rest.shape[0])).reshape(rest_rows, -1)
+    wide = first.shape[1]
+    folded = lambda m: jnp.pad(
+        m.reshape(-1, 8, m.shape[1]).transpose(1, 0, 2).reshape(8, -1), ((0, 0), (0, wide - m.size // 8))
+    )
+    rest = [folded(expand_weight[:, main:].T), folded(flip(shr_t[:, :, main:]).reshape(per * rem, co))]
+    rest = jnp.concatenate(rest, 0)
     first = jnp.concatenate([first, rest], 0)
     second = jnp.concatenate([expand_weight[:, :main], shr_t[:, :, :main].reshape(per * co, main)], 0)
     g1 = lax.all_gather(first, BOTH)
     g2 = lax.all_gather(second, BOTH).reshape(S, C, -1, main)
-    w_mix, w_out = unpack(g1, S, C, rows // 2, cm, co, D, W)
+    w_mix, w_out, r_exp, r_shr = unpack(g1, S, C, rows // 2, cm, co, D, W, rem, per)
     if rows % 16 == 0 and per * co == rows and co % 8 == 0:
         w_exp = w_shr = g2
     else:
         w_exp = g2[:, :, :rows].reshape(S, D, main)
         w_shr = g2[:, :, rows:].reshape(S, C, per, co, main).transpose(1, 2, 0, 3, 4).reshape(S, D, main)
-    flat = g1[:, rows // 2 :].reshape(S, C, -1)
-    r_exp = flat[..., : rows * rem].reshape(S, C, rows, rem).transpose(1, 2, 0, 3).reshape(D, S * rem)
-    r_shr = flat[..., rows * rem : rows * rem + per * co * rem].reshape(S, C, per, co, rem)
-    r_shr = r_shr.transpose(0, 3, 1, 2, 4).reshape(D, S * rem)
 
     def split_ff(m):
         m = m.reshape(m.shape[:-1] + (S, ce))
@@ -907,7 +947,6 @@
     pad_heads = lambda m: jnp.concatenate([padded(m[..., i * D : (i + 1) * D]) for i in range(3)], -1)
     padded = lambda m: jnp.pad(m, [(0, 0)] * (m.ndim - 1) + [(0, pad)])
     mix_up = pad_heads(mix_up)
-    flip = lambda m: jnp.swapaxes(m, -1, -2)
     entry_t = flip(entry)
     exp_main, exp_rest = split_ff(exp_up)
     hid_main, hid_rest = split_ff(flip(hid))
@@ -944,44 +983,96 @@
 
     number = jnp.broadcast_to((index.astype(F32) / C)[:, None, None], (R, rank, 128))
     early = jnp.concatenate([g1, g2_, gx0, gx1, ge, ger, gh, ghr, number], -1).reshape(R * rank, -1)
-    early = ctx_sum_rows(early, bits).astype(BF)
-    early = lax.all_gather(early, BOTH).reshape(S * R, rank, -1)
-    all_index = early[:, 0, -1].astype(jnp.int32)
-    spans = [[(i * D, D)] for i in range(4)]
-    for at in (4 * D, 4 * D + FF):
-        spans.append(
-            [p for i in range(S) for p in ((at + i * main, main), (at + S * main + i * rem, rem))]
-        )
-    entry1_g, entry2_g, exit0_g, exit1_g, expand_g, hidden_g = to_slots(all_index, early, adapters, spans)
-
-    input_grad, late, terms = None, [], []
+    swapped = turned_order(bits)
+    share = R * rank // C
+    early = jnp.concatenate([early[c * share : (c + 1) * share] for c in swapped], 0)
+
+    pairs = W // 128
+    ka_t = flip(ka)
+    late, terms, held = [], [], None
+    everything = list(range(C))
     for r in range(R):
-        dq, dk, dv = attn_bwd(meta, q, k, v, do, o, extra, ka, r)
-        if r:
-            dk, terms[r - 1] = lax.optimization_barrier((dk, terms[r - 1]))
-        parts, g = project(meta, dq, dk, dv, w_mix, mix_up, n1_parts, r)
+        grads = ()
+        cuts = [i * pairs // (len(bits) if held is None else 2) for i in range(len(bits) + 1 if held is None else 3)]
+        for i, (p0, p1) in enumerate(zip(cuts, cuts[1:])):
+            grads = attn_bwd(meta, q, k, v, do, o, extra, ka_t, r, p0, p1 - p0, grads)
+            if held is None:
+                early = ctx_sum_stage(early, bits[i])
+                if i + 1 < len(bits):
+                    do, early = lax.optimization_barrier((do, early))
+            if held is not None and i == 0:
+                held = blocks_back(held, bits[0])
+                held = {j: [block_sum(t)] if j else t for j, t in held.items()}
+                do, held = lax.optimization_barrier((do, held))
+                for bit in bits[1:]:
+                    held = blocks_back(held, bit)
+        dq, dk, dv = grads
+        if held is None:
+            dk, early = lax.optimization_barrier((dk, early))
+            early = lax.all_gather(early.astype(BF), BOTH).reshape(S * R, rank, -1)
+        if held is not None:
+            dk, held = lax.optimization_barrier((dk, held))
+            terms.append(held[0])
         if r + 1 < R:
-            do, parts = lax.optimization_barrier((do, parts))
-        terms.append(blocks_back(parts, bits))
+            parts, g = project(meta, dq, dk, dv, w_mix, mix_up, n1_parts, r, everything)
+            held = {j: [p] for j, p in enumerate(parts)}
+            do, held = lax.optimization_barrier((do, held))
+        else:
+            parts, g = project(meta, dq, dk, dv, w_mix, mix_up, n1_parts, r, everything[1:])
+            dq, parts = lax.optimization_barrier((dq, parts))
+            own, g_own = project(meta, dq, dk, dv, w_mix, mix_up, n1_parts, r, [0])
+            g = g + g_own
+            held = {j: [p] for j, p in enumerate(own + parts)}
+            held = blocks_back(held, bits[0])
+            held = {j: [block_sum(t)] if j else t for j, t in held.items()}
         g = g.reshape(4, rank, C // 4, -1).transpose(0, 2, 1, 3).reshape(C, rank, -1)
-        late.append(gather_all(ctx_sum_rows(g, bits)[0].astype(BF), S, C))
-    for r in range(R):
-        input_grad = last(r, input_grad, terms[r], dr, x, norm_gains[0][None], entry_t[0])
+        if r + 1 < R:
+            late.append(lax.all_gather(g.astype(BF), BOTH))
+        else:
+            g = jnp.concatenate([g[c : c + 1] for c in swapped], 0)
+            for bit in bits:
+                g = ctx_sum_stage(g, bit)
+            g, held = lax.optimization_barrier((g, held))
+            for bit in bits[1:]:
+                held = blocks_back(held, bit)
+            terms.append(held[0])
+            grad_of = lambda i, before: last(i, before, terms[i], dr, x, norm_gains[0][None], entry_t[0])
+            input_grad = None
+            for i in range(R - 1):
+                input_grad = grad_of(i, input_grad)
+            all_index = early[:, 0, -1].astype(jnp.int32)
+            both = []
+            for at in (4 * D, 4 * D + FF):
+                both.append([p for i in range(S) for p in ((at + i * main, main), (at + S * main + i * rem, rem))])
+            entry_g, exit_g, expand_g, hidden_g = to_slots(
+                all_index, early, adapters,
+                [[[], [(0, D)], [(D, D)]], [[(2 * D, D)], [(3 * D, D)]], [both[0]], [both[1]]],
+            )
+            early_g = (entry_g, exit_g, expand_g, hidden_g)
+            before = early_g if input_grad is None else (*early_g, input_grad)
+            last_late, order, beside = gather_all(
+                g[0].astype(BF), S, C, S.bit_length() - 1,
+                [before, lambda done: grad_of(r, done[4] if len(done) > 4 else None)],
+            )
+            entry_g, exit_g, expand_g, hidden_g = beside[0][:4]
+            input_grad = beside[1]
+            late.append(last_late)
     device = lax.axis_index("seq") * C + me
-    order = device ^ jnp.array(late[0][1], jnp.int32)
+    order = device ^ jnp.array(order, jnp.int32)
     by_row = all_index.reshape(S, R)
-    slot = jnp.concatenate([jnp.sum(jnp.where((order // C)[:, None] == jnp.arange(S), by_row[:, r], 0), 1) for r in range(R)])
-    mixing_g, entry0_g = late_slots(slot, order % C, [g for g, _ in late], adapters, C, D, W)
+    slot = [jnp.repeat(by_row[:, r], C) for r in range(R - 1)]
+    slot.append(jnp.sum(jnp.where((order // C)[:, None] == jnp.arange(S), by_row[:, R - 1], 0), 1))
+    mixing_g, entry_g = late_slots(jnp.concatenate(slot), order % C, late, entry_g, D, W)
     input_grad = flip(input_grad).reshape(tokens.shape)
 
     return (
         layer_output,
         input_grad,
-        jnp.stack([flip(entry0_g), flip(entry1_g), flip(entry2_g)]),
+        flip(entry_g),
         mixing_g,
-        expand_g,
-        flip(hidden_g),
-        jnp.stack([exit0_g, exit1_g]),
+        expand_g[0],
+        flip(hidden_g[0]),
+        exit_g,
     )
 
 

time: 694 us -> 629 us (0.906)
  starting transfers between devices: 128 us -> 79.6 us
  local copies, waits for them, and re-layouts: 56 us -> 39.8 us
    ppermute x6 -> x4, starting transfers between devices: 79.3 us -> 32.2 us  [ctx_sum_stage(): lax.ppermute(jnp.where(mine, low, high), 'ctx', [(d, d ^ bit) for d in ra...]
    ppermute x10 -> x5, waiting for transfers between devices: 35.3 us -> 1.92 us  [gather_all(): got = lax.ppermute(held, BOTH, [(d, d ^ bit) for d in range(n)])]
    ppermute x12, waiting for transfers between devices: 81.1 us -> 111 us  [swap(): return lax.ppermute(x, axis, [(d ^ bit, d) for d in range(n) if needed(d)])]
    reshape x9 -> x3, local copies, waits for them, and re-layouts: 12 us -> 0.28 us  [the longest x2 0.2 us: per_device(): m.reshape(-1, 8, m.shape[1]).transpose(1, 0, 2).reshape(8, -1)]
    all_gather x1, waiting for transfers between devices: 16.8 us -> 25.6 us  [per_device(): g2 = lax.all_gather(second, BOTH).reshape(S, C, -1, main)]
    pallas_call x5 -> x8, Pallas kernels: 131 us -> 133 us  [the longest x4 75.1 us: attn_bwd(): pl.pallas_call(functools.partial(attn_bwd_kernel, L=L, r0=r0, D=D, first=...]
    unnamed x110 -> x105, local copies, waits for them, and re-layouts: 18.3 us -> 19.4 us
    ppermute x10 -> x5, starting transfers between devices: 27.7 us -> 27 us  [gather_all(): got = lax.ppermute(held, BOTH, [(d, d ^ bit) for d in range(n)])]
  transfers between devices with their start and end apart: 31 -> 25, of which waited for: 15 -> 6; matrix products, arithmetic and copies ran while one was open for 8% -> 5% of each run, Pallas kernels for 34% -> 39%
where the time goes in v4:
time: 629 us; the launch traced here: 623 us
  Pallas kernels  323 us (51%)
  waiting for transfers between devices  142 us (23%)
  starting transfers between devices  79.6 us (13%)
  local copies, waits for them, and re-layouts  39.8 us (6%)
  other arithmetic  19.2 us (3%)
  between operations  18.8 us (3%)
    ppermute x12, waiting for transfers between devices, swap(): return lax.ppermute(x, axis, [(d ^ bit, d) for d in range(n) if needed(d)])  111 us
    pallas_call x1, Pallas kernels, ffn(): pl.pallas_call(functools.partial(ffn_kernel, R=R, per=per, co=co), grid=(...  76.3 us
    pallas_call x4, Pallas kernels, attn_bwd(): pl.pallas_call(functools.partial(attn_bwd_kernel, L=L, r0=r0, D=D, first=...  75.1 us
    pallas_call x3, Pallas kernels, project(): pl.pallas_call(functools.partial(project_kernel, W=W, js=tuple(js), r=r),...  47.9 us
    pallas_call x1, Pallas kernels, attn_fwd(): pl.pallas_call(functools.partial(attn_fwd_kernel, L=L), grid_spec=pltpu.P...  40.5 us
    ppermute x4, starting transfers between devices, ctx_sum_stage(): lax.ppermute(jnp.where(mine, low, high), 'ctx', [(d, d ^ bit) for d in ra...  32.2 us
    pallas_call x1, Pallas kernels, qkv(): pl.pallas_call(functools.partial(qkv_kernel, W=W, count=count, R=R), grid...  30.9 us
    ppermute x5, starting transfers between devices, gather_all(): got = lax.ppermute(held, BOTH, [(d, d ^ bit) for d in range(n)])  27 us
  transfers between devices with their start and end apart: 25, of which 6 were waited for; matrix products, arithmetic and copies ran while one was open for 5% of the time, Pallas kernels for 39%

profile of v4, /device:TPU:5, one launch (start us, length us, event | category | flops | bytes accessed | tf_op | source)
XLA Modules:
  0.0 622.7 jit_solution(8266598132691113606)
XLA Ops:
  13.9 3.1 collective-permute-start
  27.2 1.7 copy-done.5
  28.9 5.1 first_norm.1
  34.0 2.8 collective-permute-start.4
  40.4 1.4 fusion.28
  45.2 68.0 %collective-permute-done.4.refs_2_.refs_1_ = bf16[2,512,1152]{2,1,0:T(8,128)(2,1)} collective-permute-done((bf16[2,512,1152]{2,1,0:T(8,128)(2,1)}, bf16[2,512,1152]{2,1,0:T(8,128)(2,1)}, u32[]{:S(2)}, u32[]{:S(2)}) %collective-permute-start.4) | collective-permute-done | bytes 2359328 | tf_op jit(solution)/shard_map/ppermute | solution.py:795
  113.2 2.1 collective-permute-start.5
  124.5 1.8 copy.78.ka_ref
  127.1 9.7 %unpack.1 = (bf16[4,2,136,3456]{3,2,1,0:T(8,128)(2,1)}, bf16[4,2,136,1088]{3,2,1,0:T(8,128)(2,1)S(1)}, bf16[4,256,272]{2,1,0:T(8,128)(2,1)S(1)}, bf16[4,64,1088]{2,1,0:T(8,128)(2,1)S(1)}) custom-call(bf16[8,4,152,1088]{3,2,1,0:T(8,128)(2,1)} %bitcast.92), custom_call_target="tpu_custom_call" | custom-call | bytes 21168128 | tf_op jit(solution)/shard_map/unpack/pallas_call | solution.py:332
  136.9 1.4 copy-done
  139.2 30.9 %qkv.1 = (bf16[2,512,1152]{2,1,0:T(8,128)(2,1)}, bf16[2,2048,1152]{2,1,0:T(8,128)(2,1)}, bf16[2,2048,1152]{2,1,0:T(8,128)(2,1)}) custom-call(s32[3]{0:T(128)} %pad_add_fusion.1.meta_ref, bf16[2,512,1152]{2,1,0:T(8,128)(2,1)} %get-tuple-element.96.refs_0_, bf16[2,512,1152]{2,1,0:T(8,128)(2,1)} %collective-permute-done.3.refs_1_.refs_0_, ...), custom_call_target="tpu_custom_call" | custom-call | flops 43486543872 | bytes 35831808 | tf_op jit(solution)/shard_map/qkv/pallas_call | solution.py:384
  170.1 40.5 %attn_fwd.1 = (bf16[2,512,1088]{2,1,0:T(8,128)(2,1)S(1)}, bf16[2,9,512,128]{3,2,1,0:T(8,128)(2,1)S(1)}) custom-call(s32[3]{0:T(128)S(1)} %copy-done.22, bf16[2,512,1152]{2,1,0:T(8,128)(2,1)} %get-tuple-element.98.q_ref, bf16[2,2048,1152]{2,1,0:T(8,128)(2,1)} %get-tuple-element.99.k_ref, bf16[2,2048,1152]{2,1,0:T(8,128)(2,1)} %get-tuple-element.100.v_ref, ...), custom_call_target="tpu_custom_call" | custom-call | flops 96636764160 | bytes 23592960 | tf_op jit(solution)/shard_map/attn_fwd/pallas_call | solution.py:105
  210.6 1.4 copy-done.2
  212.1 1.4 copy-done.30
  213.5 13.0 %mid.1 = (f32[2,512,1088]{2,1,0:T(8,128)}, bf16[2,512,1152]{2,1,0:T(8,128)(2,1)S(1)}, bf16[2,512,1152]{2,1,0:T(8,128)(2,1)S(1)}, bf16[2,512,16]{2,1,0:T(8,128)(2,1)S(1)}) custom-call(bf16[2,512,1088]{2,1,0:T(8,128)(2,1)} %copy-done.2, bf16[2,512,1088]{2,1,0:T(8,128)(2,1)} %get-tuple-element.102.x_ref.refs_4_.refs_5_, ...), custom_call_target="tpu_custom_call" | custom-call | flops 2424307712 | bytes 17825792 | tf_op jit(solution)/shard_map/mid/pallas_call | solution.py:432
  226.6 1.6 copy-done.17
  228.1 1.4 copy-done.18
  230.2 25.6 %all-gather.11.cloned.1.call-done = bf16[17408,512]{1,0:T(8,128)(2,1)} async-done(((bf16[544,512]{1,0:T(8,128)(2,1)}), bf16[17408,512]{1,0:T(8,128)(2,1)}) %all-gather.11.cloned.1.call-update) | async-done | bytes 17825808 | tf_op jit(solution)/shard_map/all_gather | solution.py:926
  255.9 76.3 %ffn.1 = (bf16[2,1088,512]{2,1,0:T(8,128)(2,1)}, f32[2,512,1088]{2,1,0:T(8,128)}, bf16[2,512,1088]{2,1,0:T(8,128)(2,1)}, f32[2,16,1088]{2,1,0:T(8,128)}, f32[2,1...) custom-call(bf16[1024,1152]{1,0:T(8,128)(2,1)} %bitcast.89, ...), custom_call_target="tpu_custom_call" | custom-call | flops 77577846784 | bytes 45678592 | tf_op jit(solution)/shard_map/ffn/pallas_call | solution.py:562
  332.3 1.6 concatenate.83
  335.5 16.9 %attn_bwd.4 = (bf16[1,512,1152]{2,1,0:T(8,128)(2,1)S(1)}, bf16[1,2048,1152]{2,1,0:T(8,128)(2,1)}, bf16[1,2048,1152]{2,1,0:T(8,128)(2,1)}) custom-call(s32[3]{0:T(128)S(1)} %copy-done.22, bf16[2,512,1152]{2,1,0:T(8,128)(2,1)S(1)} %copy-done.27, bf16[2,2048,1152]{2,1,0:T(8,128)(2,1)} %get-tuple-element.99.k_ref, ...), custom_call_target="tpu_custom_call" | custom-call | flops 32212254720 | bytes 9961472 | tf_op jit(solution)/shard_map/attn_bwd/pallas_call | solution.py:225
  352.7 17.6 %collective-permute-start.7 = (f32[8,13184]{1,0:T(8,128)S(1)}, f32[8,13184]{1,0:T(8,128)S(1)}, u32[]{:S(2)}, u32[]{:S(2)}) collective-permute-start(f32[8,13184]{1,0:T(8,128)S(1)} %slice_select_fusion), channel_id=1, source_target_pairs={{0,2},{1,3},{2,0},{3,1},{4,6},{5,7},{6,4},{7,5},{8,10},{9,11},{10,... | collective-permute-start | bytes 1265672 | tf_op jit(solution)/shard_map/ppermute | solution.py:830
  370.3 20.5 %attn_bwd.5 = (bf16[1,512,1152]{2,1,0:T(8,128)(2,1)S(1)}, bf16[1,2048,1152]{2,1,0:T(8,128)(2,1)}, bf16[1,2048,1152]{2,1,0:T(8,128)(2,1)}) custom-call(s32[3]{0:T(128)S(1)} %copy-done.22, bf16[2,512,1152]{2,1,0:T(8,128)(2,1)S(1)} %copy-done.27, ...), custom_call_target="tpu_custom_call", output_to_operand_aliasing={{0}: (8, {}), {1}: (9, {}), {2}: (10, {})} | custom-call | flops 40265318400 | bytes 12451840 | tf_op jit(solution)/shard_map/attn_bwd/pallas_call | solution.py:225
  391.8 21.2 %project.3 = (f32[512,1152]{1,0:T(8,128)}, bf16[512,1152]{1,0:T(8,128)(2,1)}, bf16[512,1152]{1,0:T(8,128)(2,1)}, bf16[512,1152]{1,0:T(8,128)(2,1)}, f32[4,16,1152]{2,1,0:T(8,128)}) custom-call(s32[3]{0:T(128)} %pad_add_fusion.1.meta_ref, bf16[1,512,1152]{2,1,0:T(8,128)(2,1)} %copy-done.31, bf16[1,2048,1152]{2,1,0:T(8,128)(2,1)} %get-tuple-element.129.dk_ref, ...), custom_call_target="tpu_custom_call" | custom-call | flops 43486543872 | bytes 26394624 | tf_op jit(solution)/shard_map/project/pallas_call | solution.py:638
  413.1 1.7 collective-permute-start.9
  414.8 1.4 collective-permute-start.8
  416.2 1.7 copy-done.28
  417.8 16.9 %attn_bwd.6 = (bf16[1,512,1152]{2,1,0:T(8,128)(2,1)S(1)}, bf16[1,2048,1152]{2,1,0:T(8,128)(2,1)}, bf16[1,2048,1152]{2,1,0:T(8,128)(2,1)}) custom-call(s32[3]{0:T(128)S(1)} %copy-done.23, bf16[2,512,1152]{2,1,0:T(8,128)(2,1)S(1)} %copy-done.28, bf16[2,2048,1152]{2,1,0:T(8,128)(2,1)} %get-tuple-element.99.k_ref, ...), custom_call_target="tpu_custom_call" | custom-call | flops 32212254720 | bytes 9961472 | tf_op jit(solution)/shard_map/attn_bwd/pallas_call | solution.py:225
  435.6 2.1 add_convert_fusion.1
  440.2 20.9 %attn_bwd.7 = (bf16[1,512,1152]{2,1,0:T(8,128)(2,1)S(1)}, bf16[1,2048,1152]{2,1,0:T(8,128)(2,1)}, bf16[1,2048,1152]{2,1,0:T(8,128)(2,1)}) custom-call(s32[3]{0:T(128)S(1)} %copy-done.23, bf16[2,512,1152]{2,1,0:T(8,128)(2,1)S(1)} %copy-done.29, ...), custom_call_target="tpu_custom_call", output_to_operand_aliasing={{0}: (8, {}), {1}: (9, {}), {2}: (10, {})} | custom-call | flops 40265318400 | bytes 12451840 | tf_op jit(solution)/shard_map/attn_bwd/pallas_call | solution.py:225
  462.1 36.1 %collective-permute-done.10.refs_2_ = bf16[512,1152]{1,0:T(8,128)(2,1)S(1)} collective-permute-done((bf16[512,1152]{1,0:T(8,128)(2,1)S(1)}, bf16[512,1152]{1,0:T(8,128)(2,1)S(1)}, u32[]{:S(2)}, u32[]{:S(2)}) %collective-permute-start.10) | collective-permute-done | bytes 1179680 | tf_op jit(solution)/shard_map/ppermute | solution.py:795
  498.2 14.3 %project.4 = (bf16[512,1152]{1,0:T(8,128)(2,1)}, bf16[512,1152]{1,0:T(8,128)(2,1)}, bf16[512,1152]{1,0:T(8,128)(2,1)}, f32[4,16,1152]{2,1,0:T(8,128)}) custom-call(s32[3]{0:T(128)} %pad_add_fusion.1.meta_ref, bf16[1,512,1152]{2,1,0:T(8,128)(2,1)} %copy-done.26, bf16[1,2048,1152]{2,1,0:T(8,128)(2,1)} %get-tuple-element.149.dk_ref, ...), custom_call_target="tpu_custom_call" | custom-call | flops 32614907904 | bytes 21676032 | tf_op jit(solution)/shard_map/project/pallas_call | solution.py:638
  512.5 12.4 %project.5 = (f32[512,1152]{1,0:T(8,128)}, f32[4,16,1152]{2,1,0:T(8,128)}) custom-call(s32[3]{0:T(128)} %pad_add_fusion.1.meta_ref, bf16[1,512,1152]{2,1,0:T(8,128)(2,1)} %copy-done.26, bf16[1,2048,1152]{2,1,0:T(8,128)(2,1)} %get-tuple-element.149.dk_ref, bf16[1,2048,1152]{2,1,0:T(8,128)(2,1)} %get-tuple-element.150.dv_ref, bf16[1088,3456]{1,0:T(8,128)(2,1)} %bitcast.116, ...), custom_call_target="tpu_custom_call" | custom-call | flops 10871635968 | bytes 12238848 | tf_op jit(solution)/shard_map/project/pallas_call | solution.py:638
  526.9 2.5 collective-permute-start.13
  529.5 14.2 %collective-permute-start.12 = (f32[1,16,1152]{2,1,0:T(8,128)S(1)}, f32[1,16,1152]{2,1,0:T(8,128)S(1)}, u32[]{:S(2)}, u32[]{:S(2)}) collective-permute-start(f32[1,16,1152]{2,1,0:T(8,128)S(1)} %slice_select_fusion.1), channel_id=1, source_target_pairs={{0,2},{1,3},{2,0},{3,1},{4,6},{5,7},{6,4},{7,5},{8,10},{9,11},{10,... | collective-permute-start | bytes 221192 | tf_op jit(solution)/shard_map/ppermute | solution.py:830
  543.7 3.4 collective-permute-done.12
  547.1 1.3 add_convert_fusion
  548.4 19.7 %collective-permute-start.15 = (bf16[1,16,1152]{2,1,0:T(8,128)(2,1)S(1)}, bf16[1,16,1152]{2,1,0:T(8,128)(2,1)S(1)}, u32[]{:S(2)}, u32[]{:S(2)}) collective-permute-start(bf16[1,16,1152]{2,1,0:T(8,128)(2,1)S(1)} %select_add_fusion.3), channel_id=1, source_target_pairs={{0,16},{1,17},{2,18},{3,19},{4,20},{5,21},{6,22},{7,23},{8,24},{9,... | collective-permute-start | bytes 110600 | tf_op jit(solution)/shard_map/ppermute | solution.py:846
  568.2 1.5 collective-permute-start.19
  569.7 1.4 collective-permute-start.16
  571.0 1.9 collective-permute-done.16
  573.3 5.2 last.2.refs_0_
  579.8 7.6 %to_slots.1 = (f32[3,8,16,1088]{3,2,1,0:T(8,128)}, f32[2,8,16,1088]{3,2,1,0:T(8,128)}, f32[1,8,16,4352]{3,2,1,0:T(8,128)}, f32[1,8,16,4352]{3,2,1,0:T(8,128)}) custom-call(s32[16]{0:T(128)S(1)} %fusion.22.index_ref, bf16[16,16,13184]{2,1,0:T(8,128)(2,1)} %bitcast.95), custom_call_target="tpu_custom_call" | custom-call | flops 3375104 | bytes 13500416 | tf_op jit(solution)/shard_map/to_slots/pallas_call | solution.py:873
  587.4 3.1 collective-permute-start.18
  590.5 6.9 %collective-permute-done.19.refs_3_ = bf16[512,1152]{1,0:T(8,128)(2,1)} collective-permute-done((bf16[512,1152]{1,0:T(8,128)(2,1)}, bf16[512,1152]{1,0:T(8,128)(2,1)}, u32[]{:S(2)}, u32[]{:S(2)}) %collective-permute-start.19) | collective-permute-done | bytes 1179680 | tf_op jit(solution)/shard_map/ppermute | solution.py:795
  598.7 5.5 last.3
  604.2 2.4 collective-permute-start.20
  609.5 6.5 %late_slots.1 = (f32[8,16,3264]{2,1,0:T(8,128)}, f32[3,8,16,1088]{3,2,1,0:T(8,128)}) custom-call(s32[64]{0:T(128)} %pad_add_fusion.2.slot_ref, s32[32]{0:T(128)} %get-tuple-element.227.part_ref, bf16[32,4,16,1152]{3,2,1,0:T(8,128)(2,1)} %bitcast.97, bf16[32,16,1152]{2,1,0:T(8,128)(2,1)} %pad_maximum_fusion.refs_1_, ...), custom_call_target="tpu_custom_call", output_to_operand_aliasing={{1}: (4, {})} | custom-call | bytes 12582912 | tf_op jit(solution)/shard_map/late_slots/pallas_call | solution.py:755
  (223 shorter events, 46.5 us)
Async XLA Ops:
  7.2 120.0 %all-gather.9.cloned.1.call-start = ((), (), s32[]{:S(2)}) async-start(), calls=%async_computation | async-start | bytes 11556864 | tf_op jit(solution)/shard_map/all_gather | solution.py:925
  12.6 9.7 %copy-start.42 = (f32[2,1088]{1,0:T(2,128)S(1)}, f32[2,1088]{1,0:T(2,128)}, u32[]{:S(2)}) copy-start(f32[2,1088]{1,0:T(2,128)} %param.23) | copy-start | bytes 26116
  12.6 243.2 %all-gather.11.cloned.1.call-start = ((), (), s32[]{:S(2)}) async-start(), calls=%async_computation.1 | async-start | bytes 18382848 | tf_op jit(solution)/shard_map/all_gather | solution.py:926
  12.9 14.3 %copy-start.4 = (bf16[2,1,512,1088]{2,3,1,0:T(8,128)(2,1)S(1)}, bf16[2,1,512,1088]{2,3,1,0:T(8,128)(2,1)}, u32[]{:S(2)}) copy-start(bf16[2,1,512,1088]{2,3,1,0:T(8,128)(2,1)} %param.19) | copy-start | bytes 6684676
  13.8 564.8 %all-gather.13.cloned.1.call-start = ((), (), s32[]{:S(2)}) async-start(), calls=%async_computation.2 | async-start | bytes 6961152 | tf_op jit(solution)/shard_map/all_gather | solution.py:1012
  13.9 102.2 %collective-permute-start = (s32[2,512]{1,0:T(2,128)S(1)}, s32[2,512]{1,0:T(2,128)S(1)}, u32[]{:S(2)}, u32[]{:S(2)}) collective-permute-start(s32[2,512]{1,0:T(2,128)S(1)} %bitcast.105), channel_id=1, source_target_pairs={{0,2},{1,3},{4,6},{5,7},{8,10},{9,11},{12,14},{13,15},{16,18},{17,... | collective-permute-start | bytes 12296 | tf_op jit(solution)/shard_map/ppermute | solution.py:795
  17.0 105.4 %collective-permute-start.2 = (s32[2,512]{1,0:T(2,128)S(1)}, s32[2,512]{1,0:T(2,128)S(1)}, u32[]{:S(2)}, u32[]{:S(2)}) collective-permute-start(s32[2,512]{1,0:T(2,128)S(1)} %bitcast.106), channel_id=1, source_target_pairs={{0,1},{2,3},{4,5},{6,7},{8,9},{10,11},{12,13},{14,15},{16,17},{18,... | collective-permute-start | bytes 12296 | tf_op jit(solution)/shard_map/ppermute | solution.py:795
  27.2 186.3 %copy-start.10 = (bf16[2,16,1088]{2,1,0:T(8,128)(2,1)}, bf16[2,16,1088]{2,1,0:T(8,128)(2,1)S(1)}, u32[]{:S(2)}) copy-start(bf16[2,16,1088]{2,1,0:T(8,128)(2,1)S(1)} %get-tuple-element.254.x1_ref) | copy-start | bytes 208900
  27.2 186.3 %copy-start.11 = (bf16[2,16,1088]{2,1,0:T(8,128)(2,1)}, bf16[2,16,1088]{2,1,0:T(8,128)(2,1)S(1)}, u32[]{:S(2)}) copy-start(bf16[2,16,1088]{2,1,0:T(8,128)(2,1)S(1)} %get-tuple-element.255.x0_ref) | copy-start | bytes 208900
  28.9 9.4 %copy-start.36 = (f32[4352]{0:T(1024)S(1)}, f32[4352]{0:T(1024)}, u32[]{:S(2)}) copy-start(f32[4352]{0:T(1024)} %param.25) | copy-start | bytes 52228
  28.9 10.8 %copy-start.44 = (pred[1,1152]{1,0:T(4,128)(4,1)S(1)}, pred[1,1152]{1,0:T(4,128)(4,1)}, u32[]{:S(2)}) copy-start(pred[1,1152]{1,0:T(4,128)(4,1)} %constant.87.clone.1) | copy-start | bytes 3460
  34.0 81.3 %copy-start.47 = (s32[2,1]{0,1:T(1,128)S(1)}, s32[2,1]{0,1:T(1,128)}, u32[]{:S(2)}) copy-start(s32[2,1]{0,1:T(1,128)} %param.21) | copy-start | bytes 28
  34.0 79.2 %collective-permute-start.4 = (bf16[2,512,1152]{2,1,0:T(8,128)(2,1)}, bf16[2,512,1152]{2,1,0:T(8,128)(2,1)}, u32[]{:S(2)}, u32[]{:S(2)}) collective-permute-start(bf16[2,512,1152]{2,1,0:T(8,128)(2,1)} %get-tuple-element.96.refs_0_), channel_id=1, source_target_pairs={{0,2},{1,3},{4,6},{5,7},{8,10},{9,11},{12,14},{13,15},{16,18},{17,... | collective-permute-start | bytes 7077896 | tf_op jit(solution)/shard_map/ppermute | solution.py:795
  36.8 102.4 %collective-permute-start.3 = (bf16[2,512,1152]{2,1,0:T(8,128)(2,1)}, bf16[2,512,1152]{2,1,0:T(8,128)(2,1)}, u32[]{:S(2)}, u32[]{:S(2)}) collective-permute-start(bf16[2,512,1152]{2,1,0:T(8,128)(2,1)} %get-tuple-element.96.refs_0_), channel_id=1, source_target_pairs={{0,1},{2,3},{4,5},{6,7},{8,9},{10,11},{12,13},{14,15},{16,17},{18,... | collective-permute-start | bytes 7077896 | tf_op jit(solution)/shard_map/ppermute | solution.py:795
  113.2 26.0 %collective-permute-start.5 = (bf16[2,512,1152]{2,1,0:T(8,128)(2,1)}, bf16[2,512,1152]{2,1,0:T(8,128)(2,1)}, u32[]{:S(2)}, u32[]{:S(2)}) collective-permute-start(bf16[2,512,1152]{2,1,0:T(8,128)(2,1)} %collective-permute-done.4.refs_2_.refs_1_), channel_id=1, source_target_pairs={{3,2},{2,3},{7,6},{6,7},{11,10},{10,11},{15,14},{14,15},{19,18},{1... | collective-permute-start | bytes 7077896 | tf_op jit(solution)/shard_map/ppermute | solution.py:795
  116.1 6.3 %collective-permute-start.1 = (s32[2,512]{1,0:T(2,128)S(1)}, s32[2,512]{1,0:T(2,128)S(1)}, u32[]{:S(2)}, u32[]{:S(2)}) collective-permute-start(s32[2,512]{1,0:T(2,128)S(1)} %collective-permute-done), channel_id=1, source_target_pairs={{3,2},{2,3},{7,6},{6,7},{11,10},{10,11},{15,14},{14,15},{19,18},{1... | collective-permute-start | bytes 12296 | tf_op jit(solution)/shard_map/ppermute | solution.py:795
  139.2 30.9 %copy-start.20 = (bf16[4,64,1088]{2,1,0:T(8,128)(2,1)}, bf16[4,64,1088]{2,1,0:T(8,128)(2,1)S(1)}, u32[]{:S(2)}) copy-start(bf16[4,64,1088]{2,1,0:T(8,128)(2,1)S(1)} %get-tuple-element.110) | copy-start | bytes 1671172
  139.2 30.9 %copy-start.22 = (s32[3]{0:T(128)S(1)}, s32[3]{0:T(128)}, u32[]{:S(2)}) copy-start(s32[3]{0:T(128)} %pad_add_fusion.1.meta_ref) | copy-start | bytes 40
  170.1 43.4 %copy-start.12 = (bf16[2,16,1088]{2,1,0:T(8,128)(2,1)S(1)}, bf16[2,16,1088]{2,1,0:T(8,128)(2,1)}, u32[]{:S(2)}) copy-start(bf16[2,16,1088]{2,1,0:T(8,128)(2,1)} %get-tuple-element.268.e1_ref) | copy-start | bytes 208900
  170.1 43.4 %copy-start.13 = (bf16[2,16,1088]{2,1,0:T(8,128)(2,1)S(1)}, bf16[2,16,1088]{2,1,0:T(8,128)(2,1)}, u32[]{:S(2)}) copy-start(bf16[2,16,1088]{2,1,0:T(8,128)(2,1)} %get-tuple-element.269.e2_ref) | copy-start | bytes 208900
  170.1 43.4 %copy-start.15 = (f32[1,1088]{1,0:T(1,128)S(1)}, f32[1,1088]{1,0:T(1,128)}, u32[]{:S(2)}) copy-start(f32[1,1088]{1,0:T(1,128)} %get-tuple-element.260.gain_ref) | copy-start | bytes 13060
  170.1 43.4 %copy-start.16 = (f32[1,1088]{1,0:T(1,128)S(1)}, f32[1,1088]{1,0:T(1,128)}, u32[]{:S(2)}) copy-start(f32[1,1088]{1,0:T(1,128)} %get-tuple-element.263.shift_ref) | copy-start | bytes 13060
  255.9 76.3 %copy-start.49 = (f32[2]{0:T(128)S(1)}, f32[2]{0:T(128)}, u32[]{:S(2)}) copy-start(f32[2]{0:T(128)} %multiply_bitcast_fusion) | copy-start | bytes 28
  334.2 18.3 %collective-permute-start.6 = (f32[16,13184]{1,0:T(8,128)S(1)}, f32[16,13184]{1,0:T(8,128)S(1)}, u32[]{:S(2)}, u32[]{:S(2)}) collective-permute-start(f32[16,13184]{1,0:T(8,128)S(1)} %fusion.1), channel_id=1, source_target_pairs={{0,1},{1,0},{2,3},{3,2},{4,5},{5,4},{6,7},{7,6},{8,9},{9,8},{10,11... | collective-permute-start | bytes 2531336 | tf_op jit(solution)/shard_map/ppermute | solution.py:830
  352.7 38.1 %collective-permute-start.7 = (f32[8,13184]{1,0:T(8,128)S(1)}, f32[8,13184]{1,0:T(8,128)S(1)}, u32[]{:S(2)}, u32[]{:S(2)}) collective-permute-start(f32[8,13184]{1,0:T(8,128)S(1)} %slice_select_fusion), channel_id=1, source_target_pairs={{0,2},{1,3},{2,0},{3,1},{4,6},{5,7},{6,4},{7,5},{8,10},{9,11},{10,... | collective-permute-start | bytes 1265672 | tf_op jit(solution)/shard_map/ppermute | solution.py:830
  391.6 217.9 %all-gather.15.cloned.1.call-start = ((), (), s32[]{:S(2)}) async-start(), calls=%async_computation.3 | async-start | bytes 4866048 | tf_op jit(solution)/shard_map/all_gather | solution.py:1030
  391.8 24.3 %copy-start.23 = (s32[3]{0:T(128)S(1)}, s32[3]{0:T(128)}, u32[]{:S(2)}) copy-start(s32[3]{0:T(128)} %pad_add_fusion.1.meta_ref) | copy-start | bytes 40
  413.1 22.5 %collective-permute-start.9 = (bf16[512,1152]{1,0:T(8,128)(2,1)}, bf16[512,1152]{1,0:T(8,128)(2,1)}, u32[]{:S(2)}, u32[]{:S(2)}) collective-permute-start(bf16[512,1152]{1,0:T(8,128)(2,1)} %get-tuple-element.139), channel_id=1, source_target_pairs={{3,2},{2,3},{7,6},{6,7},{11,10},{10,11},{15,14},{14,15},{19,18},{1... | collective-permute-start | bytes 3538952 | tf_op jit(solution)/shard_map/ppermute | solution.py:795
  414.8 22.8 %collective-permute-start.8 = (bf16[512,1152]{1,0:T(8,128)(2,1)}, bf16[512,1152]{1,0:T(8,128)(2,1)S(1)}, u32[]{:S(2)}, u32[]{:S(2)}) collective-permute-start(bf16[512,1152]{1,0:T(8,128)(2,1)} %get-tuple-element.137), channel_id=1, source_target_pairs={{1,0},{3,2},{5,4},{7,6},{9,8},{11,10},{13,12},{15,14},{17,16},{19,... | collective-permute-start | bytes 3538952 | tf_op jit(solution)/shard_map/ppermute | solution.py:795
  417.8 16.9 %copy-start.35 = (f32[4,16,1152]{2,1,0:T(8,128)S(1)}, f32[4,16,1152]{2,1,0:T(8,128)}, u32[]{:S(2)}) copy-start(f32[4,16,1152]{2,1,0:T(8,128)} %get-tuple-element.177) | copy-start | bytes 884740
  437.6 60.6 %collective-permute-start.10 = (bf16[512,1152]{1,0:T(8,128)(2,1)S(1)}, bf16[512,1152]{1,0:T(8,128)(2,1)S(1)}, u32[]{:S(2)}, u32[]{:S(2)}) collective-permute-start(bf16[512,1152]{1,0:T(8,128)(2,1)S(1)} %add_convert_fusion.1), channel_id=1, source_target_pairs={{2,0},{3,1},{6,4},{7,5},{10,8},{11,9},{14,12},{15,13},{18,16},{19,... | collective-permute-start | bytes 3538952 | tf_op jit(solution)/shard_map/ppermute | solution.py:795
  512.5 12.4 %copy-start.34 = (f32[4,16,1152]{2,1,0:T(8,128)S(1)}, f32[4,16,1152]{2,1,0:T(8,128)}, u32[]{:S(2)}) copy-start(f32[4,16,1152]{2,1,0:T(8,128)} %get-tuple-element.151) | copy-start | bytes 884740
  524.9 22.2 %copy-start.32 = (bf16[512,1152]{1,0:T(8,128)(2,1)S(1)}, bf16[512,1152]{1,0:T(8,128)(2,1)}, u32[]{:S(2)}) copy-start(bf16[512,1152]{1,0:T(8,128)(2,1)} %get-tuple-element.159) | copy-start | bytes 3538948
  526.1 3.3 collective-permute-start.11
  526.2 20.9 %collective-permute-start.14 = (bf16[512,1152]{1,0:T(8,128)(2,1)}, bf16[512,1152]{1,0:T(8,128)(2,1)S(1)}, u32[]{:S(2)}, u32[]{:S(2)}) collective-permute-start(bf16[512,1152]{1,0:T(8,128)(2,1)} %get-tuple-element.160), channel_id=1, source_target_pairs={{3,2},{2,3},{7,6},{6,7},{11,10},{10,11},{15,14},{14,15},{19,18},{1... | collective-permute-start | bytes 3538952 | tf_op jit(solution)/shard_map/ppermute | solution.py:795
  526.9 21.5 %collective-permute-start.13 = (bf16[512,1152]{1,0:T(8,128)(2,1)}, bf16[512,1152]{1,0:T(8,128)(2,1)S(1)}, u32[]{:S(2)}, u32[]{:S(2)}) collective-permute-start(bf16[512,1152]{1,0:T(8,128)(2,1)} %get-tuple-element.158), channel_id=1, source_target_pairs={{1,0},{3,2},{5,4},{7,6},{9,8},{11,10},{13,12},{15,14},{17,16},{19,... | collective-permute-start | bytes 3538952 | tf_op jit(solution)/shard_map/ppermute | solution.py:795
  529.4 43.9 %copy-start.3 = (f32[512,1152]{1,0:T(8,128)S(1)}, f32[512,1152]{1,0:T(8,128)}, u32[]{:S(2)}) copy-start(f32[512,1152]{1,0:T(8,128)} %get-tuple-element.167.refs_0_) | copy-start | bytes 7077892
  529.4 43.9 %copy-start.7 = (bf16[2,16,1088]{2,1,0:T(8,128)(2,1)S(1)}, bf16[2,16,1088]{2,1,0:T(8,128)(2,1)}, u32[]{:S(2)}) copy-start(bf16[2,16,1088]{2,1,0:T(8,128)(2,1)} %copy-done.6) | copy-start | bytes 208900
  529.5 43.8 %copy-start.14 = (f32[1,1088]{1,0:T(1,128)S(1)}, f32[1,1088]{1,0:T(1,128)}, u32[]{:S(2)}) copy-start(f32[1,1088]{1,0:T(1,128)} %get-tuple-element.258.refs_5_.refs_6_) | copy-start | bytes 13060
  529.5 17.6 %collective-permute-start.12 = (f32[1,16,1152]{2,1,0:T(8,128)S(1)}, f32[1,16,1152]{2,1,0:T(8,128)S(1)}, u32[]{:S(2)}, u32[]{:S(2)}) collective-permute-start(f32[1,16,1152]{2,1,0:T(8,128)S(1)} %slice_select_fusion.1), channel_id=1, source_target_pairs={{0,2},{1,3},{2,0},{3,1},{4,6},{5,7},{6,4},{7,5},{8,10},{9,11},{10,... | collective-permute-start | bytes 221192 | tf_op jit(solution)/shard_map/ppermute | solution.py:830
  548.4 30.1 %copy-start.8 = (bf16[512,1152]{1,0:T(8,128)(2,1)}, bf16[512,1152]{1,0:T(8,128)(2,1)S(1)}, u32[]{:S(2)}) copy-start(bf16[512,1152]{1,0:T(8,128)(2,1)S(1)} %collective-permute-done.13.refs_2_) | copy-start | bytes 3538948
  548.4 21.2 %collective-permute-start.15 = (bf16[1,16,1152]{2,1,0:T(8,128)(2,1)S(1)}, bf16[1,16,1152]{2,1,0:T(8,128)(2,1)S(1)}, u32[]{:S(2)}, u32[]{:S(2)}) collective-permute-start(bf16[1,16,1152]{2,1,0:T(8,128)(2,1)S(1)} %select_add_fusion.3), channel_id=1, source_target_pairs={{0,16},{1,17},{2,18},{3,19},{4,20},{5,21},{6,22},{7,23},{8,24},{9,... | collective-permute-start | bytes 110600 | tf_op jit(solution)/shard_map/ppermute | solution.py:846
  568.2 29.2 %collective-permute-start.19 = (bf16[512,1152]{1,0:T(8,128)(2,1)}, bf16[512,1152]{1,0:T(8,128)(2,1)}, u32[]{:S(2)}, u32[]{:S(2)}) collective-permute-start(bf16[512,1152]{1,0:T(8,128)(2,1)} %add_convert_fusion), channel_id=1, source_target_pairs={{2,0},{3,1},{6,4},{7,5},{10,8},{11,9},{14,12},{15,13},{18,16},{19,... | collective-permute-start | bytes 3538952 | tf_op jit(solution)/shard_map/ppermute | solution.py:795
  569.7 3.3 collective-permute-start.16
  573.0 5.5 collective-permute-start.17
  579.8 17.6 %copy-start.1 = (f32[512,1152]{1,0:T(8,128)S(1)}, f32[512,1152]{1,0:T(8,128)}, u32[]{:S(2)}) copy-start(f32[512,1152]{1,0:T(8,128)} %get-tuple-element.173.refs_1_) | copy-start | bytes 7077892
  587.4 16.8 %collective-permute-start.18 = (bf16[8,16,1152]{2,1,0:T(8,128)(2,1)S(1)}, bf16[8,16,1152]{2,1,0:T(8,128)(2,1)S(1)}, u32[]{:S(2)}, u32[]{:S(2)}) collective-permute-start(bf16[8,16,1152]{2,1,0:T(8,128)(2,1)S(1)} %pad_maximum_fusion.8), channel_id=1, source_target_pairs={{0,2},{1,3},{2,0},{3,1},{4,6},{5,7},{6,4},{7,5},{8,10},{9,11},{10,... | collective-permute-start | bytes 884744 | tf_op jit(solution)/shard_map/ppermute | solution.py:846
  604.2 4.1 collective-permute-start.20
  (28 other events, 84.6 us)
Sparse Core Ops, SparseCore 0:
  12.7 103.4 all-gather.8
  119.6 136.1 all-gather.10
  391.7 102.9 all-gather.12
  497.5 65.9 all-gather.14

commit v5 on v4

--- a/solution.py
+++ b/solution.py
@@ -68,6 +68,29 @@
         rows = slice(h * 64, (h + 1) * 64)
         acc_ref[rows] = acc_ref[rows] * scale + product(vt_ref[rows, pl.ds(at(t), L)], p.astype(BF), 1, 0)
 
+    def triangle(h):
+        H = L // 2
+        ok = lax.broadcasted_iota(jnp.int32, (H, H), 0) <= lax.broadcasted_iota(jnp.int32, (H, H), 1)
+        s00 = jnp.where(ok, s_ref[h, :H, :H], NEG)
+        s01 = s_ref[h, :H, H:]
+        s11 = jnp.where(ok, s_ref[h, H:, H:], NEG)
+        top = lambda s: jnp.max(s, axis=0, keepdims=True)
+        add = lambda p: jnp.sum(p, axis=0, keepdims=True)
+        m = st_ref[h, 0:1]
+        new = jnp.maximum(m, jnp.concatenate([top(s00), jnp.maximum(top(s01), top(s11))], axis=1))
+        scale = jnp.exp(m - new)
+        p00 = jnp.exp(s00 - new[:, :H])
+        p01 = jnp.exp(s01 - new[:, H:])
+        p11 = jnp.exp(s11 - new[:, H:])
+        st_ref[h, 1:2] = st_ref[h, 1:2] * scale + jnp.concatenate([add(p00), add(p01) + add(p11)], axis=1)
+        st_ref[h, 0:1] = new
+        rows = slice(h * 64, (h + 1) * 64)
+        first, second = vt_ref[rows, :H], vt_ref[rows, H:L]
+        left = product(first, p00.astype(BF), 1, 0)
+        right = product(first, p01.astype(BF), 1, 0) + product(second, p11.astype(BF), 1, 0)
+        acc_ref[rows, :H] = acc_ref[rows, :H] * scale[:, :H] + left
+        acc_ref[rows, H:] = acc_ref[rows, H:] * scale[:, H:] + right
+
     scores(lo, 0)
 
     def body(t, carry):
@@ -79,21 +102,24 @@
 
     lax.fori_loop(lo, me, body, 0)
     scores(me, 1)
-    gather(me, 0, True)
-    gather(me, 1, True)
+    for h in range(2):
+        if L % 256 == 0:
+            triangle(h)
+        else:
+            gather(me, h, True)
     rows = []
     for h in range(2):
         total = st_ref[h, 1:2]
         sl = slice(h * 64, (h + 1) * 64)
         acc_ref[sl] = acc_ref[sl] / total
         rows.append(thirds(-(st_ref[h, 0:1] + jnp.log(total))))
-    o_ref[0] = acc_ref[...].T.astype(o_ref.dtype)
+    o_ref[0] = acc_ref[...].astype(BF).T
     sub = lax.broadcasted_iota(jnp.int32, (128, 1), 0)
     extra = jnp.zeros((128, L), F32)
     for h in range(2):
         for i in range(3):
             extra = jnp.where(sub == (1 - h) * 64 + 8 + i, rows[h][i].astype(F32), extra)
-    a_ref[0, 0] = (qa.astype(F32) + extra.T).astype(BF)
+    a_ref[0, 0] = qa + extra.astype(BF).T
 
 
 def attn_fwd(meta, q, k, v, qa, ka, D):
@@ -186,6 +212,24 @@
         dkt_ref[rows] = product(qt[rows], ds, 1, 0)
         dqt_ref[rows] += product(kt_ref[rows, pl.ds(at(t), L)], ds, 1, 1)
 
+    def triangle(h):
+        H = L // 2
+        ok = lax.broadcasted_iota(jnp.int32, (H, H), 1) <= lax.broadcasted_iota(jnp.int32, (H, H), 0)
+        p00 = jnp.where(ok, jnp.exp(s_ref[h, :H, :H]), 0.0)
+        p10 = jnp.exp(s_ref[h, H:, :H])
+        p11 = jnp.where(ok, jnp.exp(s_ref[h, H:, H:]), 0.0)
+        ds00 = (p00 * dp_ref[h, :H, :H]).astype(BF)
+        ds10 = (p10 * dp_ref[h, H:, :H]).astype(BF)
+        ds11 = (p11 * dp_ref[h, H:, H:]).astype(BF)
+        rows = slice(h * 64, (h + 1) * 64)
+        do_h, q_h, k_h = dot_[rows], qt[rows], kt_ref[rows, :L]
+        dvt_ref[rows, :H] = product(do_h[:, :H], p00.astype(BF), 1, 0) + product(do_h[:, H:], p10.astype(BF), 1, 0)
+        dvt_ref[rows, H:] = product(do_h[:, H:], p11.astype(BF), 1, 0)
+        dkt_ref[rows, :H] = product(q_h[:, :H], ds00, 1, 0) + product(q_h[:, H:], ds10, 1, 0)
+        dkt_ref[rows, H:] = product(q_h[:, H:], ds11, 1, 0)
+        dqt_ref[rows, :H] += product(k_h[:, :H], ds00, 1, 1)
+        dqt_ref[rows, H:] += product(k_h[:, :H], ds10, 1, 1) + product(k_h[:, H:], ds11, 1, 1)
+
     def store(t):
         here = pl.ds(at(t), L)
         dk_ref[0, here, :] = dkt_ref[...].astype(BF).T
@@ -211,8 +255,11 @@
 
     lax.fori_loop(lo, me, body, 0)
     scores(me, 1)
-    gather(me, 0, True)
-    gather(me, 1, True)
+    for h in range(2):
+        if L % 256 == 0:
+            triangle(h)
+        else:
+            gather(me, h, True)
     store(me)
     dq_ref[0] = dqt_ref[...].astype(BF).T * jnp.asarray(0.125, BF)
 
@@ -1018,11 +1065,8 @@
             held = {j: [p] for j, p in enumerate(parts)}
             do, held = lax.optimization_barrier((do, held))
         else:
-            parts, g = project(meta, dq, dk, dv, w_mix, mix_up, n1_parts, r, everything[1:])
-            dq, parts = lax.optimization_barrier((dq, parts))
-            own, g_own = project(meta, dq, dk, dv, w_mix, mix_up, n1_parts, r, [0])
-            g = g + g_own
-            held = {j: [p] for j, p in enumerate(own + parts)}
+            parts, g = project(meta, dq, dk, dv, w_mix, mix_up, n1_parts, r, everything)
+            held = {j: [p] for j, p in enumerate(parts)}
             held = blocks_back(held, bits[0])
             held = {j: [block_sum(t)] if j else t for j, t in held.items()}
         g = g.reshape(4, rank, C // 4, -1).transpose(0, 2, 1, 3).reshape(C, rank, -1)

time: 629 us -> 621 us (0.987)
  Pallas kernels: 323 us -> 315 us
    ppermute x4, starting transfers between devices: 32.2 us -> 54.6 us  [ctx_sum_stage(): lax.ppermute(jnp.where(mine, low, high), 'ctx', [(d, d ^ bit) for d in ra...]
    ppermute x5, starting transfers between devices: 27 us -> 6.27 us  [gather_all(): got = lax.ppermute(held, BOTH, [(d, d ^ bit) for d in range(n)])]
    pallas_call x3 -> x2, Pallas kernels: 47.9 us -> 42.4 us  [project(): pl.pallas_call(functools.partial(project_kernel, W=W, js=tuple(js), r=r),...]
    unnamed x105 -> x103, local copies, waits for them, and re-layouts: 19.4 us -> 19.4 us
  transfers between devices with their start and end apart: 25 -> 25, of which waited for: 6 -> 7; matrix products, arithmetic and copies ran while one was open for 5% -> 5% of each run, Pallas kernels for 39% -> 38%
where the time goes in v5:
time: 621 us; the launch traced here: 614 us
  Pallas kernels  315 us (51%)
  waiting for transfers between devices  140 us (23%)
  starting transfers between devices  81.6 us (13%)
  local copies, waits for them, and re-layouts  40.9 us (7%)
  between operations  18.7 us (3%)
  other arithmetic  18.1 us (3%)
    ppermute x12, waiting for transfers between devices, swap(): return lax.ppermute(x, axis, [(d ^ bit, d) for d in range(n) if needed(d)])  106 us
    pallas_call x1, Pallas kernels, ffn(): pl.pallas_call(functools.partial(ffn_kernel, R=R, per=per, co=co), grid=(...  76.4 us
    pallas_call x4, Pallas kernels, attn_bwd(): pl.pallas_call(functools.partial(attn_bwd_kernel, L=L, r0=r0, D=D, first=...  72.6 us
    ppermute x4, starting transfers between devices, ctx_sum_stage(): lax.ppermute(jnp.where(mine, low, high), 'ctx', [(d, d ^ bit) for d in ra...  54.6 us
    pallas_call x2, Pallas kernels, project(): pl.pallas_call(functools.partial(project_kernel, W=W, js=tuple(js), r=r),...  42.4 us
    pallas_call x1, Pallas kernels, attn_fwd(): pl.pallas_call(functools.partial(attn_fwd_kernel, L=L), grid_spec=pltpu.P...  40.4 us
    pallas_call x1, Pallas kernels, qkv(): pl.pallas_call(functools.partial(qkv_kernel, W=W, count=count, R=R), grid...  30.8 us
    all_gather x1, waiting for transfers between devices, per_device(): g2 = lax.all_gather(second, BOTH).reshape(S, C, -1, main)  25.6 us
  transfers between devices with their start and end apart: 25, of which 7 were waited for; matrix products, arithmetic and copies ran while one was open for 5% of the time, Pallas kernels for 38%

profile of v5, /device:TPU:5, one launch (start us, length us, event | category | flops | bytes accessed | tf_op | source)
XLA Modules:
  0.0 614.2 jit_solution(11117932643795339861)
XLA Ops:
  13.9 3.1 collective-permute-start
  17.0 1.3 collective-permute-start.2
  27.2 1.7 copy-done.5
  28.9 5.1 first_norm.1
  34.0 2.8 collective-permute-start.4
  40.4 1.4 fusion.28
  45.2 68.0 %collective-permute-done.4.refs_2_ = bf16[2,512,1152]{2,1,0:T(8,128)(2,1)} collective-permute-done((bf16[2,512,1152]{2,1,0:T(8,128)(2,1)}, bf16[2,512,1152]{2,1,0:T(8,128)(2,1)}, u32[]{:S(2)}, u32[]{:S(2)}) %collective-permute-start.4) | collective-permute-done | bytes 2359328 | tf_op jit(solution)/shard_map/ppermute | solution.py:842
  113.2 2.1 collective-permute-start.5
  124.5 1.8 copy.78.ka_ref
  127.2 9.7 %unpack.1 = (bf16[4,2,136,3456]{3,2,1,0:T(8,128)(2,1)}, bf16[4,2,136,1088]{3,2,1,0:T(8,128)(2,1)S(1)}, bf16[4,256,272]{2,1,0:T(8,128)(2,1)S(1)}, bf16[4,64,1088]{2,1,0:T(8,128)(2,1)S(1)}) custom-call(bf16[8,4,152,1088]{3,2,1,0:T(8,128)(2,1)} %bitcast.92), custom_call_target="tpu_custom_call" | custom-call | bytes 21168128 | tf_op jit(solution)/shard_map/unpack/pallas_call | solution.py:379
  136.9 1.5 copy-done
  139.3 30.8 %qkv.1 = (bf16[2,512,1152]{2,1,0:T(8,128)(2,1)}, bf16[2,2048,1152]{2,1,0:T(8,128)(2,1)}, bf16[2,2048,1152]{2,1,0:T(8,128)(2,1)}) custom-call(s32[3]{0:T(128)} %pad_add_fusion.1.meta_ref, bf16[2,512,1152]{2,1,0:T(8,128)(2,1)} %get-tuple-element.91.refs_0_, bf16[2,512,1152]{2,1,0:T(8,128)(2,1)} %collective-permute-done.3.refs_1_, ...), custom_call_target="tpu_custom_call" | custom-call | flops 43486543872 | bytes 35831808 | tf_op jit(solution)/shard_map/qkv/pallas_call | solution.py:431
  170.1 40.4 %attn_fwd.1 = (bf16[2,512,1088]{2,1,0:T(8,128)(2,1)S(1)}, bf16[2,9,512,128]{3,2,1,0:T(8,128)(2,1)S(1)}) custom-call(s32[3]{0:T(128)S(1)} %copy-done.22, bf16[2,512,1152]{2,1,0:T(8,128)(2,1)} %get-tuple-element.93.q_ref, bf16[2,2048,1152]{2,1,0:T(8,128)(2,1)} %get-tuple-element.94.k_ref, bf16[2,2048,1152]{2,1,0:T(8,128)(2,1)} %get-tuple-element.95.v_ref, ...), custom_call_target="tpu_custom_call" | custom-call | flops 96636764160 | bytes 23592960 | tf_op jit(solution)/shard_map/attn_fwd/pallas_call | solution.py:131
  210.6 1.4 copy-done.2
  212.0 1.4 copy-done.27
  213.5 13.1 %mid.1 = (f32[2,512,1088]{2,1,0:T(8,128)}, bf16[2,512,1152]{2,1,0:T(8,128)(2,1)S(1)}, bf16[2,512,1152]{2,1,0:T(8,128)(2,1)S(1)}, bf16[2,512,16]{2,1,0:T(8,128)(2,1)S(1)}) custom-call(bf16[2,512,1088]{2,1,0:T(8,128)(2,1)} %copy-done.2, bf16[2,512,1088]{2,1,0:T(8,128)(2,1)} %get-tuple-element.97.x_ref.refs_4_.refs_5_, ...), custom_call_target="tpu_custom_call" | custom-call | flops 2424307712 | bytes 17825792 | tf_op jit(solution)/shard_map/mid/pallas_call | solution.py:479
  226.5 1.6 copy-done.17
  228.1 1.4 copy-done.18
  230.2 25.6 %all-gather.11.cloned.1.call-done = bf16[17408,512]{1,0:T(8,128)(2,1)} async-done(((bf16[544,512]{1,0:T(8,128)(2,1)}), bf16[17408,512]{1,0:T(8,128)(2,1)}) %all-gather.11.cloned.1.call-update) | async-done | bytes 17825808 | tf_op jit(solution)/shard_map/all_gather | solution.py:973
  255.9 76.4 %ffn.1 = (bf16[2,1088,512]{2,1,0:T(8,128)(2,1)}, f32[2,512,1088]{2,1,0:T(8,128)}, bf16[2,512,1088]{2,1,0:T(8,128)(2,1)}, f32[2,16,1088]{2,1,0:T(8,128)}, f32[2,1...) custom-call(bf16[1024,1152]{1,0:T(8,128)(2,1)} %bitcast.89, ...), custom_call_target="tpu_custom_call" | custom-call | flops 77577846784 | bytes 45678592 | tf_op jit(solution)/shard_map/ffn/pallas_call | solution.py:609
  332.4 1.6 concatenate.83
  335.6 16.4 %attn_bwd.4 = (bf16[1,512,1152]{2,1,0:T(8,128)(2,1)S(1)}, bf16[1,2048,1152]{2,1,0:T(8,128)(2,1)}, bf16[1,2048,1152]{2,1,0:T(8,128)(2,1)}) custom-call(s32[3]{0:T(128)S(1)} %copy-done.22, bf16[2,512,1152]{2,1,0:T(8,128)(2,1)S(1)} %copy-done.24, bf16[2,2048,1152]{2,1,0:T(8,128)(2,1)} %get-tuple-element.94.k_ref, ...), custom_call_target="tpu_custom_call" | custom-call | flops 32212254720 | bytes 9961472 | tf_op jit(solution)/shard_map/attn_bwd/pallas_call | solution.py:272
  352.3 29.1 %collective-permute-start.7 = (f32[8,13184]{1,0:T(8,128)S(1)}, f32[8,13184]{1,0:T(8,128)S(1)}, u32[]{:S(2)}, u32[]{:S(2)}) collective-permute-start(f32[8,13184]{1,0:T(8,128)S(1)} %slice_select_fusion), channel_id=1, source_target_pairs={{0,2},{1,3},{2,0},{3,1},{4,6},{5,7},{6,4},{7,5},{8,10},{9,11},{10,... | collective-permute-start | bytes 1265672 | tf_op jit(solution)/shard_map/ppermute | solution.py:877
  381.4 19.8 %attn_bwd.5 = (bf16[1,512,1152]{2,1,0:T(8,128)(2,1)S(1)}, bf16[1,2048,1152]{2,1,0:T(8,128)(2,1)}, bf16[1,2048,1152]{2,1,0:T(8,128)(2,1)}) custom-call(s32[3]{0:T(128)S(1)} %copy-done.22, bf16[2,512,1152]{2,1,0:T(8,128)(2,1)S(1)} %copy-done.24, ...), custom_call_target="tpu_custom_call", output_to_operand_aliasing={{0}: (8, {}), {1}: (9, {}), {2}: (10, {})} | custom-call | flops 40265318400 | bytes 12451840 | tf_op jit(solution)/shard_map/attn_bwd/pallas_call | solution.py:272
  402.3 21.2 %project.2 = (f32[512,1152]{1,0:T(8,128)}, bf16[512,1152]{1,0:T(8,128)(2,1)}, bf16[512,1152]{1,0:T(8,128)(2,1)}, bf16[512,1152]{1,0:T(8,128)(2,1)}, f32[4,16,1152]{2,1,0:T(8,128)}) custom-call(s32[3]{0:T(128)} %pad_add_fusion.1.meta_ref, bf16[1,512,1152]{2,1,0:T(8,128)(2,1)} %copy-done.31, bf16[1,2048,1152]{2,1,0:T(8,128)(2,1)} %get-tuple-element.124.dk_ref, ...), custom_call_target="tpu_custom_call" | custom-call | flops 43486543872 | bytes 26394624 | tf_op jit(solution)/shard_map/project/pallas_call | solution.py:685
  423.6 1.7 collective-permute-start.9
  425.3 1.4 collective-permute-start.8
  426.7 1.7 copy-done.25
  428.3 16.4 %attn_bwd.6 = (bf16[1,512,1152]{2,1,0:T(8,128)(2,1)S(1)}, bf16[1,2048,1152]{2,1,0:T(8,128)(2,1)}, bf16[1,2048,1152]{2,1,0:T(8,128)(2,1)}) custom-call(s32[3]{0:T(128)S(1)} %copy-done.23, bf16[2,512,1152]{2,1,0:T(8,128)(2,1)S(1)} %copy-done.25, bf16[2,2048,1152]{2,1,0:T(8,128)(2,1)} %get-tuple-element.94.k_ref, ...), custom_call_target="tpu_custom_call" | custom-call | flops 32212254720 | bytes 9961472 | tf_op jit(solution)/shard_map/attn_bwd/pallas_call | solution.py:272
  445.5 2.1 add_convert_fusion.1
  450.2 20.0 %attn_bwd.7 = (bf16[1,512,1152]{2,1,0:T(8,128)(2,1)S(1)}, bf16[1,2048,1152]{2,1,0:T(8,128)(2,1)}, bf16[1,2048,1152]{2,1,0:T(8,128)(2,1)}) custom-call(s32[3]{0:T(128)S(1)} %copy-done.23, bf16[2,512,1152]{2,1,0:T(8,128)(2,1)S(1)} %copy-done.26, ...), custom_call_target="tpu_custom_call", output_to_operand_aliasing={{0}: (8, {}), {1}: (9, {}), {2}: (10, {})} | custom-call | flops 40265318400 | bytes 12451840 | tf_op jit(solution)/shard_map/attn_bwd/pallas_call | solution.py:272
  471.2 32.0 %collective-permute-done.10.refs_2_ = bf16[512,1152]{1,0:T(8,128)(2,1)S(1)} collective-permute-done((bf16[512,1152]{1,0:T(8,128)(2,1)S(1)}, bf16[512,1152]{1,0:T(8,128)(2,1)S(1)}, u32[]{:S(2)}, u32[]{:S(2)}) %collective-permute-start.10) | collective-permute-done | bytes 1179680 | tf_op jit(solution)/shard_map/ppermute | solution.py:842
  503.2 21.2 %project.3 = (f32[512,1152]{1,0:T(8,128)}, bf16[512,1152]{1,0:T(8,128)(2,1)}, bf16[512,1152]{1,0:T(8,128)(2,1)}, bf16[512,1152]{1,0:T(8,128)(2,1)}, f32[4,16,1152]{2,1,0:T(8,128)}) custom-call(s32[3]{0:T(128)} %pad_add_fusion.1.meta_ref, bf16[1,512,1152]{2,1,0:T(8,128)(2,1)} %copy-done.30, bf16[1,2048,1152]{2,1,0:T(8,128)(2,1)} %get-tuple-element.144.dk_ref, ...), custom_call_target="tpu_custom_call" | custom-call | flops 43486543872 | bytes 26394624 | tf_op jit(solution)/shard_map/project/pallas_call | solution.py:685
  526.3 2.5 collective-permute-start.13
  528.9 25.1 %collective-permute-start.12 = (f32[1,16,1152]{2,1,0:T(8,128)S(1)}, f32[1,16,1152]{2,1,0:T(8,128)S(1)}, u32[]{:S(2)}, u32[]{:S(2)}) collective-permute-start(f32[1,16,1152]{2,1,0:T(8,128)S(1)} %slice_select_fusion.1), channel_id=1, source_target_pairs={{0,2},{1,3},{2,0},{3,1},{4,6},{5,7},{6,4},{7,5},{8,10},{9,11},{10,... | collective-permute-start | bytes 221192 | tf_op jit(solution)/shard_map/ppermute | solution.py:877
  554.0 2.2 collective-permute-done.12
  556.2 1.3 add_convert_fusion
  557.5 2.2 collective-permute-start.15
  559.7 1.7 collective-permute-start.19
  561.4 2.4 collective-permute-done.15
  563.9 3.6 collective-permute-done.16
  567.8 5.2 last.2.refs_0_
  574.3 7.6 %to_slots.1 = (f32[3,8,16,1088]{3,2,1,0:T(8,128)}, f32[2,8,16,1088]{3,2,1,0:T(8,128)}, f32[1,8,16,4352]{3,2,1,0:T(8,128)}, f32[1,8,16,4352]{3,2,1,0:T(8,128)}) custom-call(s32[16]{0:T(128)S(1)} %fusion.22.index_ref, bf16[16,16,13184]{2,1,0:T(8,128)(2,1)} %bitcast.95), custom_call_target="tpu_custom_call" | custom-call | flops 3375104 | bytes 13500416 | tf_op jit(solution)/shard_map/to_slots/pallas_call | solution.py:920
  581.9 1.3 collective-permute-start.18
  583.2 5.7 collective-permute-done.19.refs_3_
  590.2 5.5 last.3
  595.8 2.4 collective-permute-start.20
  601.1 6.5 %late_slots.1 = (f32[8,16,3264]{2,1,0:T(8,128)}, f32[3,8,16,1088]{3,2,1,0:T(8,128)}) custom-call(s32[64]{0:T(128)} %pad_add_fusion.2.slot_ref, s32[32]{0:T(128)} %get-tuple-element.217.part_ref, bf16[32,4,16,1152]{3,2,1,0:T(8,128)(2,1)} %bitcast.97, bf16[32,16,1152]{2,1,0:T(8,128)(2,1)} %pad_maximum_fusion.refs_1_, ...), custom_call_target="tpu_custom_call", output_to_operand_aliasing={{1}: (4, {})} | custom-call | bytes 12582912 | tf_op jit(solution)/shard_map/late_slots/pallas_call | solution.py:802
  (219 shorter events, 45.1 us)
Async XLA Ops:
  7.2 120.0 %all-gather.9.cloned.1.call-start = ((), (), s32[]{:S(2)}) async-start(), calls=%async_computation | async-start | bytes 11556864 | tf_op jit(solution)/shard_map/all_gather | solution.py:972
  12.6 9.7 %copy-start.41 = (f32[2,1088]{1,0:T(2,128)S(1)}, f32[2,1088]{1,0:T(2,128)}, u32[]{:S(2)}) copy-start(f32[2,1088]{1,0:T(2,128)} %param.23) | copy-start | bytes 26116
  12.6 243.2 %all-gather.11.cloned.1.call-start = ((), (), s32[]{:S(2)}) async-start(), calls=%async_computation.1 | async-start | bytes 18382848 | tf_op jit(solution)/shard_map/all_gather | solution.py:973
  12.9 14.2 %copy-start.4 = (bf16[2,1,512,1088]{2,3,1,0:T(8,128)(2,1)S(1)}, bf16[2,1,512,1088]{2,3,1,0:T(8,128)(2,1)}, u32[]{:S(2)}) copy-start(bf16[2,1,512,1088]{2,3,1,0:T(8,128)(2,1)} %param.19) | copy-start | bytes 6684676
  13.8 559.3 %all-gather.13.cloned.1.call-start = ((), (), s32[]{:S(2)}) async-start(), calls=%async_computation.2 | async-start | bytes 6961152 | tf_op jit(solution)/shard_map/all_gather | solution.py:1059
  13.9 102.2 %collective-permute-start = (s32[2,512]{1,0:T(2,128)S(1)}, s32[2,512]{1,0:T(2,128)S(1)}, u32[]{:S(2)}, u32[]{:S(2)}) collective-permute-start(s32[2,512]{1,0:T(2,128)S(1)} %bitcast.105), channel_id=1, source_target_pairs={{0,2},{1,3},{4,6},{5,7},{8,10},{9,11},{12,14},{13,15},{16,18},{17,... | collective-permute-start | bytes 12296 | tf_op jit(solution)/shard_map/ppermute | solution.py:842
  17.0 105.3 %collective-permute-start.2 = (s32[2,512]{1,0:T(2,128)S(1)}, s32[2,512]{1,0:T(2,128)S(1)}, u32[]{:S(2)}, u32[]{:S(2)}) collective-permute-start(s32[2,512]{1,0:T(2,128)S(1)} %bitcast.106), channel_id=1, source_target_pairs={{0,1},{2,3},{4,5},{6,7},{8,9},{10,11},{12,13},{14,15},{16,17},{18,... | collective-permute-start | bytes 12296 | tf_op jit(solution)/shard_map/ppermute | solution.py:842
  27.2 186.3 %copy-start.10 = (bf16[2,16,1088]{2,1,0:T(8,128)(2,1)}, bf16[2,16,1088]{2,1,0:T(8,128)(2,1)S(1)}, u32[]{:S(2)}) copy-start(bf16[2,16,1088]{2,1,0:T(8,128)(2,1)S(1)} %get-tuple-element.244.x1_ref) | copy-start | bytes 208900
  27.2 186.3 %copy-start.11 = (bf16[2,16,1088]{2,1,0:T(8,128)(2,1)}, bf16[2,16,1088]{2,1,0:T(8,128)(2,1)S(1)}, u32[]{:S(2)}) copy-start(bf16[2,16,1088]{2,1,0:T(8,128)(2,1)S(1)} %get-tuple-element.245.x0_ref) | copy-start | bytes 208900
  28.9 9.2 %copy-start.40 = (f32[2,1088]{1,0:T(2,128)S(1)}, f32[2,1088]{1,0:T(2,128)}, u32[]{:S(2)}) copy-start(f32[2,1088]{1,0:T(2,128)} %param.24) | copy-start | bytes 26116
  28.9 9.4 %copy-start.35 = (f32[4352]{0:T(1024)S(1)}, f32[4352]{0:T(1024)}, u32[]{:S(2)}) copy-start(f32[4352]{0:T(1024)} %param.25) | copy-start | bytes 52228
  28.9 10.8 %copy-start.43 = (pred[1,1152]{1,0:T(4,128)(4,1)S(1)}, pred[1,1152]{1,0:T(4,128)(4,1)}, u32[]{:S(2)}) copy-start(pred[1,1152]{1,0:T(4,128)(4,1)} %constant.87.clone.1) | copy-start | bytes 3460
  34.0 81.3 %copy-start.46 = (s32[2,1]{0,1:T(1,128)S(1)}, s32[2,1]{0,1:T(1,128)}, u32[]{:S(2)}) copy-start(s32[2,1]{0,1:T(1,128)} %param.21) | copy-start | bytes 28
  34.0 79.2 %collective-permute-start.4 = (bf16[2,512,1152]{2,1,0:T(8,128)(2,1)}, bf16[2,512,1152]{2,1,0:T(8,128)(2,1)}, u32[]{:S(2)}, u32[]{:S(2)}) collective-permute-start(bf16[2,512,1152]{2,1,0:T(8,128)(2,1)} %get-tuple-element.91.refs_0_), channel_id=1, source_target_pairs={{0,2},{1,3},{4,6},{5,7},{8,10},{9,11},{12,14},{13,15},{16,18},{17,... | collective-permute-start | bytes 7077896 | tf_op jit(solution)/shard_map/ppermute | solution.py:842
  36.8 102.4 %collective-permute-start.3 = (bf16[2,512,1152]{2,1,0:T(8,128)(2,1)}, bf16[2,512,1152]{2,1,0:T(8,128)(2,1)}, u32[]{:S(2)}, u32[]{:S(2)}) collective-permute-start(bf16[2,512,1152]{2,1,0:T(8,128)(2,1)} %get-tuple-element.91.refs_0_), channel_id=1, source_target_pairs={{0,1},{2,3},{4,5},{6,7},{8,9},{10,11},{12,13},{14,15},{16,17},{18,... | collective-permute-start | bytes 7077896 | tf_op jit(solution)/shard_map/ppermute | solution.py:842
  113.2 26.1 %collective-permute-start.5 = (bf16[2,512,1152]{2,1,0:T(8,128)(2,1)}, bf16[2,512,1152]{2,1,0:T(8,128)(2,1)}, u32[]{:S(2)}, u32[]{:S(2)}) collective-permute-start(bf16[2,512,1152]{2,1,0:T(8,128)(2,1)} %collective-permute-done.4.refs_2_), channel_id=1, source_target_pairs={{3,2},{2,3},{7,6},{6,7},{11,10},{10,11},{15,14},{14,15},{19,18},{1... | collective-permute-start | bytes 7077896 | tf_op jit(solution)/shard_map/ppermute | solution.py:842
  116.1 6.3 %collective-permute-start.1 = (s32[2,512]{1,0:T(2,128)S(1)}, s32[2,512]{1,0:T(2,128)S(1)}, u32[]{:S(2)}, u32[]{:S(2)}) collective-permute-start(s32[2,512]{1,0:T(2,128)S(1)} %collective-permute-done), channel_id=1, source_target_pairs={{3,2},{2,3},{7,6},{6,7},{11,10},{10,11},{15,14},{14,15},{19,18},{1... | collective-permute-start | bytes 12296 | tf_op jit(solution)/shard_map/ppermute | solution.py:842
  139.2 30.9 %copy-start.20 = (bf16[4,64,1088]{2,1,0:T(8,128)(2,1)}, bf16[4,64,1088]{2,1,0:T(8,128)(2,1)S(1)}, u32[]{:S(2)}) copy-start(bf16[4,64,1088]{2,1,0:T(8,128)(2,1)S(1)} %get-tuple-element.105) | copy-start | bytes 1671172
  139.2 30.9 %copy-start.22 = (s32[3]{0:T(128)S(1)}, s32[3]{0:T(128)}, u32[]{:S(2)}) copy-start(s32[3]{0:T(128)} %pad_add_fusion.1.meta_ref) | copy-start | bytes 40
  170.1 43.3 %copy-start.12 = (bf16[2,16,1088]{2,1,0:T(8,128)(2,1)S(1)}, bf16[2,16,1088]{2,1,0:T(8,128)(2,1)}, u32[]{:S(2)}) copy-start(bf16[2,16,1088]{2,1,0:T(8,128)(2,1)} %get-tuple-element.258.e1_ref) | copy-start | bytes 208900
  170.1 43.3 %copy-start.13 = (bf16[2,16,1088]{2,1,0:T(8,128)(2,1)S(1)}, bf16[2,16,1088]{2,1,0:T(8,128)(2,1)}, u32[]{:S(2)}) copy-start(bf16[2,16,1088]{2,1,0:T(8,128)(2,1)} %get-tuple-element.259.e2_ref) | copy-start | bytes 208900
  170.1 43.3 %copy-start.15 = (f32[1,1088]{1,0:T(1,128)S(1)}, f32[1,1088]{1,0:T(1,128)}, u32[]{:S(2)}) copy-start(f32[1,1088]{1,0:T(1,128)} %get-tuple-element.250.gain_ref) | copy-start | bytes 13060
  170.1 43.3 %copy-start.16 = (f32[1,1088]{1,0:T(1,128)S(1)}, f32[1,1088]{1,0:T(1,128)}, u32[]{:S(2)}) copy-start(f32[1,1088]{1,0:T(1,128)} %get-tuple-element.253.shift_ref) | copy-start | bytes 13060
  255.9 76.4 %copy-start.48 = (f32[2]{0:T(128)S(1)}, f32[2]{0:T(128)}, u32[]{:S(2)}) copy-start(f32[2]{0:T(128)} %multiply_bitcast_fusion) | copy-start | bytes 28
  334.3 17.8 %collective-permute-start.6 = (f32[16,13184]{1,0:T(8,128)S(1)}, f32[16,13184]{1,0:T(8,128)S(1)}, u32[]{:S(2)}, u32[]{:S(2)}) collective-permute-start(f32[16,13184]{1,0:T(8,128)S(1)} %fusion.1), channel_id=1, source_target_pairs={{0,1},{1,0},{2,3},{3,2},{4,5},{5,4},{6,7},{7,6},{8,9},{9,8},{10,11... | collective-permute-start | bytes 2531336 | tf_op jit(solution)/shard_map/ppermute | solution.py:877
  352.3 48.9 %collective-permute-start.7 = (f32[8,13184]{1,0:T(8,128)S(1)}, f32[8,13184]{1,0:T(8,128)S(1)}, u32[]{:S(2)}, u32[]{:S(2)}) collective-permute-start(f32[8,13184]{1,0:T(8,128)S(1)} %slice_select_fusion), channel_id=1, source_target_pairs={{0,2},{1,3},{2,0},{3,1},{4,6},{5,7},{6,4},{7,5},{8,10},{9,11},{10,... | collective-permute-start | bytes 1265672 | tf_op jit(solution)/shard_map/ppermute | solution.py:877
  402.1 198.9 %all-gather.15.cloned.1.call-start = ((), (), s32[]{:S(2)}) async-start(), calls=%async_computation.3 | async-start | bytes 4866048 | tf_op jit(solution)/shard_map/all_gather | solution.py:1074
  402.3 24.3 %copy-start.23 = (s32[3]{0:T(128)S(1)}, s32[3]{0:T(128)}, u32[]{:S(2)}) copy-start(s32[3]{0:T(128)} %pad_add_fusion.1.meta_ref) | copy-start | bytes 40
  423.6 21.9 %collective-permute-start.9 = (bf16[512,1152]{1,0:T(8,128)(2,1)}, bf16[512,1152]{1,0:T(8,128)(2,1)}, u32[]{:S(2)}, u32[]{:S(2)}) collective-permute-start(bf16[512,1152]{1,0:T(8,128)(2,1)} %get-tuple-element.134), channel_id=1, source_target_pairs={{3,2},{2,3},{7,6},{6,7},{11,10},{10,11},{15,14},{14,15},{19,18},{1... | collective-permute-start | bytes 3538952 | tf_op jit(solution)/shard_map/ppermute | solution.py:842
  425.3 22.3 %collective-permute-start.8 = (bf16[512,1152]{1,0:T(8,128)(2,1)}, bf16[512,1152]{1,0:T(8,128)(2,1)S(1)}, u32[]{:S(2)}, u32[]{:S(2)}) collective-permute-start(bf16[512,1152]{1,0:T(8,128)(2,1)} %get-tuple-element.132), channel_id=1, source_target_pairs={{1,0},{3,2},{5,4},{7,6},{9,8},{11,10},{13,12},{15,14},{17,16},{19,... | collective-permute-start | bytes 3538952 | tf_op jit(solution)/shard_map/ppermute | solution.py:842
  428.3 16.4 %copy-start.34 = (f32[4,16,1152]{2,1,0:T(8,128)S(1)}, f32[4,16,1152]{2,1,0:T(8,128)}, u32[]{:S(2)}) copy-start(f32[4,16,1152]{2,1,0:T(8,128)} %get-tuple-element.167) | copy-start | bytes 884740
  447.6 55.6 %collective-permute-start.10 = (bf16[512,1152]{1,0:T(8,128)(2,1)S(1)}, bf16[512,1152]{1,0:T(8,128)(2,1)S(1)}, u32[]{:S(2)}, u32[]{:S(2)}) collective-permute-start(bf16[512,1152]{1,0:T(8,128)(2,1)S(1)} %add_convert_fusion.1), channel_id=1, source_target_pairs={{2,0},{3,1},{6,4},{7,5},{10,8},{11,9},{14,12},{15,13},{18,16},{19,... | collective-permute-start | bytes 3538952 | tf_op jit(solution)/shard_map/ppermute | solution.py:842
  524.4 31.9 %copy-start.32 = (bf16[512,1152]{1,0:T(8,128)(2,1)S(1)}, bf16[512,1152]{1,0:T(8,128)(2,1)}, u32[]{:S(2)}) copy-start(bf16[512,1152]{1,0:T(8,128)(2,1)} %get-tuple-element.149) | copy-start | bytes 3538948
  525.5 3.3 collective-permute-start.11
  525.6 30.6 %collective-permute-start.14 = (bf16[512,1152]{1,0:T(8,128)(2,1)}, bf16[512,1152]{1,0:T(8,128)(2,1)S(1)}, u32[]{:S(2)}, u32[]{:S(2)}) collective-permute-start(bf16[512,1152]{1,0:T(8,128)(2,1)} %get-tuple-element.150), channel_id=1, source_target_pairs={{3,2},{2,3},{7,6},{6,7},{11,10},{10,11},{15,14},{14,15},{19,18},{1... | collective-permute-start | bytes 3538952 | tf_op jit(solution)/shard_map/ppermute | solution.py:842
  526.3 31.2 %collective-permute-start.13 = (bf16[512,1152]{1,0:T(8,128)(2,1)}, bf16[512,1152]{1,0:T(8,128)(2,1)S(1)}, u32[]{:S(2)}, u32[]{:S(2)}) collective-permute-start(bf16[512,1152]{1,0:T(8,128)(2,1)} %get-tuple-element.148), channel_id=1, source_target_pairs={{1,0},{3,2},{5,4},{7,6},{9,8},{11,10},{13,12},{15,14},{17,16},{19,... | collective-permute-start | bytes 3538952 | tf_op jit(solution)/shard_map/ppermute | solution.py:842
  528.8 39.0 %copy-start.3 = (f32[512,1152]{1,0:T(8,128)S(1)}, f32[512,1152]{1,0:T(8,128)}, u32[]{:S(2)}) copy-start(f32[512,1152]{1,0:T(8,128)} %get-tuple-element.157.refs_0_) | copy-start | bytes 7077892
  528.8 39.0 %copy-start.7 = (bf16[2,16,1088]{2,1,0:T(8,128)(2,1)S(1)}, bf16[2,16,1088]{2,1,0:T(8,128)(2,1)}, u32[]{:S(2)}) copy-start(bf16[2,16,1088]{2,1,0:T(8,128)(2,1)} %copy-done.6) | copy-start | bytes 208900
  528.9 39.0 %copy-start.14 = (f32[1,1088]{1,0:T(1,128)S(1)}, f32[1,1088]{1,0:T(1,128)}, u32[]{:S(2)}) copy-start(f32[1,1088]{1,0:T(1,128)} %get-tuple-element.248.refs_5_.refs_6_) | copy-start | bytes 13060
  528.9 27.3 %collective-permute-start.12 = (f32[1,16,1152]{2,1,0:T(8,128)S(1)}, f32[1,16,1152]{2,1,0:T(8,128)S(1)}, u32[]{:S(2)}, u32[]{:S(2)}) collective-permute-start(f32[1,16,1152]{2,1,0:T(8,128)S(1)} %slice_select_fusion.1), channel_id=1, source_target_pairs={{0,2},{1,3},{2,0},{3,1},{4,6},{5,7},{6,4},{7,5},{8,10},{9,11},{10,... | collective-permute-start | bytes 221192 | tf_op jit(solution)/shard_map/ppermute | solution.py:877
  557.5 15.5 %copy-start.8 = (bf16[512,1152]{1,0:T(8,128)(2,1)}, bf16[512,1152]{1,0:T(8,128)(2,1)S(1)}, u32[]{:S(2)}) copy-start(bf16[512,1152]{1,0:T(8,128)(2,1)S(1)} %collective-permute-done.13.refs_2_) | copy-start | bytes 3538948
  557.5 6.3 %collective-permute-start.15 = (bf16[1,16,1152]{2,1,0:T(8,128)(2,1)S(1)}, bf16[1,16,1152]{2,1,0:T(8,128)(2,1)S(1)}, u32[]{:S(2)}, u32[]{:S(2)}) collective-permute-start(bf16[1,16,1152]{2,1,0:T(8,128)(2,1)S(1)} %select_add_fusion.3), channel_id=1, source_target_pairs={{0,16},{1,17},{2,18},{3,19},{4,20},{5,21},{6,22},{7,23},{8,24},{9,... | collective-permute-start | bytes 110600 | tf_op jit(solution)/shard_map/ppermute | solution.py:893
  559.7 29.2 %collective-permute-start.19 = (bf16[512,1152]{1,0:T(8,128)(2,1)}, bf16[512,1152]{1,0:T(8,128)(2,1)}, u32[]{:S(2)}, u32[]{:S(2)}) collective-permute-start(bf16[512,1152]{1,0:T(8,128)(2,1)} %add_convert_fusion), channel_id=1, source_target_pairs={{2,0},{3,1},{6,4},{7,5},{10,8},{11,9},{14,12},{15,13},{18,16},{19,... | collective-permute-start | bytes 3538952 | tf_op jit(solution)/shard_map/ppermute | solution.py:842
  563.8 3.7 collective-permute-start.16
  567.5 5.5 collective-permute-start.17
  574.3 14.6 %copy-start.1 = (f32[512,1152]{1,0:T(8,128)S(1)}, f32[512,1152]{1,0:T(8,128)}, u32[]{:S(2)}) copy-start(f32[512,1152]{1,0:T(8,128)} %get-tuple-element.163.refs_1_) | copy-start | bytes 7077892
  581.9 13.8 %collective-permute-start.18 = (bf16[8,16,1152]{2,1,0:T(8,128)(2,1)S(1)}, bf16[8,16,1152]{2,1,0:T(8,128)(2,1)S(1)}, u32[]{:S(2)}, u32[]{:S(2)}) collective-permute-start(bf16[8,16,1152]{2,1,0:T(8,128)(2,1)S(1)} %pad_maximum_fusion.8), channel_id=1, source_target_pairs={{0,2},{1,3},{2,0},{3,1},{4,6},{5,7},{6,4},{7,5},{8,10},{9,11},{10,... | collective-permute-start | bytes 884744 | tf_op jit(solution)/shard_map/ppermute | solution.py:893
  595.8 4.1 collective-permute-start.20
  (27 other events, 75.6 us)
Sparse Core Ops, SparseCore 0:
  12.7 103.3 all-gather.8
  119.6 136.2 all-gather.10
  402.3 85.7 all-gather.12
  490.9 75.4 all-gather.14

commit v6 on v5

--- a/solution.py
+++ b/solution.py
@@ -773,18 +773,15 @@
 
 
 def late_kernel(slot_ref, part_ref, *refs, R, parts, D, W):
-    g_refs, mix_ref, entry_ref, total = refs[:R], refs[R + 1], refs[R + 2], refs[R + 3]
-    total[...] = jnp.zeros_like(total)
+    g_refs, base_ref, mix_ref, entry_ref, total = refs[:R], refs[R], refs[R + 2], refs[R + 3], refs[R + 4]
+    total[...] = base_ref[...]
     count = g_refs[0].shape[0]
     for r in range(R):
 
         def one(i, carry):
             a = slot_ref[r * count + i]
-            if r + 1 < R:
-                total[a] = total[a] + g_refs[r][i].astype(F32)
-            else:
-                c = part_ref[i]
-                total[a, c] = total[a, c] + g_refs[r][i].astype(F32)
+            c = part_ref[i]
+            total[a, c] = total[a, c] + g_refs[r][i].astype(F32)
             return carry
 
         lax.fori_loop(0, count, one, 0)
@@ -794,7 +791,35 @@
     entry_ref[0] = wide[3][:, :, :D]
 
 
-def late_slots(slot, part, gs, entry, D, W):
+def base_kernel(slot_ref, *refs):
+    g_refs, total = refs[:-1], refs[-1]
+    total[...] = jnp.zeros_like(total)
+    count = g_refs[0].shape[0]
+    for r, g_ref in enumerate(g_refs):
+
+        def one(i, carry):
+            a = slot_ref[r * count + i]
+            total[a] = total[a] + g_ref[i].astype(F32)
+            return carry
+
+        lax.fori_loop(0, count, one, 0)
+
+
+def late_base(slot, gs, adapters):
+    shape = (adapters,) + gs[0].shape[1:]
+    return pl.pallas_call(
+        base_kernel,
+        grid_spec=pltpu.PrefetchScalarGridSpec(
+            num_scalar_prefetch=1, grid=(1,), in_specs=[whole_spec(g.shape) for g in gs], out_specs=whole_spec(shape)
+        ),
+        out_shape=jax.ShapeDtypeStruct(shape, F32),
+        compiler_params=pltpu.CompilerParams(vmem_limit_bytes=48 << 20),
+        cost_estimate=pl.CostEstimate(flops=0, bytes_accessed=8 << 20, transcendentals=0),
+        name="late_base",
+    )(slot, *gs)
+
+
+def late_slots(slot, part, gs, base, entry, D, W):
     R = len(gs)
     adapters = entry.shape[1]
     _, rank, width = gs[-1].shape
@@ -804,7 +829,7 @@
         grid_spec=pltpu.PrefetchScalarGridSpec(
             num_scalar_prefetch=2,
             grid=(1,),
-            in_specs=[whole_spec(g.shape) for g in gs] + [pl.BlockSpec(memory_space=pl.ANY)],
+            in_specs=[whole_spec(g.shape) for g in (*gs, base)] + [pl.BlockSpec(memory_space=pl.ANY)],
             out_specs=[
                 whole_spec((adapters, rank, 3 * D)),
                 pl.BlockSpec((1, adapters, rank, D), lambda i, *_: (0, 0, 0, 0)),
@@ -815,11 +840,11 @@
             jax.ShapeDtypeStruct((adapters, rank, 3 * D), F32),
             jax.ShapeDtypeStruct(entry.shape, F32),
         ],
-        input_output_aliases={2 + R: 1},
+        input_output_aliases={3 + R: 1},
         compiler_params=pltpu.CompilerParams(vmem_limit_bytes=60 << 20),
         cost_estimate=pl.CostEstimate(flops=0, bytes_accessed=12 << 20, transcendentals=0),
         name="late_slots",
-    )(slot, part, *gs, entry)
+    )(slot, part, *gs, base, entry)
 
 
 def mm(pattern, a, b):
@@ -1093,20 +1118,21 @@
                 [[[], [(0, D)], [(D, D)]], [[(2 * D, D)], [(3 * D, D)]], [both[0]], [both[1]]],
             )
             early_g = (entry_g, exit_g, expand_g, hidden_g)
-            before = early_g if input_grad is None else (*early_g, input_grad)
+            by_row = all_index.reshape(S, R)
+            slot = jnp.concatenate([jnp.repeat(by_row[:, i], C) for i in range(R - 1)])
+            before = (*early_g, input_grad, late_base(slot, late, adapters))
             last_late, order, beside = gather_all(
                 g[0].astype(BF), S, C, S.bit_length() - 1,
-                [before, lambda done: grad_of(r, done[4] if len(done) > 4 else None)],
+                [before, lambda done: grad_of(r, done[4])],
             )
             entry_g, exit_g, expand_g, hidden_g = beside[0][:4]
+            base = beside[0][5]
             input_grad = beside[1]
             late.append(last_late)
     device = lax.axis_index("seq") * C + me
     order = device ^ jnp.array(order, jnp.int32)
-    by_row = all_index.reshape(S, R)
-    slot = [jnp.repeat(by_row[:, r], C) for r in range(R - 1)]
-    slot.append(jnp.sum(jnp.where((order // C)[:, None] == jnp.arange(S), by_row[:, R - 1], 0), 1))
-    mixing_g, entry_g = late_slots(jnp.concatenate(slot), order % C, late, entry_g, D, W)
+    slot = jnp.sum(jnp.where((order // C)[:, None] == jnp.arange(S), by_row[:, R - 1], 0), 1)
+    mixing_g, entry_g = late_slots(slot, order % C, late[-1:], base, entry_g, D, W)
     input_grad = flip(input_grad).reshape(tokens.shape)
 
     return (

time: 621 us -> 622 us (level)
    unnamed x103 -> x89, local copies, waits for them, and re-layouts: 19.4 us -> 16.3 us
  transfers between devices with their start and end apart: 25 -> 25, of which waited for: 7 -> 9; matrix products, arithmetic and copies ran while one was open for 5% -> 5% of each run, Pallas kernels for 38% -> 39%
where the time goes in v6:
time: 622 us; the launch traced here: 615 us
  Pallas kernels  319 us (51%)
  waiting for transfers between devices  143 us (23%)
  starting transfers between devices  77.2 us (12%)
  local copies, waits for them, and re-layouts  39.3 us (6%)
  between operations  18.7 us (3%)
  other arithmetic  17.9 us (3%)
    ppermute x12, waiting for transfers between devices, swap(): return lax.ppermute(x, axis, [(d ^ bit, d) for d in range(n) if needed(d)])  104 us
    pallas_call x1, Pallas kernels, ffn(): pl.pallas_call(functools.partial(ffn_kernel, R=R, per=per, co=co), grid=(...  76.3 us
    pallas_call x4, Pallas kernels, attn_bwd(): pl.pallas_call(functools.partial(attn_bwd_kernel, L=L, r0=r0, D=D, first=...  72.6 us
    ppermute x4, starting transfers between devices, ctx_sum_stage(): lax.ppermute(jnp.where(mine, low, high), 'ctx', [(d, d ^ bit) for d in ra...  52.4 us
    pallas_call x2, Pallas kernels, project(): pl.pallas_call(functools.partial(project_kernel, W=W, js=tuple(js), r=r),...  42.5 us
    pallas_call x1, Pallas kernels, attn_fwd(): pl.pallas_call(functools.partial(attn_fwd_kernel, L=L), grid_spec=pltpu.P...  40.4 us
    pallas_call x1, Pallas kernels, qkv(): pl.pallas_call(functools.partial(qkv_kernel, W=W, count=count, R=R), grid...  30.5 us
    all_gather x1, waiting for transfers between devices, per_device(): g2 = lax.all_gather(second, BOTH).reshape(S, C, -1, main)  28.4 us
  transfers between devices with their start and end apart: 25, of which 9 were waited for; matrix products, arithmetic and copies ran while one was open for 5% of the time, Pallas kernels for 39%

profile of v6, /device:TPU:5, one launch (start us, length us, event | category | flops | bytes accessed | tf_op | source)
XLA Modules:
  0.0 614.8 jit_solution(12722048888004891046)
XLA Ops:
  15.2 3.1 collective-permute-start
  26.1 1.7 copy-done.6
  27.8 5.1 first_norm.1
  32.9 1.4 collective-permute-start.3
  34.3 2.7 collective-permute-start.4
  39.3 1.4 fusion.28
  44.1 66.5 %collective-permute-done.4.refs_2_ = bf16[2,512,1152]{2,1,0:T(8,128)(2,1)} collective-permute-done((bf16[2,512,1152]{2,1,0:T(8,128)(2,1)}, bf16[2,512,1152]{2,1,0:T(8,128)(2,1)}, u32[]{:S(2)}, u32[]{:S(2)}) %collective-permute-start.4) | collective-permute-done | bytes 2359328 | tf_op jit(solution)/shard_map/ppermute | solution.py:867
  110.6 2.1 collective-permute-start.5
  121.1 2.1 copy.78.ka_ref
  124.0 9.7 %unpack.1 = (bf16[4,2,136,3456]{3,2,1,0:T(8,128)(2,1)}, bf16[4,2,136,1088]{3,2,1,0:T(8,128)(2,1)S(1)}, bf16[4,256,272]{2,1,0:T(8,128)(2,1)S(1)}, bf16[4,64,1088]{2,1,0:T(8,128)(2,1)S(1)}) custom-call(bf16[8,4,152,1088]{3,2,1,0:T(8,128)(2,1)} %bitcast.92), custom_call_target="tpu_custom_call" | custom-call | bytes 21168128 | tf_op jit(solution)/shard_map/unpack/pallas_call | solution.py:379
  133.8 1.5 copy-done.1
  136.1 30.5 %qkv.1 = (bf16[2,512,1152]{2,1,0:T(8,128)(2,1)}, bf16[2,2048,1152]{2,1,0:T(8,128)(2,1)}, bf16[2,2048,1152]{2,1,0:T(8,128)(2,1)}) custom-call(s32[3]{0:T(128)} %pad_add_fusion.1.meta_ref, bf16[2,512,1152]{2,1,0:T(8,128)(2,1)} %get-tuple-element.92.refs_0_, bf16[2,512,1152]{2,1,0:T(8,128)(2,1)} %collective-permute-done.3.refs_1_, ...), custom_call_target="tpu_custom_call" | custom-call | flops 43486543872 | bytes 35831808 | tf_op jit(solution)/shard_map/qkv/pallas_call | solution.py:431
  166.7 40.4 %attn_fwd.1 = (bf16[2,512,1088]{2,1,0:T(8,128)(2,1)S(1)}, bf16[2,9,512,128]{3,2,1,0:T(8,128)(2,1)S(1)}) custom-call(s32[3]{0:T(128)S(1)} %copy-done.21, bf16[2,512,1152]{2,1,0:T(8,128)(2,1)} %get-tuple-element.94.q_ref, bf16[2,2048,1152]{2,1,0:T(8,128)(2,1)} %get-tuple-element.95.k_ref, bf16[2,2048,1152]{2,1,0:T(8,128)(2,1)} %get-tuple-element.96.v_ref, ...), custom_call_target="tpu_custom_call" | custom-call | flops 96636764160 | bytes 23592960 | tf_op jit(solution)/shard_map/attn_fwd/pallas_call | solution.py:131
  207.1 1.4 copy-done.3
  208.5 1.4 copy-done.26
  209.9 13.2 %mid.1 = (f32[2,512,1088]{2,1,0:T(8,128)}, bf16[2,512,1152]{2,1,0:T(8,128)(2,1)S(1)}, bf16[2,512,1152]{2,1,0:T(8,128)(2,1)S(1)}, bf16[2,512,16]{2,1,0:T(8,128)(2,1)S(1)}) custom-call(bf16[2,512,1088]{2,1,0:T(8,128)(2,1)} %copy-done.3, bf16[2,512,1088]{2,1,0:T(8,128)(2,1)} %get-tuple-element.98.x_ref.refs_4_.refs_5_, ...), custom_call_target="tpu_custom_call" | custom-call | flops 2424307712 | bytes 17825792 | tf_op jit(solution)/shard_map/mid/pallas_call | solution.py:479
  223.1 1.6 copy-done.16
  224.7 1.4 copy-done.17
  226.8 28.4 %all-gather.11.cloned.1.call-done = bf16[17408,512]{1,0:T(8,128)(2,1)} async-done(((bf16[544,512]{1,0:T(8,128)(2,1)}), bf16[17408,512]{1,0:T(8,128)(2,1)}) %all-gather.11.cloned.1.call-update) | async-done | bytes 17825808 | tf_op jit(solution)/shard_map/all_gather | solution.py:998
  255.2 76.3 %ffn.1 = (bf16[2,1088,512]{2,1,0:T(8,128)(2,1)}, f32[2,512,1088]{2,1,0:T(8,128)}, bf16[2,512,1088]{2,1,0:T(8,128)(2,1)}, f32[2,16,1088]{2,1,0:T(8,128)}, f32[2,1...) custom-call(bf16[1024,1152]{1,0:T(8,128)(2,1)} %bitcast.89, ...), custom_call_target="tpu_custom_call" | custom-call | flops 77577846784 | bytes 45678592 | tf_op jit(solution)/shard_map/ffn/pallas_call | solution.py:609
  331.6 2.5 concatenate.80
  334.1 1.6 fusion.24
  336.3 16.4 %attn_bwd.4 = (bf16[1,512,1152]{2,1,0:T(8,128)(2,1)S(1)}, bf16[1,2048,1152]{2,1,0:T(8,128)(2,1)}, bf16[1,2048,1152]{2,1,0:T(8,128)(2,1)}) custom-call(s32[3]{0:T(128)S(1)} %copy-done.21, bf16[2,512,1152]{2,1,0:T(8,128)(2,1)S(1)} %copy-done.23, bf16[2,2048,1152]{2,1,0:T(8,128)(2,1)} %get-tuple-element.95.k_ref, ...), custom_call_target="tpu_custom_call" | custom-call | flops 32212254720 | bytes 9961472 | tf_op jit(solution)/shard_map/attn_bwd/pallas_call | solution.py:272
  352.9 29.3 %collective-permute-start.7 = (f32[8,13184]{1,0:T(8,128)S(1)}, f32[8,13184]{1,0:T(8,128)S(1)}, u32[]{:S(2)}, u32[]{:S(2)}) collective-permute-start(f32[8,13184]{1,0:T(8,128)S(1)} %slice_select_fusion), channel_id=1, source_target_pairs={{0,2},{1,3},{2,0},{3,1},{4,6},{5,7},{6,4},{7,5},{8,10},{9,11},{10,... | collective-permute-start | bytes 1265672 | tf_op jit(solution)/shard_map/ppermute | solution.py:902
  382.2 19.8 %attn_bwd.5 = (bf16[1,512,1152]{2,1,0:T(8,128)(2,1)S(1)}, bf16[1,2048,1152]{2,1,0:T(8,128)(2,1)}, bf16[1,2048,1152]{2,1,0:T(8,128)(2,1)}) custom-call(s32[3]{0:T(128)S(1)} %copy-done.21, bf16[2,512,1152]{2,1,0:T(8,128)(2,1)S(1)} %copy-done.23, ...), custom_call_target="tpu_custom_call", output_to_operand_aliasing={{0}: (8, {}), {1}: (9, {}), {2}: (10, {})} | custom-call | flops 40265318400 | bytes 12451840 | tf_op jit(solution)/shard_map/attn_bwd/pallas_call | solution.py:272
  403.1 21.2 %project.2 = (f32[512,1152]{1,0:T(8,128)}, bf16[512,1152]{1,0:T(8,128)(2,1)}, bf16[512,1152]{1,0:T(8,128)(2,1)}, bf16[512,1152]{1,0:T(8,128)(2,1)}, f32[4,16,1152]{2,1,0:T(8,128)}) custom-call(s32[3]{0:T(128)} %pad_add_fusion.1.meta_ref, bf16[1,512,1152]{2,1,0:T(8,128)(2,1)} %copy-done.28, bf16[1,2048,1152]{2,1,0:T(8,128)(2,1)} %get-tuple-element.125.dk_ref, ...), custom_call_target="tpu_custom_call" | custom-call | flops 43486543872 | bytes 26394624 | tf_op jit(solution)/shard_map/project/pallas_call | solution.py:685
  424.4 1.4 collective-permute-start.8
  425.7 1.7 collective-permute-start.9
  427.4 1.7 copy-done.24
  429.1 16.4 %attn_bwd.6 = (bf16[1,512,1152]{2,1,0:T(8,128)(2,1)S(1)}, bf16[1,2048,1152]{2,1,0:T(8,128)(2,1)}, bf16[1,2048,1152]{2,1,0:T(8,128)(2,1)}) custom-call(s32[3]{0:T(128)S(1)} %copy-done.22, bf16[2,512,1152]{2,1,0:T(8,128)(2,1)S(1)} %copy-done.24, bf16[2,2048,1152]{2,1,0:T(8,128)(2,1)} %get-tuple-element.95.k_ref, ...), custom_call_target="tpu_custom_call" | custom-call | flops 32212254720 | bytes 9961472 | tf_op jit(solution)/shard_map/attn_bwd/pallas_call | solution.py:272
  446.2 2.1 add_convert_fusion.1
  449.6 20.0 %attn_bwd.7 = (bf16[1,512,1152]{2,1,0:T(8,128)(2,1)S(1)}, bf16[1,2048,1152]{2,1,0:T(8,128)(2,1)}, bf16[1,2048,1152]{2,1,0:T(8,128)(2,1)}) custom-call(s32[3]{0:T(128)S(1)} %copy-done.22, bf16[2,512,1152]{2,1,0:T(8,128)(2,1)S(1)} %copy-done.25, ...), custom_call_target="tpu_custom_call", output_to_operand_aliasing={{0}: (8, {}), {1}: (9, {}), {2}: (10, {})} | custom-call | flops 40265318400 | bytes 12451840 | tf_op jit(solution)/shard_map/attn_bwd/pallas_call | solution.py:272
  470.7 33.3 %collective-permute-done.10.refs_2_ = bf16[512,1152]{1,0:T(8,128)(2,1)S(1)} collective-permute-done((bf16[512,1152]{1,0:T(8,128)(2,1)S(1)}, bf16[512,1152]{1,0:T(8,128)(2,1)S(1)}, u32[]{:S(2)}, u32[]{:S(2)}) %collective-permute-start.10) | collective-permute-done | bytes 1179680 | tf_op jit(solution)/shard_map/ppermute | solution.py:867
  505.0 21.3 %project.3 = (f32[512,1152]{1,0:T(8,128)}, bf16[512,1152]{1,0:T(8,128)(2,1)}, bf16[512,1152]{1,0:T(8,128)(2,1)}, bf16[512,1152]{1,0:T(8,128)(2,1)}, f32[4,16,1152]{2,1,0:T(8,128)}) custom-call(s32[3]{0:T(128)} %pad_add_fusion.1.meta_ref, bf16[1,512,1152]{2,1,0:T(8,128)(2,1)} %copy-done.27, bf16[1,2048,1152]{2,1,0:T(8,128)(2,1)} %get-tuple-element.145.dk_ref, ...), custom_call_target="tpu_custom_call" | custom-call | flops 43486543872 | bytes 26394624 | tf_op jit(solution)/shard_map/project/pallas_call | solution.py:685
  527.5 2.5 collective-permute-start.13
  530.8 22.7 %collective-permute-start.12 = (f32[1,16,1152]{2,1,0:T(8,128)S(1)}, f32[1,16,1152]{2,1,0:T(8,128)S(1)}, u32[]{:S(2)}, u32[]{:S(2)}) collective-permute-start(f32[1,16,1152]{2,1,0:T(8,128)S(1)} %slice_select_fusion.1), channel_id=1, source_target_pairs={{0,2},{1,3},{2,0},{3,1},{4,6},{5,7},{6,4},{7,5},{8,10},{9,11},{10,... | collective-permute-start | bytes 221192 | tf_op jit(solution)/shard_map/ppermute | solution.py:902
  553.5 2.2 collective-permute-done.12
  557.0 5.5 collective-permute-done.15
  562.6 1.5 collective-permute-start.19
  564.1 1.7 collective-permute-done.16
  566.0 5.2 last.2.refs_0_
  573.0 4.1 late_base.1.refs_1_
  577.0 8.5 %to_slots.1 = (f32[3,8,16,1088]{3,2,1,0:T(8,128)}, f32[2,8,16,1088]{3,2,1,0:T(8,128)}, f32[1,8,16,4352]{3,2,1,0:T(8,128)}, f32[1,8,16,4352]{3,2,1,0:T(8,128)}) custom-call(s32[16]{0:T(128)S(1)} %fusion.22.index_ref, bf16[16,16,13184]{2,1,0:T(8,128)(2,1)} %bitcast.95), custom_call_target="tpu_custom_call" | custom-call | flops 3375104 | bytes 13500416 | tf_op jit(solution)/shard_map/to_slots/pallas_call | solution.py:945
  585.5 1.5 collective-permute-start.18
  587.0 4.4 collective-permute-done.19.refs_3_
  591.4 5.5 last.3
  597.7 2.6 collective-permute-start.20
  603.1 4.9 late_slots.1
  (205 shorter events, 42.8 us)
Async XLA Ops:
  7.2 116.8 %all-gather.9.cloned.1.call-start = ((), (), s32[]{:S(2)}) async-start(), calls=%async_computation | async-start | bytes 11556864 | tf_op jit(solution)/shard_map/all_gather | solution.py:997
  12.6 8.9 %copy-start.35 = (f32[2,1088]{1,0:T(2,128)S(1)}, f32[2,1088]{1,0:T(2,128)}, u32[]{:S(2)}) copy-start(f32[2,1088]{1,0:T(2,128)} %param.22) | copy-start | bytes 26116
  12.6 9.1 %copy-start.34 = (f32[2,1088]{1,0:T(2,128)S(1)}, f32[2,1088]{1,0:T(2,128)}, u32[]{:S(2)}) copy-start(f32[2,1088]{1,0:T(2,128)} %param.23) | copy-start | bytes 26116
  12.6 242.6 %all-gather.11.cloned.1.call-start = ((), (), s32[]{:S(2)}) async-start(), calls=%async_computation.1 | async-start | bytes 18382848 | tf_op jit(solution)/shard_map/all_gather | solution.py:998
  12.9 13.2 %copy-start.5 = (bf16[2,1,512,1088]{2,3,1,0:T(8,128)(2,1)S(1)}, bf16[2,1,512,1088]{2,3,1,0:T(8,128)(2,1)}, u32[]{:S(2)}) copy-start(bf16[2,1,512,1088]{2,3,1,0:T(8,128)(2,1)} %param.19) | copy-start | bytes 6684676
  13.8 557.5 %all-gather.13.cloned.1.call-start = ((), (), s32[]{:S(2)}) async-start(), calls=%async_computation.2 | async-start | bytes 6961152 | tf_op jit(solution)/shard_map/all_gather | solution.py:1084
  13.9 105.8 %collective-permute-start.2 = (s32[2,512]{1,0:T(2,128)S(1)}, s32[2,512]{1,0:T(2,128)S(1)}, u32[]{:S(2)}, u32[]{:S(2)}) collective-permute-start(s32[2,512]{1,0:T(2,128)S(1)} %bitcast.105), channel_id=1, source_target_pairs={{0,1},{2,3},{4,5},{6,7},{8,9},{10,11},{12,13},{14,15},{16,17},{18,... | collective-permute-start | bytes 12296 | tf_op jit(solution)/shard_map/ppermute | solution.py:867
  15.2 98.3 %collective-permute-start = (s32[2,512]{1,0:T(2,128)S(1)}, s32[2,512]{1,0:T(2,128)S(1)}, u32[]{:S(2)}, u32[]{:S(2)}) collective-permute-start(s32[2,512]{1,0:T(2,128)S(1)} %bitcast.106), channel_id=1, source_target_pairs={{0,2},{1,3},{4,6},{5,7},{8,10},{9,11},{12,14},{13,15},{16,18},{17,... | collective-permute-start | bytes 12296 | tf_op jit(solution)/shard_map/ppermute | solution.py:867
  21.5 188.4 %copy-start.15 = (f32[1,1088]{1,0:T(1,128)}, f32[1,1088]{1,0:T(1,128)S(1)}, u32[]{:S(2)}) copy-start(f32[1,1088]{1,0:T(1,128)S(1)} %get-tuple-element.252.gain_ref) | copy-start | bytes 13060
  26.1 183.9 %copy-start.11 = (bf16[2,16,1088]{2,1,0:T(8,128)(2,1)}, bf16[2,16,1088]{2,1,0:T(8,128)(2,1)S(1)}, u32[]{:S(2)}) copy-start(bf16[2,16,1088]{2,1,0:T(8,128)(2,1)S(1)} %get-tuple-element.246.x1_ref) | copy-start | bytes 208900
  26.1 183.9 %copy-start.12 = (bf16[2,16,1088]{2,1,0:T(8,128)(2,1)}, bf16[2,16,1088]{2,1,0:T(8,128)(2,1)S(1)}, u32[]{:S(2)}) copy-start(bf16[2,16,1088]{2,1,0:T(8,128)(2,1)S(1)} %get-tuple-element.247.x0_ref) | copy-start | bytes 208900
  27.8 9.2 %copy-start.33 = (f32[2,1088]{1,0:T(2,128)S(1)}, f32[2,1088]{1,0:T(2,128)}, u32[]{:S(2)}) copy-start(f32[2,1088]{1,0:T(2,128)} %param.24) | copy-start | bytes 26116
  27.8 9.4 %copy-start.32 = (f32[4352]{0:T(1024)S(1)}, f32[4352]{0:T(1024)}, u32[]{:S(2)}) copy-start(f32[4352]{0:T(1024)} %param.25) | copy-start | bytes 52228
  27.8 10.8 %copy-start.36 = (pred[1,1152]{1,0:T(4,128)(4,1)S(1)}, pred[1,1152]{1,0:T(4,128)(4,1)}, u32[]{:S(2)}) copy-start(pred[1,1152]{1,0:T(4,128)(4,1)} %constant.87.clone.1) | copy-start | bytes 3460
  32.9 79.8 %copy-start.39 = (s32[2,1]{0,1:T(1,128)S(1)}, s32[2,1]{0,1:T(1,128)}, u32[]{:S(2)}) copy-start(s32[2,1]{0,1:T(1,128)} %param.21) | copy-start | bytes 28
  32.9 103.2 %collective-permute-start.3 = (bf16[2,512,1152]{2,1,0:T(8,128)(2,1)}, bf16[2,512,1152]{2,1,0:T(8,128)(2,1)}, u32[]{:S(2)}, u32[]{:S(2)}) collective-permute-start(bf16[2,512,1152]{2,1,0:T(8,128)(2,1)} %get-tuple-element.92.refs_0_), channel_id=1, source_target_pairs={{0,1},{2,3},{4,5},{6,7},{8,9},{10,11},{12,13},{14,15},{16,17},{18,... | collective-permute-start | bytes 7077896 | tf_op jit(solution)/shard_map/ppermute | solution.py:867
  34.3 76.3 %collective-permute-start.4 = (bf16[2,512,1152]{2,1,0:T(8,128)(2,1)}, bf16[2,512,1152]{2,1,0:T(8,128)(2,1)}, u32[]{:S(2)}, u32[]{:S(2)}) collective-permute-start(bf16[2,512,1152]{2,1,0:T(8,128)(2,1)} %get-tuple-element.92.refs_0_), channel_id=1, source_target_pairs={{0,2},{1,3},{4,6},{5,7},{8,10},{9,11},{12,14},{13,15},{16,18},{17,... | collective-permute-start | bytes 7077896 | tf_op jit(solution)/shard_map/ppermute | solution.py:867
  110.6 25.5 %collective-permute-start.5 = (bf16[2,512,1152]{2,1,0:T(8,128)(2,1)}, bf16[2,512,1152]{2,1,0:T(8,128)(2,1)}, u32[]{:S(2)}, u32[]{:S(2)}) collective-permute-start(bf16[2,512,1152]{2,1,0:T(8,128)(2,1)} %collective-permute-done.4.refs_2_), channel_id=1, source_target_pairs={{3,2},{2,3},{7,6},{6,7},{11,10},{10,11},{15,14},{14,15},{19,18},{1... | collective-permute-start | bytes 7077896 | tf_op jit(solution)/shard_map/ppermute | solution.py:867
  113.5 6.2 %collective-permute-start.1 = (s32[2,512]{1,0:T(2,128)S(1)}, s32[2,512]{1,0:T(2,128)S(1)}, u32[]{:S(2)}, u32[]{:S(2)}) collective-permute-start(s32[2,512]{1,0:T(2,128)S(1)} %collective-permute-done), channel_id=1, source_target_pairs={{3,2},{2,3},{7,6},{6,7},{11,10},{10,11},{15,14},{14,15},{19,18},{1... | collective-permute-start | bytes 12296 | tf_op jit(solution)/shard_map/ppermute | solution.py:867
  136.1 30.5 %copy-start.19 = (bf16[4,64,1088]{2,1,0:T(8,128)(2,1)}, bf16[4,64,1088]{2,1,0:T(8,128)(2,1)S(1)}, u32[]{:S(2)}) copy-start(bf16[4,64,1088]{2,1,0:T(8,128)(2,1)S(1)} %get-tuple-element.106) | copy-start | bytes 1671172
  136.1 30.5 %copy-start.21 = (s32[3]{0:T(128)S(1)}, s32[3]{0:T(128)}, u32[]{:S(2)}) copy-start(s32[3]{0:T(128)} %pad_add_fusion.1.meta_ref) | copy-start | bytes 40
  166.6 43.3 %copy-start.13 = (bf16[2,16,1088]{2,1,0:T(8,128)(2,1)S(1)}, bf16[2,16,1088]{2,1,0:T(8,128)(2,1)}, u32[]{:S(2)}) copy-start(bf16[2,16,1088]{2,1,0:T(8,128)(2,1)} %get-tuple-element.260.e1_ref) | copy-start | bytes 208900
  166.6 43.3 %copy-start.14 = (bf16[2,16,1088]{2,1,0:T(8,128)(2,1)S(1)}, bf16[2,16,1088]{2,1,0:T(8,128)(2,1)}, u32[]{:S(2)}) copy-start(bf16[2,16,1088]{2,1,0:T(8,128)(2,1)} %get-tuple-element.261.e2_ref) | copy-start | bytes 208900
  255.2 76.3 %copy-start.41 = (f32[2]{0:T(128)S(1)}, f32[2]{0:T(128)}, u32[]{:S(2)}) copy-start(f32[2]{0:T(128)} %multiply_bitcast_fusion) | copy-start | bytes 28
  335.9 16.7 %collective-permute-start.6 = (f32[16,13184]{1,0:T(8,128)S(1)}, f32[16,13184]{1,0:T(8,128)S(1)}, u32[]{:S(2)}, u32[]{:S(2)}) collective-permute-start(f32[16,13184]{1,0:T(8,128)S(1)} %fusion.1), channel_id=1, source_target_pairs={{0,1},{1,0},{2,3},{3,2},{4,5},{5,4},{6,7},{7,6},{8,9},{9,8},{10,11... | collective-permute-start | bytes 2531336 | tf_op jit(solution)/shard_map/ppermute | solution.py:902
  352.9 49.1 %collective-permute-start.7 = (f32[8,13184]{1,0:T(8,128)S(1)}, f32[8,13184]{1,0:T(8,128)S(1)}, u32[]{:S(2)}, u32[]{:S(2)}) collective-permute-start(f32[8,13184]{1,0:T(8,128)S(1)} %slice_select_fusion), channel_id=1, source_target_pairs={{0,2},{1,3},{2,0},{3,1},{4,6},{5,7},{6,4},{7,5},{8,10},{9,11},{10,... | collective-permute-start | bytes 1265672 | tf_op jit(solution)/shard_map/ppermute | solution.py:902
  403.0 170.0 %all-gather.15.cloned.1.call-start = ((), (), s32[]{:S(2)}) async-start(), calls=%async_computation.3 | async-start | bytes 4866048 | tf_op jit(solution)/shard_map/all_gather | solution.py:1099
  403.1 24.3 %copy-start.22 = (s32[3]{0:T(128)S(1)}, s32[3]{0:T(128)}, u32[]{:S(2)}) copy-start(s32[3]{0:T(128)} %pad_add_fusion.1.meta_ref) | copy-start | bytes 40
  424.4 24.0 %collective-permute-start.8 = (bf16[512,1152]{1,0:T(8,128)(2,1)}, bf16[512,1152]{1,0:T(8,128)(2,1)S(1)}, u32[]{:S(2)}, u32[]{:S(2)}) collective-permute-start(bf16[512,1152]{1,0:T(8,128)(2,1)} %get-tuple-element.133), channel_id=1, source_target_pairs={{1,0},{3,2},{5,4},{7,6},{9,8},{11,10},{13,12},{15,14},{17,16},{19,... | collective-permute-start | bytes 3538952 | tf_op jit(solution)/shard_map/ppermute | solution.py:867
  425.7 20.5 %collective-permute-start.9 = (bf16[512,1152]{1,0:T(8,128)(2,1)}, bf16[512,1152]{1,0:T(8,128)(2,1)}, u32[]{:S(2)}, u32[]{:S(2)}) collective-permute-start(bf16[512,1152]{1,0:T(8,128)(2,1)} %get-tuple-element.135), channel_id=1, source_target_pairs={{3,2},{2,3},{7,6},{6,7},{11,10},{10,11},{15,14},{14,15},{19,18},{1... | collective-permute-start | bytes 3538952 | tf_op jit(solution)/shard_map/ppermute | solution.py:867
  429.1 16.4 %copy-start.31 = (f32[4,16,1152]{2,1,0:T(8,128)S(1)}, f32[4,16,1152]{2,1,0:T(8,128)}, u32[]{:S(2)}) copy-start(f32[4,16,1152]{2,1,0:T(8,128)} %get-tuple-element.162) | copy-start | bytes 884740
  448.3 55.6 %collective-permute-start.10 = (bf16[512,1152]{1,0:T(8,128)(2,1)S(1)}, bf16[512,1152]{1,0:T(8,128)(2,1)S(1)}, u32[]{:S(2)}, u32[]{:S(2)}) collective-permute-start(bf16[512,1152]{1,0:T(8,128)(2,1)S(1)} %add_convert_fusion.1), channel_id=1, source_target_pairs={{2,0},{3,1},{6,4},{7,5},{10,8},{11,9},{14,12},{15,13},{18,16},{19,... | collective-permute-start | bytes 3538952 | tf_op jit(solution)/shard_map/ppermute | solution.py:867
  526.2 29.4 %copy-start.29 = (bf16[512,1152]{1,0:T(8,128)(2,1)S(1)}, bf16[512,1152]{1,0:T(8,128)(2,1)}, u32[]{:S(2)}) copy-start(bf16[512,1152]{1,0:T(8,128)(2,1)} %get-tuple-element.150) | copy-start | bytes 3538948
  527.4 3.3 collective-permute-start.11
  527.5 29.5 %collective-permute-start.13 = (bf16[512,1152]{1,0:T(8,128)(2,1)}, bf16[512,1152]{1,0:T(8,128)(2,1)S(1)}, u32[]{:S(2)}, u32[]{:S(2)}) collective-permute-start(bf16[512,1152]{1,0:T(8,128)(2,1)} %get-tuple-element.149), channel_id=1, source_target_pairs={{1,0},{3,2},{5,4},{7,6},{9,8},{11,10},{13,12},{15,14},{17,16},{19,... | collective-permute-start | bytes 3538952 | tf_op jit(solution)/shard_map/ppermute | solution.py:867
  529.9 25.7 %collective-permute-start.14 = (bf16[512,1152]{1,0:T(8,128)(2,1)}, bf16[512,1152]{1,0:T(8,128)(2,1)S(1)}, u32[]{:S(2)}, u32[]{:S(2)}) collective-permute-start(bf16[512,1152]{1,0:T(8,128)(2,1)} %get-tuple-element.151), channel_id=1, source_target_pairs={{3,2},{2,3},{7,6},{6,7},{11,10},{10,11},{15,14},{14,15},{19,18},{1... | collective-permute-start | bytes 3538952 | tf_op jit(solution)/shard_map/ppermute | solution.py:867
  530.7 35.3 %copy-start.4 = (f32[512,1152]{1,0:T(8,128)S(1)}, f32[512,1152]{1,0:T(8,128)}, u32[]{:S(2)}) copy-start(f32[512,1152]{1,0:T(8,128)} %get-tuple-element.158.refs_0_) | copy-start | bytes 7077892
  530.7 35.3 %copy-start.8 = (bf16[2,16,1088]{2,1,0:T(8,128)(2,1)S(1)}, bf16[2,16,1088]{2,1,0:T(8,128)(2,1)}, u32[]{:S(2)}) copy-start(bf16[2,16,1088]{2,1,0:T(8,128)(2,1)} %copy-done.7) | copy-start | bytes 208900
  530.7 35.3 %copy-start.10 = (bf16[512,1152]{1,0:T(8,128)(2,1)S(1)}, bf16[512,1152]{1,0:T(8,128)(2,1)}, u32[]{:S(2)}) copy-start(bf16[512,1152]{1,0:T(8,128)(2,1)} %copy-done.9) | copy-start | bytes 3538948
  530.8 24.9 %collective-permute-start.12 = (f32[1,16,1152]{2,1,0:T(8,128)S(1)}, f32[1,16,1152]{2,1,0:T(8,128)S(1)}, u32[]{:S(2)}, u32[]{:S(2)}) collective-permute-start(f32[1,16,1152]{2,1,0:T(8,128)S(1)} %slice_select_fusion.1), channel_id=1, source_target_pairs={{0,2},{1,3},{2,0},{3,1},{4,6},{5,7},{6,4},{7,5},{8,10},{9,11},{10,... | collective-permute-start | bytes 221192 | tf_op jit(solution)/shard_map/ppermute | solution.py:902
  557.0 5.6 collective-permute-start.15
  562.6 3.3 collective-permute-start.16
  562.6 28.8 %collective-permute-start.19 = (bf16[512,1152]{1,0:T(8,128)(2,1)}, bf16[512,1152]{1,0:T(8,128)(2,1)}, u32[]{:S(2)}, u32[]{:S(2)}) collective-permute-start(bf16[512,1152]{1,0:T(8,128)(2,1)} %add_convert_fusion), channel_id=1, source_target_pairs={{2,0},{3,1},{6,4},{7,5},{10,8},{11,9},{14,12},{15,13},{18,16},{19,... | collective-permute-start | bytes 3538952 | tf_op jit(solution)/shard_map/ppermute | solution.py:867
  565.8 5.4 collective-permute-start.17
  577.0 14.4 %copy-start.2 = (f32[512,1152]{1,0:T(8,128)S(1)}, f32[512,1152]{1,0:T(8,128)}, u32[]{:S(2)}) copy-start(f32[512,1152]{1,0:T(8,128)} %get-tuple-element.165.refs_1_) | copy-start | bytes 7077892
  585.5 14.8 %copy-start.40 = (s32[32]{0:T(128)S(1)}, s32[32]{0:T(128)}, u32[]{:S(2)}) copy-start(s32[32]{0:T(128)} %constant.97.clone) | copy-start | bytes 388
  585.5 12.1 %collective-permute-start.18 = (bf16[8,16,1152]{2,1,0:T(8,128)(2,1)S(1)}, bf16[8,16,1152]{2,1,0:T(8,128)(2,1)S(1)}, u32[]{:S(2)}, u32[]{:S(2)}) collective-permute-start(bf16[8,16,1152]{2,1,0:T(8,128)(2,1)S(1)} %pad_maximum_fusion.8), channel_id=1, source_target_pairs={{0,2},{1,3},{2,0},{3,1},{4,6},{5,7},{6,4},{7,5},{8,10},{9,11},{10,... | collective-permute-start | bytes 884744 | tf_op jit(solution)/shard_map/ppermute | solution.py:918
  597.7 4.3 collective-permute-start.20
  (20 other events, 50.1 us)
Sparse Core Ops, SparseCore 0:
  12.7 102.7 all-gather.8
  118.9 136.1 all-gather.10
  403.1 89.0 all-gather.12
  494.9 69.6 all-gather.14
